TPU v7x, 32 devices: a whole 2x2x4 slice. The times are simulated.
32 devices in a mesh: ctx: 8 (over z, x), tp: 4 (over y, core).
Axes of the slice: x: 2, y: 2, z: 4, core: 2. Of those that a mesh axis runs over, the one named last changes fastest.
Arguments:
- queries: bfloat16 [256, 8192], P('ctx', 'tp'), may hold values from -15 to 15
- new_keys: bfloat16 [256, 1024], P('ctx', 'tp'), may hold values from -6 to 6
- new_values: bfloat16 [256, 1024], P('ctx', 'tp'), may hold values from -6 to 6
- cache_keys: bfloat16 [32768, 1024], P('ctx', 'tp'), may hold values from -6 to 6
- cache_values: bfloat16 [32768, 1024], P('ctx', 'tp'), may hold values from -6 to 6
- keep_tiles: int32 [8, 8, 24], P('ctx', 'tp'), may hold values from 0 to 31, as said below
- tile_count: int32 [8, 8], P('ctx', 'tp'), may hold values from 1 to 24
- owner_slot: int32 [8], replicated, may hold values from 0 to 7, each once
- out_weight: bfloat16 [8192, 8192], P('tp', 'ctx'), may hold values from -0.0625 to 0.0625
Outputs:
- projected_out: float32 [256, 8192], P('tp', 'ctx')
Inputs may be any that keep to these rules, and one draw needn't show every extreme that they name: `keep_tiles`: the 24 entries of each keep list are distinct tile numbers; entries at or past tile_count are ignored.
All inputs are finite; a program needn't handle non-finite values.
Results may differ from a plain program's by a relative error of at most 0.0055.
Values may be sent and summed in bfloat16 or wider, within the bound.
No kernel may reach another device: no remote copies, remote signals or barrier semaphores. Data moves between devices by JAX's collectives and lax.ppermute only.
A program may use at most 128 MiB of HBM per device.

v0:
```python
import functools
import math

import jax
import jax.numpy as jnp
from jax import lax
from jax.experimental import pallas as pl
from jax.experimental.pallas import tpu as pltpu
from jax.sharding import PartitionSpec as P

DH = 128
TILE = 128
LANES = 128
CHUNK = 4
LOW = -1e30
LOW_SIZE = 2
VMEM_ATTN = 24 * 2**20
VMEM_MERGE = 8 * 2**20
VMEM_PROJ = 16 * 2**20


def flipped(me, count, step, flip):
    high = count // LOW_SIZE
    return lax.rem(me // LOW_SIZE + step, high) * LOW_SIZE + lax.rem(me + flip, LOW_SIZE)


def attention_kernel(
    members, ctx_count, group, kv_local, slots, table_ref, new_ref, k_ref, v_ref, *rest
):
    blocks = len(members)
    q_refs, rest = rest[:blocks], rest[blocks:]
    out_refs, rest = rest[:blocks], rest[blocks:]
    q_ref, acc_ref, max_ref = rest
    q_dev = q_refs[0].shape[0]
    heads = kv_local * group
    rows = q_dev * group
    span = CHUNK * TILE
    scale = math.log2(math.e) / math.sqrt(DH)
    me = lax.axis_index("ctx")

    def count_of(g):
        return table_ref[kv_local * slots + g]

    def slot_of(ctx):
        return table_ref[kv_local * (slots + 1) + ctx]

    lane = lax.broadcasted_iota(jnp.int32, (q_dev, LANES), 1)
    ones_new = jnp.ones((q_dev, LANES), jnp.bfloat16)
    ones_tile = jnp.ones((TILE, LANES), jnp.bfloat16)
    place_row = lax.broadcasted_iota(jnp.int32, (rows, q_dev), 0) % q_dev
    place_key = lax.broadcasted_iota(jnp.int32, (rows, q_dev), 1)
    contract_last = (((1,), (1,)), ((), ()))

    for g in range(kv_local):
        cols = slice(g * DH, (g + 1) * DH)
        fresh_keys = new_ref[:, cols]
        fresh_values = jnp.concatenate(
            [new_ref[:, (kv_local + g) * DH : (kv_local + g + 1) * DH], ones_new], 1
        )
        for b in range(blocks):
            for h in range(group):
                head = g * group + h
                q_ref[g, b, h * q_dev : (h + 1) * q_dev, :] = q_refs[b][
                    :, head * DH : (head + 1) * DH
                ]
            s = lax.dot_general(
                q_ref[g, b], fresh_keys, contract_last, preferred_element_type=jnp.float32
            )
            shift = (slot_of(flipped(me, ctx_count, *members[b])) - slot_of(me)) * q_dev
            s = jnp.where(place_row - place_key + shift >= 0, s * scale, LOW)
            top = jnp.broadcast_to(jnp.max(s, axis=1, keepdims=True), (rows, LANES))
            p = jnp.exp2(s - top[:, :q_dev]).astype(jnp.bfloat16)
            max_ref[g, b] = top
            acc_ref[g, b] = jnp.dot(p, fresh_values, preferred_element_type=jnp.float32)

    def load_chunk(g, chunk):
        cols = slice(g * DH, (g + 1) * DH)
        key_parts, value_parts = [], []
        for i in range(CHUNK):
            slot = chunk * CHUNK + i
            live = slot < count_of(g)
            tile = table_ref[g * slots + jnp.where(live, slot, 0)]
            at = pl.ds(pl.multiple_of(tile * TILE, TILE), TILE)
            key_parts.append(k_ref[at, cols])
            tail = jnp.concatenate([v_ref[at, cols], ones_tile], 1)
            value_parts.append(jnp.where(live, tail, jnp.zeros_like(tail)))
        return jnp.concatenate(key_parts, 0), jnp.concatenate(value_parts, 0)

    def run(kv_heads, chunk):
        loaded = {g: load_chunk(g, chunk) for g in kv_heads}
        chains = [(g, b) for b in range(blocks) for g in kv_heads]

        def score(g, b):
            return lax.dot_general(
                q_ref[g, b], loaded[g][0], contract_last, preferred_element_type=jnp.float32
            )

        ahead = score(*chains[0])
        for at, (g, b) in enumerate(chains):
            s = ahead
            if at + 1 < len(chains):
                ahead = score(*chains[at + 1])
            old = max_ref[g, b]
            top = jnp.maximum(old, jnp.max(s, axis=1, keepdims=True) * scale)
            p = jnp.concatenate(
                [
                    jnp.exp2(s[:, j * LANES : (j + 1) * LANES] * scale - top)
                    for j in range(span // LANES)
                ],
                1,
            ).astype(jnp.bfloat16)
            shrink = jnp.exp2(old - top)
            max_ref[g, b] = top
            acc_ref[g, b] = acc_ref[g, b] * jnp.concatenate([shrink, shrink], 1) + jnp.dot(
                p, loaded[g][1], preferred_element_type=jnp.float32
            )

    ends = [(count_of(g) + CHUNK - 1) // CHUNK for g in range(kv_local)]
    shared = functools.reduce(jnp.minimum, ends)

    def step_all(chunk, carry):
        run(range(kv_local), chunk)
        return carry

    lax.fori_loop(0, shared, step_all, 0)
    for g in range(kv_local):

        def step_one(chunk, carry, g=g):
            run([g], chunk)
            return carry

        lax.fori_loop(shared, ends[g], step_one, 0)

    stats = [jnp.zeros((q_dev, LANES), jnp.float32) for _ in range(blocks)]
    for b in range(blocks):
        for g in range(kv_local):
            total = acc_ref[g, b, :, DH:]
            mean = acc_ref[g, b, :, :DH] / total
            level = max_ref[g, b] + jnp.log2(total)
            for h in range(group):
                head = g * group + h
                part = slice(h * q_dev, (h + 1) * q_dev)
                out_refs[b][:, head * DH : (head + 1) * DH] = mean[part].astype(jnp.bfloat16)
                stats[b] = jnp.where(lane % heads == head, level[part], stats[b])

    for b in range(blocks):
        high = stats[b].astype(jnp.bfloat16).astype(jnp.float32)
        middle = (stats[b] - high).astype(jnp.bfloat16).astype(jnp.float32)
        low = stats[b] - high - middle
        packed = jnp.where(lane < heads, high, jnp.where(lane < 2 * heads, middle, low))
        out_refs[b][:, heads * DH :] = packed.astype(jnp.bfloat16)


def attention_call(members, ctx_count, kv_local, slots, blocks, table, new_rows, keys, values):
    n = len(blocks)
    q_dev, width = blocks[0].shape
    group = width // DH // kv_local
    rows = q_dev * group
    smem = pl.BlockSpec(memory_space=pltpu.SMEM)
    vmem = pl.BlockSpec(memory_space=pltpu.VMEM)
    work = n * rows * kv_local * slots * TILE
    return pl.pallas_call(
        functools.partial(attention_kernel, members, ctx_count, group, kv_local, slots),
        out_shape=[jax.ShapeDtypeStruct((q_dev, width + LANES), jnp.bfloat16)] * n,
        in_specs=[smem] + [vmem] * (3 + n),
        out_specs=[vmem] * n,
        scratch_shapes=[
            pltpu.VMEM((kv_local, n, rows, DH), jnp.bfloat16),
            pltpu.VMEM((kv_local, n, rows, DH + LANES), jnp.float32),
            pltpu.VMEM((kv_local, n, rows, LANES), jnp.float32),
        ],
        compiler_params=pltpu.CompilerParams(vmem_limit_bytes=VMEM_ATTN),
        cost_estimate=pl.CostEstimate(
            flops=work * DH * 8, bytes_accessed=8 * 2**20, transcendentals=work
        ),
        name="attention",
    )(table, new_rows, keys, values, *blocks)


def merge_kernel(parts, *refs):
    in_refs, out_ref = refs[:parts], refs[parts]
    width = out_ref.shape[1]
    heads = width // DH
    levels = []
    for ref in in_refs:
        packed = ref[:, width:].astype(jnp.float32)
        levels.append(
            packed
            + pltpu.roll(packed, LANES - heads, 1)
            + pltpu.roll(packed, LANES - 2 * heads, 1)
        )
    top = functools.reduce(jnp.maximum, levels)
    shares = [jnp.exp2(level - top) for level in levels]
    total = functools.reduce(jnp.add, shares)
    shares = [share / total for share in shares]
    for h in range(heads):
        cols = slice(h * DH, (h + 1) * DH)
        mixed = functools.reduce(
            jnp.add,
            [share[:, h : h + 1] * ref[:, cols].astype(jnp.float32) for share, ref in zip(shares, in_refs)],
        )
        out_ref[:, cols] = mixed.astype(jnp.bfloat16)


def merge_call(parts):
    q_dev, wide = parts[0].shape
    vmem = pl.BlockSpec(memory_space=pltpu.VMEM)
    return pl.pallas_call(
        functools.partial(merge_kernel, len(parts)),
        out_shape=jax.ShapeDtypeStruct((q_dev, wide - LANES), jnp.bfloat16),
        in_specs=[vmem] * len(parts),
        out_specs=vmem,
        compiler_params=pltpu.CompilerParams(vmem_limit_bytes=VMEM_MERGE),
        cost_estimate=pl.CostEstimate(
            flops=len(parts) * q_dev * wide * 2,
            bytes_accessed=len(parts) * q_dev * wide * 2,
            transcendentals=0,
        ),
        name="merge",
    )(*parts)


def projection_kernel(members, ctx_count, peers, w_ref, *rest):
    blocks = len(members)
    in_refs, rest = rest[:blocks], rest[blocks:]
    own_ref, send_refs, (rows_ref, sum_ref) = rest[0], rest[1:peers], rest[peers:]
    q_dev = in_refs[0].shape[0]
    me = lax.axis_index("ctx")
    for member, ref in zip(members, in_refs):
        at = flipped(me, ctx_count, *member) * q_dev
        rows_ref[pl.ds(pl.multiple_of(at, q_dev), q_dev), :] = ref[...]
    part = own_ref.shape[0]
    my_tp = lax.axis_index("tp")
    sum_ref[...] = jnp.dot(rows_ref[...], w_ref[...], preferred_element_type=jnp.float32)
    own_ref[...] = sum_ref[pl.ds(pl.multiple_of(my_tp * part, part), part), :]
    for j in range(1, peers):
        at = pl.multiple_of((my_tp ^ j) * part, part)
        send_refs[j - 1][...] = sum_ref[pl.ds(at, part), :].astype(jnp.bfloat16)


def projection_call(members, ctx_count, blocks, weight, peers):
    n = len(blocks)
    q_dev, width = blocks[0].shape
    columns = weight.shape[1]
    part = n * q_dev // peers
    vmem = pl.BlockSpec(memory_space=pltpu.VMEM)
    return pl.pallas_call(
        functools.partial(projection_kernel, members, ctx_count, peers),
        out_shape=[jax.ShapeDtypeStruct((part, columns), jnp.float32)]
        + [jax.ShapeDtypeStruct((part, columns), jnp.bfloat16)] * (peers - 1),
        in_specs=[vmem] * (1 + n),
        out_specs=[vmem] * peers,
        scratch_shapes=[
            pltpu.VMEM((n * q_dev, width), jnp.bfloat16),
            pltpu.VMEM((n * q_dev, columns), jnp.float32),
        ],
        compiler_params=pltpu.CompilerParams(vmem_limit_bytes=VMEM_PROJ),
        cost_estimate=pl.CostEstimate(
            flops=2 * n * q_dev * width * columns,
            bytes_accessed=2 * width * columns,
            transcendentals=0,
        ),
        name="projection",
    )(weight, *blocks)


def body(
    queries,
    new_keys,
    new_values,
    cache_keys,
    cache_values,
    keep_tiles,
    tile_count,
    owner_slot,
    out_weight,
):
    ctx_count = lax.axis_size("ctx")
    peers = lax.axis_size("tp")
    low = LOW_SIZE
    high = ctx_count // low

    def move(x, step, flip):
        pairs = [
            (i, (i // low + step) % high * low + (i % low + flip) % low) for i in range(ctx_count)
        ]
        return lax.ppermute(x, "ctx", pairs)

    steps = sorted(range(1, high), key=lambda k: (min(k, high - k), k))
    order = [(k, 0) for k in (0, *steps)] + [(k, 1) for k in (0, *steps)]

    def gather(x, chained):
        held = {(0, 0): x, (0, 1): move(x, 0, 1)}
        for k in steps:
            held[k, 0] = move(x, -k, 0)
        behind = None
        for k in steps:
            block = held[k, 0]
            if chained and 2 * k == high and behind is not None:
                block, held[behind] = lax.optimization_barrier((block, held[behind]))
            held[k, 1] = move(block, 0, 1)
            behind = (k, 1)
        return held

    held = gather(queries, False)
    near = [m for m in order[1:] if not m[1]]
    far = sorted((m for m in order if m[1]), key=lambda m: -min(m[0], high - m[0]))
    groups = [order[:1]] + [near[i : i + 3] for i in range(0, len(near), 3)]
    groups += [far[i : i + 2] for i in range(0, len(far), 2)]
    kv_local = new_keys.shape[1] // DH
    table = jnp.concatenate([keep_tiles.reshape(-1), tile_count.reshape(-1), owner_slot])
    new_rows = jnp.concatenate([new_keys, new_values], 1)

    def attend(members, blocks):
        return attention_call(
            members,
            ctx_count,
            kv_local,
            keep_tiles.shape[2],
            blocks,
            table,
            new_rows,
            cache_keys,
            cache_values,
        )

    parts, back = {}, {}
    last = None
    for index, members in enumerate(groups):
        blocks = [held[m] for m in members]
        if last is not None:
            blocks, parts[last] = lax.optimization_barrier((blocks, parts[last]))
        if index >= 3:
            returned = {m: back[m] for m in groups[index - 2] if 2 * m[0] != high}
            blocks, returned = lax.optimization_barrier((blocks, returned))
            back.update(returned)
        parts.update(zip(members, attend(members, blocks)))
        last = members[-1]
        for m in members:
            back[m] = parts[m] if m == (0, 0) else move(parts[m], *m)
    attn = merge_call([back[m] for m in order])

    held = gather(attn, True)
    own, *sends = projection_call(order, ctx_count, [held[m] for m in order], out_weight, peers)
    for j, piece in enumerate(sends, 1):
        got = lax.ppermute(piece, "tp", [(i, i ^ j) for i in range(peers)])
        own = own + got.astype(jnp.float32)
    return own


def solution(mesh):
    return jax.shard_map(
        body,
        mesh=mesh,
        in_specs=(
            P("ctx", "tp"),
            P("ctx", "tp"),
            P("ctx", "tp"),
            P("ctx", "tp"),
            P("ctx", "tp"),
            P("ctx", "tp", None),
            P("ctx", "tp"),
            P(),
            P("tp", "ctx"),
        ),
        out_specs=P("tp", "ctx"),
        check_vma=False,
    )
```

profile of v0, /device:TPU:0, one launch (start us, length us, event | category | flops | bytes accessed | tf_op | source)
XLA Modules:
  0.0 89.7 jit_solution(14493128575641178436)
XLA Ops:
  0.0 2.9 %collective-permute-start.2 = (bf16[32,2048]{1,0:T(8,128)(2,1)}, bf16[32,2048]{1,0:T(8,128)(2,1)S(1)}, u32[]{:S(2)}, u32[]{:S(2)}) collective-permute-start(bf16[32,2048]{1,0:T(8,128)(2,1)} %rest_0_.1), channel_id=1, source_target_pairs={{0,4},{4,0},{8,12},{12,8},{16,20},{20,16},{24,28},{28,24},{1,5},{5... | collective-permute-start | bytes 393224 | tf_op jit(solution)/shard_map/ppermute | solution.py:287
  2.9 1.6 %collective-permute-start = (bf16[32,2048]{1,0:T(8,128)(2,1)}, bf16[32,2048]{1,0:T(8,128)(2,1)S(1)}, u32[]{:S(2)}, u32[]{:S(2)}) collective-permute-start(bf16[32,2048]{1,0:T(8,128)(2,1)} %rest_0_.1), channel_id=1, source_target_pairs={{0,8},{4,12},{8,16},{12,20},{16,24},{20,28},{24,0},{28,4},{1,9},{5... | collective-permute-start | bytes 393224 | tf_op jit(solution)/shard_map/ppermute | solution.py:287
  4.5 2.2 %collective-permute-start.5 = (bf16[32,2048]{1,0:T(8,128)(2,1)}, bf16[32,2048]{1,0:T(8,128)(2,1)S(1)}, u32[]{:S(2)}, u32[]{:S(2)}) collective-permute-start(bf16[32,2048]{1,0:T(8,128)(2,1)} %rest_0_.1), channel_id=1, source_target_pairs={{0,24},{4,28},{8,0},{12,4},{16,8},{20,12},{24,16},{28,20},{1,25},{... | collective-permute-start | bytes 393224 | tf_op jit(solution)/shard_map/ppermute | solution.py:287
  6.8 0.8 collective-permute-start.3
  7.6 0.8 reshape.6
  8.3 0.7 constant_dynamic-update-slice_fusion.1
  9.0 0.7 constant_dynamic-update-slice_fusion.new_ref
  9.8 0.7 pad_add_fusion.table_ref
  10.5 0.0 copy-start.1
  10.5 1.6 %copy-done.1 = bf16[4096,256]{1,0:T(8,128)(2,1)S(1)} copy-done((bf16[4096,256]{1,0:T(8,128)(2,1)S(1)}, bf16[4096,256]{1,0:T(8,128)(2,1)}, u32[]{:S(2)}) %copy-start.1) | copy-done | bytes 2097176
  12.1 1.6 %copy-done.2 = bf16[4096,256]{1,0:T(8,128)(2,1)S(1)} copy-done((bf16[4096,256]{1,0:T(8,128)(2,1)S(1)}, bf16[4096,256]{1,0:T(8,128)(2,1)}, u32[]{:S(2)}) %copy-start.2) | copy-done | bytes 2097176
  13.7 0.9 %copy-done.3 = bf16[32,2048]{1,0:T(8,128)(2,1)S(1)} copy-done((bf16[32,2048]{1,0:T(8,128)(2,1)S(1)}, bf16[32,2048]{1,0:T(8,128)(2,1)}, u32[]{:S(2)}) %copy-start.3) | copy-done | bytes 131096
  14.6 3.1 %attention.4.refs_0_ = bf16[32,2176]{1,0:T(8,128)(2,1)S(1)} custom-call(s32[58]{0:T(128)S(1)} %pad_add_fusion.table_ref, bf16[32,512]{1,0:T(8,128)(2,1)S(1)} %constant_dynamic-update-slice_fusion.new_ref, bf16[4096,256]{1,0:T(8,128)(2,1)S(1)} %copy-done.1, bf16[4096,256]{1,0:T(8,128)(2,1)S(1)} %copy-done.2, bf16[32,2048]{1,0:T(8,128)(2,1)S(1)} %copy-done.3), custom_call_target="tpu_custom_call" | custom-call | flops 1610612736 | bytes 8388608 | tf_op jit(solution)/shard_map/attention/pallas_call | solution.py:162
  17.7 0.0 collective-permute-done.rest_1_
  17.7 0.0 collective-permute-done.5.rest_0_
  17.7 0.7 collective-permute-done.3.rest_2_
  18.4 1.0 %collective-permute-start.6 = (bf16[32,2048]{1,0:T(8,128)(2,1)S(1)}, bf16[32,2048]{1,0:T(8,128)(2,1)S(1)}, u32[]{:S(2)}, u32[]{:S(2)}) collective-permute-start(bf16[32,2048]{1,0:T(8,128)(2,1)S(1)} %collective-permute-done.5.rest_0_), channel_id=1, source_target_pairs={{0,4},{4,0},{8,12},{12,8},{16,20},{20,16},{24,28},{28,24},{1,5},{5... | collective-permute-start | bytes 393224 | tf_op jit(solution)/shard_map/ppermute | solution.py:287
  19.5 1.0 %collective-permute-start.4 = (bf16[32,2048]{1,0:T(8,128)(2,1)S(1)}, bf16[32,2048]{1,0:T(8,128)(2,1)S(1)}, u32[]{:S(2)}, u32[]{:S(2)}) collective-permute-start(bf16[32,2048]{1,0:T(8,128)(2,1)S(1)} %collective-permute-done.3.rest_2_), channel_id=1, source_target_pairs={{0,4},{4,0},{8,12},{12,8},{16,20},{20,16},{24,28},{28,24},{1,5},{5... | collective-permute-start | bytes 393224 | tf_op jit(solution)/shard_map/ppermute | solution.py:287
  20.5 6.2 %attention.5 = (bf16[32,2176]{1,0:T(8,128)(2,1)S(1)}, bf16[32,2176]{1,0:T(8,128)(2,1)S(1)}, bf16[32,2176]{1,0:T(8,128)(2,1)S(1)}) custom-call(s32[58]{0:T(128)S(1)} %pad_add_fusion.table_ref, bf16[32,512]{1,0:T(8,128)(2,1)S(1)} %constant_dynamic-update-slice_fusion.new_ref, bf16[4096,256]{1,0:T(8,128)(2,1)S(1)} %copy-done.1, ...), custom_call_target="tpu_custom_call" | custom-call | flops 4831838208 | bytes 8388608 | tf_op jit(solution)/shard_map/attention/pallas_call | solution.py:162
  26.7 2.4 %collective-permute-start.7 = (bf16[32,2176]{1,0:T(8,128)(2,1)S(1)}, bf16[32,2176]{1,0:T(8,128)(2,1)S(1)}, u32[]{:S(2)}, u32[]{:S(2)}) collective-permute-start(bf16[32,2176]{1,0:T(8,128)(2,1)S(1)} %get-tuple-element.38), channel_id=1, source_target_pairs={{0,8},{4,12},{8,16},{12,20},{16,24},{20,28},{24,0},{28,4},{1,9},{5... | collective-permute-start | bytes 417800 | tf_op jit(solution)/shard_map/ppermute | solution.py:287
  29.0 1.5 %collective-permute-start.8 = (bf16[32,2176]{1,0:T(8,128)(2,1)S(1)}, bf16[32,2176]{1,0:T(8,128)(2,1)S(1)}, u32[]{:S(2)}, u32[]{:S(2)}) collective-permute-start(bf16[32,2176]{1,0:T(8,128)(2,1)S(1)} %get-tuple-element.39), channel_id=1, source_target_pairs={{0,24},{4,28},{8,0},{12,4},{16,8},{20,12},{24,16},{28,20},{1,25},{... | collective-permute-start | bytes 417800 | tf_op jit(solution)/shard_map/ppermute | solution.py:287
  30.5 0.0 collective-permute-done.6.rest_1_
  30.5 2.4 %collective-permute-start.9 = (bf16[32,2176]{1,0:T(8,128)(2,1)S(1)}, bf16[32,2176]{1,0:T(8,128)(2,1)S(1)}, u32[]{:S(2)}, u32[]{:S(2)}) collective-permute-start(bf16[32,2176]{1,0:T(8,128)(2,1)S(1)} %get-tuple-element.32), channel_id=1, source_target_pairs={{0,16},{4,20},{8,24},{12,28},{16,0},{20,4},{24,8},{28,12},{1,17},{... | collective-permute-start | bytes 417800 | tf_op jit(solution)/shard_map/ppermute | solution.py:287
  33.0 0.0 collective-permute-done.4.rest_0_
  33.0 1.5 %collective-permute-start.1 = (bf16[32,2048]{1,0:T(8,128)(2,1)S(1)}, bf16[32,2048]{1,0:T(8,128)(2,1)S(1)}, u32[]{:S(2)}, u32[]{:S(2)}) collective-permute-start(bf16[32,2048]{1,0:T(8,128)(2,1)S(1)} %collective-permute-done.rest_1_), channel_id=1, source_target_pairs={{0,4},{4,0},{8,12},{12,8},{16,20},{20,16},{24,28},{28,24},{1,5},{5... | collective-permute-start | bytes 393224 | tf_op jit(solution)/shard_map/ppermute | solution.py:287
  34.5 4.6 %attention.6 = (bf16[32,2176]{1,0:T(8,128)(2,1)S(1)}, bf16[32,2176]{1,0:T(8,128)(2,1)S(1)}) custom-call(s32[58]{0:T(128)S(1)} %pad_add_fusion.table_ref, bf16[32,512]{1,0:T(8,128)(2,1)S(1)} %constant_dynamic-update-slice_fusion.new_ref, bf16[4096,256]{1,0:T(8,128)(2,1)S(1)} %copy-done.1, bf16[4096,256]{1,0:T(8,128)(2,1)S(1)} %copy-done.2, ...), custom_call_target="tpu_custom_call" | custom-call | flops 3221225472 | bytes 8388608 | tf_op jit(solution)/shard_map/attention/pallas_call | solution.py:162
  39.1 0.0 collective-permute-done.2.rest_1_
  39.1 2.3 %collective-permute-start.11 = (bf16[32,2176]{1,0:T(8,128)(2,1)S(1)}, bf16[32,2176]{1,0:T(8,128)(2,1)S(1)}, u32[]{:S(2)}, u32[]{:S(2)}) collective-permute-start(bf16[32,2176]{1,0:T(8,128)(2,1)S(1)} %get-tuple-element.35), channel_id=1, source_target_pairs={{0,12},{4,8},{8,20},{12,16},{16,28},{20,24},{24,4},{28,0},{1,13},{... | collective-permute-start | bytes 417800 | tf_op jit(solution)/shard_map/ppermute | solution.py:287
  41.5 0.0 collective-permute-done.1.rest_0_
  41.5 3.3 %collective-permute-start.13 = (bf16[32,2176]{1,0:T(8,128)(2,1)S(1)}, bf16[32,2176]{1,0:T(8,128)(2,1)S(1)}, u32[]{:S(2)}, u32[]{:S(2)}) collective-permute-start(bf16[32,2176]{1,0:T(8,128)(2,1)S(1)} %get-tuple-element.46), channel_id=1, source_target_pairs={{0,20},{4,16},{8,28},{12,24},{16,4},{20,0},{24,12},{28,8},{1,21},{... | collective-permute-start | bytes 417800 | tf_op jit(solution)/shard_map/ppermute | solution.py:287
  44.7 0.0 collective-permute-done.7.refs_1_
  44.8 0.0 collective-permute-done.8.refs_2_
  44.8 4.7 %attention.7 = (bf16[32,2176]{1,0:T(8,128)(2,1)S(1)}, bf16[32,2176]{1,0:T(8,128)(2,1)S(1)}) custom-call(s32[58]{0:T(128)S(1)} %pad_add_fusion.table_ref, bf16[32,512]{1,0:T(8,128)(2,1)S(1)} %constant_dynamic-update-slice_fusion.new_ref, bf16[4096,256]{1,0:T(8,128)(2,1)S(1)} %copy-done.1, bf16[4096,256]{1,0:T(8,128)(2,1)S(1)} %copy-done.2, ...), custom_call_target="tpu_custom_call" | custom-call | flops 3221225472 | bytes 8388608 | tf_op jit(solution)/shard_map/attention/pallas_call | solution.py:162
  49.4 0.1 collective-permute-start.10
  49.6 3.7 %collective-permute-start.12 = (bf16[32,2176]{1,0:T(8,128)(2,1)S(1)}, bf16[32,2176]{1,0:T(8,128)(2,1)S(1)}, u32[]{:S(2)}, u32[]{:S(2)}) collective-permute-start(bf16[32,2176]{1,0:T(8,128)(2,1)S(1)} %get-tuple-element.45), channel_id=1, source_target_pairs={{0,28},{4,24},{8,4},{12,0},{16,12},{20,8},{24,20},{28,16},{1,29},{... | collective-permute-start | bytes 417800 | tf_op jit(solution)/shard_map/ppermute | solution.py:287
  53.3 0.0 collective-permute-done.9.refs_3_
  53.3 0.0 collective-permute-done.13.refs_7_
  53.3 0.0 collective-permute-done.11.refs_5_
  53.3 4.9 %collective-permute-done.10.refs_4_ = bf16[32,2176]{1,0:T(8,128)(2,1)S(1)} collective-permute-done((bf16[32,2176]{1,0:T(8,128)(2,1)S(1)}, bf16[32,2176]{1,0:T(8,128)(2,1)S(1)}, u32[]{:S(2)}, u32[]{:S(2)}) %collective-permute-start.10) | collective-permute-done | bytes 139296 | tf_op jit(solution)/shard_map/ppermute | solution.py:287
  58.2 0.0 collective-permute-done.12.refs_6_
  58.2 0.8 merge.1.rest_0_
  59.0 1.0 %collective-permute-start.15 = (bf16[32,2048]{1,0:T(8,128)(2,1)S(1)}, bf16[32,2048]{1,0:T(8,128)(2,1)S(1)}, u32[]{:S(2)}, u32[]{:S(2)}) collective-permute-start(bf16[32,2048]{1,0:T(8,128)(2,1)S(1)} %merge.1.rest_0_), channel_id=1, source_target_pairs={{0,8},{4,12},{8,16},{12,20},{16,24},{20,28},{24,0},{28,4},{1,9},{5... | collective-permute-start | bytes 393224 | tf_op jit(solution)/shard_map/ppermute | solution.py:287
  60.0 2.9 %collective-permute-start.14 = (bf16[32,2048]{1,0:T(8,128)(2,1)S(1)}, bf16[32,2048]{1,0:T(8,128)(2,1)S(1)}, u32[]{:S(2)}, u32[]{:S(2)}) collective-permute-start(bf16[32,2048]{1,0:T(8,128)(2,1)S(1)} %merge.1.rest_0_), channel_id=1, source_target_pairs={{0,24},{4,28},{8,0},{12,4},{16,8},{20,12},{24,16},{28,20},{1,25},{... | collective-permute-start | bytes 393224 | tf_op jit(solution)/shard_map/ppermute | solution.py:287
  62.9 0.0 collective-permute-start.16
  62.9 4.3 %collective-permute-done.15.rest_2_ = bf16[32,2048]{1,0:T(8,128)(2,1)S(1)} collective-permute-done((bf16[32,2048]{1,0:T(8,128)(2,1)S(1)}, bf16[32,2048]{1,0:T(8,128)(2,1)S(1)}, u32[]{:S(2)}, u32[]{:S(2)}) %collective-permute-start.15) | collective-permute-done | bytes 131104 | tf_op jit(solution)/shard_map/ppermute | solution.py:287
  67.2 1.7 %collective-permute-start.19 = (bf16[32,2048]{1,0:T(8,128)(2,1)S(1)}, bf16[32,2048]{1,0:T(8,128)(2,1)S(1)}, u32[]{:S(2)}, u32[]{:S(2)}) collective-permute-start(bf16[32,2048]{1,0:T(8,128)(2,1)S(1)} %collective-permute-done.15.rest_2_), channel_id=1, source_target_pairs={{0,4},{4,0},{8,12},{12,8},{16,20},{20,16},{24,28},{28,24},{1,5},{5... | collective-permute-start | bytes 393224 | tf_op jit(solution)/shard_map/ppermute | solution.py:287
  68.9 0.4 collective-permute-start.17
  69.3 0.0 collective-permute-done.14.rest_1_
  69.3 1.7 %collective-permute-start.18 = (bf16[32,2048]{1,0:T(8,128)(2,1)S(1)}, bf16[32,2048]{1,0:T(8,128)(2,1)S(1)}, u32[]{:S(2)}, u32[]{:S(2)}) collective-permute-start(bf16[32,2048]{1,0:T(8,128)(2,1)S(1)} %collective-permute-done.14.rest_1_), channel_id=1, source_target_pairs={{0,4},{4,0},{8,12},{12,8},{16,20},{20,16},{24,28},{28,24},{1,5},{5... | collective-permute-start | bytes 393224 | tf_op jit(solution)/shard_map/ppermute | solution.py:287
  71.0 2.2 %collective-permute-done.16.rest_3_ = bf16[32,2048]{1,0:T(8,128)(2,1)S(1)} collective-permute-done((bf16[32,2048]{1,0:T(8,128)(2,1)S(1)}, bf16[32,2048]{1,0:T(8,128)(2,1)S(1)}, u32[]{:S(2)}, u32[]{:S(2)}) %collective-permute-start.16) | collective-permute-done | bytes 131104 | tf_op jit(solution)/shard_map/ppermute | solution.py:287
  73.1 0.4 collective-permute-done.19.rest_6_
  73.5 0.8 collective-permute-start.20
  74.3 0.6 collective-permute-done.17.rest_4_
  74.9 2.8 %collective-permute-done.18.rest_5_ = bf16[32,2048]{1,0:T(8,128)(2,1)S(1)} collective-permute-done((bf16[32,2048]{1,0:T(8,128)(2,1)S(1)}, bf16[32,2048]{1,0:T(8,128)(2,1)S(1)}, u32[]{:S(2)}, u32[]{:S(2)}) %collective-permute-start.18) | collective-permute-done | bytes 131104 | tf_op jit(solution)/shard_map/ppermute | solution.py:287
  77.7 1.4 %collective-permute-done.20.rest_7_ = bf16[32,2048]{1,0:T(8,128)(2,1)S(1)} collective-permute-done((bf16[32,2048]{1,0:T(8,128)(2,1)S(1)}, bf16[32,2048]{1,0:T(8,128)(2,1)S(1)}, u32[]{:S(2)}, u32[]{:S(2)}) %collective-permute-start.20) | collective-permute-done | bytes 131104 | tf_op jit(solution)/shard_map/ppermute | solution.py:287
  79.2 0.0 copy-done
  79.2 1.4 %projection.1 = (f32[64,1024]{1,0:T(8,128)S(1)}, bf16[64,1024]{1,0:T(8,128)(2,1)S(1)}, bf16[64,1024]{1,0:T(8,128)(2,1)S(1)}, bf16[64,1024]{1,0:T(8,128)(2,1)S(1)}) custom-call(bf16[2048,1024]{1,0:T(8,128)(2,1)S(1)} %copy-done, bf16[32,2048]{1,0:T(8,128)(2,1)S(1)} %merge.1.rest_0_, bf16[32,2048]{1,0:T(8,128)(2,1)S(1)} %collective-permute-done.14.rest_1_, ...), custom_call_target="tpu_custom_call" | custom-call | flops 1073741824 | bytes 4194304 | tf_op jit(solution)/shard_map/projection/pallas_call | solution.py:247
  80.6 0.1 collective-permute-start.21
  80.6 0.1 collective-permute-start.22
  80.7 1.8 %collective-permute-start.23 = (bf16[64,1024]{1,0:T(8,128)(2,1)S(1)}, bf16[64,1024]{1,0:T(8,128)(2,1)S(1)}, u32[]{:S(2)}, u32[]{:S(2)}) collective-permute-start(bf16[64,1024]{1,0:T(8,128)(2,1)S(1)} %get-tuple-element.52), channel_id=1, source_target_pairs={{0,3},{1,2},{2,1},{3,0},{4,7},{5,6},{6,5},{7,4},{8,11},{9,10},{10,... | collective-permute-start | bytes 393224 | tf_op jit(solution)/shard_map/ppermute | solution.py:346
  82.5 0.0 collective-permute-done.21
  82.5 4.5 %collective-permute-done.22 = bf16[64,1024]{1,0:T(8,128)(2,1)S(1)} collective-permute-done((bf16[64,1024]{1,0:T(8,128)(2,1)S(1)}, bf16[64,1024]{1,0:T(8,128)(2,1)S(1)}, u32[]{:S(2)}, u32[]{:S(2)}) %collective-permute-start.22) | collective-permute-done | bytes 131104 | tf_op jit(solution)/shard_map/ppermute | solution.py:346
  87.0 1.9 %collective-permute-done.23 = bf16[64,1024]{1,0:T(8,128)(2,1)S(1)} collective-permute-done((bf16[64,1024]{1,0:T(8,128)(2,1)S(1)}, bf16[64,1024]{1,0:T(8,128)(2,1)S(1)}, u32[]{:S(2)}, u32[]{:S(2)}) %collective-permute-start.23) | collective-permute-done | bytes 131104 | tf_op jit(solution)/shard_map/ppermute | solution.py:346
  88.9 0.8 convert_add_fusion
  (3 shorter events, 0.0 us)
Async XLA Ops:
  0.0 39.1 %collective-permute-start.2 = (bf16[32,2048]{1,0:T(8,128)(2,1)}, bf16[32,2048]{1,0:T(8,128)(2,1)S(1)}, u32[]{:S(2)}, u32[]{:S(2)}) collective-permute-start(bf16[32,2048]{1,0:T(8,128)(2,1)} %rest_0_.1), channel_id=1, source_target_pairs={{0,4},{4,0},{8,12},{12,8},{16,20},{20,16},{24,28},{28,24},{1,5},{5... | collective-permute-start | bytes 393224 | tf_op jit(solution)/shard_map/ppermute | solution.py:287
  2.9 14.8 %collective-permute-start = (bf16[32,2048]{1,0:T(8,128)(2,1)}, bf16[32,2048]{1,0:T(8,128)(2,1)S(1)}, u32[]{:S(2)}, u32[]{:S(2)}) collective-permute-start(bf16[32,2048]{1,0:T(8,128)(2,1)} %rest_0_.1), channel_id=1, source_target_pairs={{0,8},{4,12},{8,16},{12,20},{16,24},{20,28},{24,0},{28,4},{1,9},{5... | collective-permute-start | bytes 393224 | tf_op jit(solution)/shard_map/ppermute | solution.py:287
  4.5 13.2 %collective-permute-start.5 = (bf16[32,2048]{1,0:T(8,128)(2,1)}, bf16[32,2048]{1,0:T(8,128)(2,1)S(1)}, u32[]{:S(2)}, u32[]{:S(2)}) collective-permute-start(bf16[32,2048]{1,0:T(8,128)(2,1)} %rest_0_.1), channel_id=1, source_target_pairs={{0,24},{4,28},{8,0},{12,4},{16,8},{20,12},{24,16},{28,20},{1,25},{... | collective-permute-start | bytes 393224 | tf_op jit(solution)/shard_map/ppermute | solution.py:287
  6.8 11.7 %collective-permute-start.3 = (bf16[32,2048]{1,0:T(8,128)(2,1)}, bf16[32,2048]{1,0:T(8,128)(2,1)S(1)}, u32[]{:S(2)}, u32[]{:S(2)}) collective-permute-start(bf16[32,2048]{1,0:T(8,128)(2,1)} %rest_0_.1), channel_id=1, source_target_pairs={{0,16},{4,20},{8,24},{12,28},{16,0},{20,4},{24,8},{28,12},{1,17},{... | collective-permute-start | bytes 393224 | tf_op jit(solution)/shard_map/ppermute | solution.py:287
  10.5 1.6 %copy-start.1 = (bf16[4096,256]{1,0:T(8,128)(2,1)S(1)}, bf16[4096,256]{1,0:T(8,128)(2,1)}, u32[]{:S(2)}) copy-start(bf16[4096,256]{1,0:T(8,128)(2,1)} %k_ref.7) | copy-start | bytes 6291460
  12.1 1.6 %copy-start.2 = (bf16[4096,256]{1,0:T(8,128)(2,1)S(1)}, bf16[4096,256]{1,0:T(8,128)(2,1)}, u32[]{:S(2)}) copy-start(bf16[4096,256]{1,0:T(8,128)(2,1)} %v_ref.7) | copy-start | bytes 6291460
  13.7 0.9 %copy-start.3 = (bf16[32,2048]{1,0:T(8,128)(2,1)S(1)}, bf16[32,2048]{1,0:T(8,128)(2,1)}, u32[]{:S(2)}) copy-start(bf16[32,2048]{1,0:T(8,128)(2,1)} %rest_0_.1) | copy-start | bytes 393220
  18.4 12.1 %collective-permute-start.6 = (bf16[32,2048]{1,0:T(8,128)(2,1)S(1)}, bf16[32,2048]{1,0:T(8,128)(2,1)S(1)}, u32[]{:S(2)}, u32[]{:S(2)}) collective-permute-start(bf16[32,2048]{1,0:T(8,128)(2,1)S(1)} %collective-permute-done.5.rest_0_), channel_id=1, source_target_pairs={{0,4},{4,0},{8,12},{12,8},{16,20},{20,16},{24,28},{28,24},{1,5},{5... | collective-permute-start | bytes 393224 | tf_op jit(solution)/shard_map/ppermute | solution.py:287
  19.5 13.5 %collective-permute-start.4 = (bf16[32,2048]{1,0:T(8,128)(2,1)S(1)}, bf16[32,2048]{1,0:T(8,128)(2,1)S(1)}, u32[]{:S(2)}, u32[]{:S(2)}) collective-permute-start(bf16[32,2048]{1,0:T(8,128)(2,1)S(1)} %collective-permute-done.3.rest_2_), channel_id=1, source_target_pairs={{0,4},{4,0},{8,12},{12,8},{16,20},{20,16},{24,28},{28,24},{1,5},{5... | collective-permute-start | bytes 393224 | tf_op jit(solution)/shard_map/ppermute | solution.py:287
  26.7 18.1 %collective-permute-start.7 = (bf16[32,2176]{1,0:T(8,128)(2,1)S(1)}, bf16[32,2176]{1,0:T(8,128)(2,1)S(1)}, u32[]{:S(2)}, u32[]{:S(2)}) collective-permute-start(bf16[32,2176]{1,0:T(8,128)(2,1)S(1)} %get-tuple-element.38), channel_id=1, source_target_pairs={{0,8},{4,12},{8,16},{12,20},{16,24},{20,28},{24,0},{28,4},{1,9},{5... | collective-permute-start | bytes 417800 | tf_op jit(solution)/shard_map/ppermute | solution.py:287
  29.0 15.7 %collective-permute-start.8 = (bf16[32,2176]{1,0:T(8,128)(2,1)S(1)}, bf16[32,2176]{1,0:T(8,128)(2,1)S(1)}, u32[]{:S(2)}, u32[]{:S(2)}) collective-permute-start(bf16[32,2176]{1,0:T(8,128)(2,1)S(1)} %get-tuple-element.39), channel_id=1, source_target_pairs={{0,24},{4,28},{8,0},{12,4},{16,8},{20,12},{24,16},{28,20},{1,25},{... | collective-permute-start | bytes 417800 | tf_op jit(solution)/shard_map/ppermute | solution.py:287
  30.5 22.8 %collective-permute-start.9 = (bf16[32,2176]{1,0:T(8,128)(2,1)S(1)}, bf16[32,2176]{1,0:T(8,128)(2,1)S(1)}, u32[]{:S(2)}, u32[]{:S(2)}) collective-permute-start(bf16[32,2176]{1,0:T(8,128)(2,1)S(1)} %get-tuple-element.32), channel_id=1, source_target_pairs={{0,16},{4,20},{8,24},{12,28},{16,0},{20,4},{24,8},{28,12},{1,17},{... | collective-permute-start | bytes 417800 | tf_op jit(solution)/shard_map/ppermute | solution.py:287
  33.0 8.5 %collective-permute-start.1 = (bf16[32,2048]{1,0:T(8,128)(2,1)S(1)}, bf16[32,2048]{1,0:T(8,128)(2,1)S(1)}, u32[]{:S(2)}, u32[]{:S(2)}) collective-permute-start(bf16[32,2048]{1,0:T(8,128)(2,1)S(1)} %collective-permute-done.rest_1_), channel_id=1, source_target_pairs={{0,4},{4,0},{8,12},{12,8},{16,20},{20,16},{24,28},{28,24},{1,5},{5... | collective-permute-start | bytes 393224 | tf_op jit(solution)/shard_map/ppermute | solution.py:287
  39.1 14.2 %collective-permute-start.11 = (bf16[32,2176]{1,0:T(8,128)(2,1)S(1)}, bf16[32,2176]{1,0:T(8,128)(2,1)S(1)}, u32[]{:S(2)}, u32[]{:S(2)}) collective-permute-start(bf16[32,2176]{1,0:T(8,128)(2,1)S(1)} %get-tuple-element.35), channel_id=1, source_target_pairs={{0,12},{4,8},{8,20},{12,16},{16,28},{20,24},{24,4},{28,0},{1,13},{... | collective-permute-start | bytes 417800 | tf_op jit(solution)/shard_map/ppermute | solution.py:287
  41.5 11.8 %collective-permute-start.13 = (bf16[32,2176]{1,0:T(8,128)(2,1)S(1)}, bf16[32,2176]{1,0:T(8,128)(2,1)S(1)}, u32[]{:S(2)}, u32[]{:S(2)}) collective-permute-start(bf16[32,2176]{1,0:T(8,128)(2,1)S(1)} %get-tuple-element.46), channel_id=1, source_target_pairs={{0,20},{4,16},{8,28},{12,24},{16,4},{20,0},{24,12},{28,8},{1,21},{... | collective-permute-start | bytes 417800 | tf_op jit(solution)/shard_map/ppermute | solution.py:287
  44.8 34.4 %copy-start = (bf16[2048,1024]{1,0:T(8,128)(2,1)S(1)}, bf16[2048,1024]{1,0:T(8,128)(2,1)}, u32[]{:S(2)}) copy-start(bf16[2048,1024]{1,0:T(8,128)(2,1)} %w_ref.1) | copy-start | bytes 12582916
  49.4 8.8 %collective-permute-start.10 = (bf16[32,2176]{1,0:T(8,128)(2,1)S(1)}, bf16[32,2176]{1,0:T(8,128)(2,1)S(1)}, u32[]{:S(2)}, u32[]{:S(2)}) collective-permute-start(bf16[32,2176]{1,0:T(8,128)(2,1)S(1)} %get-tuple-element.44), channel_id=1, source_target_pairs={{0,4},{4,0},{8,12},{12,8},{16,20},{20,16},{24,28},{28,24},{1,5},{5... | collective-permute-start | bytes 417800 | tf_op jit(solution)/shard_map/ppermute | solution.py:287
  49.6 8.7 %collective-permute-start.12 = (bf16[32,2176]{1,0:T(8,128)(2,1)S(1)}, bf16[32,2176]{1,0:T(8,128)(2,1)S(1)}, u32[]{:S(2)}, u32[]{:S(2)}) collective-permute-start(bf16[32,2176]{1,0:T(8,128)(2,1)S(1)} %get-tuple-element.45), channel_id=1, source_target_pairs={{0,28},{4,24},{8,4},{12,0},{16,12},{20,8},{24,20},{28,16},{1,29},{... | collective-permute-start | bytes 417800 | tf_op jit(solution)/shard_map/ppermute | solution.py:287
  59.0 8.2 %collective-permute-start.15 = (bf16[32,2048]{1,0:T(8,128)(2,1)S(1)}, bf16[32,2048]{1,0:T(8,128)(2,1)S(1)}, u32[]{:S(2)}, u32[]{:S(2)}) collective-permute-start(bf16[32,2048]{1,0:T(8,128)(2,1)S(1)} %merge.1.rest_0_), channel_id=1, source_target_pairs={{0,8},{4,12},{8,16},{12,20},{16,24},{20,28},{24,0},{28,4},{1,9},{5... | collective-permute-start | bytes 393224 | tf_op jit(solution)/shard_map/ppermute | solution.py:287
  60.0 9.3 %collective-permute-start.14 = (bf16[32,2048]{1,0:T(8,128)(2,1)S(1)}, bf16[32,2048]{1,0:T(8,128)(2,1)S(1)}, u32[]{:S(2)}, u32[]{:S(2)}) collective-permute-start(bf16[32,2048]{1,0:T(8,128)(2,1)S(1)} %merge.1.rest_0_), channel_id=1, source_target_pairs={{0,24},{4,28},{8,0},{12,4},{16,8},{20,12},{24,16},{28,20},{1,25},{... | collective-permute-start | bytes 393224 | tf_op jit(solution)/shard_map/ppermute | solution.py:287
  62.9 10.2 %collective-permute-start.16 = (bf16[32,2048]{1,0:T(8,128)(2,1)S(1)}, bf16[32,2048]{1,0:T(8,128)(2,1)S(1)}, u32[]{:S(2)}, u32[]{:S(2)}) collective-permute-start(bf16[32,2048]{1,0:T(8,128)(2,1)S(1)} %merge.1.rest_0_), channel_id=1, source_target_pairs={{0,16},{4,20},{8,24},{12,28},{16,0},{20,4},{24,8},{28,12},{1,17},{... | collective-permute-start | bytes 393224 | tf_op jit(solution)/shard_map/ppermute | solution.py:287
  67.2 6.3 %collective-permute-start.19 = (bf16[32,2048]{1,0:T(8,128)(2,1)S(1)}, bf16[32,2048]{1,0:T(8,128)(2,1)S(1)}, u32[]{:S(2)}, u32[]{:S(2)}) collective-permute-start(bf16[32,2048]{1,0:T(8,128)(2,1)S(1)} %collective-permute-done.15.rest_2_), channel_id=1, source_target_pairs={{0,4},{4,0},{8,12},{12,8},{16,20},{20,16},{24,28},{28,24},{1,5},{5... | collective-permute-start | bytes 393224 | tf_op jit(solution)/shard_map/ppermute | solution.py:287
  68.9 6.0 %collective-permute-start.17 = (bf16[32,2048]{1,0:T(8,128)(2,1)S(1)}, bf16[32,2048]{1,0:T(8,128)(2,1)S(1)}, u32[]{:S(2)}, u32[]{:S(2)}) collective-permute-start(bf16[32,2048]{1,0:T(8,128)(2,1)S(1)} %merge.1.rest_0_), channel_id=1, source_target_pairs={{0,4},{4,0},{8,12},{12,8},{16,20},{20,16},{24,28},{28,24},{1,5},{5... | collective-permute-start | bytes 393224 | tf_op jit(solution)/shard_map/ppermute | solution.py:287
  69.3 8.5 %collective-permute-start.18 = (bf16[32,2048]{1,0:T(8,128)(2,1)S(1)}, bf16[32,2048]{1,0:T(8,128)(2,1)S(1)}, u32[]{:S(2)}, u32[]{:S(2)}) collective-permute-start(bf16[32,2048]{1,0:T(8,128)(2,1)S(1)} %collective-permute-done.14.rest_1_), channel_id=1, source_target_pairs={{0,4},{4,0},{8,12},{12,8},{16,20},{20,16},{24,28},{28,24},{1,5},{5... | collective-permute-start | bytes 393224 | tf_op jit(solution)/shard_map/ppermute | solution.py:287
  73.5 5.6 %collective-permute-start.20 = (bf16[32,2048]{1,0:T(8,128)(2,1)S(1)}, bf16[32,2048]{1,0:T(8,128)(2,1)S(1)}, u32[]{:S(2)}, u32[]{:S(2)}) collective-permute-start(bf16[32,2048]{1,0:T(8,128)(2,1)S(1)} %collective-permute-done.16.rest_3_), channel_id=1, source_target_pairs={{0,4},{4,0},{8,12},{12,8},{16,20},{20,16},{24,28},{28,24},{1,5},{5... | collective-permute-start | bytes 393224 | tf_op jit(solution)/shard_map/ppermute | solution.py:287
  80.6 1.9 %collective-permute-start.21 = (bf16[64,1024]{1,0:T(8,128)(2,1)S(1)}, bf16[64,1024]{1,0:T(8,128)(2,1)S(1)}, u32[]{:S(2)}, u32[]{:S(2)}) collective-permute-start(bf16[64,1024]{1,0:T(8,128)(2,1)S(1)} %get-tuple-element.50), channel_id=1, source_target_pairs={{0,1},{1,0},{2,3},{3,2},{4,5},{5,4},{6,7},{7,6},{8,9},{9,8},{10,11... | collective-permute-start | bytes 393224 | tf_op jit(solution)/shard_map/ppermute | solution.py:346
  80.6 6.4 %collective-permute-start.22 = (bf16[64,1024]{1,0:T(8,128)(2,1)S(1)}, bf16[64,1024]{1,0:T(8,128)(2,1)S(1)}, u32[]{:S(2)}, u32[]{:S(2)}) collective-permute-start(bf16[64,1024]{1,0:T(8,128)(2,1)S(1)} %get-tuple-element.51), channel_id=1, source_target_pairs={{0,2},{1,3},{2,0},{3,1},{4,6},{5,7},{6,4},{7,5},{8,10},{9,11},{10,... | collective-permute-start | bytes 393224 | tf_op jit(solution)/shard_map/ppermute | solution.py:346
  80.7 8.2 %collective-permute-start.23 = (bf16[64,1024]{1,0:T(8,128)(2,1)S(1)}, bf16[64,1024]{1,0:T(8,128)(2,1)S(1)}, u32[]{:S(2)}, u32[]{:S(2)}) collective-permute-start(bf16[64,1024]{1,0:T(8,128)(2,1)S(1)} %get-tuple-element.52), channel_id=1, source_target_pairs={{0,3},{1,2},{2,1},{3,0},{4,7},{5,6},{6,5},{7,4},{8,11},{9,10},{10,... | collective-permute-start | bytes 393224 | tf_op jit(solution)/shard_map/ppermute | solution.py:346
where the time goes:
time: 89.1 us; the launch traced here: 89.7 us
  starting transfers between devices  37.2 us (42%)
  waiting for transfers between devices  23.8 us (27%)
  Pallas kernels  20.8 us (23%)
  local copies, waits for them, and re-layouts  6.29 us (7%)
  other arithmetic  1.51 us (2%)
    ppermute x21, starting transfers between devices, move(): return lax.ppermute(x, 'ctx', pairs)  35.2 us
    pallas_call x4, Pallas kernels, attention_call(): pl.pallas_call(functools.partial(attention_kernel, members, ctx_count, gr...  18.6 us
    ppermute x21, waiting for transfers between devices, move(): return lax.ppermute(x, 'ctx', pairs)  17.4 us
    ppermute x3, waiting for transfers between devices, body(): got = lax.ppermute(piece, 'tp', [(i, i ^ j) for i in range(peers)])  6.4 us
    unnamed x9, local copies, waits for them, and re-layouts  4.81 us
    ppermute x3, starting transfers between devices, body(): got = lax.ppermute(piece, 'tp', [(i, i ^ j) for i in range(peers)])  1.93 us
  transfers between devices with their start and end apart: 24, of which 10 were waited for; matrix products, arithmetic and copies ran while one was open for 3% of the time, Pallas kernels for 21%

commit v1 on v0

--- a/solution.py
+++ b/solution.py
@@ -13,6 +13,7 @@
 LANES = 128
 CHUNK = 4
 LOW = -1e30
+ONES = 16
 LOW_SIZE = 2
 VMEM_ATTN = 24 * 2**20
 VMEM_MERGE = 8 * 2**20
@@ -30,7 +31,7 @@
     blocks = len(members)
     q_refs, rest = rest[:blocks], rest[blocks:]
     out_refs, rest = rest[:blocks], rest[blocks:]
-    q_ref, acc_ref, max_ref = rest
+    q_ref, turned_ref, acc_ref, max_ref = rest
     q_dev = q_refs[0].shape[0]
     heads = kv_local * group
     rows = q_dev * group
@@ -44,34 +45,41 @@
     def slot_of(ctx):
         return table_ref[kv_local * (slots + 1) + ctx]
 
-    lane = lax.broadcasted_iota(jnp.int32, (q_dev, LANES), 1)
-    ones_new = jnp.ones((q_dev, LANES), jnp.bfloat16)
-    ones_tile = jnp.ones((TILE, LANES), jnp.bfloat16)
-    place_row = lax.broadcasted_iota(jnp.int32, (rows, q_dev), 0) % q_dev
-    place_key = lax.broadcasted_iota(jnp.int32, (rows, q_dev), 1)
-    contract_last = (((1,), (1,)), ((), ()))
+    def turned(x):
+        return x.astype(jnp.float32).T.astype(jnp.bfloat16)
+
+    def fold(g, b, s, values, first=False):
+        peak = jnp.max(s, axis=0, keepdims=True) * scale
+        top = peak if first else jnp.maximum(max_ref[g, b, :1], peak)
+        p = jnp.exp2(s * scale - top).astype(jnp.bfloat16)
+        mixed = jnp.dot(values, p, preferred_element_type=jnp.float32)
+        if not first:
+            mixed += acc_ref[g, b] * jnp.exp2(max_ref[g, b, :1] - top)
+        max_ref[g, b] = jnp.broadcast_to(top, max_ref.shape[2:])
+        acc_ref[g, b] = mixed
+
+    ones_tile = jnp.ones((ONES, TILE), jnp.bfloat16)
+    place_key = lax.broadcasted_iota(jnp.int32, (TILE, rows), 0)
+    place_row = lax.broadcasted_iota(jnp.int32, (TILE, rows), 1) % q_dev
+    padding = jnp.zeros((TILE - q_dev, DH), jnp.bfloat16)
 
     for g in range(kv_local):
-        cols = slice(g * DH, (g + 1) * DH)
-        fresh_keys = new_ref[:, cols]
+        fresh_keys = jnp.concatenate([new_ref[:, g * DH : (g + 1) * DH], padding], 0)
+        fresh_values = new_ref[:, (kv_local + g) * DH : (kv_local + g + 1) * DH]
         fresh_values = jnp.concatenate(
-            [new_ref[:, (kv_local + g) * DH : (kv_local + g + 1) * DH], ones_new], 1
+            [turned(jnp.concatenate([fresh_values, padding], 0)), ones_tile], 0
         )
         for b in range(blocks):
             for h in range(group):
                 head = g * group + h
-                q_ref[g, b, h * q_dev : (h + 1) * q_dev, :] = q_refs[b][
+                q_ref[h * q_dev : (h + 1) * q_dev, :] = q_refs[b][
                     :, head * DH : (head + 1) * DH
-                ]
-            s = lax.dot_general(
-                q_ref[g, b], fresh_keys, contract_last, preferred_element_type=jnp.float32
-            )
+                ].astype(jnp.float32)
+            turned_ref[g, b] = q_ref[...].T.astype(jnp.bfloat16)
+            s = jnp.dot(fresh_keys, turned_ref[g, b], preferred_element_type=jnp.float32)
             shift = (slot_of(flipped(me, ctx_count, *members[b])) - slot_of(me)) * q_dev
-            s = jnp.where(place_row - place_key + shift >= 0, s * scale, LOW)
-            top = jnp.broadcast_to(jnp.max(s, axis=1, keepdims=True), (rows, LANES))
-            p = jnp.exp2(s - top[:, :q_dev]).astype(jnp.bfloat16)
-            max_ref[g, b] = top
-            acc_ref[g, b] = jnp.dot(p, fresh_values, preferred_element_type=jnp.float32)
+            live = (place_key < q_dev) & (place_row - place_key + shift >= 0)
+            fold(g, b, jnp.where(live, s, LOW), fresh_values, first=True)
 
     def load_chunk(g, chunk):
         cols = slice(g * DH, (g + 1) * DH)
@@ -82,38 +90,23 @@
             tile = table_ref[g * slots + jnp.where(live, slot, 0)]
             at = pl.ds(pl.multiple_of(tile * TILE, TILE), TILE)
             key_parts.append(k_ref[at, cols])
-            tail = jnp.concatenate([v_ref[at, cols], ones_tile], 1)
+            tail = jnp.concatenate([turned(v_ref[at, cols]), ones_tile], 0)
             value_parts.append(jnp.where(live, tail, jnp.zeros_like(tail)))
-        return jnp.concatenate(key_parts, 0), jnp.concatenate(value_parts, 0)
+        return jnp.concatenate(key_parts, 0), jnp.concatenate(value_parts, 1)
 
     def run(kv_heads, chunk):
         loaded = {g: load_chunk(g, chunk) for g in kv_heads}
         chains = [(g, b) for b in range(blocks) for g in kv_heads]
 
         def score(g, b):
-            return lax.dot_general(
-                q_ref[g, b], loaded[g][0], contract_last, preferred_element_type=jnp.float32
-            )
+            return jnp.dot(loaded[g][0], turned_ref[g, b], preferred_element_type=jnp.float32)
 
         ahead = score(*chains[0])
         for at, (g, b) in enumerate(chains):
             s = ahead
             if at + 1 < len(chains):
                 ahead = score(*chains[at + 1])
-            old = max_ref[g, b]
-            top = jnp.maximum(old, jnp.max(s, axis=1, keepdims=True) * scale)
-            p = jnp.concatenate(
-                [
-                    jnp.exp2(s[:, j * LANES : (j + 1) * LANES] * scale - top)
-                    for j in range(span // LANES)
-                ],
-                1,
-            ).astype(jnp.bfloat16)
-            shrink = jnp.exp2(old - top)
-            max_ref[g, b] = top
-            acc_ref[g, b] = acc_ref[g, b] * jnp.concatenate([shrink, shrink], 1) + jnp.dot(
-                p, loaded[g][1], preferred_element_type=jnp.float32
-            )
+            fold(g, b, s, loaded[g][1])
 
     ends = [(count_of(g) + CHUNK - 1) // CHUNK for g in range(kv_local)]
     shared = functools.reduce(jnp.minimum, ends)
@@ -131,24 +124,24 @@
 
         lax.fori_loop(shared, ends[g], step_one, 0)
 
-    stats = [jnp.zeros((q_dev, LANES), jnp.float32) for _ in range(blocks)]
+    sublane = lax.broadcasted_iota(jnp.int32, (q_dev, LANES), 0)
+    parts = rows // LANES
     for b in range(blocks):
+        stats = jnp.zeros((q_dev, LANES), jnp.float32)
         for g in range(kv_local):
-            total = acc_ref[g, b, :, DH:]
-            mean = acc_ref[g, b, :, :DH] / total
-            level = max_ref[g, b] + jnp.log2(total)
+            total = acc_ref[g, b, DH : DH + 1, :]
+            mean = (acc_ref[g, b, :DH, :] / total).T.astype(jnp.bfloat16)
             for h in range(group):
                 head = g * group + h
-                part = slice(h * q_dev, (h + 1) * q_dev)
-                out_refs[b][:, head * DH : (head + 1) * DH] = mean[part].astype(jnp.bfloat16)
-                stats[b] = jnp.where(lane % heads == head, level[part], stats[b])
-
-    for b in range(blocks):
-        high = stats[b].astype(jnp.bfloat16).astype(jnp.float32)
-        middle = (stats[b] - high).astype(jnp.bfloat16).astype(jnp.float32)
-        low = stats[b] - high - middle
-        packed = jnp.where(lane < heads, high, jnp.where(lane < 2 * heads, middle, low))
-        out_refs[b][:, heads * DH :] = packed.astype(jnp.bfloat16)
+                out_refs[b][:, head * DH : (head + 1) * DH] = mean[h * q_dev : (h + 1) * q_dev]
+            level = max_ref[g, b, :1] + jnp.log2(total)
+            high = level.astype(jnp.bfloat16).astype(jnp.float32)
+            middle = (level - high).astype(jnp.bfloat16).astype(jnp.float32)
+            for i, term in enumerate((high, middle, level - high - middle)):
+                for j in range(parts):
+                    at = (g * 3 + i) * parts + j
+                    stats = jnp.where(sublane == at, term[:, j * LANES : (j + 1) * LANES], stats)
+        out_refs[b][:, heads * DH :] = stats.astype(jnp.bfloat16)
 
 
 def attention_call(members, ctx_count, kv_local, slots, blocks, table, new_rows, keys, values):
@@ -165,9 +158,10 @@
         in_specs=[smem] + [vmem] * (3 + n),
         out_specs=[vmem] * n,
         scratch_shapes=[
-            pltpu.VMEM((kv_local, n, rows, DH), jnp.bfloat16),
-            pltpu.VMEM((kv_local, n, rows, DH + LANES), jnp.float32),
-            pltpu.VMEM((kv_local, n, rows, LANES), jnp.float32),
+            pltpu.VMEM((rows, DH), jnp.float32),
+            pltpu.VMEM((kv_local, n, DH, rows), jnp.bfloat16),
+            pltpu.VMEM((kv_local, n, DH + ONES, rows), jnp.float32),
+            pltpu.VMEM((kv_local, n, 8, rows), jnp.float32),
         ],
         compiler_params=pltpu.CompilerParams(vmem_limit_bytes=VMEM_ATTN),
         cost_estimate=pl.CostEstimate(
@@ -177,36 +171,47 @@
     )(table, new_rows, keys, values, *blocks)
 
 
-def merge_kernel(parts, *refs):
+def merge_kernel(parts, kv_local, *refs):
     in_refs, out_ref = refs[:parts], refs[parts]
-    width = out_ref.shape[1]
-    heads = width // DH
-    levels = []
-    for ref in in_refs:
-        packed = ref[:, width:].astype(jnp.float32)
-        levels.append(
-            packed
-            + pltpu.roll(packed, LANES - heads, 1)
-            + pltpu.roll(packed, LANES - 2 * heads, 1)
-        )
-    top = functools.reduce(jnp.maximum, levels)
-    shares = [jnp.exp2(level - top) for level in levels]
-    total = functools.reduce(jnp.add, shares)
-    shares = [share / total for share in shares]
-    for h in range(heads):
-        cols = slice(h * DH, (h + 1) * DH)
-        mixed = functools.reduce(
-            jnp.add,
-            [share[:, h : h + 1] * ref[:, cols].astype(jnp.float32) for share, ref in zip(shares, in_refs)],
-        )
-        out_ref[:, cols] = mixed.astype(jnp.bfloat16)
-
-
-def merge_call(parts):
+    q_dev, width = out_ref.shape
+    group = width // DH // kv_local
+    lane_parts = q_dev * group // LANES
+    per_part = LANES // q_dev
+    stats = [ref[:, width:].astype(jnp.float32) for ref in in_refs]
+    sublane = lax.broadcasted_iota(jnp.int32, (LANES, LANES), 0)
+    for j in range(lane_parts):
+        table = jnp.zeros((LANES, LANES), jnp.float32)
+        for g in range(kv_local):
+            at = [(g * 3 + i) * lane_parts + j for i in range(3)]
+            levels = [stat[at[0]] + stat[at[1]] + stat[at[2]] for stat in stats]
+            levels = [level.reshape(1, LANES) for level in levels]
+            top = functools.reduce(jnp.maximum, levels)
+            shares = [jnp.exp2(level - top) for level in levels]
+            total = functools.reduce(jnp.add, shares)
+            for c, share in enumerate(shares):
+                table = jnp.where(sublane == g * parts + c, share / total, table)
+        table = table.T
+        for g in range(kv_local):
+            for i in range(per_part):
+                head = g * group + j * per_part + i
+                cols = slice(head * DH, (head + 1) * DH)
+                share = table[i * q_dev : (i + 1) * q_dev]
+                mixed = functools.reduce(
+                    jnp.add,
+                    [
+                        share[:, g * parts + c : g * parts + c + 1]
+                        * in_refs[c][:, cols].astype(jnp.float32)
+                        for c in range(parts)
+                    ],
+                )
+                out_ref[:, cols] = mixed.astype(jnp.bfloat16)
+
+
+def merge_call(parts, kv_local):
     q_dev, wide = parts[0].shape
     vmem = pl.BlockSpec(memory_space=pltpu.VMEM)
     return pl.pallas_call(
-        functools.partial(merge_kernel, len(parts)),
+        functools.partial(merge_kernel, len(parts), kv_local),
         out_shape=jax.ShapeDtypeStruct((q_dev, wide - LANES), jnp.bfloat16),
         in_specs=[vmem] * len(parts),
         out_specs=vmem,
@@ -338,7 +343,7 @@
         last = members[-1]
         for m in members:
             back[m] = parts[m] if m == (0, 0) else move(parts[m], *m)
-    attn = merge_call([back[m] for m in order])
+    attn = merge_call([back[m] for m in order], kv_local)
 
     held = gather(attn, True)
     own, *sends = projection_call(order, ctx_count, [held[m] for m in order], out_weight, peers)

time: 89.1 us -> 88.2 us (0.990)
  waiting for transfers between devices: 23.8 us -> 18.9 us
  starting transfers between devices: 37.2 us -> 39.8 us
    ppermute x21, waiting for transfers between devices: 17.4 us -> 12.3 us  [move(): return lax.ppermute(x, 'ctx', pairs)]
    ppermute x3, starting transfers between devices: 1.93 us -> 3.3 us  [body(): got = lax.ppermute(piece, 'tp', [(i, i ^ j) for i in range(peers)])]
    ppermute x21, starting transfers between devices: 35.2 us -> 36.5 us  [move(): return lax.ppermute(x, 'ctx', pairs)]
  transfers between devices with their start and end apart: 24 -> 24, of which waited for: 10 -> 11; matrix products, arithmetic and copies ran while one was open for 3% -> 3% of each run, Pallas kernels for 21% -> 22%
where the time goes in v1:
time: 88.2 us
  starting transfers between devices  39.8 us (45%)
  Pallas kernels  21.6 us (24%)
  waiting for transfers between devices  18.9 us (21%)
  local copies, waits for them, and re-layouts  6.29 us (7%)
  other arithmetic  1.51 us (2%)
    ppermute x21, starting transfers between devices, move(): return lax.ppermute(x, 'ctx', pairs)  36.5 us
    pallas_call x4, Pallas kernels, attention_call(): pl.pallas_call(functools.partial(attention_kernel, members, ctx_count, gr...  19.3 us
    ppermute x21, waiting for transfers between devices, move(): return lax.ppermute(x, 'ctx', pairs)  12.3 us
    ppermute x3, waiting for transfers between devices, body(): got = lax.ppermute(piece, 'tp', [(i, i ^ j) for i in range(peers)])  6.56 us
    unnamed x9, local copies, waits for them, and re-layouts  4.81 us
    ppermute x3, starting transfers between devices, body(): got = lax.ppermute(piece, 'tp', [(i, i ^ j) for i in range(peers)])  3.3 us
  transfers between devices with their start and end apart: 24, of which 11 were waited for; matrix products, arithmetic and copies ran while one was open for 3% of the time, Pallas kernels for 22%

profile of v1, /device:TPU:0, one launch (start us, length us, event | category | flops | bytes accessed | tf_op | source)
XLA Modules:
  0.0 88.2 jit_solution(14778455604217813512)
XLA Ops:
  0.0 2.9 %collective-permute-start.2 = (bf16[32,2048]{1,0:T(8,128)(2,1)}, bf16[32,2048]{1,0:T(8,128)(2,1)S(1)}, u32[]{:S(2)}, u32[]{:S(2)}) collective-permute-start(bf16[32,2048]{1,0:T(8,128)(2,1)} %rest_0_.1), channel_id=1, source_target_pairs={{0,4},{4,0},{8,12},{12,8},{16,20},{20,16},{24,28},{28,24},{1,5},{5... | collective-permute-start | bytes 393224 | tf_op jit(solution)/shard_map/ppermute | solution.py:292
  2.9 1.6 %collective-permute-start = (bf16[32,2048]{1,0:T(8,128)(2,1)}, bf16[32,2048]{1,0:T(8,128)(2,1)S(1)}, u32[]{:S(2)}, u32[]{:S(2)}) collective-permute-start(bf16[32,2048]{1,0:T(8,128)(2,1)} %rest_0_.1), channel_id=1, source_target_pairs={{0,8},{4,12},{8,16},{12,20},{16,24},{20,28},{24,0},{28,4},{1,9},{5... | collective-permute-start | bytes 393224 | tf_op jit(solution)/shard_map/ppermute | solution.py:292
  4.5 2.2 %collective-permute-start.5 = (bf16[32,2048]{1,0:T(8,128)(2,1)}, bf16[32,2048]{1,0:T(8,128)(2,1)S(1)}, u32[]{:S(2)}, u32[]{:S(2)}) collective-permute-start(bf16[32,2048]{1,0:T(8,128)(2,1)} %rest_0_.1), channel_id=1, source_target_pairs={{0,24},{4,28},{8,0},{12,4},{16,8},{20,12},{24,16},{28,20},{1,25},{... | collective-permute-start | bytes 393224 | tf_op jit(solution)/shard_map/ppermute | solution.py:292
  6.8 0.8 collective-permute-start.3
  7.6 0.8 reshape.6
  8.3 0.7 constant_dynamic-update-slice_fusion.1
  9.0 0.7 constant_dynamic-update-slice_fusion.new_ref
  9.8 0.7 pad_add_fusion.table_ref
  10.5 0.0 copy-start.1
  10.5 1.6 %copy-done.1 = bf16[4096,256]{1,0:T(8,128)(2,1)S(1)} copy-done((bf16[4096,256]{1,0:T(8,128)(2,1)S(1)}, bf16[4096,256]{1,0:T(8,128)(2,1)}, u32[]{:S(2)}) %copy-start.1) | copy-done | bytes 2097176
  12.1 1.6 %copy-done.2 = bf16[4096,256]{1,0:T(8,128)(2,1)S(1)} copy-done((bf16[4096,256]{1,0:T(8,128)(2,1)S(1)}, bf16[4096,256]{1,0:T(8,128)(2,1)}, u32[]{:S(2)}) %copy-start.2) | copy-done | bytes 2097176
  13.7 0.9 %copy-done.3 = bf16[32,2048]{1,0:T(8,128)(2,1)S(1)} copy-done((bf16[32,2048]{1,0:T(8,128)(2,1)S(1)}, bf16[32,2048]{1,0:T(8,128)(2,1)}, u32[]{:S(2)}) %copy-start.3) | copy-done | bytes 131096
  14.6 3.7 %attention.4.refs_0_ = bf16[32,2176]{1,0:T(8,128)(2,1)S(1)} custom-call(s32[58]{0:T(128)S(1)} %pad_add_fusion.table_ref, bf16[32,512]{1,0:T(8,128)(2,1)S(1)} %constant_dynamic-update-slice_fusion.new_ref, bf16[4096,256]{1,0:T(8,128)(2,1)S(1)} %copy-done.1, bf16[4096,256]{1,0:T(8,128)(2,1)S(1)} %copy-done.2, bf16[32,2048]{1,0:T(8,128)(2,1)S(1)} %copy-done.3), custom_call_target="tpu_custom_call" | custom-call | flops 1610612736 | bytes 8388608 | tf_op jit(solution)/shard_map/attention/pallas_call | solution.py:155
  18.3 0.0 collective-permute-done.rest_1_
  18.3 0.0 collective-permute-done.5.rest_0_
  18.3 0.1 collective-permute-done.3.rest_2_
  18.4 0.6 collective-permute-start.6
  19.1 1.4 %collective-permute-start.4 = (bf16[32,2048]{1,0:T(8,128)(2,1)S(1)}, bf16[32,2048]{1,0:T(8,128)(2,1)S(1)}, u32[]{:S(2)}, u32[]{:S(2)}) collective-permute-start(bf16[32,2048]{1,0:T(8,128)(2,1)S(1)} %collective-permute-done.3.rest_2_), channel_id=1, source_target_pairs={{0,4},{4,0},{8,12},{12,8},{16,20},{20,16},{24,28},{28,24},{1,5},{5... | collective-permute-start | bytes 393224 | tf_op jit(solution)/shard_map/ppermute | solution.py:292
  20.5 6.1 %attention.5 = (bf16[32,2176]{1,0:T(8,128)(2,1)S(1)}, bf16[32,2176]{1,0:T(8,128)(2,1)S(1)}, bf16[32,2176]{1,0:T(8,128)(2,1)S(1)}) custom-call(s32[58]{0:T(128)S(1)} %pad_add_fusion.table_ref, bf16[32,512]{1,0:T(8,128)(2,1)S(1)} %constant_dynamic-update-slice_fusion.new_ref, bf16[4096,256]{1,0:T(8,128)(2,1)S(1)} %copy-done.1, ...), custom_call_target="tpu_custom_call" | custom-call | flops 4831838208 | bytes 8388608 | tf_op jit(solution)/shard_map/attention/pallas_call | solution.py:155
  26.6 2.5 %collective-permute-start.7 = (bf16[32,2176]{1,0:T(8,128)(2,1)S(1)}, bf16[32,2176]{1,0:T(8,128)(2,1)S(1)}, u32[]{:S(2)}, u32[]{:S(2)}) collective-permute-start(bf16[32,2176]{1,0:T(8,128)(2,1)S(1)} %get-tuple-element.38), channel_id=1, source_target_pairs={{0,8},{4,12},{8,16},{12,20},{16,24},{20,28},{24,0},{28,4},{1,9},{5... | collective-permute-start | bytes 417800 | tf_op jit(solution)/shard_map/ppermute | solution.py:292
  29.0 1.4 %collective-permute-start.8 = (bf16[32,2176]{1,0:T(8,128)(2,1)S(1)}, bf16[32,2176]{1,0:T(8,128)(2,1)S(1)}, u32[]{:S(2)}, u32[]{:S(2)}) collective-permute-start(bf16[32,2176]{1,0:T(8,128)(2,1)S(1)} %get-tuple-element.39), channel_id=1, source_target_pairs={{0,24},{4,28},{8,0},{12,4},{16,8},{20,12},{24,16},{28,20},{1,25},{... | collective-permute-start | bytes 417800 | tf_op jit(solution)/shard_map/ppermute | solution.py:292
  30.4 0.0 collective-permute-done.6.rest_1_
  30.4 1.2 %collective-permute-start.9 = (bf16[32,2176]{1,0:T(8,128)(2,1)S(1)}, bf16[32,2176]{1,0:T(8,128)(2,1)S(1)}, u32[]{:S(2)}, u32[]{:S(2)}) collective-permute-start(bf16[32,2176]{1,0:T(8,128)(2,1)S(1)} %get-tuple-element.32), channel_id=1, source_target_pairs={{0,16},{4,20},{8,24},{12,28},{16,0},{20,4},{24,8},{28,12},{1,17},{... | collective-permute-start | bytes 417800 | tf_op jit(solution)/shard_map/ppermute | solution.py:292
  31.6 0.0 collective-permute-done.4.rest_0_
  31.6 3.2 %collective-permute-start.1 = (bf16[32,2048]{1,0:T(8,128)(2,1)S(1)}, bf16[32,2048]{1,0:T(8,128)(2,1)S(1)}, u32[]{:S(2)}, u32[]{:S(2)}) collective-permute-start(bf16[32,2048]{1,0:T(8,128)(2,1)S(1)} %collective-permute-done.rest_1_), channel_id=1, source_target_pairs={{0,4},{4,0},{8,12},{12,8},{16,20},{20,16},{24,28},{28,24},{1,5},{5... | collective-permute-start | bytes 393224 | tf_op jit(solution)/shard_map/ppermute | solution.py:292
  34.8 4.7 %attention.6 = (bf16[32,2176]{1,0:T(8,128)(2,1)S(1)}, bf16[32,2176]{1,0:T(8,128)(2,1)S(1)}) custom-call(s32[58]{0:T(128)S(1)} %pad_add_fusion.table_ref, bf16[32,512]{1,0:T(8,128)(2,1)S(1)} %constant_dynamic-update-slice_fusion.new_ref, bf16[4096,256]{1,0:T(8,128)(2,1)S(1)} %copy-done.1, bf16[4096,256]{1,0:T(8,128)(2,1)S(1)} %copy-done.2, ...), custom_call_target="tpu_custom_call" | custom-call | flops 3221225472 | bytes 8388608 | tf_op jit(solution)/shard_map/attention/pallas_call | solution.py:155
  39.5 0.0 collective-permute-done.2.rest_1_
  39.5 2.2 %collective-permute-start.11 = (bf16[32,2176]{1,0:T(8,128)(2,1)S(1)}, bf16[32,2176]{1,0:T(8,128)(2,1)S(1)}, u32[]{:S(2)}, u32[]{:S(2)}) collective-permute-start(bf16[32,2176]{1,0:T(8,128)(2,1)S(1)} %get-tuple-element.35), channel_id=1, source_target_pairs={{0,12},{4,8},{8,20},{12,16},{16,28},{20,24},{24,4},{28,0},{1,13},{... | collective-permute-start | bytes 417800 | tf_op jit(solution)/shard_map/ppermute | solution.py:292
  41.8 0.0 collective-permute-done.1.rest_0_
  41.8 2.9 %collective-permute-start.13 = (bf16[32,2176]{1,0:T(8,128)(2,1)S(1)}, bf16[32,2176]{1,0:T(8,128)(2,1)S(1)}, u32[]{:S(2)}, u32[]{:S(2)}) collective-permute-start(bf16[32,2176]{1,0:T(8,128)(2,1)S(1)} %get-tuple-element.46), channel_id=1, source_target_pairs={{0,20},{4,16},{8,28},{12,24},{16,4},{20,0},{24,12},{28,8},{1,21},{... | collective-permute-start | bytes 417800 | tf_op jit(solution)/shard_map/ppermute | solution.py:292
  44.7 0.0 collective-permute-done.7.refs_1_
  44.7 0.0 collective-permute-done.8.refs_2_
  44.7 4.7 %attention.7 = (bf16[32,2176]{1,0:T(8,128)(2,1)S(1)}, bf16[32,2176]{1,0:T(8,128)(2,1)S(1)}) custom-call(s32[58]{0:T(128)S(1)} %pad_add_fusion.table_ref, bf16[32,512]{1,0:T(8,128)(2,1)S(1)} %constant_dynamic-update-slice_fusion.new_ref, bf16[4096,256]{1,0:T(8,128)(2,1)S(1)} %copy-done.1, bf16[4096,256]{1,0:T(8,128)(2,1)S(1)} %copy-done.2, ...), custom_call_target="tpu_custom_call" | custom-call | flops 3221225472 | bytes 8388608 | tf_op jit(solution)/shard_map/attention/pallas_call | solution.py:155
  49.5 0.5 collective-permute-start.10
  49.9 2.4 %collective-permute-start.12 = (bf16[32,2176]{1,0:T(8,128)(2,1)S(1)}, bf16[32,2176]{1,0:T(8,128)(2,1)S(1)}, u32[]{:S(2)}, u32[]{:S(2)}) collective-permute-start(bf16[32,2176]{1,0:T(8,128)(2,1)S(1)} %get-tuple-element.45), channel_id=1, source_target_pairs={{0,28},{4,24},{8,4},{12,0},{16,12},{20,8},{24,20},{28,16},{1,29},{... | collective-permute-start | bytes 417800 | tf_op jit(solution)/shard_map/ppermute | solution.py:292
  52.3 0.0 collective-permute-done.9.refs_3_
  52.3 0.0 collective-permute-done.13.refs_7_
  52.3 0.0 collective-permute-done.11.refs_5_
  52.3 3.8 %collective-permute-done.10.refs_4_ = bf16[32,2176]{1,0:T(8,128)(2,1)S(1)} collective-permute-done((bf16[32,2176]{1,0:T(8,128)(2,1)S(1)}, bf16[32,2176]{1,0:T(8,128)(2,1)S(1)}, u32[]{:S(2)}, u32[]{:S(2)}) %collective-permute-start.10) | collective-permute-done | bytes 139296 | tf_op jit(solution)/shard_map/ppermute | solution.py:292
  56.1 0.2 collective-permute-done.12.refs_6_
  56.2 0.9 %merge.1.rest_0_ = bf16[32,2048]{1,0:T(8,128)(2,1)S(1)} custom-call(bf16[32,2176]{1,0:T(8,128)(2,1)S(1)} %attention.4.refs_0_, bf16[32,2176]{1,0:T(8,128)(2,1)S(1)} %collective-permute-done.7.refs_1_, bf16[32,2176]{1,0:T(8,128)(2,1)S(1)} %collective-permute-done.8.refs_2_, bf16[32,2176]{1,0:T(8,128)(2,1)S(1)} %collective-permute-done.9.refs_3_, ...), custom_call_target="tpu_custom_call" | custom-call | flops 1114112 | bytes 1114112 | tf_op jit(solution)/shard_map/merge/pallas_call | solution.py:213
  57.2 6.2 %collective-permute-start.15 = (bf16[32,2048]{1,0:T(8,128)(2,1)S(1)}, bf16[32,2048]{1,0:T(8,128)(2,1)S(1)}, u32[]{:S(2)}, u32[]{:S(2)}) collective-permute-start(bf16[32,2048]{1,0:T(8,128)(2,1)S(1)} %merge.1.rest_0_), channel_id=1, source_target_pairs={{0,8},{4,12},{8,16},{12,20},{16,24},{20,28},{24,0},{28,4},{1,9},{5... | collective-permute-start | bytes 393224 | tf_op jit(solution)/shard_map/ppermute | solution.py:292
  63.4 0.0 collective-permute-start.14
  63.4 1.5 %collective-permute-start.16 = (bf16[32,2048]{1,0:T(8,128)(2,1)S(1)}, bf16[32,2048]{1,0:T(8,128)(2,1)S(1)}, u32[]{:S(2)}, u32[]{:S(2)}) collective-permute-start(bf16[32,2048]{1,0:T(8,128)(2,1)S(1)} %merge.1.rest_0_), channel_id=1, source_target_pairs={{0,16},{4,20},{8,24},{12,28},{16,0},{20,4},{24,8},{28,12},{1,17},{... | collective-permute-start | bytes 393224 | tf_op jit(solution)/shard_map/ppermute | solution.py:292
  64.9 1.0 %collective-permute-done.15.rest_2_ = bf16[32,2048]{1,0:T(8,128)(2,1)S(1)} collective-permute-done((bf16[32,2048]{1,0:T(8,128)(2,1)S(1)}, bf16[32,2048]{1,0:T(8,128)(2,1)S(1)}, u32[]{:S(2)}, u32[]{:S(2)}) %collective-permute-start.15) | collective-permute-done | bytes 131104 | tf_op jit(solution)/shard_map/ppermute | solution.py:292
  65.9 0.2 collective-permute-start.19
  66.1 1.8 %collective-permute-start.17 = (bf16[32,2048]{1,0:T(8,128)(2,1)S(1)}, bf16[32,2048]{1,0:T(8,128)(2,1)S(1)}, u32[]{:S(2)}, u32[]{:S(2)}) collective-permute-start(bf16[32,2048]{1,0:T(8,128)(2,1)S(1)} %merge.1.rest_0_), channel_id=1, source_target_pairs={{0,4},{4,0},{8,12},{12,8},{16,20},{20,16},{24,28},{28,24},{1,5},{5... | collective-permute-start | bytes 393224 | tf_op jit(solution)/shard_map/ppermute | solution.py:292
  68.0 1.8 %collective-permute-done.14.rest_1_ = bf16[32,2048]{1,0:T(8,128)(2,1)S(1)} collective-permute-done((bf16[32,2048]{1,0:T(8,128)(2,1)S(1)}, bf16[32,2048]{1,0:T(8,128)(2,1)S(1)}, u32[]{:S(2)}, u32[]{:S(2)}) %collective-permute-start.14) | collective-permute-done | bytes 131104 | tf_op jit(solution)/shard_map/ppermute | solution.py:292
  69.8 0.0 collective-permute-start.18
  69.8 0.0 collective-permute-done.16.rest_3_
  69.8 1.1 %collective-permute-done.19.rest_6_ = bf16[32,2048]{1,0:T(8,128)(2,1)S(1)} collective-permute-done((bf16[32,2048]{1,0:T(8,128)(2,1)S(1)}, bf16[32,2048]{1,0:T(8,128)(2,1)S(1)}, u32[]{:S(2)}, u32[]{:S(2)}) %collective-permute-start.19) | collective-permute-done | bytes 131104 | tf_op jit(solution)/shard_map/ppermute | solution.py:292
  70.9 0.9 %collective-permute-start.20 = (bf16[32,2048]{1,0:T(8,128)(2,1)S(1)}, bf16[32,2048]{1,0:T(8,128)(2,1)S(1)}, u32[]{:S(2)}, u32[]{:S(2)}) collective-permute-start(bf16[32,2048]{1,0:T(8,128)(2,1)S(1)} %collective-permute-done.16.rest_3_), channel_id=1, source_target_pairs={{0,4},{4,0},{8,12},{12,8},{16,20},{20,16},{24,28},{28,24},{1,5},{5... | collective-permute-start | bytes 393224 | tf_op jit(solution)/shard_map/ppermute | solution.py:292
  71.8 0.5 collective-permute-done.17.rest_4_
  72.3 2.4 %collective-permute-done.18.rest_5_ = bf16[32,2048]{1,0:T(8,128)(2,1)S(1)} collective-permute-done((bf16[32,2048]{1,0:T(8,128)(2,1)S(1)}, bf16[32,2048]{1,0:T(8,128)(2,1)S(1)}, u32[]{:S(2)}, u32[]{:S(2)}) %collective-permute-start.18) | collective-permute-done | bytes 131104 | tf_op jit(solution)/shard_map/ppermute | solution.py:292
  74.8 1.4 %collective-permute-done.20.rest_7_ = bf16[32,2048]{1,0:T(8,128)(2,1)S(1)} collective-permute-done((bf16[32,2048]{1,0:T(8,128)(2,1)S(1)}, bf16[32,2048]{1,0:T(8,128)(2,1)S(1)}, u32[]{:S(2)}, u32[]{:S(2)}) %collective-permute-start.20) | collective-permute-done | bytes 131104 | tf_op jit(solution)/shard_map/ppermute | solution.py:292
  76.2 0.0 copy-done
  76.2 1.4 %projection.1 = (f32[64,1024]{1,0:T(8,128)S(1)}, bf16[64,1024]{1,0:T(8,128)(2,1)S(1)}, bf16[64,1024]{1,0:T(8,128)(2,1)S(1)}, bf16[64,1024]{1,0:T(8,128)(2,1)S(1)}) custom-call(bf16[2048,1024]{1,0:T(8,128)(2,1)S(1)} %copy-done, bf16[32,2048]{1,0:T(8,128)(2,1)S(1)} %merge.1.rest_0_, bf16[32,2048]{1,0:T(8,128)(2,1)S(1)} %collective-permute-done.14.rest_1_, ...), custom_call_target="tpu_custom_call" | custom-call | flops 1073741824 | bytes 4194304 | tf_op jit(solution)/shard_map/projection/pallas_call | solution.py:252
  77.6 0.1 collective-permute-start.21
  77.6 3.2 %collective-permute-start.22 = (bf16[64,1024]{1,0:T(8,128)(2,1)S(1)}, bf16[64,1024]{1,0:T(8,128)(2,1)S(1)}, u32[]{:S(2)}, u32[]{:S(2)}) collective-permute-start(bf16[64,1024]{1,0:T(8,128)(2,1)S(1)} %get-tuple-element.51), channel_id=1, source_target_pairs={{0,2},{1,3},{2,0},{3,1},{4,6},{5,7},{6,4},{7,5},{8,10},{9,11},{10,... | collective-permute-start | bytes 393224 | tf_op jit(solution)/shard_map/ppermute | solution.py:351
  80.8 0.1 collective-permute-start.23
  80.9 0.0 collective-permute-done.21
  80.9 4.3 %collective-permute-done.22 = bf16[64,1024]{1,0:T(8,128)(2,1)S(1)} collective-permute-done((bf16[64,1024]{1,0:T(8,128)(2,1)S(1)}, bf16[64,1024]{1,0:T(8,128)(2,1)S(1)}, u32[]{:S(2)}, u32[]{:S(2)}) %collective-permute-start.22) | collective-permute-done | bytes 131104 | tf_op jit(solution)/shard_map/ppermute | solution.py:351
  85.2 2.3 %collective-permute-done.23 = bf16[64,1024]{1,0:T(8,128)(2,1)S(1)} collective-permute-done((bf16[64,1024]{1,0:T(8,128)(2,1)S(1)}, bf16[64,1024]{1,0:T(8,128)(2,1)S(1)}, u32[]{:S(2)}, u32[]{:S(2)}) %collective-permute-start.23) | collective-permute-done | bytes 131104 | tf_op jit(solution)/shard_map/ppermute | solution.py:351
  87.4 0.8 convert_add_fusion
  (3 shorter events, 0.0 us)
Async XLA Ops:
  0.0 39.5 %collective-permute-start.2 = (bf16[32,2048]{1,0:T(8,128)(2,1)}, bf16[32,2048]{1,0:T(8,128)(2,1)S(1)}, u32[]{:S(2)}, u32[]{:S(2)}) collective-permute-start(bf16[32,2048]{1,0:T(8,128)(2,1)} %rest_0_.1), channel_id=1, source_target_pairs={{0,4},{4,0},{8,12},{12,8},{16,20},{20,16},{24,28},{28,24},{1,5},{5... | collective-permute-start | bytes 393224 | tf_op jit(solution)/shard_map/ppermute | solution.py:292
  2.9 15.4 %collective-permute-start = (bf16[32,2048]{1,0:T(8,128)(2,1)}, bf16[32,2048]{1,0:T(8,128)(2,1)S(1)}, u32[]{:S(2)}, u32[]{:S(2)}) collective-permute-start(bf16[32,2048]{1,0:T(8,128)(2,1)} %rest_0_.1), channel_id=1, source_target_pairs={{0,8},{4,12},{8,16},{12,20},{16,24},{20,28},{24,0},{28,4},{1,9},{5... | collective-permute-start | bytes 393224 | tf_op jit(solution)/shard_map/ppermute | solution.py:292
  4.5 13.8 %collective-permute-start.5 = (bf16[32,2048]{1,0:T(8,128)(2,1)}, bf16[32,2048]{1,0:T(8,128)(2,1)S(1)}, u32[]{:S(2)}, u32[]{:S(2)}) collective-permute-start(bf16[32,2048]{1,0:T(8,128)(2,1)} %rest_0_.1), channel_id=1, source_target_pairs={{0,24},{4,28},{8,0},{12,4},{16,8},{20,12},{24,16},{28,20},{1,25},{... | collective-permute-start | bytes 393224 | tf_op jit(solution)/shard_map/ppermute | solution.py:292
  6.8 11.7 %collective-permute-start.3 = (bf16[32,2048]{1,0:T(8,128)(2,1)}, bf16[32,2048]{1,0:T(8,128)(2,1)S(1)}, u32[]{:S(2)}, u32[]{:S(2)}) collective-permute-start(bf16[32,2048]{1,0:T(8,128)(2,1)} %rest_0_.1), channel_id=1, source_target_pairs={{0,16},{4,20},{8,24},{12,28},{16,0},{20,4},{24,8},{28,12},{1,17},{... | collective-permute-start | bytes 393224 | tf_op jit(solution)/shard_map/ppermute | solution.py:292
  10.5 1.6 %copy-start.1 = (bf16[4096,256]{1,0:T(8,128)(2,1)S(1)}, bf16[4096,256]{1,0:T(8,128)(2,1)}, u32[]{:S(2)}) copy-start(bf16[4096,256]{1,0:T(8,128)(2,1)} %k_ref.7) | copy-start | bytes 6291460
  12.1 1.6 %copy-start.2 = (bf16[4096,256]{1,0:T(8,128)(2,1)S(1)}, bf16[4096,256]{1,0:T(8,128)(2,1)}, u32[]{:S(2)}) copy-start(bf16[4096,256]{1,0:T(8,128)(2,1)} %v_ref.7) | copy-start | bytes 6291460
  13.7 0.9 %copy-start.3 = (bf16[32,2048]{1,0:T(8,128)(2,1)S(1)}, bf16[32,2048]{1,0:T(8,128)(2,1)}, u32[]{:S(2)}) copy-start(bf16[32,2048]{1,0:T(8,128)(2,1)} %rest_0_.1) | copy-start | bytes 393220
  18.4 12.0 %collective-permute-start.6 = (bf16[32,2048]{1,0:T(8,128)(2,1)S(1)}, bf16[32,2048]{1,0:T(8,128)(2,1)S(1)}, u32[]{:S(2)}, u32[]{:S(2)}) collective-permute-start(bf16[32,2048]{1,0:T(8,128)(2,1)S(1)} %collective-permute-done.5.rest_0_), channel_id=1, source_target_pairs={{0,4},{4,0},{8,12},{12,8},{16,20},{20,16},{24,28},{28,24},{1,5},{5... | collective-permute-start | bytes 393224 | tf_op jit(solution)/shard_map/ppermute | solution.py:292
  19.1 12.5 %collective-permute-start.4 = (bf16[32,2048]{1,0:T(8,128)(2,1)S(1)}, bf16[32,2048]{1,0:T(8,128)(2,1)S(1)}, u32[]{:S(2)}, u32[]{:S(2)}) collective-permute-start(bf16[32,2048]{1,0:T(8,128)(2,1)S(1)} %collective-permute-done.3.rest_2_), channel_id=1, source_target_pairs={{0,4},{4,0},{8,12},{12,8},{16,20},{20,16},{24,28},{28,24},{1,5},{5... | collective-permute-start | bytes 393224 | tf_op jit(solution)/shard_map/ppermute | solution.py:292
  26.6 18.1 %collective-permute-start.7 = (bf16[32,2176]{1,0:T(8,128)(2,1)S(1)}, bf16[32,2176]{1,0:T(8,128)(2,1)S(1)}, u32[]{:S(2)}, u32[]{:S(2)}) collective-permute-start(bf16[32,2176]{1,0:T(8,128)(2,1)S(1)} %get-tuple-element.38), channel_id=1, source_target_pairs={{0,8},{4,12},{8,16},{12,20},{16,24},{20,28},{24,0},{28,4},{1,9},{5... | collective-permute-start | bytes 417800 | tf_op jit(solution)/shard_map/ppermute | solution.py:292
  29.0 15.7 %collective-permute-start.8 = (bf16[32,2176]{1,0:T(8,128)(2,1)S(1)}, bf16[32,2176]{1,0:T(8,128)(2,1)S(1)}, u32[]{:S(2)}, u32[]{:S(2)}) collective-permute-start(bf16[32,2176]{1,0:T(8,128)(2,1)S(1)} %get-tuple-element.39), channel_id=1, source_target_pairs={{0,24},{4,28},{8,0},{12,4},{16,8},{20,12},{24,16},{28,20},{1,25},{... | collective-permute-start | bytes 417800 | tf_op jit(solution)/shard_map/ppermute | solution.py:292
  30.4 21.8 %collective-permute-start.9 = (bf16[32,2176]{1,0:T(8,128)(2,1)S(1)}, bf16[32,2176]{1,0:T(8,128)(2,1)S(1)}, u32[]{:S(2)}, u32[]{:S(2)}) collective-permute-start(bf16[32,2176]{1,0:T(8,128)(2,1)S(1)} %get-tuple-element.32), channel_id=1, source_target_pairs={{0,16},{4,20},{8,24},{12,28},{16,0},{20,4},{24,8},{28,12},{1,17},{... | collective-permute-start | bytes 417800 | tf_op jit(solution)/shard_map/ppermute | solution.py:292
  31.6 10.1 %collective-permute-start.1 = (bf16[32,2048]{1,0:T(8,128)(2,1)S(1)}, bf16[32,2048]{1,0:T(8,128)(2,1)S(1)}, u32[]{:S(2)}, u32[]{:S(2)}) collective-permute-start(bf16[32,2048]{1,0:T(8,128)(2,1)S(1)} %collective-permute-done.rest_1_), channel_id=1, source_target_pairs={{0,4},{4,0},{8,12},{12,8},{16,20},{20,16},{24,28},{28,24},{1,5},{5... | collective-permute-start | bytes 393224 | tf_op jit(solution)/shard_map/ppermute | solution.py:292
  39.5 12.8 %collective-permute-start.11 = (bf16[32,2176]{1,0:T(8,128)(2,1)S(1)}, bf16[32,2176]{1,0:T(8,128)(2,1)S(1)}, u32[]{:S(2)}, u32[]{:S(2)}) collective-permute-start(bf16[32,2176]{1,0:T(8,128)(2,1)S(1)} %get-tuple-element.35), channel_id=1, source_target_pairs={{0,12},{4,8},{8,20},{12,16},{16,28},{20,24},{24,4},{28,0},{1,13},{... | collective-permute-start | bytes 417800 | tf_op jit(solution)/shard_map/ppermute | solution.py:292
  41.8 10.5 %collective-permute-start.13 = (bf16[32,2176]{1,0:T(8,128)(2,1)S(1)}, bf16[32,2176]{1,0:T(8,128)(2,1)S(1)}, u32[]{:S(2)}, u32[]{:S(2)}) collective-permute-start(bf16[32,2176]{1,0:T(8,128)(2,1)S(1)} %get-tuple-element.46), channel_id=1, source_target_pairs={{0,20},{4,16},{8,28},{12,24},{16,4},{20,0},{24,12},{28,8},{1,21},{... | collective-permute-start | bytes 417800 | tf_op jit(solution)/shard_map/ppermute | solution.py:292
  44.7 31.5 %copy-start = (bf16[2048,1024]{1,0:T(8,128)(2,1)S(1)}, bf16[2048,1024]{1,0:T(8,128)(2,1)}, u32[]{:S(2)}) copy-start(bf16[2048,1024]{1,0:T(8,128)(2,1)} %w_ref.1) | copy-start | bytes 12582916
  49.5 6.6 %collective-permute-start.10 = (bf16[32,2176]{1,0:T(8,128)(2,1)S(1)}, bf16[32,2176]{1,0:T(8,128)(2,1)S(1)}, u32[]{:S(2)}, u32[]{:S(2)}) collective-permute-start(bf16[32,2176]{1,0:T(8,128)(2,1)S(1)} %get-tuple-element.44), channel_id=1, source_target_pairs={{0,4},{4,0},{8,12},{12,8},{16,20},{20,16},{24,28},{28,24},{1,5},{5... | collective-permute-start | bytes 417800 | tf_op jit(solution)/shard_map/ppermute | solution.py:292
  49.9 6.3 %collective-permute-start.12 = (bf16[32,2176]{1,0:T(8,128)(2,1)S(1)}, bf16[32,2176]{1,0:T(8,128)(2,1)S(1)}, u32[]{:S(2)}, u32[]{:S(2)}) collective-permute-start(bf16[32,2176]{1,0:T(8,128)(2,1)S(1)} %get-tuple-element.45), channel_id=1, source_target_pairs={{0,28},{4,24},{8,4},{12,0},{16,12},{20,8},{24,20},{28,16},{1,29},{... | collective-permute-start | bytes 417800 | tf_op jit(solution)/shard_map/ppermute | solution.py:292
  57.2 8.8 %collective-permute-start.15 = (bf16[32,2048]{1,0:T(8,128)(2,1)S(1)}, bf16[32,2048]{1,0:T(8,128)(2,1)S(1)}, u32[]{:S(2)}, u32[]{:S(2)}) collective-permute-start(bf16[32,2048]{1,0:T(8,128)(2,1)S(1)} %merge.1.rest_0_), channel_id=1, source_target_pairs={{0,8},{4,12},{8,16},{12,20},{16,24},{20,28},{24,0},{28,4},{1,9},{5... | collective-permute-start | bytes 393224 | tf_op jit(solution)/shard_map/ppermute | solution.py:292
  63.4 6.4 %collective-permute-start.14 = (bf16[32,2048]{1,0:T(8,128)(2,1)S(1)}, bf16[32,2048]{1,0:T(8,128)(2,1)S(1)}, u32[]{:S(2)}, u32[]{:S(2)}) collective-permute-start(bf16[32,2048]{1,0:T(8,128)(2,1)S(1)} %merge.1.rest_0_), channel_id=1, source_target_pairs={{0,24},{4,28},{8,0},{12,4},{16,8},{20,12},{24,16},{28,20},{1,25},{... | collective-permute-start | bytes 393224 | tf_op jit(solution)/shard_map/ppermute | solution.py:292
  63.4 6.4 %collective-permute-start.16 = (bf16[32,2048]{1,0:T(8,128)(2,1)S(1)}, bf16[32,2048]{1,0:T(8,128)(2,1)S(1)}, u32[]{:S(2)}, u32[]{:S(2)}) collective-permute-start(bf16[32,2048]{1,0:T(8,128)(2,1)S(1)} %merge.1.rest_0_), channel_id=1, source_target_pairs={{0,16},{4,20},{8,24},{12,28},{16,0},{20,4},{24,8},{28,12},{1,17},{... | collective-permute-start | bytes 393224 | tf_op jit(solution)/shard_map/ppermute | solution.py:292
  65.9 5.0 %collective-permute-start.19 = (bf16[32,2048]{1,0:T(8,128)(2,1)S(1)}, bf16[32,2048]{1,0:T(8,128)(2,1)S(1)}, u32[]{:S(2)}, u32[]{:S(2)}) collective-permute-start(bf16[32,2048]{1,0:T(8,128)(2,1)S(1)} %collective-permute-done.15.rest_2_), channel_id=1, source_target_pairs={{0,4},{4,0},{8,12},{12,8},{16,20},{20,16},{24,28},{28,24},{1,5},{5... | collective-permute-start | bytes 393224 | tf_op jit(solution)/shard_map/ppermute | solution.py:292
  66.1 6.2 %collective-permute-start.17 = (bf16[32,2048]{1,0:T(8,128)(2,1)S(1)}, bf16[32,2048]{1,0:T(8,128)(2,1)S(1)}, u32[]{:S(2)}, u32[]{:S(2)}) collective-permute-start(bf16[32,2048]{1,0:T(8,128)(2,1)S(1)} %merge.1.rest_0_), channel_id=1, source_target_pairs={{0,4},{4,0},{8,12},{12,8},{16,20},{20,16},{24,28},{28,24},{1,5},{5... | collective-permute-start | bytes 393224 | tf_op jit(solution)/shard_map/ppermute | solution.py:292
  69.8 5.0 %collective-permute-start.18 = (bf16[32,2048]{1,0:T(8,128)(2,1)S(1)}, bf16[32,2048]{1,0:T(8,128)(2,1)S(1)}, u32[]{:S(2)}, u32[]{:S(2)}) collective-permute-start(bf16[32,2048]{1,0:T(8,128)(2,1)S(1)} %collective-permute-done.14.rest_1_), channel_id=1, source_target_pairs={{0,4},{4,0},{8,12},{12,8},{16,20},{20,16},{24,28},{28,24},{1,5},{5... | collective-permute-start | bytes 393224 | tf_op jit(solution)/shard_map/ppermute | solution.py:292
  70.9 5.3 %collective-permute-start.20 = (bf16[32,2048]{1,0:T(8,128)(2,1)S(1)}, bf16[32,2048]{1,0:T(8,128)(2,1)S(1)}, u32[]{:S(2)}, u32[]{:S(2)}) collective-permute-start(bf16[32,2048]{1,0:T(8,128)(2,1)S(1)} %collective-permute-done.16.rest_3_), channel_id=1, source_target_pairs={{0,4},{4,0},{8,12},{12,8},{16,20},{20,16},{24,28},{28,24},{1,5},{5... | collective-permute-start | bytes 393224 | tf_op jit(solution)/shard_map/ppermute | solution.py:292
  77.6 3.3 %collective-permute-start.21 = (bf16[64,1024]{1,0:T(8,128)(2,1)S(1)}, bf16[64,1024]{1,0:T(8,128)(2,1)S(1)}, u32[]{:S(2)}, u32[]{:S(2)}) collective-permute-start(bf16[64,1024]{1,0:T(8,128)(2,1)S(1)} %get-tuple-element.50), channel_id=1, source_target_pairs={{0,1},{1,0},{2,3},{3,2},{4,5},{5,4},{6,7},{7,6},{8,9},{9,8},{10,11... | collective-permute-start | bytes 393224 | tf_op jit(solution)/shard_map/ppermute | solution.py:351
  77.6 7.5 %collective-permute-start.22 = (bf16[64,1024]{1,0:T(8,128)(2,1)S(1)}, bf16[64,1024]{1,0:T(8,128)(2,1)S(1)}, u32[]{:S(2)}, u32[]{:S(2)}) collective-permute-start(bf16[64,1024]{1,0:T(8,128)(2,1)S(1)} %get-tuple-element.51), channel_id=1, source_target_pairs={{0,2},{1,3},{2,0},{3,1},{4,6},{5,7},{6,4},{7,5},{8,10},{9,11},{10,... | collective-permute-start | bytes 393224 | tf_op jit(solution)/shard_map/ppermute | solution.py:351
  80.8 6.6 %collective-permute-start.23 = (bf16[64,1024]{1,0:T(8,128)(2,1)S(1)}, bf16[64,1024]{1,0:T(8,128)(2,1)S(1)}, u32[]{:S(2)}, u32[]{:S(2)}) collective-permute-start(bf16[64,1024]{1,0:T(8,128)(2,1)S(1)} %get-tuple-element.52), channel_id=1, source_target_pairs={{0,3},{1,2},{2,1},{3,0},{4,7},{5,6},{6,5},{7,4},{8,11},{9,10},{10,... | collective-permute-start | bytes 393224 | tf_op jit(solution)/shard_map/ppermute | solution.py:351

commit v2 on v1

--- a/solution.py
+++ b/solution.py
@@ -308,10 +308,13 @@
         return held
 
     held = gather(queries, False)
-    near = [m for m in order[1:] if not m[1]]
-    far = sorted((m for m in order if m[1]), key=lambda m: -min(m[0], high - m[0]))
-    groups = [order[:1]] + [near[i : i + 3] for i in range(0, len(near), 3)]
-    groups += [far[i : i + 2] for i in range(0, len(far), 2)]
+    near = [m for m in order[1:] if not m[1] and 2 * m[0] != high]
+    middle = [m for m in order[1:] if not m[1] and 2 * m[0] == high]
+    flip = [m for m in order if m[1] and m[0] and 2 * m[0] != high]
+    late = [m for m in order if m[1] and 2 * m[0] == high] + [(0, 1)]
+    groups = [near[i : i + 2] for i in range(0, len(near), 2)]
+    groups += [middle + flip[:2]] + [flip[i : i + 2] for i in range(2, len(flip), 2)]
+    groups += [late, order[:1]]
     kv_local = new_keys.shape[1] // DH
     table = jnp.concatenate([keep_tiles.reshape(-1), tile_count.reshape(-1), owner_slot])
     new_rows = jnp.concatenate([new_keys, new_values], 1)
@@ -335,7 +338,7 @@
         blocks = [held[m] for m in members]
         if last is not None:
             blocks, parts[last] = lax.optimization_barrier((blocks, parts[last]))
-        if index >= 3:
+        if 2 <= index < len(groups) - 1:
             returned = {m: back[m] for m in groups[index - 2] if 2 * m[0] != high}
             blocks, returned = lax.optimization_barrier((blocks, returned))
             back.update(returned)

time: 88.2 us -> 90.5 us (1.026)
  starting transfers between devices: 39.8 us -> 31.8 us
  waiting for transfers between devices: 18.9 us -> 25.4 us
  Pallas kernels: 21.6 us -> 26.1 us
    ppermute x21, waiting for transfers between devices: 12.3 us -> 19 us  [move(): return lax.ppermute(x, 'ctx', pairs)]
    ppermute x21, starting transfers between devices: 36.5 us -> 29.9 us  [move(): return lax.ppermute(x, 'ctx', pairs)]
    pallas_call x4, Pallas kernels: 19.3 us -> 23.7 us  [attention_call(): pl.pallas_call(functools.partial(attention_kernel, members, ctx_count, gr...]
    ppermute x3, starting transfers between devices: 3.3 us -> 1.93 us  [body(): got = lax.ppermute(piece, 'tp', [(i, i ^ j) for i in range(peers)])]
  transfers between devices with their start and end apart: 24 -> 24, of which waited for: 11 -> 9; matrix products, arithmetic and copies ran while one was open for 3% -> 3% of each run, Pallas kernels for 22% -> 26%
where the time goes in v2:
time: 90.5 us; the launch traced here: 90.2 us
  starting transfers between devices  31.8 us (35%)
  Pallas kernels  26.1 us (29%)
  waiting for transfers between devices  25.4 us (28%)
  local copies, waits for them, and re-layouts  5.39 us (6%)
  other arithmetic  1.51 us (2%)
    ppermute x21, starting transfers between devices, move(): return lax.ppermute(x, 'ctx', pairs)  29.9 us
    pallas_call x4, Pallas kernels, attention_call(): pl.pallas_call(functools.partial(attention_kernel, members, ctx_count, gr...  23.7 us
    ppermute x21, waiting for transfers between devices, move(): return lax.ppermute(x, 'ctx', pairs)  19 us
    ppermute x3, waiting for transfers between devices, body(): got = lax.ppermute(piece, 'tp', [(i, i ^ j) for i in range(peers)])  6.4 us
    unnamed x9, local copies, waits for them, and re-layouts  3.91 us
    ppermute x3, starting transfers between devices, body(): got = lax.ppermute(piece, 'tp', [(i, i ^ j) for i in range(peers)])  1.93 us
  transfers between devices with their start and end apart: 24, of which 9 were waited for; matrix products, arithmetic and copies ran while one was open for 3% of the time, Pallas kernels for 26%

profile of v2, /device:TPU:0, one launch (start us, length us, event | category | flops | bytes accessed | tf_op | source)
XLA Modules:
  0.0 90.2 jit_solution(11010453841170255222)
XLA Ops:
  0.0 5.0 %collective-permute-start.3 = (bf16[32,2048]{1,0:T(8,128)(2,1)}, bf16[32,2048]{1,0:T(8,128)(2,1)S(1)}, u32[]{:S(2)}, u32[]{:S(2)}) collective-permute-start(bf16[32,2048]{1,0:T(8,128)(2,1)} %rest_0_), channel_id=1, source_target_pairs={{0,24},{4,28},{8,0},{12,4},{16,8},{20,12},{24,16},{28,20},{1,25},{... | collective-permute-start | bytes 393224 | tf_op jit(solution)/shard_map/ppermute | solution.py:292
  5.0 1.5 %collective-permute-start.2 = (bf16[32,2048]{1,0:T(8,128)(2,1)}, bf16[32,2048]{1,0:T(8,128)(2,1)S(1)}, u32[]{:S(2)}, u32[]{:S(2)}) collective-permute-start(bf16[32,2048]{1,0:T(8,128)(2,1)} %rest_0_), channel_id=1, source_target_pairs={{0,4},{4,0},{8,12},{12,8},{16,20},{20,16},{24,28},{28,24},{1,5},{5... | collective-permute-start | bytes 393224 | tf_op jit(solution)/shard_map/ppermute | solution.py:292
  6.5 0.0 collective-permute-start
  6.5 1.0 %collective-permute-start.5 = (bf16[32,2048]{1,0:T(8,128)(2,1)}, bf16[32,2048]{1,0:T(8,128)(2,1)S(1)}, u32[]{:S(2)}, u32[]{:S(2)}) collective-permute-start(bf16[32,2048]{1,0:T(8,128)(2,1)} %rest_0_), channel_id=1, source_target_pairs={{0,8},{4,12},{8,16},{12,20},{16,24},{20,28},{24,0},{28,4},{1,9},{5... | collective-permute-start | bytes 393224 | tf_op jit(solution)/shard_map/ppermute | solution.py:292
  7.6 0.8 reshape.6
  8.3 0.7 constant_dynamic-update-slice_fusion.1
  9.0 0.7 pad_add_fusion.table_ref
  9.8 0.7 constant_dynamic-update-slice_fusion.new_ref
  10.5 0.0 collective-permute-done.3.rest_0_
  10.5 0.5 collective-permute-start.4
  11.0 3.6 %collective-permute-done.5.rest_1_ = bf16[32,2048]{1,0:T(8,128)(2,1)S(1)} collective-permute-done((bf16[32,2048]{1,0:T(8,128)(2,1)}, bf16[32,2048]{1,0:T(8,128)(2,1)S(1)}, u32[]{:S(2)}, u32[]{:S(2)}) %collective-permute-start.5) | collective-permute-done | bytes 131104 | tf_op jit(solution)/shard_map/ppermute | solution.py:292
  14.6 1.5 %collective-permute-start.6 = (bf16[32,2048]{1,0:T(8,128)(2,1)S(1)}, bf16[32,2048]{1,0:T(8,128)(2,1)S(1)}, u32[]{:S(2)}, u32[]{:S(2)}) collective-permute-start(bf16[32,2048]{1,0:T(8,128)(2,1)S(1)} %collective-permute-done.5.rest_1_), channel_id=1, source_target_pairs={{0,4},{4,0},{8,12},{12,8},{16,20},{20,16},{24,28},{28,24},{1,5},{5... | collective-permute-start | bytes 393224 | tf_op jit(solution)/shard_map/ppermute | solution.py:292
  16.1 1.6 %copy-done.1 = bf16[4096,256]{1,0:T(8,128)(2,1)S(1)} copy-done((bf16[4096,256]{1,0:T(8,128)(2,1)S(1)}, bf16[4096,256]{1,0:T(8,128)(2,1)}, u32[]{:S(2)}) %copy-start.1) | copy-done | bytes 2097176
  17.7 1.6 %copy-done.2 = bf16[4096,256]{1,0:T(8,128)(2,1)S(1)} copy-done((bf16[4096,256]{1,0:T(8,128)(2,1)S(1)}, bf16[4096,256]{1,0:T(8,128)(2,1)}, u32[]{:S(2)}) %copy-start.2) | copy-done | bytes 2097176
  19.3 5.8 %attention.4 = (bf16[32,2176]{1,0:T(8,128)(2,1)S(1)}, bf16[32,2176]{1,0:T(8,128)(2,1)S(1)}) custom-call(s32[58]{0:T(128)S(1)} %pad_add_fusion.table_ref, bf16[32,512]{1,0:T(8,128)(2,1)S(1)} %constant_dynamic-update-slice_fusion.new_ref, bf16[4096,256]{1,0:T(8,128)(2,1)S(1)} %copy-done.1, bf16[4096,256]{1,0:T(8,128)(2,1)S(1)} %copy-done.2, ...), custom_call_target="tpu_custom_call" | custom-call | flops 3221225472 | bytes 8388608 | tf_op jit(solution)/shard_map/attention/pallas_call | solution.py:155
  25.1 3.3 %collective-permute-start.7 = (bf16[32,2176]{1,0:T(8,128)(2,1)S(1)}, bf16[32,2176]{1,0:T(8,128)(2,1)S(1)}, u32[]{:S(2)}, u32[]{:S(2)}) collective-permute-start(bf16[32,2176]{1,0:T(8,128)(2,1)S(1)} %get-tuple-element.35), channel_id=1, source_target_pairs={{0,8},{4,12},{8,16},{12,20},{16,24},{20,28},{24,0},{28,4},{1,9},{5... | collective-permute-start | bytes 417800 | tf_op jit(solution)/shard_map/ppermute | solution.py:292
  28.5 0.0 collective-permute-done.rest_0_
  28.5 0.5 collective-permute-start.8
  29.0 0.0 collective-permute-done.4.rest_1_
  29.0 0.9 %collective-permute-start.1 = (bf16[32,2048]{1,0:T(8,128)(2,1)S(1)}, bf16[32,2048]{1,0:T(8,128)(2,1)S(1)}, u32[]{:S(2)}, u32[]{:S(2)}) collective-permute-start(bf16[32,2048]{1,0:T(8,128)(2,1)S(1)} %collective-permute-done.rest_0_), channel_id=1, source_target_pairs={{0,4},{4,0},{8,12},{12,8},{16,20},{20,16},{24,28},{28,24},{1,5},{5... | collective-permute-start | bytes 393224 | tf_op jit(solution)/shard_map/ppermute | solution.py:292
  29.9 0.0 collective-permute-done.6.rest_2_
  30.0 7.7 %attention.5 = (bf16[32,2176]{1,0:T(8,128)(2,1)S(1)}, bf16[32,2176]{1,0:T(8,128)(2,1)S(1)}, bf16[32,2176]{1,0:T(8,128)(2,1)S(1)}) custom-call(s32[58]{0:T(128)S(1)} %pad_add_fusion.table_ref, bf16[32,512]{1,0:T(8,128)(2,1)S(1)} %constant_dynamic-update-slice_fusion.new_ref, bf16[4096,256]{1,0:T(8,128)(2,1)S(1)} %copy-done.1, ...), custom_call_target="tpu_custom_call" | custom-call | flops 4831838208 | bytes 8388608 | tf_op jit(solution)/shard_map/attention/pallas_call | solution.py:155
  37.6 3.9 %collective-permute-start.12 = (bf16[32,2176]{1,0:T(8,128)(2,1)S(1)}, bf16[32,2176]{1,0:T(8,128)(2,1)S(1)}, u32[]{:S(2)}, u32[]{:S(2)}) collective-permute-start(bf16[32,2176]{1,0:T(8,128)(2,1)S(1)} %get-tuple-element.32), channel_id=1, source_target_pairs={{0,28},{4,24},{8,4},{12,0},{16,12},{20,8},{24,20},{28,16},{1,29},{... | collective-permute-start | bytes 417800 | tf_op jit(solution)/shard_map/ppermute | solution.py:292
  41.5 0.0 collective-permute-done.2.rest_1_
  41.5 0.0 collective-permute-done.1.rest_0_
  41.5 0.0 collective-permute-start.9
  41.5 0.0 copy-start.3
  41.5 1.2 %collective-permute-start.11 = (bf16[32,2176]{1,0:T(8,128)(2,1)S(1)}, bf16[32,2176]{1,0:T(8,128)(2,1)S(1)}, u32[]{:S(2)}, u32[]{:S(2)}) collective-permute-start(bf16[32,2176]{1,0:T(8,128)(2,1)S(1)} %get-tuple-element.43), channel_id=1, source_target_pairs={{0,12},{4,8},{8,20},{12,16},{16,28},{20,24},{24,4},{28,0},{1,13},{... | collective-permute-start | bytes 417800 | tf_op jit(solution)/shard_map/ppermute | solution.py:292
  42.8 0.0 collective-permute-done.7.refs_1_
  42.8 0.0 collective-permute-done.8.refs_2_
  42.8 5.8 %attention.6 = (bf16[32,2176]{1,0:T(8,128)(2,1)S(1)}, bf16[32,2176]{1,0:T(8,128)(2,1)S(1)}) custom-call(s32[58]{0:T(128)S(1)} %pad_add_fusion.table_ref, bf16[32,512]{1,0:T(8,128)(2,1)S(1)} %constant_dynamic-update-slice_fusion.new_ref, bf16[4096,256]{1,0:T(8,128)(2,1)S(1)} %copy-done.1, bf16[4096,256]{1,0:T(8,128)(2,1)S(1)} %copy-done.2, ...), custom_call_target="tpu_custom_call" | custom-call | flops 3221225472 | bytes 8388608 | tf_op jit(solution)/shard_map/attention/pallas_call | solution.py:155
  48.6 1.6 %collective-permute-start.10 = (bf16[32,2176]{1,0:T(8,128)(2,1)S(1)}, bf16[32,2176]{1,0:T(8,128)(2,1)S(1)}, u32[]{:S(2)}, u32[]{:S(2)}) collective-permute-start(bf16[32,2176]{1,0:T(8,128)(2,1)S(1)} %get-tuple-element.38), channel_id=1, source_target_pairs={{0,4},{4,0},{8,12},{12,8},{16,20},{20,16},{24,28},{28,24},{1,5},{5... | collective-permute-start | bytes 417800 | tf_op jit(solution)/shard_map/ppermute | solution.py:292
  50.2 0.9 collective-permute-start.13
  51.1 0.0 copy-done.3
  51.1 4.4 %attention.7.refs_0_ = bf16[32,2176]{1,0:T(8,128)(2,1)S(1)} custom-call(s32[58]{0:T(128)S(1)} %pad_add_fusion.table_ref, bf16[32,512]{1,0:T(8,128)(2,1)S(1)} %constant_dynamic-update-slice_fusion.new_ref, bf16[4096,256]{1,0:T(8,128)(2,1)S(1)} %copy-done.1, bf16[4096,256]{1,0:T(8,128)(2,1)S(1)} %copy-done.2, bf16[32,2048]{1,0:T(8,128)(2,1)S(1)} %copy-done.3), custom_call_target="tpu_custom_call" | custom-call | flops 1610612736 | bytes 8388608 | tf_op jit(solution)/shard_map/attention/pallas_call | solution.py:155
  55.6 0.0 collective-permute-done.9.refs_3_
  55.6 0.0 collective-permute-done.11.refs_5_
  55.6 0.0 collective-permute-done.12.refs_6_
  55.6 3.7 %collective-permute-done.13.refs_7_ = bf16[32,2176]{1,0:T(8,128)(2,1)S(1)} collective-permute-done((bf16[32,2176]{1,0:T(8,128)(2,1)S(1)}, bf16[32,2176]{1,0:T(8,128)(2,1)S(1)}, u32[]{:S(2)}, u32[]{:S(2)}) %collective-permute-start.13) | collective-permute-done | bytes 139296 | tf_op jit(solution)/shard_map/ppermute | solution.py:292
  59.3 0.0 collective-permute-done.10.refs_4_
  59.3 0.9 %merge.1.rest_0_ = bf16[32,2048]{1,0:T(8,128)(2,1)S(1)} custom-call(bf16[32,2176]{1,0:T(8,128)(2,1)S(1)} %attention.7.refs_0_, bf16[32,2176]{1,0:T(8,128)(2,1)S(1)} %collective-permute-done.7.refs_1_, bf16[32,2176]{1,0:T(8,128)(2,1)S(1)} %collective-permute-done.8.refs_2_, bf16[32,2176]{1,0:T(8,128)(2,1)S(1)} %collective-permute-done.9.refs_3_, ...), custom_call_target="tpu_custom_call" | custom-call | flops 1114112 | bytes 1114112 | tf_op jit(solution)/shard_map/merge/pallas_call | solution.py:213
  60.2 0.8 collective-permute-start.15
  61.0 3.1 %collective-permute-start.14 = (bf16[32,2048]{1,0:T(8,128)(2,1)S(1)}, bf16[32,2048]{1,0:T(8,128)(2,1)S(1)}, u32[]{:S(2)}, u32[]{:S(2)}) collective-permute-start(bf16[32,2048]{1,0:T(8,128)(2,1)S(1)} %merge.1.rest_0_), channel_id=1, source_target_pairs={{0,24},{4,28},{8,0},{12,4},{16,8},{20,12},{24,16},{28,20},{1,25},{... | collective-permute-start | bytes 393224 | tf_op jit(solution)/shard_map/ppermute | solution.py:292
  64.1 0.0 collective-permute-start.16
  64.1 4.4 %collective-permute-done.15.rest_2_ = bf16[32,2048]{1,0:T(8,128)(2,1)S(1)} collective-permute-done((bf16[32,2048]{1,0:T(8,128)(2,1)S(1)}, bf16[32,2048]{1,0:T(8,128)(2,1)S(1)}, u32[]{:S(2)}, u32[]{:S(2)}) %collective-permute-start.15) | collective-permute-done | bytes 131104 | tf_op jit(solution)/shard_map/ppermute | solution.py:292
  68.5 1.1 %collective-permute-start.19 = (bf16[32,2048]{1,0:T(8,128)(2,1)S(1)}, bf16[32,2048]{1,0:T(8,128)(2,1)S(1)}, u32[]{:S(2)}, u32[]{:S(2)}) collective-permute-start(bf16[32,2048]{1,0:T(8,128)(2,1)S(1)} %collective-permute-done.15.rest_2_), channel_id=1, source_target_pairs={{0,4},{4,0},{8,12},{12,8},{16,20},{20,16},{24,28},{28,24},{1,5},{5... | collective-permute-start | bytes 393224 | tf_op jit(solution)/shard_map/ppermute | solution.py:292
  69.6 1.0 %collective-permute-start.17 = (bf16[32,2048]{1,0:T(8,128)(2,1)S(1)}, bf16[32,2048]{1,0:T(8,128)(2,1)S(1)}, u32[]{:S(2)}, u32[]{:S(2)}) collective-permute-start(bf16[32,2048]{1,0:T(8,128)(2,1)S(1)} %merge.1.rest_0_), channel_id=1, source_target_pairs={{0,4},{4,0},{8,12},{12,8},{16,20},{20,16},{24,28},{28,24},{1,5},{5... | collective-permute-start | bytes 393224 | tf_op jit(solution)/shard_map/ppermute | solution.py:292
  70.5 0.0 collective-permute-done.14.rest_1_
  70.5 1.1 %collective-permute-start.18 = (bf16[32,2048]{1,0:T(8,128)(2,1)S(1)}, bf16[32,2048]{1,0:T(8,128)(2,1)S(1)}, u32[]{:S(2)}, u32[]{:S(2)}) collective-permute-start(bf16[32,2048]{1,0:T(8,128)(2,1)S(1)} %collective-permute-done.14.rest_1_), channel_id=1, source_target_pairs={{0,4},{4,0},{8,12},{12,8},{16,20},{20,16},{24,28},{28,24},{1,5},{5... | collective-permute-start | bytes 393224 | tf_op jit(solution)/shard_map/ppermute | solution.py:292
  71.6 2.8 %collective-permute-done.16.rest_3_ = bf16[32,2048]{1,0:T(8,128)(2,1)S(1)} collective-permute-done((bf16[32,2048]{1,0:T(8,128)(2,1)S(1)}, bf16[32,2048]{1,0:T(8,128)(2,1)S(1)}, u32[]{:S(2)}, u32[]{:S(2)}) %collective-permute-start.16) | collective-permute-done | bytes 131104 | tf_op jit(solution)/shard_map/ppermute | solution.py:292
  74.5 0.0 collective-permute-done.19.rest_6_
  74.5 0.9 collective-permute-start.20
  75.4 0.1 collective-permute-done.17.rest_4_
  75.5 1.4 %collective-permute-done.18.rest_5_ = bf16[32,2048]{1,0:T(8,128)(2,1)S(1)} collective-permute-done((bf16[32,2048]{1,0:T(8,128)(2,1)S(1)}, bf16[32,2048]{1,0:T(8,128)(2,1)S(1)}, u32[]{:S(2)}, u32[]{:S(2)}) %collective-permute-start.18) | collective-permute-done | bytes 131104 | tf_op jit(solution)/shard_map/ppermute | solution.py:292
  76.9 2.9 %collective-permute-done.20.rest_7_ = bf16[32,2048]{1,0:T(8,128)(2,1)S(1)} collective-permute-done((bf16[32,2048]{1,0:T(8,128)(2,1)S(1)}, bf16[32,2048]{1,0:T(8,128)(2,1)S(1)}, u32[]{:S(2)}, u32[]{:S(2)}) %collective-permute-start.20) | collective-permute-done | bytes 131104 | tf_op jit(solution)/shard_map/ppermute | solution.py:292
  79.7 0.0 copy-done
  79.8 1.4 %projection.1 = (f32[64,1024]{1,0:T(8,128)S(1)}, bf16[64,1024]{1,0:T(8,128)(2,1)S(1)}, bf16[64,1024]{1,0:T(8,128)(2,1)S(1)}, bf16[64,1024]{1,0:T(8,128)(2,1)S(1)}) custom-call(bf16[2048,1024]{1,0:T(8,128)(2,1)S(1)} %copy-done, bf16[32,2048]{1,0:T(8,128)(2,1)S(1)} %merge.1.rest_0_, bf16[32,2048]{1,0:T(8,128)(2,1)S(1)} %collective-permute-done.14.rest_1_, ...), custom_call_target="tpu_custom_call" | custom-call | flops 1073741824 | bytes 4194304 | tf_op jit(solution)/shard_map/projection/pallas_call | solution.py:252
  81.1 0.1 collective-permute-start.21
  81.2 0.9 %collective-permute-start.22 = (bf16[64,1024]{1,0:T(8,128)(2,1)S(1)}, bf16[64,1024]{1,0:T(8,128)(2,1)S(1)}, u32[]{:S(2)}, u32[]{:S(2)}) collective-permute-start(bf16[64,1024]{1,0:T(8,128)(2,1)S(1)} %get-tuple-element.49), channel_id=1, source_target_pairs={{0,2},{1,3},{2,0},{3,1},{4,6},{5,7},{6,4},{7,5},{8,10},{9,11},{10,... | collective-permute-start | bytes 393224 | tf_op jit(solution)/shard_map/ppermute | solution.py:354
  82.1 0.9 %collective-permute-start.23 = (bf16[64,1024]{1,0:T(8,128)(2,1)S(1)}, bf16[64,1024]{1,0:T(8,128)(2,1)S(1)}, u32[]{:S(2)}, u32[]{:S(2)}) collective-permute-start(bf16[64,1024]{1,0:T(8,128)(2,1)S(1)} %get-tuple-element.50), channel_id=1, source_target_pairs={{0,3},{1,2},{2,1},{3,0},{4,7},{5,6},{6,5},{7,4},{8,11},{9,10},{10,... | collective-permute-start | bytes 393224 | tf_op jit(solution)/shard_map/ppermute | solution.py:354
  83.1 0.0 collective-permute-done.21
  83.1 4.5 %collective-permute-done.22 = bf16[64,1024]{1,0:T(8,128)(2,1)S(1)} collective-permute-done((bf16[64,1024]{1,0:T(8,128)(2,1)S(1)}, bf16[64,1024]{1,0:T(8,128)(2,1)S(1)}, u32[]{:S(2)}, u32[]{:S(2)}) %collective-permute-start.22) | collective-permute-done | bytes 131104 | tf_op jit(solution)/shard_map/ppermute | solution.py:354
  87.6 1.9 %collective-permute-done.23 = bf16[64,1024]{1,0:T(8,128)(2,1)S(1)} collective-permute-done((bf16[64,1024]{1,0:T(8,128)(2,1)S(1)}, bf16[64,1024]{1,0:T(8,128)(2,1)S(1)}, u32[]{:S(2)}, u32[]{:S(2)}) %collective-permute-start.23) | collective-permute-done | bytes 131104 | tf_op jit(solution)/shard_map/ppermute | solution.py:354
  89.5 0.8 convert_add_fusion
  (3 shorter events, 0.0 us)
Async XLA Ops:
  0.0 10.5 %collective-permute-start.3 = (bf16[32,2048]{1,0:T(8,128)(2,1)}, bf16[32,2048]{1,0:T(8,128)(2,1)S(1)}, u32[]{:S(2)}, u32[]{:S(2)}) collective-permute-start(bf16[32,2048]{1,0:T(8,128)(2,1)} %rest_0_), channel_id=1, source_target_pairs={{0,24},{4,28},{8,0},{12,4},{16,8},{20,12},{24,16},{28,20},{1,25},{... | collective-permute-start | bytes 393224 | tf_op jit(solution)/shard_map/ppermute | solution.py:292
  5.0 36.4 %collective-permute-start.2 = (bf16[32,2048]{1,0:T(8,128)(2,1)}, bf16[32,2048]{1,0:T(8,128)(2,1)S(1)}, u32[]{:S(2)}, u32[]{:S(2)}) collective-permute-start(bf16[32,2048]{1,0:T(8,128)(2,1)} %rest_0_), channel_id=1, source_target_pairs={{0,4},{4,0},{8,12},{12,8},{16,20},{20,16},{24,28},{28,24},{1,5},{5... | collective-permute-start | bytes 393224 | tf_op jit(solution)/shard_map/ppermute | solution.py:292
  6.5 21.9 %collective-permute-start = (bf16[32,2048]{1,0:T(8,128)(2,1)}, bf16[32,2048]{1,0:T(8,128)(2,1)S(1)}, u32[]{:S(2)}, u32[]{:S(2)}) collective-permute-start(bf16[32,2048]{1,0:T(8,128)(2,1)} %rest_0_), channel_id=1, source_target_pairs={{0,16},{4,20},{8,24},{12,28},{16,0},{20,4},{24,8},{28,12},{1,17},{... | collective-permute-start | bytes 393224 | tf_op jit(solution)/shard_map/ppermute | solution.py:292
  6.5 8.1 %collective-permute-start.5 = (bf16[32,2048]{1,0:T(8,128)(2,1)}, bf16[32,2048]{1,0:T(8,128)(2,1)S(1)}, u32[]{:S(2)}, u32[]{:S(2)}) collective-permute-start(bf16[32,2048]{1,0:T(8,128)(2,1)} %rest_0_), channel_id=1, source_target_pairs={{0,8},{4,12},{8,16},{12,20},{16,24},{20,28},{24,0},{28,4},{1,9},{5... | collective-permute-start | bytes 393224 | tf_op jit(solution)/shard_map/ppermute | solution.py:292
  10.5 18.5 %collective-permute-start.4 = (bf16[32,2048]{1,0:T(8,128)(2,1)S(1)}, bf16[32,2048]{1,0:T(8,128)(2,1)S(1)}, u32[]{:S(2)}, u32[]{:S(2)}) collective-permute-start(bf16[32,2048]{1,0:T(8,128)(2,1)S(1)} %collective-permute-done.3.rest_0_), channel_id=1, source_target_pairs={{0,4},{4,0},{8,12},{12,8},{16,20},{20,16},{24,28},{28,24},{1,5},{5... | collective-permute-start | bytes 393224 | tf_op jit(solution)/shard_map/ppermute | solution.py:292
  14.6 15.3 %collective-permute-start.6 = (bf16[32,2048]{1,0:T(8,128)(2,1)S(1)}, bf16[32,2048]{1,0:T(8,128)(2,1)S(1)}, u32[]{:S(2)}, u32[]{:S(2)}) collective-permute-start(bf16[32,2048]{1,0:T(8,128)(2,1)S(1)} %collective-permute-done.5.rest_1_), channel_id=1, source_target_pairs={{0,4},{4,0},{8,12},{12,8},{16,20},{20,16},{24,28},{28,24},{1,5},{5... | collective-permute-start | bytes 393224 | tf_op jit(solution)/shard_map/ppermute | solution.py:292
  16.1 1.6 %copy-start.1 = (bf16[4096,256]{1,0:T(8,128)(2,1)S(1)}, bf16[4096,256]{1,0:T(8,128)(2,1)}, u32[]{:S(2)}) copy-start(bf16[4096,256]{1,0:T(8,128)(2,1)} %k_ref.7) | copy-start | bytes 6291460
  17.7 1.6 %copy-start.2 = (bf16[4096,256]{1,0:T(8,128)(2,1)S(1)}, bf16[4096,256]{1,0:T(8,128)(2,1)}, u32[]{:S(2)}) copy-start(bf16[4096,256]{1,0:T(8,128)(2,1)} %v_ref.7) | copy-start | bytes 6291460
  25.1 17.6 %collective-permute-start.7 = (bf16[32,2176]{1,0:T(8,128)(2,1)S(1)}, bf16[32,2176]{1,0:T(8,128)(2,1)S(1)}, u32[]{:S(2)}, u32[]{:S(2)}) collective-permute-start(bf16[32,2176]{1,0:T(8,128)(2,1)S(1)} %get-tuple-element.35), channel_id=1, source_target_pairs={{0,8},{4,12},{8,16},{12,20},{16,24},{20,28},{24,0},{28,4},{1,9},{5... | collective-permute-start | bytes 417800 | tf_op jit(solution)/shard_map/ppermute | solution.py:292
  28.5 14.3 %collective-permute-start.8 = (bf16[32,2176]{1,0:T(8,128)(2,1)S(1)}, bf16[32,2176]{1,0:T(8,128)(2,1)S(1)}, u32[]{:S(2)}, u32[]{:S(2)}) collective-permute-start(bf16[32,2176]{1,0:T(8,128)(2,1)S(1)} %get-tuple-element.28), channel_id=1, source_target_pairs={{0,24},{4,28},{8,0},{12,4},{16,8},{20,12},{24,16},{28,20},{1,25},{... | collective-permute-start | bytes 417800 | tf_op jit(solution)/shard_map/ppermute | solution.py:292
  29.0 12.5 %collective-permute-start.1 = (bf16[32,2048]{1,0:T(8,128)(2,1)S(1)}, bf16[32,2048]{1,0:T(8,128)(2,1)S(1)}, u32[]{:S(2)}, u32[]{:S(2)}) collective-permute-start(bf16[32,2048]{1,0:T(8,128)(2,1)S(1)} %collective-permute-done.rest_0_), channel_id=1, source_target_pairs={{0,4},{4,0},{8,12},{12,8},{16,20},{20,16},{24,28},{28,24},{1,5},{5... | collective-permute-start | bytes 393224 | tf_op jit(solution)/shard_map/ppermute | solution.py:292
  37.6 18.0 %collective-permute-start.12 = (bf16[32,2176]{1,0:T(8,128)(2,1)S(1)}, bf16[32,2176]{1,0:T(8,128)(2,1)S(1)}, u32[]{:S(2)}, u32[]{:S(2)}) collective-permute-start(bf16[32,2176]{1,0:T(8,128)(2,1)S(1)} %get-tuple-element.32), channel_id=1, source_target_pairs={{0,28},{4,24},{8,4},{12,0},{16,12},{20,8},{24,20},{28,16},{1,29},{... | collective-permute-start | bytes 417800 | tf_op jit(solution)/shard_map/ppermute | solution.py:292
  41.5 14.1 %collective-permute-start.9 = (bf16[32,2176]{1,0:T(8,128)(2,1)S(1)}, bf16[32,2176]{1,0:T(8,128)(2,1)S(1)}, u32[]{:S(2)}, u32[]{:S(2)}) collective-permute-start(bf16[32,2176]{1,0:T(8,128)(2,1)S(1)} %get-tuple-element.42), channel_id=1, source_target_pairs={{0,16},{4,20},{8,24},{12,28},{16,0},{20,4},{24,8},{28,12},{1,17},{... | collective-permute-start | bytes 417800 | tf_op jit(solution)/shard_map/ppermute | solution.py:292
  41.5 9.6 %copy-start.3 = (bf16[32,2048]{1,0:T(8,128)(2,1)S(1)}, bf16[32,2048]{1,0:T(8,128)(2,1)}, u32[]{:S(2)}) copy-start(bf16[32,2048]{1,0:T(8,128)(2,1)} %rest_0_) | copy-start | bytes 393220
  41.5 14.0 %collective-permute-start.11 = (bf16[32,2176]{1,0:T(8,128)(2,1)S(1)}, bf16[32,2176]{1,0:T(8,128)(2,1)S(1)}, u32[]{:S(2)}, u32[]{:S(2)}) collective-permute-start(bf16[32,2176]{1,0:T(8,128)(2,1)S(1)} %get-tuple-element.43), channel_id=1, source_target_pairs={{0,12},{4,8},{8,20},{12,16},{16,28},{20,24},{24,4},{28,0},{1,13},{... | collective-permute-start | bytes 417800 | tf_op jit(solution)/shard_map/ppermute | solution.py:292
  48.6 10.7 %collective-permute-start.10 = (bf16[32,2176]{1,0:T(8,128)(2,1)S(1)}, bf16[32,2176]{1,0:T(8,128)(2,1)S(1)}, u32[]{:S(2)}, u32[]{:S(2)}) collective-permute-start(bf16[32,2176]{1,0:T(8,128)(2,1)S(1)} %get-tuple-element.38), channel_id=1, source_target_pairs={{0,4},{4,0},{8,12},{12,8},{16,20},{20,16},{24,28},{28,24},{1,5},{5... | collective-permute-start | bytes 417800 | tf_op jit(solution)/shard_map/ppermute | solution.py:292
  50.2 9.1 %collective-permute-start.13 = (bf16[32,2176]{1,0:T(8,128)(2,1)S(1)}, bf16[32,2176]{1,0:T(8,128)(2,1)S(1)}, u32[]{:S(2)}, u32[]{:S(2)}) collective-permute-start(bf16[32,2176]{1,0:T(8,128)(2,1)S(1)} %get-tuple-element.44), channel_id=1, source_target_pairs={{0,20},{4,16},{8,28},{12,24},{16,4},{20,0},{24,12},{28,8},{1,21},{... | collective-permute-start | bytes 417800 | tf_op jit(solution)/shard_map/ppermute | solution.py:292
  51.1 28.6 %copy-start = (bf16[2048,1024]{1,0:T(8,128)(2,1)S(1)}, bf16[2048,1024]{1,0:T(8,128)(2,1)}, u32[]{:S(2)}) copy-start(bf16[2048,1024]{1,0:T(8,128)(2,1)} %w_ref.1) | copy-start | bytes 12582916
  60.2 8.3 %collective-permute-start.15 = (bf16[32,2048]{1,0:T(8,128)(2,1)S(1)}, bf16[32,2048]{1,0:T(8,128)(2,1)S(1)}, u32[]{:S(2)}, u32[]{:S(2)}) collective-permute-start(bf16[32,2048]{1,0:T(8,128)(2,1)S(1)} %merge.1.rest_0_), channel_id=1, source_target_pairs={{0,8},{4,12},{8,16},{12,20},{16,24},{20,28},{24,0},{28,4},{1,9},{5... | collective-permute-start | bytes 393224 | tf_op jit(solution)/shard_map/ppermute | solution.py:292
  61.0 9.5 %collective-permute-start.14 = (bf16[32,2048]{1,0:T(8,128)(2,1)S(1)}, bf16[32,2048]{1,0:T(8,128)(2,1)S(1)}, u32[]{:S(2)}, u32[]{:S(2)}) collective-permute-start(bf16[32,2048]{1,0:T(8,128)(2,1)S(1)} %merge.1.rest_0_), channel_id=1, source_target_pairs={{0,24},{4,28},{8,0},{12,4},{16,8},{20,12},{24,16},{28,20},{1,25},{... | collective-permute-start | bytes 393224 | tf_op jit(solution)/shard_map/ppermute | solution.py:292
  64.1 10.3 %collective-permute-start.16 = (bf16[32,2048]{1,0:T(8,128)(2,1)S(1)}, bf16[32,2048]{1,0:T(8,128)(2,1)S(1)}, u32[]{:S(2)}, u32[]{:S(2)}) collective-permute-start(bf16[32,2048]{1,0:T(8,128)(2,1)S(1)} %merge.1.rest_0_), channel_id=1, source_target_pairs={{0,16},{4,20},{8,24},{12,28},{16,0},{20,4},{24,8},{28,12},{1,17},{... | collective-permute-start | bytes 393224 | tf_op jit(solution)/shard_map/ppermute | solution.py:292
  68.5 6.0 %collective-permute-start.19 = (bf16[32,2048]{1,0:T(8,128)(2,1)S(1)}, bf16[32,2048]{1,0:T(8,128)(2,1)S(1)}, u32[]{:S(2)}, u32[]{:S(2)}) collective-permute-start(bf16[32,2048]{1,0:T(8,128)(2,1)S(1)} %collective-permute-done.15.rest_2_), channel_id=1, source_target_pairs={{0,4},{4,0},{8,12},{12,8},{16,20},{20,16},{24,28},{28,24},{1,5},{5... | collective-permute-start | bytes 393224 | tf_op jit(solution)/shard_map/ppermute | solution.py:292
  69.6 5.9 %collective-permute-start.17 = (bf16[32,2048]{1,0:T(8,128)(2,1)S(1)}, bf16[32,2048]{1,0:T(8,128)(2,1)S(1)}, u32[]{:S(2)}, u32[]{:S(2)}) collective-permute-start(bf16[32,2048]{1,0:T(8,128)(2,1)S(1)} %merge.1.rest_0_), channel_id=1, source_target_pairs={{0,4},{4,0},{8,12},{12,8},{16,20},{20,16},{24,28},{28,24},{1,5},{5... | collective-permute-start | bytes 393224 | tf_op jit(solution)/shard_map/ppermute | solution.py:292
  70.5 6.3 %collective-permute-start.18 = (bf16[32,2048]{1,0:T(8,128)(2,1)S(1)}, bf16[32,2048]{1,0:T(8,128)(2,1)S(1)}, u32[]{:S(2)}, u32[]{:S(2)}) collective-permute-start(bf16[32,2048]{1,0:T(8,128)(2,1)S(1)} %collective-permute-done.14.rest_1_), channel_id=1, source_target_pairs={{0,4},{4,0},{8,12},{12,8},{16,20},{20,16},{24,28},{28,24},{1,5},{5... | collective-permute-start | bytes 393224 | tf_op jit(solution)/shard_map/ppermute | solution.py:292
  74.5 5.3 %collective-permute-start.20 = (bf16[32,2048]{1,0:T(8,128)(2,1)S(1)}, bf16[32,2048]{1,0:T(8,128)(2,1)S(1)}, u32[]{:S(2)}, u32[]{:S(2)}) collective-permute-start(bf16[32,2048]{1,0:T(8,128)(2,1)S(1)} %collective-permute-done.16.rest_3_), channel_id=1, source_target_pairs={{0,4},{4,0},{8,12},{12,8},{16,20},{20,16},{24,28},{28,24},{1,5},{5... | collective-permute-start | bytes 393224 | tf_op jit(solution)/shard_map/ppermute | solution.py:292
  81.1 1.9 %collective-permute-start.21 = (bf16[64,1024]{1,0:T(8,128)(2,1)S(1)}, bf16[64,1024]{1,0:T(8,128)(2,1)S(1)}, u32[]{:S(2)}, u32[]{:S(2)}) collective-permute-start(bf16[64,1024]{1,0:T(8,128)(2,1)S(1)} %get-tuple-element.48), channel_id=1, source_target_pairs={{0,1},{1,0},{2,3},{3,2},{4,5},{5,4},{6,7},{7,6},{8,9},{9,8},{10,11... | collective-permute-start | bytes 393224 | tf_op jit(solution)/shard_map/ppermute | solution.py:354
  81.2 6.4 %collective-permute-start.22 = (bf16[64,1024]{1,0:T(8,128)(2,1)S(1)}, bf16[64,1024]{1,0:T(8,128)(2,1)S(1)}, u32[]{:S(2)}, u32[]{:S(2)}) collective-permute-start(bf16[64,1024]{1,0:T(8,128)(2,1)S(1)} %get-tuple-element.49), channel_id=1, source_target_pairs={{0,2},{1,3},{2,0},{3,1},{4,6},{5,7},{6,4},{7,5},{8,10},{9,11},{10,... | collective-permute-start | bytes 393224 | tf_op jit(solution)/shard_map/ppermute | solution.py:354
  82.1 7.3 %collective-permute-start.23 = (bf16[64,1024]{1,0:T(8,128)(2,1)S(1)}, bf16[64,1024]{1,0:T(8,128)(2,1)S(1)}, u32[]{:S(2)}, u32[]{:S(2)}) collective-permute-start(bf16[64,1024]{1,0:T(8,128)(2,1)S(1)} %get-tuple-element.50), channel_id=1, source_target_pairs={{0,3},{1,2},{2,1},{3,0},{4,7},{5,6},{6,5},{7,4},{8,11},{9,10},{10,... | collective-permute-start | bytes 393224 | tf_op jit(solution)/shard_map/ppermute | solution.py:354

commit v3 on v2

--- a/solution.py
+++ b/solution.py
@@ -142,6 +142,22 @@
                     at = (g * 3 + i) * parts + j
                     stats = jnp.where(sublane == at, term[:, j * LANES : (j + 1) * LANES], stats)
         out_refs[b][:, heads * DH :] = stats.astype(jnp.bfloat16)
+
+
+def hand_on_kernel(in_ref, k_ref, v_ref, out_ref):
+    out_ref[...] = in_ref[...]
+
+
+def hand_on_call(new_rows, keys, values):
+    vmem = pl.BlockSpec(memory_space=pltpu.VMEM)
+    return pl.pallas_call(
+        hand_on_kernel,
+        out_shape=jax.ShapeDtypeStruct(new_rows.shape, new_rows.dtype),
+        in_specs=[vmem] * 3,
+        out_specs=vmem,
+        compiler_params=pltpu.CompilerParams(vmem_limit_bytes=VMEM_ATTN),
+        name="hand_on",
+    )(new_rows, keys, values)
 
 
 def attention_call(members, ctx_count, kv_local, slots, blocks, table, new_rows, keys, values):
@@ -297,7 +313,12 @@
     def gather(x, chained):
         held = {(0, 0): x, (0, 1): move(x, 0, 1)}
         for k in steps:
-            held[k, 0] = move(x, -k, 0)
+            block = x
+            if not chained and 2 * k == high:
+                ready = {m: held[m] for m in held if m[0]}
+                block, ready = lax.optimization_barrier((block, ready))
+                held.update(ready)
+            held[k, 0] = move(block, -k, 0)
         behind = None
         for k in steps:
             block = held[k, 0]
@@ -318,6 +339,7 @@
     kv_local = new_keys.shape[1] // DH
     table = jnp.concatenate([keep_tiles.reshape(-1), tile_count.reshape(-1), owner_slot])
     new_rows = jnp.concatenate([new_keys, new_values], 1)
+    new_rows = hand_on_call(new_rows, cache_keys, cache_values)
 
     def attend(members, blocks):
         return attention_call(

time: 90.5 us -> 88.4 us (0.977)
  waiting for transfers between devices: 25.4 us -> 21.1 us
  starting transfers between devices: 31.8 us -> 35.4 us
    ppermute x21, waiting for transfers between devices: 19 us -> 14.5 us  [move(): return lax.ppermute(x, 'ctx', pairs)]
    ppermute x3, starting transfers between devices: 1.93 us -> 4.2 us  [body(): got = lax.ppermute(piece, 'tp', [(i, i ^ j) for i in range(peers)])]
    ppermute x21, starting transfers between devices: 29.9 us -> 31.2 us  [move(): return lax.ppermute(x, 'ctx', pairs)]
    unnamed x9 -> x16, local copies, waits for them, and re-layouts: 3.91 us -> 3.85 us
  transfers between devices with their start and end apart: 24 -> 24, of which waited for: 9 -> 8; matrix products, arithmetic and copies ran while one was open for 3% -> 2% of each run, Pallas kernels for 26% -> 27%
where the time goes in v3:
time: 88.4 us; the launch traced here: 88.6 us
  starting transfers between devices  35.4 us (40%)
  Pallas kernels  25.9 us (29%)
  waiting for transfers between devices  21.1 us (24%)
  local copies, waits for them, and re-layouts  4.6 us (5%)
  other arithmetic  1.57 us (2%)
    ppermute x21, starting transfers between devices, move(): return lax.ppermute(x, 'ctx', pairs)  31.2 us
    pallas_call x4, Pallas kernels, attention_call(): pl.pallas_call(functools.partial(attention_kernel, members, ctx_count, gr...  23.6 us
    ppermute x21, waiting for transfers between devices, move(): return lax.ppermute(x, 'ctx', pairs)  14.5 us
    ppermute x3, waiting for transfers between devices, body(): got = lax.ppermute(piece, 'tp', [(i, i ^ j) for i in range(peers)])  6.56 us
    ppermute x3, starting transfers between devices, body(): got = lax.ppermute(piece, 'tp', [(i, i ^ j) for i in range(peers)])  4.2 us
    unnamed x16, local copies, waits for them, and re-layouts  3.85 us
  transfers between devices with their start and end apart: 24, of which 8 were waited for; matrix products, arithmetic and copies ran while one was open for 2% of the time, Pallas kernels for 27%

profile of v3, /device:TPU:0, one launch (start us, length us, event | category | flops | bytes accessed | tf_op | source)
XLA Modules:
  0.0 88.6 jit_solution(8189511619313597743)
XLA Ops:
  0.0 3.0 %collective-permute-start.1 = (bf16[32,2048]{1,0:T(8,128)(2,1)}, bf16[32,2048]{1,0:T(8,128)(2,1)S(1)}, u32[]{:S(2)}, u32[]{:S(2)}) collective-permute-start(bf16[32,2048]{1,0:T(8,128)(2,1)} %rest_0_), channel_id=1, source_target_pairs={{0,8},{4,12},{8,16},{12,20},{16,24},{20,28},{24,0},{28,4},{1,9},{5... | collective-permute-start | bytes 393224 | tf_op jit(solution)/shard_map/ppermute | solution.py:308
  3.0 2.0 %collective-permute-start = (bf16[32,2048]{1,0:T(8,128)(2,1)}, bf16[32,2048]{1,0:T(8,128)(2,1)S(1)}, u32[]{:S(2)}, u32[]{:S(2)}) collective-permute-start(bf16[32,2048]{1,0:T(8,128)(2,1)} %rest_0_), channel_id=1, source_target_pairs={{0,24},{4,28},{8,0},{12,4},{16,8},{20,12},{24,16},{28,20},{1,25},{... | collective-permute-start | bytes 393224 | tf_op jit(solution)/shard_map/ppermute | solution.py:308
  5.1 1.7 %collective-permute-start.4 = (bf16[32,2048]{1,0:T(8,128)(2,1)}, bf16[32,2048]{1,0:T(8,128)(2,1)S(1)}, u32[]{:S(2)}, u32[]{:S(2)}) collective-permute-start(bf16[32,2048]{1,0:T(8,128)(2,1)} %rest_0_), channel_id=1, source_target_pairs={{0,4},{4,0},{8,12},{12,8},{16,20},{20,16},{24,28},{28,24},{1,5},{5... | collective-permute-start | bytes 393224 | tf_op jit(solution)/shard_map/ppermute | solution.py:308
  6.8 0.7 pad_maximum_fusion.in_ref
  7.5 0.8 reshape.6
  8.3 1.6 %copy-done.1 = bf16[4096,256]{1,0:T(8,128)(2,1)S(1)} copy-done((bf16[4096,256]{1,0:T(8,128)(2,1)S(1)}, bf16[4096,256]{1,0:T(8,128)(2,1)}, u32[]{:S(2)}) %copy-start.1) | copy-done | bytes 2097176
  9.9 1.6 %copy-done.3 = bf16[4096,256]{1,0:T(8,128)(2,1)S(1)} copy-done((bf16[4096,256]{1,0:T(8,128)(2,1)S(1)}, bf16[4096,256]{1,0:T(8,128)(2,1)}, u32[]{:S(2)}) %copy-start.3) | copy-done | bytes 2097176
  11.5 0.6 copy-done.6
  12.1 0.0 copy-done.7
  12.1 0.1 pad_add_fusion.table_ref
  12.2 0.0 collective-permute-done.1.rest_1_
  12.2 0.0 collective-permute-done.rest_0_
  12.2 0.8 collective-permute-start.2
  13.0 0.8 collective-permute-start.5
  13.8 1.3 %collective-permute-start.6 = (bf16[32,2048]{1,0:T(8,128)(2,1)S(1)}, bf16[32,2048]{1,0:T(8,128)(2,1)S(1)}, u32[]{:S(2)}, u32[]{:S(2)}) collective-permute-start(bf16[32,2048]{1,0:T(8,128)(2,1)S(1)} %collective-permute-done.1.rest_1_), channel_id=1, source_target_pairs={{0,4},{4,0},{8,12},{12,8},{16,20},{20,16},{24,28},{28,24},{1,5},{5... | collective-permute-start | bytes 393224 | tf_op jit(solution)/shard_map/ppermute | solution.py:308
  15.1 0.0 copy-done.2
  15.1 5.8 %attention.4 = (bf16[32,2176]{1,0:T(8,128)(2,1)S(1)}, bf16[32,2176]{1,0:T(8,128)(2,1)S(1)}) custom-call(s32[58]{0:T(128)S(1)} %pad_add_fusion.table_ref, bf16[32,512]{1,0:T(8,128)(2,1)S(1)} %hand_on.1.new_ref, bf16[4096,256]{1,0:T(8,128)(2,1)S(1)} %copy-done.2, bf16[4096,256]{1,0:T(8,128)(2,1)S(1)} %copy-done.4, ...), custom_call_target="tpu_custom_call" | custom-call | flops 3221225472 | bytes 8388608 | tf_op jit(solution)/shard_map/attention/pallas_call | solution.py:171
  20.9 1.6 %collective-permute-start.7 = (bf16[32,2176]{1,0:T(8,128)(2,1)S(1)}, bf16[32,2176]{1,0:T(8,128)(2,1)S(1)}, u32[]{:S(2)}, u32[]{:S(2)}) collective-permute-start(bf16[32,2176]{1,0:T(8,128)(2,1)S(1)} %get-tuple-element.41), channel_id=1, source_target_pairs={{0,8},{4,12},{8,16},{12,20},{16,24},{20,28},{24,0},{28,4},{1,9},{5... | collective-permute-start | bytes 417800 | tf_op jit(solution)/shard_map/ppermute | solution.py:308
  22.5 0.0 collective-permute-done.2.rest_0_
  22.5 2.3 %collective-permute-start.8 = (bf16[32,2176]{1,0:T(8,128)(2,1)S(1)}, bf16[32,2176]{1,0:T(8,128)(2,1)S(1)}, u32[]{:S(2)}, u32[]{:S(2)}) collective-permute-start(bf16[32,2176]{1,0:T(8,128)(2,1)S(1)} %get-tuple-element.34), channel_id=1, source_target_pairs={{0,24},{4,28},{8,0},{12,4},{16,8},{20,12},{24,16},{28,20},{1,25},{... | collective-permute-start | bytes 417800 | tf_op jit(solution)/shard_map/ppermute | solution.py:308
  24.7 0.0 collective-permute-done.5.rest_1_
  24.7 0.0 collective-permute-done.6.rest_2_
  24.7 1.4 %collective-permute-start.3 = (bf16[32,2048]{1,0:T(8,128)(2,1)S(1)}, bf16[32,2048]{1,0:T(8,128)(2,1)S(1)}, u32[]{:S(2)}, u32[]{:S(2)}) collective-permute-start(bf16[32,2048]{1,0:T(8,128)(2,1)S(1)} %collective-permute-done.2.rest_0_), channel_id=1, source_target_pairs={{0,4},{4,0},{8,12},{12,8},{16,20},{20,16},{24,28},{28,24},{1,5},{5... | collective-permute-start | bytes 393224 | tf_op jit(solution)/shard_map/ppermute | solution.py:308
  26.2 7.6 %attention.5 = (bf16[32,2176]{1,0:T(8,128)(2,1)S(1)}, bf16[32,2176]{1,0:T(8,128)(2,1)S(1)}, bf16[32,2176]{1,0:T(8,128)(2,1)S(1)}) custom-call(s32[58]{0:T(128)S(1)} %pad_add_fusion.table_ref, bf16[32,512]{1,0:T(8,128)(2,1)S(1)} %hand_on.1.new_ref, bf16[4096,256]{1,0:T(8,128)(2,1)S(1)} %copy-done.2, bf16[4096,256]{1,0:T(8,128)(2,1)S(1)} %copy-done.4, ...), custom_call_target="tpu_custom_call" | custom-call | flops 4831838208 | bytes 8388608 | tf_op jit(solution)/shard_map/attention/pallas_call | solution.py:171
  33.8 0.4 collective-permute-start.9
  34.2 0.0 collective-permute-done.4.rest_1_
  34.2 2.0 %collective-permute-start.11 = (bf16[32,2176]{1,0:T(8,128)(2,1)S(1)}, bf16[32,2176]{1,0:T(8,128)(2,1)S(1)}, u32[]{:S(2)}, u32[]{:S(2)}) collective-permute-start(bf16[32,2176]{1,0:T(8,128)(2,1)S(1)} %get-tuple-element.49), channel_id=1, source_target_pairs={{0,12},{4,8},{8,20},{12,16},{16,28},{20,24},{24,4},{28,0},{1,13},{... | collective-permute-start | bytes 417800 | tf_op jit(solution)/shard_map/ppermute | solution.py:308
  36.1 0.0 collective-permute-done.3.rest_0_
  36.1 2.8 %collective-permute-start.12 = (bf16[32,2176]{1,0:T(8,128)(2,1)S(1)}, bf16[32,2176]{1,0:T(8,128)(2,1)S(1)}, u32[]{:S(2)}, u32[]{:S(2)}) collective-permute-start(bf16[32,2176]{1,0:T(8,128)(2,1)S(1)} %get-tuple-element.38), channel_id=1, source_target_pairs={{0,28},{4,24},{8,4},{12,0},{16,12},{20,8},{24,20},{28,16},{1,29},{... | collective-permute-start | bytes 417800 | tf_op jit(solution)/shard_map/ppermute | solution.py:308
  38.9 0.0 collective-permute-done.7.refs_1_
  38.9 0.0 collective-permute-done.8.refs_2_
  38.9 5.8 %attention.6 = (bf16[32,2176]{1,0:T(8,128)(2,1)S(1)}, bf16[32,2176]{1,0:T(8,128)(2,1)S(1)}) custom-call(s32[58]{0:T(128)S(1)} %pad_add_fusion.table_ref, bf16[32,512]{1,0:T(8,128)(2,1)S(1)} %hand_on.1.new_ref, bf16[4096,256]{1,0:T(8,128)(2,1)S(1)} %copy-done.2, bf16[4096,256]{1,0:T(8,128)(2,1)S(1)} %copy-done.4, ...), custom_call_target="tpu_custom_call" | custom-call | flops 3221225472 | bytes 8388608 | tf_op jit(solution)/shard_map/attention/pallas_call | solution.py:171
  44.7 2.5 %collective-permute-start.10 = (bf16[32,2176]{1,0:T(8,128)(2,1)S(1)}, bf16[32,2176]{1,0:T(8,128)(2,1)S(1)}, u32[]{:S(2)}, u32[]{:S(2)}) collective-permute-start(bf16[32,2176]{1,0:T(8,128)(2,1)S(1)} %get-tuple-element.44), channel_id=1, source_target_pairs={{0,4},{4,0},{8,12},{12,8},{16,20},{20,16},{24,28},{28,24},{1,5},{5... | collective-permute-start | bytes 417800 | tf_op jit(solution)/shard_map/ppermute | solution.py:308
  47.2 0.2 collective-permute-start.13
  47.4 0.0 copy-done.5
  47.5 4.4 %attention.7.refs_0_ = bf16[32,2176]{1,0:T(8,128)(2,1)S(1)} custom-call(s32[58]{0:T(128)S(1)} %pad_add_fusion.table_ref, bf16[32,512]{1,0:T(8,128)(2,1)S(1)} %hand_on.1.new_ref, bf16[4096,256]{1,0:T(8,128)(2,1)S(1)} %copy-done.2, bf16[4096,256]{1,0:T(8,128)(2,1)S(1)} %copy-done.4, bf16[32,2048]{1,0:T(8,128)(2,1)S(1)} %copy-done.5), custom_call_target="tpu_custom_call" | custom-call | flops 1610612736 | bytes 8388608 | tf_op jit(solution)/shard_map/attention/pallas_call | solution.py:171
  51.9 0.0 collective-permute-done.9.refs_3_
  51.9 0.0 collective-permute-done.11.refs_5_
  51.9 0.0 collective-permute-done.12.refs_6_
  51.9 3.3 %collective-permute-done.13.refs_7_ = bf16[32,2176]{1,0:T(8,128)(2,1)S(1)} collective-permute-done((bf16[32,2176]{1,0:T(8,128)(2,1)S(1)}, bf16[32,2176]{1,0:T(8,128)(2,1)S(1)}, u32[]{:S(2)}, u32[]{:S(2)}) %collective-permute-start.13) | collective-permute-done | bytes 139296 | tf_op jit(solution)/shard_map/ppermute | solution.py:308
  55.2 0.0 collective-permute-done.10.refs_4_
  55.2 0.9 %merge.1.rest_0_ = bf16[32,2048]{1,0:T(8,128)(2,1)S(1)} custom-call(bf16[32,2176]{1,0:T(8,128)(2,1)S(1)} %attention.7.refs_0_, bf16[32,2176]{1,0:T(8,128)(2,1)S(1)} %collective-permute-done.7.refs_1_, bf16[32,2176]{1,0:T(8,128)(2,1)S(1)} %collective-permute-done.8.refs_2_, bf16[32,2176]{1,0:T(8,128)(2,1)S(1)} %collective-permute-done.9.refs_3_, ...), custom_call_target="tpu_custom_call" | custom-call | flops 1114112 | bytes 1114112 | tf_op jit(solution)/shard_map/merge/pallas_call | solution.py:229
  56.1 0.2 collective-permute-start.15
  56.3 3.7 %collective-permute-start.14 = (bf16[32,2048]{1,0:T(8,128)(2,1)S(1)}, bf16[32,2048]{1,0:T(8,128)(2,1)S(1)}, u32[]{:S(2)}, u32[]{:S(2)}) collective-permute-start(bf16[32,2048]{1,0:T(8,128)(2,1)S(1)} %merge.1.rest_0_), channel_id=1, source_target_pairs={{0,24},{4,28},{8,0},{12,4},{16,8},{20,12},{24,16},{28,20},{1,25},{... | collective-permute-start | bytes 393224 | tf_op jit(solution)/shard_map/ppermute | solution.py:308
  60.0 0.0 collective-permute-start.16
  60.0 4.4 %collective-permute-done.15.rest_2_ = bf16[32,2048]{1,0:T(8,128)(2,1)S(1)} collective-permute-done((bf16[32,2048]{1,0:T(8,128)(2,1)S(1)}, bf16[32,2048]{1,0:T(8,128)(2,1)S(1)}, u32[]{:S(2)}, u32[]{:S(2)}) %collective-permute-start.15) | collective-permute-done | bytes 131104 | tf_op jit(solution)/shard_map/ppermute | solution.py:308
  64.4 0.9 %collective-permute-start.19 = (bf16[32,2048]{1,0:T(8,128)(2,1)S(1)}, bf16[32,2048]{1,0:T(8,128)(2,1)S(1)}, u32[]{:S(2)}, u32[]{:S(2)}) collective-permute-start(bf16[32,2048]{1,0:T(8,128)(2,1)S(1)} %collective-permute-done.15.rest_2_), channel_id=1, source_target_pairs={{0,4},{4,0},{8,12},{12,8},{16,20},{20,16},{24,28},{28,24},{1,5},{5... | collective-permute-start | bytes 393224 | tf_op jit(solution)/shard_map/ppermute | solution.py:308
  65.2 1.1 %collective-permute-start.17 = (bf16[32,2048]{1,0:T(8,128)(2,1)S(1)}, bf16[32,2048]{1,0:T(8,128)(2,1)S(1)}, u32[]{:S(2)}, u32[]{:S(2)}) collective-permute-start(bf16[32,2048]{1,0:T(8,128)(2,1)S(1)} %merge.1.rest_0_), channel_id=1, source_target_pairs={{0,4},{4,0},{8,12},{12,8},{16,20},{20,16},{24,28},{28,24},{1,5},{5... | collective-permute-start | bytes 393224 | tf_op jit(solution)/shard_map/ppermute | solution.py:308
  66.4 0.0 collective-permute-done.14.rest_1_
  66.4 0.9 %collective-permute-start.18 = (bf16[32,2048]{1,0:T(8,128)(2,1)S(1)}, bf16[32,2048]{1,0:T(8,128)(2,1)S(1)}, u32[]{:S(2)}, u32[]{:S(2)}) collective-permute-start(bf16[32,2048]{1,0:T(8,128)(2,1)S(1)} %collective-permute-done.14.rest_1_), channel_id=1, source_target_pairs={{0,4},{4,0},{8,12},{12,8},{16,20},{20,16},{24,28},{28,24},{1,5},{5... | collective-permute-start | bytes 393224 | tf_op jit(solution)/shard_map/ppermute | solution.py:308
  67.3 2.4 %collective-permute-done.16.rest_3_ = bf16[32,2048]{1,0:T(8,128)(2,1)S(1)} collective-permute-done((bf16[32,2048]{1,0:T(8,128)(2,1)S(1)}, bf16[32,2048]{1,0:T(8,128)(2,1)S(1)}, u32[]{:S(2)}, u32[]{:S(2)}) %collective-permute-start.16) | collective-permute-done | bytes 131104 | tf_op jit(solution)/shard_map/ppermute | solution.py:308
  69.7 0.4 collective-permute-done.19.rest_6_
  70.1 1.6 %collective-permute-start.20 = (bf16[32,2048]{1,0:T(8,128)(2,1)S(1)}, bf16[32,2048]{1,0:T(8,128)(2,1)S(1)}, u32[]{:S(2)}, u32[]{:S(2)}) collective-permute-start(bf16[32,2048]{1,0:T(8,128)(2,1)S(1)} %collective-permute-done.16.rest_3_), channel_id=1, source_target_pairs={{0,4},{4,0},{8,12},{12,8},{16,20},{20,16},{24,28},{28,24},{1,5},{5... | collective-permute-start | bytes 393224 | tf_op jit(solution)/shard_map/ppermute | solution.py:308
  71.7 0.0 collective-permute-done.17.rest_4_
  71.7 2.2 %collective-permute-done.18.rest_5_ = bf16[32,2048]{1,0:T(8,128)(2,1)S(1)} collective-permute-done((bf16[32,2048]{1,0:T(8,128)(2,1)S(1)}, bf16[32,2048]{1,0:T(8,128)(2,1)S(1)}, u32[]{:S(2)}, u32[]{:S(2)}) %collective-permute-start.18) | collective-permute-done | bytes 131104 | tf_op jit(solution)/shard_map/ppermute | solution.py:308
  73.8 1.8 %collective-permute-done.20.rest_7_ = bf16[32,2048]{1,0:T(8,128)(2,1)S(1)} collective-permute-done((bf16[32,2048]{1,0:T(8,128)(2,1)S(1)}, bf16[32,2048]{1,0:T(8,128)(2,1)S(1)}, u32[]{:S(2)}, u32[]{:S(2)}) %collective-permute-start.20) | collective-permute-done | bytes 131104 | tf_op jit(solution)/shard_map/ppermute | solution.py:308
  75.7 1.4 %projection.1 = (f32[64,1024]{1,0:T(8,128)S(1)}, bf16[64,1024]{1,0:T(8,128)(2,1)S(1)}, bf16[64,1024]{1,0:T(8,128)(2,1)S(1)}, bf16[64,1024]{1,0:T(8,128)(2,1)S(1)}) custom-call(bf16[2048,1024]{1,0:T(8,128)(2,1)S(1)} %copy-done, bf16[32,2048]{1,0:T(8,128)(2,1)S(1)} %merge.1.rest_0_, bf16[32,2048]{1,0:T(8,128)(2,1)S(1)} %collective-permute-done.14.rest_1_, ...), custom_call_target="tpu_custom_call" | custom-call | flops 1073741824 | bytes 4194304 | tf_op jit(solution)/shard_map/projection/pallas_call | solution.py:268
  77.1 0.1 collective-permute-start.21
  77.2 4.1 %collective-permute-start.22 = (bf16[64,1024]{1,0:T(8,128)(2,1)S(1)}, bf16[64,1024]{1,0:T(8,128)(2,1)S(1)}, u32[]{:S(2)}, u32[]{:S(2)}) collective-permute-start(bf16[64,1024]{1,0:T(8,128)(2,1)S(1)} %get-tuple-element.55), channel_id=1, source_target_pairs={{0,2},{1,3},{2,0},{3,1},{4,6},{5,7},{6,4},{7,5},{8,10},{9,11},{10,... | collective-permute-start | bytes 393224 | tf_op jit(solution)/shard_map/ppermute | solution.py:376
  81.2 0.1 collective-permute-start.23
  81.3 0.0 collective-permute-done.21
  81.3 4.3 %collective-permute-done.22 = bf16[64,1024]{1,0:T(8,128)(2,1)S(1)} collective-permute-done((bf16[64,1024]{1,0:T(8,128)(2,1)S(1)}, bf16[64,1024]{1,0:T(8,128)(2,1)S(1)}, u32[]{:S(2)}, u32[]{:S(2)}) %collective-permute-start.22) | collective-permute-done | bytes 131104 | tf_op jit(solution)/shard_map/ppermute | solution.py:376
  85.6 2.3 %collective-permute-done.23 = bf16[64,1024]{1,0:T(8,128)(2,1)S(1)} collective-permute-done((bf16[64,1024]{1,0:T(8,128)(2,1)S(1)}, bf16[64,1024]{1,0:T(8,128)(2,1)S(1)}, u32[]{:S(2)}, u32[]{:S(2)}) %collective-permute-start.23) | collective-permute-done | bytes 131104 | tf_op jit(solution)/shard_map/ppermute | solution.py:376
  87.9 0.8 convert_add_fusion
  (11 shorter events, 0.0 us)
Async XLA Ops:
  0.0 12.2 %collective-permute-start.1 = (bf16[32,2048]{1,0:T(8,128)(2,1)}, bf16[32,2048]{1,0:T(8,128)(2,1)S(1)}, u32[]{:S(2)}, u32[]{:S(2)}) collective-permute-start(bf16[32,2048]{1,0:T(8,128)(2,1)} %rest_0_), channel_id=1, source_target_pairs={{0,8},{4,12},{8,16},{12,20},{16,24},{20,28},{24,0},{28,4},{1,9},{5... | collective-permute-start | bytes 393224 | tf_op jit(solution)/shard_map/ppermute | solution.py:308
  3.0 9.2 %collective-permute-start = (bf16[32,2048]{1,0:T(8,128)(2,1)}, bf16[32,2048]{1,0:T(8,128)(2,1)S(1)}, u32[]{:S(2)}, u32[]{:S(2)}) collective-permute-start(bf16[32,2048]{1,0:T(8,128)(2,1)} %rest_0_), channel_id=1, source_target_pairs={{0,24},{4,28},{8,0},{12,4},{16,8},{20,12},{24,16},{28,20},{1,25},{... | collective-permute-start | bytes 393224 | tf_op jit(solution)/shard_map/ppermute | solution.py:308
  5.1 29.1 %collective-permute-start.4 = (bf16[32,2048]{1,0:T(8,128)(2,1)}, bf16[32,2048]{1,0:T(8,128)(2,1)S(1)}, u32[]{:S(2)}, u32[]{:S(2)}) collective-permute-start(bf16[32,2048]{1,0:T(8,128)(2,1)} %rest_0_), channel_id=1, source_target_pairs={{0,4},{4,0},{8,12},{12,8},{16,20},{20,16},{24,28},{28,24},{1,5},{5... | collective-permute-start | bytes 393224 | tf_op jit(solution)/shard_map/ppermute | solution.py:308
  8.3 1.6 %copy-start.1 = (bf16[4096,256]{1,0:T(8,128)(2,1)S(1)}, bf16[4096,256]{1,0:T(8,128)(2,1)}, u32[]{:S(2)}) copy-start(bf16[4096,256]{1,0:T(8,128)(2,1)} %k_ref.9) | copy-start | bytes 6291460
  9.9 1.6 %copy-start.3 = (bf16[4096,256]{1,0:T(8,128)(2,1)S(1)}, bf16[4096,256]{1,0:T(8,128)(2,1)}, u32[]{:S(2)}) copy-start(bf16[4096,256]{1,0:T(8,128)(2,1)} %v_ref.9) | copy-start | bytes 6291460
  11.4 0.7 copy-start.6
  11.4 0.7 copy-start.7
  11.4 3.6 %copy-start.2 = (bf16[4096,256]{1,0:T(8,128)(2,1)S(1)}, bf16[4096,256]{1,0:T(8,128)(2,1)}, u32[]{:S(2)}) copy-start(bf16[4096,256]{1,0:T(8,128)(2,1)} %k_ref.9) | copy-start | bytes 6291460
  11.5 3.6 %copy-start.4 = (bf16[4096,256]{1,0:T(8,128)(2,1)S(1)}, bf16[4096,256]{1,0:T(8,128)(2,1)}, u32[]{:S(2)}) copy-start(bf16[4096,256]{1,0:T(8,128)(2,1)} %v_ref.9) | copy-start | bytes 6291460
  12.2 10.3 %collective-permute-start.2 = (bf16[32,2048]{1,0:T(8,128)(2,1)}, bf16[32,2048]{1,0:T(8,128)(2,1)S(1)}, u32[]{:S(2)}, u32[]{:S(2)}) collective-permute-start(bf16[32,2048]{1,0:T(8,128)(2,1)} %rest_0_), channel_id=1, source_target_pairs={{0,16},{4,20},{8,24},{12,28},{16,0},{20,4},{24,8},{28,12},{1,17},{... | collective-permute-start | bytes 393224 | tf_op jit(solution)/shard_map/ppermute | solution.py:308
  13.0 11.7 %collective-permute-start.5 = (bf16[32,2048]{1,0:T(8,128)(2,1)S(1)}, bf16[32,2048]{1,0:T(8,128)(2,1)S(1)}, u32[]{:S(2)}, u32[]{:S(2)}) collective-permute-start(bf16[32,2048]{1,0:T(8,128)(2,1)S(1)} %collective-permute-done.rest_0_), channel_id=1, source_target_pairs={{0,4},{4,0},{8,12},{12,8},{16,20},{20,16},{24,28},{28,24},{1,5},{5... | collective-permute-start | bytes 393224 | tf_op jit(solution)/shard_map/ppermute | solution.py:308
  13.8 11.0 %collective-permute-start.6 = (bf16[32,2048]{1,0:T(8,128)(2,1)S(1)}, bf16[32,2048]{1,0:T(8,128)(2,1)S(1)}, u32[]{:S(2)}, u32[]{:S(2)}) collective-permute-start(bf16[32,2048]{1,0:T(8,128)(2,1)S(1)} %collective-permute-done.1.rest_1_), channel_id=1, source_target_pairs={{0,4},{4,0},{8,12},{12,8},{16,20},{20,16},{24,28},{28,24},{1,5},{5... | collective-permute-start | bytes 393224 | tf_op jit(solution)/shard_map/ppermute | solution.py:308
  20.9 18.0 %collective-permute-start.7 = (bf16[32,2176]{1,0:T(8,128)(2,1)S(1)}, bf16[32,2176]{1,0:T(8,128)(2,1)S(1)}, u32[]{:S(2)}, u32[]{:S(2)}) collective-permute-start(bf16[32,2176]{1,0:T(8,128)(2,1)S(1)} %get-tuple-element.41), channel_id=1, source_target_pairs={{0,8},{4,12},{8,16},{12,20},{16,24},{20,28},{24,0},{28,4},{1,9},{5... | collective-permute-start | bytes 417800 | tf_op jit(solution)/shard_map/ppermute | solution.py:308
  22.5 16.4 %collective-permute-start.8 = (bf16[32,2176]{1,0:T(8,128)(2,1)S(1)}, bf16[32,2176]{1,0:T(8,128)(2,1)S(1)}, u32[]{:S(2)}, u32[]{:S(2)}) collective-permute-start(bf16[32,2176]{1,0:T(8,128)(2,1)S(1)} %get-tuple-element.34), channel_id=1, source_target_pairs={{0,24},{4,28},{8,0},{12,4},{16,8},{20,12},{24,16},{28,20},{1,25},{... | collective-permute-start | bytes 417800 | tf_op jit(solution)/shard_map/ppermute | solution.py:308
  24.7 11.4 %collective-permute-start.3 = (bf16[32,2048]{1,0:T(8,128)(2,1)S(1)}, bf16[32,2048]{1,0:T(8,128)(2,1)S(1)}, u32[]{:S(2)}, u32[]{:S(2)}) collective-permute-start(bf16[32,2048]{1,0:T(8,128)(2,1)S(1)} %collective-permute-done.2.rest_0_), channel_id=1, source_target_pairs={{0,4},{4,0},{8,12},{12,8},{16,20},{20,16},{24,28},{28,24},{1,5},{5... | collective-permute-start | bytes 393224 | tf_op jit(solution)/shard_map/ppermute | solution.py:308
  33.8 18.0 %collective-permute-start.9 = (bf16[32,2176]{1,0:T(8,128)(2,1)S(1)}, bf16[32,2176]{1,0:T(8,128)(2,1)S(1)}, u32[]{:S(2)}, u32[]{:S(2)}) collective-permute-start(bf16[32,2176]{1,0:T(8,128)(2,1)S(1)} %get-tuple-element.48), channel_id=1, source_target_pairs={{0,16},{4,20},{8,24},{12,28},{16,0},{20,4},{24,8},{28,12},{1,17},{... | collective-permute-start | bytes 417800 | tf_op jit(solution)/shard_map/ppermute | solution.py:308
  34.2 17.7 %collective-permute-start.11 = (bf16[32,2176]{1,0:T(8,128)(2,1)S(1)}, bf16[32,2176]{1,0:T(8,128)(2,1)S(1)}, u32[]{:S(2)}, u32[]{:S(2)}) collective-permute-start(bf16[32,2176]{1,0:T(8,128)(2,1)S(1)} %get-tuple-element.49), channel_id=1, source_target_pairs={{0,12},{4,8},{8,20},{12,16},{16,28},{20,24},{24,4},{28,0},{1,13},{... | collective-permute-start | bytes 417800 | tf_op jit(solution)/shard_map/ppermute | solution.py:308
  36.1 11.3 %copy-start.5 = (bf16[32,2048]{1,0:T(8,128)(2,1)S(1)}, bf16[32,2048]{1,0:T(8,128)(2,1)}, u32[]{:S(2)}) copy-start(bf16[32,2048]{1,0:T(8,128)(2,1)} %rest_0_) | copy-start | bytes 393220
  36.1 15.7 %collective-permute-start.12 = (bf16[32,2176]{1,0:T(8,128)(2,1)S(1)}, bf16[32,2176]{1,0:T(8,128)(2,1)S(1)}, u32[]{:S(2)}, u32[]{:S(2)}) collective-permute-start(bf16[32,2176]{1,0:T(8,128)(2,1)S(1)} %get-tuple-element.38), channel_id=1, source_target_pairs={{0,28},{4,24},{8,4},{12,0},{16,12},{20,8},{24,20},{28,16},{1,29},{... | collective-permute-start | bytes 417800 | tf_op jit(solution)/shard_map/ppermute | solution.py:308
  44.7 10.4 %collective-permute-start.10 = (bf16[32,2176]{1,0:T(8,128)(2,1)S(1)}, bf16[32,2176]{1,0:T(8,128)(2,1)S(1)}, u32[]{:S(2)}, u32[]{:S(2)}) collective-permute-start(bf16[32,2176]{1,0:T(8,128)(2,1)S(1)} %get-tuple-element.44), channel_id=1, source_target_pairs={{0,4},{4,0},{8,12},{12,8},{16,20},{20,16},{24,28},{28,24},{1,5},{5... | collective-permute-start | bytes 417800 | tf_op jit(solution)/shard_map/ppermute | solution.py:308
  47.2 7.9 %collective-permute-start.13 = (bf16[32,2176]{1,0:T(8,128)(2,1)S(1)}, bf16[32,2176]{1,0:T(8,128)(2,1)S(1)}, u32[]{:S(2)}, u32[]{:S(2)}) collective-permute-start(bf16[32,2176]{1,0:T(8,128)(2,1)S(1)} %get-tuple-element.50), channel_id=1, source_target_pairs={{0,20},{4,16},{8,28},{12,24},{16,4},{20,0},{24,12},{28,8},{1,21},{... | collective-permute-start | bytes 417800 | tf_op jit(solution)/shard_map/ppermute | solution.py:308
  47.4 28.2 %copy-start = (bf16[2048,1024]{1,0:T(8,128)(2,1)S(1)}, bf16[2048,1024]{1,0:T(8,128)(2,1)}, u32[]{:S(2)}) copy-start(bf16[2048,1024]{1,0:T(8,128)(2,1)} %w_ref.1) | copy-start | bytes 12582916
  56.1 8.3 %collective-permute-start.15 = (bf16[32,2048]{1,0:T(8,128)(2,1)S(1)}, bf16[32,2048]{1,0:T(8,128)(2,1)S(1)}, u32[]{:S(2)}, u32[]{:S(2)}) collective-permute-start(bf16[32,2048]{1,0:T(8,128)(2,1)S(1)} %merge.1.rest_0_), channel_id=1, source_target_pairs={{0,8},{4,12},{8,16},{12,20},{16,24},{20,28},{24,0},{28,4},{1,9},{5... | collective-permute-start | bytes 393224 | tf_op jit(solution)/shard_map/ppermute | solution.py:308
  56.3 10.1 %collective-permute-start.14 = (bf16[32,2048]{1,0:T(8,128)(2,1)S(1)}, bf16[32,2048]{1,0:T(8,128)(2,1)S(1)}, u32[]{:S(2)}, u32[]{:S(2)}) collective-permute-start(bf16[32,2048]{1,0:T(8,128)(2,1)S(1)} %merge.1.rest_0_), channel_id=1, source_target_pairs={{0,24},{4,28},{8,0},{12,4},{16,8},{20,12},{24,16},{28,20},{1,25},{... | collective-permute-start | bytes 393224 | tf_op jit(solution)/shard_map/ppermute | solution.py:308
  60.0 9.7 %collective-permute-start.16 = (bf16[32,2048]{1,0:T(8,128)(2,1)S(1)}, bf16[32,2048]{1,0:T(8,128)(2,1)S(1)}, u32[]{:S(2)}, u32[]{:S(2)}) collective-permute-start(bf16[32,2048]{1,0:T(8,128)(2,1)S(1)} %merge.1.rest_0_), channel_id=1, source_target_pairs={{0,16},{4,20},{8,24},{12,28},{16,0},{20,4},{24,8},{28,12},{1,17},{... | collective-permute-start | bytes 393224 | tf_op jit(solution)/shard_map/ppermute | solution.py:308
  64.4 5.7 %collective-permute-start.19 = (bf16[32,2048]{1,0:T(8,128)(2,1)S(1)}, bf16[32,2048]{1,0:T(8,128)(2,1)S(1)}, u32[]{:S(2)}, u32[]{:S(2)}) collective-permute-start(bf16[32,2048]{1,0:T(8,128)(2,1)S(1)} %collective-permute-done.15.rest_2_), channel_id=1, source_target_pairs={{0,4},{4,0},{8,12},{12,8},{16,20},{20,16},{24,28},{28,24},{1,5},{5... | collective-permute-start | bytes 393224 | tf_op jit(solution)/shard_map/ppermute | solution.py:308
  65.2 6.4 %collective-permute-start.17 = (bf16[32,2048]{1,0:T(8,128)(2,1)S(1)}, bf16[32,2048]{1,0:T(8,128)(2,1)S(1)}, u32[]{:S(2)}, u32[]{:S(2)}) collective-permute-start(bf16[32,2048]{1,0:T(8,128)(2,1)S(1)} %merge.1.rest_0_), channel_id=1, source_target_pairs={{0,4},{4,0},{8,12},{12,8},{16,20},{20,16},{24,28},{28,24},{1,5},{5... | collective-permute-start | bytes 393224 | tf_op jit(solution)/shard_map/ppermute | solution.py:308
  66.4 7.5 %collective-permute-start.18 = (bf16[32,2048]{1,0:T(8,128)(2,1)S(1)}, bf16[32,2048]{1,0:T(8,128)(2,1)S(1)}, u32[]{:S(2)}, u32[]{:S(2)}) collective-permute-start(bf16[32,2048]{1,0:T(8,128)(2,1)S(1)} %collective-permute-done.14.rest_1_), channel_id=1, source_target_pairs={{0,4},{4,0},{8,12},{12,8},{16,20},{20,16},{24,28},{28,24},{1,5},{5... | collective-permute-start | bytes 393224 | tf_op jit(solution)/shard_map/ppermute | solution.py:308
  70.1 5.6 %collective-permute-start.20 = (bf16[32,2048]{1,0:T(8,128)(2,1)S(1)}, bf16[32,2048]{1,0:T(8,128)(2,1)S(1)}, u32[]{:S(2)}, u32[]{:S(2)}) collective-permute-start(bf16[32,2048]{1,0:T(8,128)(2,1)S(1)} %collective-permute-done.16.rest_3_), channel_id=1, source_target_pairs={{0,4},{4,0},{8,12},{12,8},{16,20},{20,16},{24,28},{28,24},{1,5},{5... | collective-permute-start | bytes 393224 | tf_op jit(solution)/shard_map/ppermute | solution.py:308
  77.1 4.2 %collective-permute-start.21 = (bf16[64,1024]{1,0:T(8,128)(2,1)S(1)}, bf16[64,1024]{1,0:T(8,128)(2,1)S(1)}, u32[]{:S(2)}, u32[]{:S(2)}) collective-permute-start(bf16[64,1024]{1,0:T(8,128)(2,1)S(1)} %get-tuple-element.54), channel_id=1, source_target_pairs={{0,1},{1,0},{2,3},{3,2},{4,5},{5,4},{6,7},{7,6},{8,9},{9,8},{10,11... | collective-permute-start | bytes 393224 | tf_op jit(solution)/shard_map/ppermute | solution.py:376
  77.2 8.4 %collective-permute-start.22 = (bf16[64,1024]{1,0:T(8,128)(2,1)S(1)}, bf16[64,1024]{1,0:T(8,128)(2,1)S(1)}, u32[]{:S(2)}, u32[]{:S(2)}) collective-permute-start(bf16[64,1024]{1,0:T(8,128)(2,1)S(1)} %get-tuple-element.55), channel_id=1, source_target_pairs={{0,2},{1,3},{2,0},{3,1},{4,6},{5,7},{6,4},{7,5},{8,10},{9,11},{10,... | collective-permute-start | bytes 393224 | tf_op jit(solution)/shard_map/ppermute | solution.py:376
  81.2 6.6 %collective-permute-start.23 = (bf16[64,1024]{1,0:T(8,128)(2,1)S(1)}, bf16[64,1024]{1,0:T(8,128)(2,1)S(1)}, u32[]{:S(2)}, u32[]{:S(2)}) collective-permute-start(bf16[64,1024]{1,0:T(8,128)(2,1)S(1)} %get-tuple-element.56), channel_id=1, source_target_pairs={{0,3},{1,2},{2,1},{3,0},{4,7},{5,6},{6,5},{7,4},{8,11},{9,10},{10,... | collective-permute-start | bytes 393224 | tf_op jit(solution)/shard_map/ppermute | solution.py:376

commit v4 on v2

--- a/solution.py
+++ b/solution.py
@@ -15,6 +15,7 @@
 LOW = -1e30
 ONES = 16
 LOW_SIZE = 2
+VMEM_PACK = 58 * 2**20
 VMEM_ATTN = 24 * 2**20
 VMEM_MERGE = 8 * 2**20
 VMEM_PROJ = 16 * 2**20
@@ -142,6 +143,38 @@
                     at = (g * 3 + i) * parts + j
                     stats = jnp.where(sublane == at, term[:, j * LANES : (j + 1) * LANES], stats)
         out_refs[b][:, heads * DH :] = stats.astype(jnp.bfloat16)
+
+
+def pack_kernel(slot_ref, keep_ref, count_ref, nk_ref, nv_ref, k_hbm, v_hbm, table_ref, rows_ref):
+    kv_local, slots = keep_ref.shape
+    for g in range(kv_local):
+        for t in range(slots):
+            table_ref[g * slots + t] = keep_ref[g, t]
+        table_ref[kv_local * slots + g] = count_ref[g]
+    for c in range(slot_ref.shape[0]):
+        table_ref[kv_local * (slots + 1) + c] = slot_ref[c]
+    width = nk_ref.shape[1]
+    rows_ref[:, :width] = nk_ref[...]
+    rows_ref[:, width:] = nv_ref[...]
+
+
+def pack_call(slot, keep, count, new_keys, new_values, keys, values):
+    smem = pl.BlockSpec(memory_space=pltpu.SMEM)
+    vmem = pl.BlockSpec(memory_space=pltpu.VMEM)
+    hbm = pl.BlockSpec(memory_space=pltpu.HBM)
+    q_dev, width = new_keys.shape
+    entries = keep.size + count.size + slot.size
+    return pl.pallas_call(
+        pack_kernel,
+        out_shape=[
+            jax.ShapeDtypeStruct((entries,), jnp.int32),
+            jax.ShapeDtypeStruct((q_dev, 2 * width), new_keys.dtype),
+        ],
+        in_specs=[smem] * 3 + [vmem] * 2 + [hbm] * 2,
+        out_specs=[smem, vmem],
+        compiler_params=pltpu.CompilerParams(vmem_limit_bytes=VMEM_PACK),
+        name="pack",
+    )(slot, keep, count, new_keys, new_values, keys, values)
 
 
 def attention_call(members, ctx_count, kv_local, slots, blocks, table, new_rows, keys, values):
@@ -228,19 +261,22 @@
 def projection_kernel(members, ctx_count, peers, w_ref, *rest):
     blocks = len(members)
     in_refs, rest = rest[:blocks], rest[blocks:]
-    own_ref, send_refs, (rows_ref, sum_ref) = rest[0], rest[1:peers], rest[peers:]
+    own_ref, send_ref, rows_ref, sum_ref = rest
     q_dev = in_refs[0].shape[0]
     me = lax.axis_index("ctx")
     for member, ref in zip(members, in_refs):
         at = flipped(me, ctx_count, *member) * q_dev
         rows_ref[pl.ds(pl.multiple_of(at, q_dev), q_dev), :] = ref[...]
-    part = own_ref.shape[0]
+    steps, part = own_ref.shape[:2]
     my_tp = lax.axis_index("tp")
     sum_ref[...] = jnp.dot(rows_ref[...], w_ref[...], preferred_element_type=jnp.float32)
-    own_ref[...] = sum_ref[pl.ds(pl.multiple_of(my_tp * part, part), part), :]
-    for j in range(1, peers):
-        at = pl.multiple_of((my_tp ^ j) * part, part)
-        send_refs[j - 1][...] = sum_ref[pl.ds(at, part), :].astype(jnp.bfloat16)
+
+    def piece(peer):
+        return sum_ref[pl.ds(pl.multiple_of(peer * part, part), part), :]
+
+    for j in range(steps):
+        own_ref[j] = piece(my_tp ^ (2 * j))
+        send_ref[j] = piece(my_tp ^ (2 * j + 1)).astype(jnp.bfloat16)
 
 
 def projection_call(members, ctx_count, blocks, weight, peers):
@@ -251,10 +287,12 @@
     vmem = pl.BlockSpec(memory_space=pltpu.VMEM)
     return pl.pallas_call(
         functools.partial(projection_kernel, members, ctx_count, peers),
-        out_shape=[jax.ShapeDtypeStruct((part, columns), jnp.float32)]
-        + [jax.ShapeDtypeStruct((part, columns), jnp.bfloat16)] * (peers - 1),
+        out_shape=[
+            jax.ShapeDtypeStruct((peers // 2, part, columns), jnp.float32),
+            jax.ShapeDtypeStruct((peers // 2, part, columns), jnp.bfloat16),
+        ],
         in_specs=[vmem] * (1 + n),
-        out_specs=[vmem] * peers,
+        out_specs=[vmem] * 2,
         scratch_shapes=[
             pltpu.VMEM((n * q_dev, width), jnp.bfloat16),
             pltpu.VMEM((n * q_dev, columns), jnp.float32),
@@ -297,7 +335,12 @@
     def gather(x, chained):
         held = {(0, 0): x, (0, 1): move(x, 0, 1)}
         for k in steps:
-            held[k, 0] = move(x, -k, 0)
+            block = x
+            if not chained and 2 * k == high:
+                ready = {m: held[m] for m in held if m[0]}
+                block, ready = lax.optimization_barrier((block, ready))
+                held.update(ready)
+            held[k, 0] = move(block, -k, 0)
         behind = None
         for k in steps:
             block = held[k, 0]
@@ -316,8 +359,15 @@
     groups += [middle + flip[:2]] + [flip[i : i + 2] for i in range(2, len(flip), 2)]
     groups += [late, order[:1]]
     kv_local = new_keys.shape[1] // DH
-    table = jnp.concatenate([keep_tiles.reshape(-1), tile_count.reshape(-1), owner_slot])
-    new_rows = jnp.concatenate([new_keys, new_values], 1)
+    table, new_rows = pack_call(
+        owner_slot,
+        keep_tiles[0],
+        tile_count[0],
+        new_keys,
+        new_values,
+        cache_keys,
+        cache_values,
+    )
 
     def attend(members, blocks):
         return attention_call(
@@ -349,11 +399,14 @@
     attn = merge_call([back[m] for m in order], kv_local)
 
     held = gather(attn, True)
-    own, *sends = projection_call(order, ctx_count, [held[m] for m in order], out_weight, peers)
-    for j, piece in enumerate(sends, 1):
-        got = lax.ppermute(piece, "tp", [(i, i ^ j) for i in range(peers)])
-        own = own + got.astype(jnp.float32)
-    return own
+    own, send = projection_call(order, ctx_count, [held[m] for m in order], out_weight, peers)
+    got = lax.ppermute(send, "tp", [(i, i ^ 1) for i in range(peers)])
+    total = own[0] + got[0].astype(jnp.float32)
+    for j in range(1, peers // 2):
+        piece = (own[j] + got[j].astype(jnp.float32)).astype(jnp.bfloat16)
+        piece = lax.ppermute(piece, "tp", [(i, i ^ (2 * j)) for i in range(peers)])
+        total = total + piece.astype(jnp.float32)
+    return total
 
 
 def solution(mesh):

time: 90.5 us -> 87.2 us (0.964)
  waiting for transfers between devices: 25.4 us -> 20.3 us
  Pallas kernels: 26.1 us -> 30.5 us
  local copies, waits for them, and re-layouts: 5.39 us -> 1.41 us
  starting transfers between devices: 31.8 us -> 34.1 us
    ppermute x21, waiting for transfers between devices: 19 us -> 15 us  [move(): return lax.ppermute(x, 'ctx', pairs)]
    ppermute x3 -> x2, starting transfers between devices: 1.93 us -> 5.14 us  [the longest x1 5.07 us: body(): piece = lax.ppermute(piece, 'tp', [(i, i ^ 2 * j) for i in range(peers)])]
    pallas_call x4, Pallas kernels: 23.7 us -> 26.7 us  [attention_call(): pl.pallas_call(functools.partial(attention_kernel, members, ctx_count, gr...]
    unnamed x9 -> x14, local copies, waits for them, and re-layouts: 3.91 us -> 1.41 us
    pallas_call x0 -> x1, Pallas kernels: none -> 1.55 us  [pack_call(): pl.pallas_call(pack_kernel, out_shape=[jax.ShapeDtypeStruct((entries,), j...]
    ppermute x3 -> x2, waiting for transfers between devices: 6.4 us -> 5.32 us  [the longest x1 3.8 us: body(): piece = lax.ppermute(piece, 'tp', [(i, i ^ 2 * j) for i in range(peers)])]
    ppermute x21, starting transfers between devices: 29.9 us -> 29 us  [move(): return lax.ppermute(x, 'ctx', pairs)]
  transfers between devices with their start and end apart: 24 -> 23, of which waited for: 9 -> 11; matrix products, arithmetic and copies ran while one was open for 3% -> 0% of each run, Pallas kernels for 26% -> 32%
where the time goes in v4:
time: 87.2 us; the launch traced here: 87.3 us
  starting transfers between devices  34.1 us (39%)
  Pallas kernels  30.5 us (35%)
  waiting for transfers between devices  20.3 us (23%)
  local copies, waits for them, and re-layouts  1.41 us (2%)
    ppermute x21, starting transfers between devices, move(): return lax.ppermute(x, 'ctx', pairs)  29 us
    pallas_call x4, Pallas kernels, attention_call(): pl.pallas_call(functools.partial(attention_kernel, members, ctx_count, gr...  26.7 us
    ppermute x21, waiting for transfers between devices, move(): return lax.ppermute(x, 'ctx', pairs)  15 us
    ppermute x1, starting transfers between devices, body(): piece = lax.ppermute(piece, 'tp', [(i, i ^ 2 * j) for i in range(peers)])  5.07 us
    ppermute x1, waiting for transfers between devices, body(): piece = lax.ppermute(piece, 'tp', [(i, i ^ 2 * j) for i in range(peers)])  3.8 us
  transfers between devices with their start and end apart: 23, of which 11 were waited for; matrix products, arithmetic and copies ran while one was open for 0% of the time, Pallas kernels for 32%

profile of v4, /device:TPU:0, one launch (start us, length us, event | category | flops | bytes accessed | tf_op | source)
XLA Modules:
  0.0 87.3 jit_solution(588214418911927119)
XLA Ops:
  0.0 3.0 %collective-permute-start.1 = (bf16[32,2048]{1,0:T(8,128)(2,1)}, bf16[32,2048]{1,0:T(8,128)(2,1)S(1)}, u32[]{:S(2)}, u32[]{:S(2)}) collective-permute-start(bf16[32,2048]{1,0:T(8,128)(2,1)} %rest_0_), channel_id=1, source_target_pairs={{0,8},{4,12},{8,16},{12,20},{16,24},{20,28},{24,0},{28,4},{1,9},{5... | collective-permute-start | bytes 393224 | tf_op jit(solution)/shard_map/ppermute | solution.py:330
  3.0 2.0 %collective-permute-start = (bf16[32,2048]{1,0:T(8,128)(2,1)}, bf16[32,2048]{1,0:T(8,128)(2,1)S(1)}, u32[]{:S(2)}, u32[]{:S(2)}) collective-permute-start(bf16[32,2048]{1,0:T(8,128)(2,1)} %rest_0_), channel_id=1, source_target_pairs={{0,24},{4,28},{8,0},{12,4},{16,8},{20,12},{24,16},{28,20},{1,25},{... | collective-permute-start | bytes 393224 | tf_op jit(solution)/shard_map/ppermute | solution.py:330
  5.1 1.7 %collective-permute-start.4 = (bf16[32,2048]{1,0:T(8,128)(2,1)}, bf16[32,2048]{1,0:T(8,128)(2,1)S(1)}, u32[]{:S(2)}, u32[]{:S(2)}) collective-permute-start(bf16[32,2048]{1,0:T(8,128)(2,1)} %rest_0_), channel_id=1, source_target_pairs={{0,4},{4,0},{8,12},{12,8},{16,20},{20,16},{24,28},{28,24},{1,5},{5... | collective-permute-start | bytes 393224 | tf_op jit(solution)/shard_map/ppermute | solution.py:330
  6.8 0.0 copy-start.1
  6.8 0.0 copy-start.2
  6.8 1.6 %pack.1 = (s32[58]{0:T(128)}, bf16[32,512]{1,0:T(8,128)(2,1)}) custom-call(s32[8]{0:T(128)} %slot_ref.1, s32[2,24]{1,0:T(2,128)} %bitcast.6, s32[2]{0:T(128)} %bitcast.7, bf16[32,256]{1,0:T(8,128)(2,1)} %nk_ref.1, bf16[32,256]{1,0:T(8,128)(2,1)} %nv_ref.1, bf16[4096,256]{1,0:T(8,128)(2,1)} %k_ref.7, bf16[4096,256]{1,0:T(8,128)(2,1)} %v_ref.7), custom_call_target="tpu_custom_call" | custom-call | tf_op jit(solution)/shard_map/pack/pallas_call | solution.py:167
  8.3 1.3 %collective-permute-done.1.rest_1_ = bf16[32,2048]{1,0:T(8,128)(2,1)S(1)} collective-permute-done((bf16[32,2048]{1,0:T(8,128)(2,1)}, bf16[32,2048]{1,0:T(8,128)(2,1)S(1)}, u32[]{:S(2)}, u32[]{:S(2)}) %collective-permute-start.1) | collective-permute-done | bytes 131104 | tf_op jit(solution)/shard_map/ppermute | solution.py:330
  9.6 1.4 %collective-permute-done.rest_0_ = bf16[32,2048]{1,0:T(8,128)(2,1)S(1)} collective-permute-done((bf16[32,2048]{1,0:T(8,128)(2,1)}, bf16[32,2048]{1,0:T(8,128)(2,1)S(1)}, u32[]{:S(2)}, u32[]{:S(2)}) %collective-permute-start) | collective-permute-done | bytes 131104 | tf_op jit(solution)/shard_map/ppermute | solution.py:330
  11.0 1.3 %collective-permute-start.2 = (bf16[32,2048]{1,0:T(8,128)(2,1)}, bf16[32,2048]{1,0:T(8,128)(2,1)S(1)}, u32[]{:S(2)}, u32[]{:S(2)}) collective-permute-start(bf16[32,2048]{1,0:T(8,128)(2,1)} %rest_0_), channel_id=1, source_target_pairs={{0,16},{4,20},{8,24},{12,28},{16,0},{20,4},{24,8},{28,12},{1,17},{... | collective-permute-start | bytes 393224 | tf_op jit(solution)/shard_map/ppermute | solution.py:330
  12.3 1.5 %collective-permute-start.5 = (bf16[32,2048]{1,0:T(8,128)(2,1)S(1)}, bf16[32,2048]{1,0:T(8,128)(2,1)S(1)}, u32[]{:S(2)}, u32[]{:S(2)}) collective-permute-start(bf16[32,2048]{1,0:T(8,128)(2,1)S(1)} %collective-permute-done.rest_0_), channel_id=1, source_target_pairs={{0,4},{4,0},{8,12},{12,8},{16,20},{20,16},{24,28},{28,24},{1,5},{5... | collective-permute-start | bytes 393224 | tf_op jit(solution)/shard_map/ppermute | solution.py:330
  13.8 0.5 collective-permute-start.6
  14.3 0.0 copy-done.1
  14.3 0.0 copy-done.2
  14.3 0.0 copy-start.4
  14.3 0.8 copy-done.4
  15.1 0.6 copy-done.5
  15.7 6.5 %attention.4 = (bf16[32,2176]{1,0:T(8,128)(2,1)S(1)}, bf16[32,2176]{1,0:T(8,128)(2,1)S(1)}) custom-call(s32[58]{0:T(128)S(1)} %copy-done.5, bf16[32,512]{1,0:T(8,128)(2,1)S(1)} %copy-done.4, bf16[4096,256]{1,0:T(8,128)(2,1)S(1)} %copy-done.1, bf16[4096,256]{1,0:T(8,128)(2,1)S(1)} %copy-done.2, bf16[32,2048]{1,0:T(8,128)(2,1)S(1)} %collective-permute-done.rest_0_, ...), custom_call_target="tpu_custom_call" | custom-call | flops 3221225472 | bytes 8388608 | tf_op jit(solution)/shard_map/attention/pallas_call | solution.py:188
  22.2 0.6 collective-permute-start.7
  22.8 0.0 collective-permute-done.2.rest_0_
  22.8 3.3 %collective-permute-start.8 = (bf16[32,2176]{1,0:T(8,128)(2,1)S(1)}, bf16[32,2176]{1,0:T(8,128)(2,1)S(1)}, u32[]{:S(2)}, u32[]{:S(2)}) collective-permute-start(bf16[32,2176]{1,0:T(8,128)(2,1)S(1)} %get-tuple-element.36), channel_id=1, source_target_pairs={{0,24},{4,28},{8,0},{12,4},{16,8},{20,12},{24,16},{28,20},{1,25},{... | collective-permute-start | bytes 417800 | tf_op jit(solution)/shard_map/ppermute | solution.py:330
  26.1 0.0 collective-permute-done.5.rest_1_
  26.1 0.0 collective-permute-done.6.rest_2_
  26.1 1.5 %collective-permute-start.3 = (bf16[32,2048]{1,0:T(8,128)(2,1)S(1)}, bf16[32,2048]{1,0:T(8,128)(2,1)S(1)}, u32[]{:S(2)}, u32[]{:S(2)}) collective-permute-start(bf16[32,2048]{1,0:T(8,128)(2,1)S(1)} %collective-permute-done.2.rest_0_), channel_id=1, source_target_pairs={{0,4},{4,0},{8,12},{12,8},{16,20},{20,16},{24,28},{28,24},{1,5},{5... | collective-permute-start | bytes 393224 | tf_op jit(solution)/shard_map/ppermute | solution.py:330
  27.6 9.0 %attention.5 = (bf16[32,2176]{1,0:T(8,128)(2,1)S(1)}, bf16[32,2176]{1,0:T(8,128)(2,1)S(1)}, bf16[32,2176]{1,0:T(8,128)(2,1)S(1)}) custom-call(s32[58]{0:T(128)S(1)} %copy-done.5, bf16[32,512]{1,0:T(8,128)(2,1)S(1)} %copy-done.4, bf16[4096,256]{1,0:T(8,128)(2,1)S(1)} %copy-done.1, bf16[4096,256]{1,0:T(8,128)(2,1)S(1)} %copy-done.2, ...), custom_call_target="tpu_custom_call" | custom-call | flops 4831838208 | bytes 8388608 | tf_op jit(solution)/shard_map/attention/pallas_call | solution.py:188
  36.6 0.1 collective-permute-start.9
  36.7 0.0 collective-permute-done.4.rest_1_
  36.7 1.6 %collective-permute-start.11 = (bf16[32,2176]{1,0:T(8,128)(2,1)S(1)}, bf16[32,2176]{1,0:T(8,128)(2,1)S(1)}, u32[]{:S(2)}, u32[]{:S(2)}) collective-permute-start(bf16[32,2176]{1,0:T(8,128)(2,1)S(1)} %get-tuple-element.51), channel_id=1, source_target_pairs={{0,12},{4,8},{8,20},{12,16},{16,28},{20,24},{24,4},{28,0},{1,13},{... | collective-permute-start | bytes 417800 | tf_op jit(solution)/shard_map/ppermute | solution.py:330
  38.3 0.0 collective-permute-done.3.rest_0_
  38.3 3.2 %collective-permute-start.12 = (bf16[32,2176]{1,0:T(8,128)(2,1)S(1)}, bf16[32,2176]{1,0:T(8,128)(2,1)S(1)}, u32[]{:S(2)}, u32[]{:S(2)}) collective-permute-start(bf16[32,2176]{1,0:T(8,128)(2,1)S(1)} %get-tuple-element.40), channel_id=1, source_target_pairs={{0,28},{4,24},{8,4},{12,0},{16,12},{20,8},{24,20},{28,16},{1,29},{... | collective-permute-start | bytes 417800 | tf_op jit(solution)/shard_map/ppermute | solution.py:330
  41.5 0.0 collective-permute-done.7.refs_1_
  41.5 0.0 collective-permute-done.8.refs_2_
  41.5 0.0 copy-done.6
  41.5 6.5 %attention.6 = (bf16[32,2176]{1,0:T(8,128)(2,1)S(1)}, bf16[32,2176]{1,0:T(8,128)(2,1)S(1)}) custom-call(s32[58]{0:T(128)S(1)} %copy-done.6, bf16[32,512]{1,0:T(8,128)(2,1)S(1)} %copy-done.4, bf16[4096,256]{1,0:T(8,128)(2,1)S(1)} %copy-done.1, bf16[4096,256]{1,0:T(8,128)(2,1)S(1)} %copy-done.2, bf16[32,2048]{1,0:T(8,128)(2,1)S(1)} %collective-permute-done.3.rest_0_, ...), custom_call_target="tpu_custom_call" | custom-call | flops 3221225472 | bytes 8388608 | tf_op jit(solution)/shard_map/attention/pallas_call | solution.py:188
  48.0 0.6 collective-permute-start.10
  48.6 1.2 %collective-permute-start.13 = (bf16[32,2176]{1,0:T(8,128)(2,1)S(1)}, bf16[32,2176]{1,0:T(8,128)(2,1)S(1)}, u32[]{:S(2)}, u32[]{:S(2)}) collective-permute-start(bf16[32,2176]{1,0:T(8,128)(2,1)S(1)} %get-tuple-element.52), channel_id=1, source_target_pairs={{0,20},{4,16},{8,28},{12,24},{16,4},{20,0},{24,12},{28,8},{1,21},{... | collective-permute-start | bytes 417800 | tf_op jit(solution)/shard_map/ppermute | solution.py:330
  49.8 0.0 copy-done.3
  49.8 4.7 %attention.7.refs_0_ = bf16[32,2176]{1,0:T(8,128)(2,1)S(1)} custom-call(s32[58]{0:T(128)S(1)} %copy-done.6, bf16[32,512]{1,0:T(8,128)(2,1)S(1)} %copy-done.4, bf16[4096,256]{1,0:T(8,128)(2,1)S(1)} %copy-done.1, bf16[4096,256]{1,0:T(8,128)(2,1)S(1)} %copy-done.2, bf16[32,2048]{1,0:T(8,128)(2,1)S(1)} %copy-done.3), custom_call_target="tpu_custom_call" | custom-call | flops 1610612736 | bytes 8388608 | tf_op jit(solution)/shard_map/attention/pallas_call | solution.py:188
  54.5 0.0 collective-permute-done.9.refs_3_
  54.5 0.0 collective-permute-done.11.refs_5_
  54.5 0.0 collective-permute-done.12.refs_6_
  54.5 2.4 %collective-permute-done.13.refs_7_ = bf16[32,2176]{1,0:T(8,128)(2,1)S(1)} collective-permute-done((bf16[32,2176]{1,0:T(8,128)(2,1)S(1)}, bf16[32,2176]{1,0:T(8,128)(2,1)S(1)}, u32[]{:S(2)}, u32[]{:S(2)}) %collective-permute-start.13) | collective-permute-done | bytes 139296 | tf_op jit(solution)/shard_map/ppermute | solution.py:330
  56.9 0.0 collective-permute-done.10.refs_4_
  56.9 0.9 %merge.1.rest_0_ = bf16[32,2048]{1,0:T(8,128)(2,1)S(1)} custom-call(bf16[32,2176]{1,0:T(8,128)(2,1)S(1)} %attention.7.refs_0_, bf16[32,2176]{1,0:T(8,128)(2,1)S(1)} %collective-permute-done.7.refs_1_, bf16[32,2176]{1,0:T(8,128)(2,1)S(1)} %collective-permute-done.8.refs_2_, bf16[32,2176]{1,0:T(8,128)(2,1)S(1)} %collective-permute-done.9.refs_3_, ...), custom_call_target="tpu_custom_call" | custom-call | flops 1114112 | bytes 1114112 | tf_op jit(solution)/shard_map/merge/pallas_call | solution.py:246
  57.9 0.1 collective-permute-start.15
  57.9 3.8 %collective-permute-start.14 = (bf16[32,2048]{1,0:T(8,128)(2,1)S(1)}, bf16[32,2048]{1,0:T(8,128)(2,1)S(1)}, u32[]{:S(2)}, u32[]{:S(2)}) collective-permute-start(bf16[32,2048]{1,0:T(8,128)(2,1)S(1)} %merge.1.rest_0_), channel_id=1, source_target_pairs={{0,24},{4,28},{8,0},{12,4},{16,8},{20,12},{24,16},{28,20},{1,25},{... | collective-permute-start | bytes 393224 | tf_op jit(solution)/shard_map/ppermute | solution.py:330
  61.7 0.0 collective-permute-start.16
  61.8 2.9 %collective-permute-done.15.rest_2_ = bf16[32,2048]{1,0:T(8,128)(2,1)S(1)} collective-permute-done((bf16[32,2048]{1,0:T(8,128)(2,1)S(1)}, bf16[32,2048]{1,0:T(8,128)(2,1)S(1)}, u32[]{:S(2)}, u32[]{:S(2)}) %collective-permute-start.15) | collective-permute-done | bytes 131104 | tf_op jit(solution)/shard_map/ppermute | solution.py:330
  64.7 0.3 collective-permute-start.19
  64.9 1.8 %collective-permute-start.17 = (bf16[32,2048]{1,0:T(8,128)(2,1)S(1)}, bf16[32,2048]{1,0:T(8,128)(2,1)S(1)}, u32[]{:S(2)}, u32[]{:S(2)}) collective-permute-start(bf16[32,2048]{1,0:T(8,128)(2,1)S(1)} %merge.1.rest_0_), channel_id=1, source_target_pairs={{0,4},{4,0},{8,12},{12,8},{16,20},{20,16},{24,28},{28,24},{1,5},{5... | collective-permute-start | bytes 393224 | tf_op jit(solution)/shard_map/ppermute | solution.py:330
  66.7 0.0 collective-permute-done.14.rest_1_
  66.7 0.3 collective-permute-start.18
  67.0 1.9 %collective-permute-done.16.rest_3_ = bf16[32,2048]{1,0:T(8,128)(2,1)S(1)} collective-permute-done((bf16[32,2048]{1,0:T(8,128)(2,1)S(1)}, bf16[32,2048]{1,0:T(8,128)(2,1)S(1)}, u32[]{:S(2)}, u32[]{:S(2)}) %collective-permute-start.16) | collective-permute-done | bytes 131104 | tf_op jit(solution)/shard_map/ppermute | solution.py:330
  68.9 0.8 collective-permute-done.19.rest_6_
  69.7 0.7 collective-permute-start.20
  70.4 0.7 collective-permute-done.17.rest_4_
  71.1 1.4 %collective-permute-done.18.rest_5_ = bf16[32,2048]{1,0:T(8,128)(2,1)S(1)} collective-permute-done((bf16[32,2048]{1,0:T(8,128)(2,1)S(1)}, bf16[32,2048]{1,0:T(8,128)(2,1)S(1)}, u32[]{:S(2)}, u32[]{:S(2)}) %collective-permute-start.18) | collective-permute-done | bytes 131104 | tf_op jit(solution)/shard_map/ppermute | solution.py:330
  72.5 2.2 %collective-permute-done.20.rest_7_ = bf16[32,2048]{1,0:T(8,128)(2,1)S(1)} collective-permute-done((bf16[32,2048]{1,0:T(8,128)(2,1)S(1)}, bf16[32,2048]{1,0:T(8,128)(2,1)S(1)}, u32[]{:S(2)}, u32[]{:S(2)}) %collective-permute-start.20) | collective-permute-done | bytes 131104 | tf_op jit(solution)/shard_map/ppermute | solution.py:330
  74.6 0.0 copy-done
  74.6 1.4 %projection.1 = (f32[2,64,1024]{2,1,0:T(8,128)S(1)}, bf16[2,64,1024]{2,1,0:T(8,128)(2,1)S(1)}) custom-call(bf16[2048,1024]{1,0:T(8,128)(2,1)S(1)} %copy-done, bf16[32,2048]{1,0:T(8,128)(2,1)S(1)} %merge.1.rest_0_, bf16[32,2048]{1,0:T(8,128)(2,1)S(1)} %collective-permute-done.14.rest_1_, bf16[32,2048]{1,0:T(8,128)(2,1)S(1)} %collective-permute-done.15.rest_2_, ...), custom_call_target="tpu_custom_call" | custom-call | flops 1073741824 | bytes 4194304 | tf_op jit(solution)/shard_map/projection/pallas_call | solution.py:288
  76.0 0.1 collective-permute-start.21
  76.1 1.5 %collective-permute-done.21 = bf16[2,64,1024]{2,1,0:T(8,128)(2,1)S(1)} collective-permute-done((bf16[2,64,1024]{2,1,0:T(8,128)(2,1)S(1)}, bf16[2,64,1024]{2,1,0:T(8,128)(2,1)S(1)}, u32[]{:S(2)}, u32[]{:S(2)}) %collective-permute-start.21) | collective-permute-done | bytes 262176 | tf_op jit(solution)/shard_map/ppermute | solution.py:403
  77.6 5.1 %collective-permute-start.22 = (bf16[64,1024]{1,0:T(8,128)(2,1)S(1)}, bf16[64,1024]{1,0:T(8,128)(2,1)S(1)}, u32[]{:S(2)}, u32[]{:S(2)}) collective-permute-start(bf16[64,1024]{1,0:T(8,128)(2,1)S(1)} %fusion), channel_id=1, source_target_pairs={{0,2},{1,3},{2,0},{3,1},{4,6},{5,7},{6,4},{7,5},{8,10},{9,11},{10,... | collective-permute-start | bytes 393224 | tf_op jit(solution)/shard_map/ppermute | solution.py:407
  82.7 3.8 %collective-permute-done.22 = bf16[64,1024]{1,0:T(8,128)(2,1)S(1)} collective-permute-done((bf16[64,1024]{1,0:T(8,128)(2,1)S(1)}, bf16[64,1024]{1,0:T(8,128)(2,1)S(1)}, u32[]{:S(2)}, u32[]{:S(2)}) %collective-permute-start.22) | collective-permute-done | bytes 131104 | tf_op jit(solution)/shard_map/ppermute | solution.py:407
  86.5 0.7 bitcast_add_fusion
  (5 shorter events, 0.0 us)
Async XLA Ops:
  0.0 9.6 %collective-permute-start.1 = (bf16[32,2048]{1,0:T(8,128)(2,1)}, bf16[32,2048]{1,0:T(8,128)(2,1)S(1)}, u32[]{:S(2)}, u32[]{:S(2)}) collective-permute-start(bf16[32,2048]{1,0:T(8,128)(2,1)} %rest_0_), channel_id=1, source_target_pairs={{0,8},{4,12},{8,16},{12,20},{16,24},{20,28},{24,0},{28,4},{1,9},{5... | collective-permute-start | bytes 393224 | tf_op jit(solution)/shard_map/ppermute | solution.py:330
  3.0 8.0 %collective-permute-start = (bf16[32,2048]{1,0:T(8,128)(2,1)}, bf16[32,2048]{1,0:T(8,128)(2,1)S(1)}, u32[]{:S(2)}, u32[]{:S(2)}) collective-permute-start(bf16[32,2048]{1,0:T(8,128)(2,1)} %rest_0_), channel_id=1, source_target_pairs={{0,24},{4,28},{8,0},{12,4},{16,8},{20,12},{24,16},{28,20},{1,25},{... | collective-permute-start | bytes 393224 | tf_op jit(solution)/shard_map/ppermute | solution.py:330
  5.1 31.6 %collective-permute-start.4 = (bf16[32,2048]{1,0:T(8,128)(2,1)}, bf16[32,2048]{1,0:T(8,128)(2,1)S(1)}, u32[]{:S(2)}, u32[]{:S(2)}) collective-permute-start(bf16[32,2048]{1,0:T(8,128)(2,1)} %rest_0_), channel_id=1, source_target_pairs={{0,4},{4,0},{8,12},{12,8},{16,20},{20,16},{24,28},{28,24},{1,5},{5... | collective-permute-start | bytes 393224 | tf_op jit(solution)/shard_map/ppermute | solution.py:330
  6.8 7.6 %copy-start.1 = (bf16[4096,256]{1,0:T(8,128)(2,1)S(1)}, bf16[4096,256]{1,0:T(8,128)(2,1)}, u32[]{:S(2)}) copy-start(bf16[4096,256]{1,0:T(8,128)(2,1)} %k_ref.7) | copy-start | bytes 6291460
  6.8 7.6 %copy-start.2 = (bf16[4096,256]{1,0:T(8,128)(2,1)S(1)}, bf16[4096,256]{1,0:T(8,128)(2,1)}, u32[]{:S(2)}) copy-start(bf16[4096,256]{1,0:T(8,128)(2,1)} %v_ref.7) | copy-start | bytes 6291460
  11.0 11.8 %collective-permute-start.2 = (bf16[32,2048]{1,0:T(8,128)(2,1)}, bf16[32,2048]{1,0:T(8,128)(2,1)S(1)}, u32[]{:S(2)}, u32[]{:S(2)}) collective-permute-start(bf16[32,2048]{1,0:T(8,128)(2,1)} %rest_0_), channel_id=1, source_target_pairs={{0,16},{4,20},{8,24},{12,28},{16,0},{20,4},{24,8},{28,12},{1,17},{... | collective-permute-start | bytes 393224 | tf_op jit(solution)/shard_map/ppermute | solution.py:330
  12.3 13.8 %collective-permute-start.5 = (bf16[32,2048]{1,0:T(8,128)(2,1)S(1)}, bf16[32,2048]{1,0:T(8,128)(2,1)S(1)}, u32[]{:S(2)}, u32[]{:S(2)}) collective-permute-start(bf16[32,2048]{1,0:T(8,128)(2,1)S(1)} %collective-permute-done.rest_0_), channel_id=1, source_target_pairs={{0,4},{4,0},{8,12},{12,8},{16,20},{20,16},{24,28},{28,24},{1,5},{5... | collective-permute-start | bytes 393224 | tf_op jit(solution)/shard_map/ppermute | solution.py:330
  13.8 12.3 %collective-permute-start.6 = (bf16[32,2048]{1,0:T(8,128)(2,1)S(1)}, bf16[32,2048]{1,0:T(8,128)(2,1)S(1)}, u32[]{:S(2)}, u32[]{:S(2)}) collective-permute-start(bf16[32,2048]{1,0:T(8,128)(2,1)S(1)} %collective-permute-done.1.rest_1_), channel_id=1, source_target_pairs={{0,4},{4,0},{8,12},{12,8},{16,20},{20,16},{24,28},{28,24},{1,5},{5... | collective-permute-start | bytes 393224 | tf_op jit(solution)/shard_map/ppermute | solution.py:330
  14.3 0.8 copy-start.4
  15.1 0.6 copy-start.5
  22.2 19.2 %collective-permute-start.7 = (bf16[32,2176]{1,0:T(8,128)(2,1)S(1)}, bf16[32,2176]{1,0:T(8,128)(2,1)S(1)}, u32[]{:S(2)}, u32[]{:S(2)}) collective-permute-start(bf16[32,2176]{1,0:T(8,128)(2,1)S(1)} %get-tuple-element.43), channel_id=1, source_target_pairs={{0,8},{4,12},{8,16},{12,20},{16,24},{20,28},{24,0},{28,4},{1,9},{5... | collective-permute-start | bytes 417800 | tf_op jit(solution)/shard_map/ppermute | solution.py:330
  22.8 18.7 %copy-start.6 = (s32[58]{0:T(128)S(1)}, s32[58]{0:T(128)}, u32[]{:S(2)}) copy-start(s32[58]{0:T(128)} %get-tuple-element.31.table_ref) | copy-start | bytes 700
  22.8 18.7 %collective-permute-start.8 = (bf16[32,2176]{1,0:T(8,128)(2,1)S(1)}, bf16[32,2176]{1,0:T(8,128)(2,1)S(1)}, u32[]{:S(2)}, u32[]{:S(2)}) collective-permute-start(bf16[32,2176]{1,0:T(8,128)(2,1)S(1)} %get-tuple-element.36), channel_id=1, source_target_pairs={{0,24},{4,28},{8,0},{12,4},{16,8},{20,12},{24,16},{28,20},{1,25},{... | collective-permute-start | bytes 417800 | tf_op jit(solution)/shard_map/ppermute | solution.py:330
  26.1 12.2 %collective-permute-start.3 = (bf16[32,2048]{1,0:T(8,128)(2,1)S(1)}, bf16[32,2048]{1,0:T(8,128)(2,1)S(1)}, u32[]{:S(2)}, u32[]{:S(2)}) collective-permute-start(bf16[32,2048]{1,0:T(8,128)(2,1)S(1)} %collective-permute-done.2.rest_0_), channel_id=1, source_target_pairs={{0,4},{4,0},{8,12},{12,8},{16,20},{20,16},{24,28},{28,24},{1,5},{5... | collective-permute-start | bytes 393224 | tf_op jit(solution)/shard_map/ppermute | solution.py:330
  36.6 17.9 %collective-permute-start.9 = (bf16[32,2176]{1,0:T(8,128)(2,1)S(1)}, bf16[32,2176]{1,0:T(8,128)(2,1)S(1)}, u32[]{:S(2)}, u32[]{:S(2)}) collective-permute-start(bf16[32,2176]{1,0:T(8,128)(2,1)S(1)} %get-tuple-element.50), channel_id=1, source_target_pairs={{0,16},{4,20},{8,24},{12,28},{16,0},{20,4},{24,8},{28,12},{1,17},{... | collective-permute-start | bytes 417800 | tf_op jit(solution)/shard_map/ppermute | solution.py:330
  36.7 17.8 %collective-permute-start.11 = (bf16[32,2176]{1,0:T(8,128)(2,1)S(1)}, bf16[32,2176]{1,0:T(8,128)(2,1)S(1)}, u32[]{:S(2)}, u32[]{:S(2)}) collective-permute-start(bf16[32,2176]{1,0:T(8,128)(2,1)S(1)} %get-tuple-element.51), channel_id=1, source_target_pairs={{0,12},{4,8},{8,20},{12,16},{16,28},{20,24},{24,4},{28,0},{1,13},{... | collective-permute-start | bytes 417800 | tf_op jit(solution)/shard_map/ppermute | solution.py:330
  38.3 11.5 %copy-start.3 = (bf16[32,2048]{1,0:T(8,128)(2,1)S(1)}, bf16[32,2048]{1,0:T(8,128)(2,1)}, u32[]{:S(2)}) copy-start(bf16[32,2048]{1,0:T(8,128)(2,1)} %rest_0_) | copy-start | bytes 393220
  38.3 16.2 %collective-permute-start.12 = (bf16[32,2176]{1,0:T(8,128)(2,1)S(1)}, bf16[32,2176]{1,0:T(8,128)(2,1)S(1)}, u32[]{:S(2)}, u32[]{:S(2)}) collective-permute-start(bf16[32,2176]{1,0:T(8,128)(2,1)S(1)} %get-tuple-element.40), channel_id=1, source_target_pairs={{0,28},{4,24},{8,4},{12,0},{16,12},{20,8},{24,20},{28,16},{1,29},{... | collective-permute-start | bytes 417800 | tf_op jit(solution)/shard_map/ppermute | solution.py:330
  48.0 8.9 %collective-permute-start.10 = (bf16[32,2176]{1,0:T(8,128)(2,1)S(1)}, bf16[32,2176]{1,0:T(8,128)(2,1)S(1)}, u32[]{:S(2)}, u32[]{:S(2)}) collective-permute-start(bf16[32,2176]{1,0:T(8,128)(2,1)S(1)} %get-tuple-element.46), channel_id=1, source_target_pairs={{0,4},{4,0},{8,12},{12,8},{16,20},{20,16},{24,28},{28,24},{1,5},{5... | collective-permute-start | bytes 417800 | tf_op jit(solution)/shard_map/ppermute | solution.py:330
  48.6 8.3 %collective-permute-start.13 = (bf16[32,2176]{1,0:T(8,128)(2,1)S(1)}, bf16[32,2176]{1,0:T(8,128)(2,1)S(1)}, u32[]{:S(2)}, u32[]{:S(2)}) collective-permute-start(bf16[32,2176]{1,0:T(8,128)(2,1)S(1)} %get-tuple-element.52), channel_id=1, source_target_pairs={{0,20},{4,16},{8,28},{12,24},{16,4},{20,0},{24,12},{28,8},{1,21},{... | collective-permute-start | bytes 417800 | tf_op jit(solution)/shard_map/ppermute | solution.py:330
  49.8 24.8 %copy-start = (bf16[2048,1024]{1,0:T(8,128)(2,1)S(1)}, bf16[2048,1024]{1,0:T(8,128)(2,1)}, u32[]{:S(2)}) copy-start(bf16[2048,1024]{1,0:T(8,128)(2,1)} %w_ref.1) | copy-start | bytes 12582916
  57.9 6.8 %collective-permute-start.15 = (bf16[32,2048]{1,0:T(8,128)(2,1)S(1)}, bf16[32,2048]{1,0:T(8,128)(2,1)S(1)}, u32[]{:S(2)}, u32[]{:S(2)}) collective-permute-start(bf16[32,2048]{1,0:T(8,128)(2,1)S(1)} %merge.1.rest_0_), channel_id=1, source_target_pairs={{0,8},{4,12},{8,16},{12,20},{16,24},{20,28},{24,0},{28,4},{1,9},{5... | collective-permute-start | bytes 393224 | tf_op jit(solution)/shard_map/ppermute | solution.py:330
  57.9 8.8 %collective-permute-start.14 = (bf16[32,2048]{1,0:T(8,128)(2,1)S(1)}, bf16[32,2048]{1,0:T(8,128)(2,1)S(1)}, u32[]{:S(2)}, u32[]{:S(2)}) collective-permute-start(bf16[32,2048]{1,0:T(8,128)(2,1)S(1)} %merge.1.rest_0_), channel_id=1, source_target_pairs={{0,24},{4,28},{8,0},{12,4},{16,8},{20,12},{24,16},{28,20},{1,25},{... | collective-permute-start | bytes 393224 | tf_op jit(solution)/shard_map/ppermute | solution.py:330
  61.7 7.2 %collective-permute-start.16 = (bf16[32,2048]{1,0:T(8,128)(2,1)S(1)}, bf16[32,2048]{1,0:T(8,128)(2,1)S(1)}, u32[]{:S(2)}, u32[]{:S(2)}) collective-permute-start(bf16[32,2048]{1,0:T(8,128)(2,1)S(1)} %merge.1.rest_0_), channel_id=1, source_target_pairs={{0,16},{4,20},{8,24},{12,28},{16,0},{20,4},{24,8},{28,12},{1,17},{... | collective-permute-start | bytes 393224 | tf_op jit(solution)/shard_map/ppermute | solution.py:330
  64.7 5.0 %collective-permute-start.19 = (bf16[32,2048]{1,0:T(8,128)(2,1)S(1)}, bf16[32,2048]{1,0:T(8,128)(2,1)S(1)}, u32[]{:S(2)}, u32[]{:S(2)}) collective-permute-start(bf16[32,2048]{1,0:T(8,128)(2,1)S(1)} %collective-permute-done.15.rest_2_), channel_id=1, source_target_pairs={{0,4},{4,0},{8,12},{12,8},{16,20},{20,16},{24,28},{28,24},{1,5},{5... | collective-permute-start | bytes 393224 | tf_op jit(solution)/shard_map/ppermute | solution.py:330
  64.9 6.1 %collective-permute-start.17 = (bf16[32,2048]{1,0:T(8,128)(2,1)S(1)}, bf16[32,2048]{1,0:T(8,128)(2,1)S(1)}, u32[]{:S(2)}, u32[]{:S(2)}) collective-permute-start(bf16[32,2048]{1,0:T(8,128)(2,1)S(1)} %merge.1.rest_0_), channel_id=1, source_target_pairs={{0,4},{4,0},{8,12},{12,8},{16,20},{20,16},{24,28},{28,24},{1,5},{5... | collective-permute-start | bytes 393224 | tf_op jit(solution)/shard_map/ppermute | solution.py:330
  66.7 5.7 %collective-permute-start.18 = (bf16[32,2048]{1,0:T(8,128)(2,1)S(1)}, bf16[32,2048]{1,0:T(8,128)(2,1)S(1)}, u32[]{:S(2)}, u32[]{:S(2)}) collective-permute-start(bf16[32,2048]{1,0:T(8,128)(2,1)S(1)} %collective-permute-done.14.rest_1_), channel_id=1, source_target_pairs={{0,4},{4,0},{8,12},{12,8},{16,20},{20,16},{24,28},{28,24},{1,5},{5... | collective-permute-start | bytes 393224 | tf_op jit(solution)/shard_map/ppermute | solution.py:330
  69.7 5.0 %collective-permute-start.20 = (bf16[32,2048]{1,0:T(8,128)(2,1)S(1)}, bf16[32,2048]{1,0:T(8,128)(2,1)S(1)}, u32[]{:S(2)}, u32[]{:S(2)}) collective-permute-start(bf16[32,2048]{1,0:T(8,128)(2,1)S(1)} %collective-permute-done.16.rest_3_), channel_id=1, source_target_pairs={{0,4},{4,0},{8,12},{12,8},{16,20},{20,16},{24,28},{28,24},{1,5},{5... | collective-permute-start | bytes 393224 | tf_op jit(solution)/shard_map/ppermute | solution.py:330
  76.0 1.6 %collective-permute-start.21 = (bf16[2,64,1024]{2,1,0:T(8,128)(2,1)S(1)}, bf16[2,64,1024]{2,1,0:T(8,128)(2,1)S(1)}, u32[]{:S(2)}, u32[]{:S(2)}) collective-permute-start(bf16[2,64,1024]{2,1,0:T(8,128)(2,1)S(1)} %get-tuple-element.56), channel_id=1, source_target_pairs={{0,1},{1,0},{2,3},{3,2},{4,5},{5,4},{6,7},{7,6},{8,9},{9,8},{10,11... | collective-permute-start | bytes 786440 | tf_op jit(solution)/shard_map/ppermute | solution.py:403
  77.6 8.9 %collective-permute-start.22 = (bf16[64,1024]{1,0:T(8,128)(2,1)S(1)}, bf16[64,1024]{1,0:T(8,128)(2,1)S(1)}, u32[]{:S(2)}, u32[]{:S(2)}) collective-permute-start(bf16[64,1024]{1,0:T(8,128)(2,1)S(1)} %fusion), channel_id=1, source_target_pairs={{0,2},{1,3},{2,0},{3,1},{4,6},{5,7},{6,4},{7,5},{8,10},{9,11},{10,... | collective-permute-start | bytes 393224 | tf_op jit(solution)/shard_map/ppermute | solution.py:407

commit v5 on v4

--- a/solution.py
+++ b/solution.py
@@ -27,12 +27,14 @@
 
 
 def attention_kernel(
-    members, ctx_count, group, kv_local, slots, table_ref, new_ref, k_ref, v_ref, *rest
+    members, ctx_count, group, kv_local, slots, turn, table_ref, new_ref, k_ref, v_ref, *rest
 ):
     blocks = len(members)
     q_refs, rest = rest[:blocks], rest[blocks:]
     out_refs, rest = rest[:blocks], rest[blocks:]
-    q_ref, turned_ref, acc_ref, max_ref = rest
+    turned_ref, acc_ref, max_ref = rest[-3:]
+    kept_ref = rest[0] if turn else v_ref
+    last = kept_ref.shape[2] - TILE
     q_dev = q_refs[0].shape[0]
     heads = kv_local * group
     rows = q_dev * group
@@ -47,7 +49,7 @@
         return table_ref[kv_local * (slots + 1) + ctx]
 
     def turned(x):
-        return x.astype(jnp.float32).T.astype(jnp.bfloat16)
+        return x.T
 
     def fold(g, b, s, values, first=False):
         peak = jnp.max(s, axis=0, keepdims=True) * scale
@@ -66,17 +68,20 @@
 
     for g in range(kv_local):
         fresh_keys = jnp.concatenate([new_ref[:, g * DH : (g + 1) * DH], padding], 0)
-        fresh_values = new_ref[:, (kv_local + g) * DH : (kv_local + g + 1) * DH]
-        fresh_values = jnp.concatenate(
-            [turned(jnp.concatenate([fresh_values, padding], 0)), ones_tile], 0
-        )
+        if turn:
+            fresh_values = new_ref[:, (kv_local + g) * DH : (kv_local + g + 1) * DH]
+            fresh_values = jnp.concatenate(
+                [turned(jnp.concatenate([fresh_values, padding], 0)), ones_tile], 0
+            )
+            kept_ref[g, :, last:] = fresh_values
+        else:
+            fresh_values = kept_ref[g, :, last:]
         for b in range(blocks):
-            for h in range(group):
-                head = g * group + h
-                q_ref[h * q_dev : (h + 1) * q_dev, :] = q_refs[b][
-                    :, head * DH : (head + 1) * DH
-                ].astype(jnp.float32)
-            turned_ref[g, b] = q_ref[...].T.astype(jnp.bfloat16)
+            columns = [
+                q_refs[b][:, (g * group + h) * DH : (g * group + h + 1) * DH]
+                for h in range(group)
+            ]
+            turned_ref[g, b] = turned(jnp.concatenate(columns, 0))
             s = jnp.dot(fresh_keys, turned_ref[g, b], preferred_element_type=jnp.float32)
             shift = (slot_of(flipped(me, ctx_count, *members[b])) - slot_of(me)) * q_dev
             live = (place_key < q_dev) & (place_row - place_key + shift >= 0)
@@ -84,6 +89,7 @@
 
     def load_chunk(g, chunk):
         cols = slice(g * DH, (g + 1) * DH)
+        whole = pl.ds(pl.multiple_of(chunk * span, span), span)
         key_parts, value_parts = [], []
         for i in range(CHUNK):
             slot = chunk * CHUNK + i
@@ -91,9 +97,15 @@
             tile = table_ref[g * slots + jnp.where(live, slot, 0)]
             at = pl.ds(pl.multiple_of(tile * TILE, TILE), TILE)
             key_parts.append(k_ref[at, cols])
-            tail = jnp.concatenate([turned(v_ref[at, cols]), ones_tile], 0)
-            value_parts.append(jnp.where(live, tail, jnp.zeros_like(tail)))
-        return jnp.concatenate(key_parts, 0), jnp.concatenate(value_parts, 1)
+            if turn:
+                tail = jnp.concatenate([turned(v_ref[at, cols]), ones_tile], 0)
+                value_parts.append(jnp.where(live, tail, jnp.zeros_like(tail)))
+        keys = jnp.concatenate(key_parts, 0)
+        if not turn:
+            return keys, kept_ref[g, :, whole]
+        values = jnp.concatenate(value_parts, 1)
+        kept_ref[g, :, whole] = values
+        return keys, values
 
     def run(kv_heads, chunk):
         loaded = {g: load_chunk(g, chunk) for g in kv_heads}
@@ -177,7 +189,9 @@
     )(slot, keep, count, new_keys, new_values, keys, values)
 
 
-def attention_call(members, ctx_count, kv_local, slots, blocks, table, new_rows, keys, values):
+def attention_call(
+    members, ctx_count, kv_local, slots, turn, blocks, table, new_rows, keys, values
+):
     n = len(blocks)
     q_dev, width = blocks[0].shape
     group = width // DH // kv_local
@@ -185,13 +199,16 @@
     smem = pl.BlockSpec(memory_space=pltpu.SMEM)
     vmem = pl.BlockSpec(memory_space=pltpu.VMEM)
     work = n * rows * kv_local * slots * TILE
+    kept = -(-slots // CHUNK) * CHUNK + 1
     return pl.pallas_call(
-        functools.partial(attention_kernel, members, ctx_count, group, kv_local, slots),
-        out_shape=[jax.ShapeDtypeStruct((q_dev, width + LANES), jnp.bfloat16)] * n,
+        functools.partial(
+            attention_kernel, members, ctx_count, group, kv_local, slots, turn
+        ),
+        out_shape=[jax.ShapeDtypeStruct((q_dev, width + LANES), jnp.bfloat16)] * n
+        + [jax.ShapeDtypeStruct((kv_local, DH + ONES, kept * TILE), jnp.bfloat16)] * turn,
         in_specs=[smem] + [vmem] * (3 + n),
-        out_specs=[vmem] * n,
+        out_specs=[vmem] * (n + turn),
         scratch_shapes=[
-            pltpu.VMEM((rows, DH), jnp.float32),
             pltpu.VMEM((kv_local, n, DH, rows), jnp.bfloat16),
             pltpu.VMEM((kv_local, n, DH + ONES, rows), jnp.float32),
             pltpu.VMEM((kv_local, n, 8, rows), jnp.float32),
@@ -369,19 +386,21 @@
         cache_values,
     )
 
-    def attend(members, blocks):
+    def attend(members, blocks, turn, values):
         return attention_call(
             members,
             ctx_count,
             kv_local,
             keep_tiles.shape[2],
+            turn,
             blocks,
             table,
             new_rows,
             cache_keys,
-            cache_values,
+            values,
         )
 
+    values = cache_values
     parts, back = {}, {}
     last = None
     for index, members in enumerate(groups):
@@ -392,7 +411,10 @@
             returned = {m: back[m] for m in groups[index - 2] if 2 * m[0] != high}
             blocks, returned = lax.optimization_barrier((blocks, returned))
             back.update(returned)
-        parts.update(zip(members, attend(members, blocks)))
+        outs = attend(members, blocks, index == 0, values)
+        parts.update(zip(members, outs))
+        if index == 0:
+            values = outs[-1]
         last = members[-1]
         for m in members:
             back[m] = parts[m] if m == (0, 0) else move(parts[m], *m)

time: 87.2 us -> 85.7 us (0.983)
  Pallas kernels: 30.5 us -> 24.3 us
  starting transfers between devices: 34.1 us -> 38.2 us
    pallas_call x4, Pallas kernels: 26.7 us -> 20.4 us  [attention_call(): pl.pallas_call(functools.partial(attention_kernel, members, ctx_count, gr...]
    ppermute x21, starting transfers between devices: 29 us -> 32.1 us  [move(): return lax.ppermute(x, 'ctx', pairs)]
    ppermute x1, starting transfers between devices: 5.07 us -> 6.01 us  [body(): piece = lax.ppermute(piece, 'tp', [(i, i ^ 2 * j) for i in range(peers)])]
  transfers between devices with their start and end apart: 23 -> 23, of which waited for: 11 -> 10; matrix products, arithmetic and copies ran while one was open for 0% -> 0% of each run, Pallas kernels for 32% -> 26%
where the time goes in v5:
time: 85.7 us; the launch traced here: 85.8 us
  starting transfers between devices  38.2 us (45%)
  Pallas kernels  24.3 us (28%)
  waiting for transfers between devices  20.9 us (24%)
  local copies, waits for them, and re-layouts  1.38 us (2%)
    ppermute x21, starting transfers between devices, move(): return lax.ppermute(x, 'ctx', pairs)  32.1 us
    pallas_call x4, Pallas kernels, attention_call(): pl.pallas_call(functools.partial(attention_kernel, members, ctx_count, gr...  20.4 us
    ppermute x21, waiting for transfers between devices, move(): return lax.ppermute(x, 'ctx', pairs)  15.6 us
    ppermute x1, starting transfers between devices, body(): piece = lax.ppermute(piece, 'tp', [(i, i ^ 2 * j) for i in range(peers)])  6.01 us
    ppermute x1, waiting for transfers between devices, body(): piece = lax.ppermute(piece, 'tp', [(i, i ^ 2 * j) for i in range(peers)])  3.8 us
  transfers between devices with their start and end apart: 23, of which 10 were waited for; matrix products, arithmetic and copies ran while one was open for 0% of the time, Pallas kernels for 26%

profile of v5, /device:TPU:0, one launch (start us, length us, event | category | flops | bytes accessed | tf_op | source)
XLA Modules:
  0.0 85.8 jit_solution(7004837606237790513)
XLA Ops:
  0.0 5.0 %collective-permute-start = (bf16[32,2048]{1,0:T(8,128)(2,1)}, bf16[32,2048]{1,0:T(8,128)(2,1)S(1)}, u32[]{:S(2)}, u32[]{:S(2)}) collective-permute-start(bf16[32,2048]{1,0:T(8,128)(2,1)} %rest_0_), channel_id=1, source_target_pairs={{0,24},{4,28},{8,0},{12,4},{16,8},{20,12},{24,16},{28,20},{1,25},{... | collective-permute-start | bytes 393224 | tf_op jit(solution)/shard_map/ppermute | solution.py:347
  5.0 0.0 collective-permute-start.1
  5.1 1.5 %collective-permute-start.4 = (bf16[32,2048]{1,0:T(8,128)(2,1)}, bf16[32,2048]{1,0:T(8,128)(2,1)S(1)}, u32[]{:S(2)}, u32[]{:S(2)}) collective-permute-start(bf16[32,2048]{1,0:T(8,128)(2,1)} %rest_0_), channel_id=1, source_target_pairs={{0,4},{4,0},{8,12},{12,8},{16,20},{20,16},{24,28},{28,24},{1,5},{5... | collective-permute-start | bytes 393224 | tf_op jit(solution)/shard_map/ppermute | solution.py:347
  6.5 0.0 copy-start.1
  6.5 0.0 copy-start.2
  6.5 1.6 %pack.1 = (s32[58]{0:T(128)}, bf16[32,512]{1,0:T(8,128)(2,1)}) custom-call(s32[8]{0:T(128)} %slot_ref.1, s32[2,24]{1,0:T(2,128)} %bitcast.6, s32[2]{0:T(128)} %bitcast.7, bf16[32,256]{1,0:T(8,128)(2,1)} %nk_ref.1, bf16[32,256]{1,0:T(8,128)(2,1)} %nv_ref.1, bf16[4096,256]{1,0:T(8,128)(2,1)} %k_ref.7, bf16[4096,256]{1,0:T(8,128)(2,1)} %v_ref.1), custom_call_target="tpu_custom_call" | custom-call | tf_op jit(solution)/shard_map/pack/pallas_call | solution.py:179
  8.1 1.2 %collective-permute-done.rest_0_ = bf16[32,2048]{1,0:T(8,128)(2,1)S(1)} collective-permute-done((bf16[32,2048]{1,0:T(8,128)(2,1)}, bf16[32,2048]{1,0:T(8,128)(2,1)S(1)}, u32[]{:S(2)}, u32[]{:S(2)}) %collective-permute-start) | collective-permute-done | bytes 131104 | tf_op jit(solution)/shard_map/ppermute | solution.py:347
  9.3 2.8 %collective-permute-done.1.rest_1_ = bf16[32,2048]{1,0:T(8,128)(2,1)S(1)} collective-permute-done((bf16[32,2048]{1,0:T(8,128)(2,1)}, bf16[32,2048]{1,0:T(8,128)(2,1)S(1)}, u32[]{:S(2)}, u32[]{:S(2)}) %collective-permute-start.1) | collective-permute-done | bytes 131104 | tf_op jit(solution)/shard_map/ppermute | solution.py:347
  12.0 0.4 collective-permute-start.2
  12.4 1.5 %collective-permute-start.5 = (bf16[32,2048]{1,0:T(8,128)(2,1)S(1)}, bf16[32,2048]{1,0:T(8,128)(2,1)S(1)}, u32[]{:S(2)}, u32[]{:S(2)}) collective-permute-start(bf16[32,2048]{1,0:T(8,128)(2,1)S(1)} %collective-permute-done.rest_0_), channel_id=1, source_target_pairs={{0,4},{4,0},{8,12},{12,8},{16,20},{20,16},{24,28},{28,24},{1,5},{5... | collective-permute-start | bytes 393224 | tf_op jit(solution)/shard_map/ppermute | solution.py:347
  13.9 0.5 collective-permute-start.6
  14.4 0.0 copy-done.1
  14.4 0.0 copy-done.2
  14.4 0.8 copy-done.4
  15.2 0.6 copy-done.6
  15.8 5.0 %attention.4 = (bf16[32,2176]{1,0:T(8,128)(2,1)S(1)}, bf16[32,2176]{1,0:T(8,128)(2,1)S(1)}, bf16[2,144,3200]{2,1,0:T(8,128)(2,1)S(1)}) custom-call(s32[58]{0:T(128)S(1)} %copy-done.6, bf16[32,512]{1,0:T(8,128)(2,1)S(1)} %copy-done.4, bf16[4096,256]{1,0:T(8,128)(2,1)S(1)} %copy-done.2, bf16[4096,256]{1,0:T(8,128)(2,1)S(1)} %copy-done.1, ...), custom_call_target="tpu_custom_call" | custom-call | flops 3221225472 | bytes 8388608 | tf_op jit(solution)/shard_map/attention/pallas_call | solution.py:203
  20.8 2.7 %collective-permute-start.8 = (bf16[32,2176]{1,0:T(8,128)(2,1)S(1)}, bf16[32,2176]{1,0:T(8,128)(2,1)S(1)}, u32[]{:S(2)}, u32[]{:S(2)}) collective-permute-start(bf16[32,2176]{1,0:T(8,128)(2,1)S(1)} %get-tuple-element.38), channel_id=1, source_target_pairs={{0,24},{4,28},{8,0},{12,4},{16,8},{20,12},{24,16},{28,20},{1,25},{... | collective-permute-start | bytes 417800 | tf_op jit(solution)/shard_map/ppermute | solution.py:347
  23.5 0.0 collective-permute-done.2.rest_0_
  23.5 0.0 collective-permute-start.7
  23.5 0.0 collective-permute-done.5.rest_1_
  23.5 0.0 collective-permute-done.6.rest_2_
  23.6 2.9 %collective-permute-start.3 = (bf16[32,2048]{1,0:T(8,128)(2,1)S(1)}, bf16[32,2048]{1,0:T(8,128)(2,1)S(1)}, u32[]{:S(2)}, u32[]{:S(2)}) collective-permute-start(bf16[32,2048]{1,0:T(8,128)(2,1)S(1)} %collective-permute-done.2.rest_0_), channel_id=1, source_target_pairs={{0,4},{4,0},{8,12},{12,8},{16,20},{20,16},{24,28},{28,24},{1,5},{5... | collective-permute-start | bytes 393224 | tf_op jit(solution)/shard_map/ppermute | solution.py:347
  26.4 6.7 %attention.5 = (bf16[32,2176]{1,0:T(8,128)(2,1)S(1)}, bf16[32,2176]{1,0:T(8,128)(2,1)S(1)}, bf16[32,2176]{1,0:T(8,128)(2,1)S(1)}) custom-call(s32[58]{0:T(128)S(1)} %copy-done.6, bf16[32,512]{1,0:T(8,128)(2,1)S(1)} %copy-done.4, bf16[4096,256]{1,0:T(8,128)(2,1)S(1)} %copy-done.2, bf16[2,144,3200]{2,1,0:T(8,128)(2,1)S(1)} %get-tuple-element.36.v_ref, ...), custom_call_target="tpu_custom_call" | custom-call | flops 4831838208 | bytes 8388608 | tf_op jit(solution)/shard_map/attention/pallas_call | solution.py:203
  33.2 0.1 collective-permute-start.11
  33.2 0.0 collective-permute-done.4.rest_1_
  33.2 4.7 %collective-permute-start.12 = (bf16[32,2176]{1,0:T(8,128)(2,1)S(1)}, bf16[32,2176]{1,0:T(8,128)(2,1)S(1)}, u32[]{:S(2)}, u32[]{:S(2)}) collective-permute-start(bf16[32,2176]{1,0:T(8,128)(2,1)S(1)} %get-tuple-element.42), channel_id=1, source_target_pairs={{0,28},{4,24},{8,4},{12,0},{16,12},{20,8},{24,20},{28,16},{1,29},{... | collective-permute-start | bytes 417800 | tf_op jit(solution)/shard_map/ppermute | solution.py:347
  37.9 0.0 collective-permute-done.3.rest_0_
  37.9 0.0 collective-permute-start.9
  38.0 0.0 collective-permute-done.8.refs_2_
  38.0 0.0 collective-permute-done.7.refs_1_
  38.0 0.0 copy-done.7
  38.0 5.0 %attention.6 = (bf16[32,2176]{1,0:T(8,128)(2,1)S(1)}, bf16[32,2176]{1,0:T(8,128)(2,1)S(1)}) custom-call(s32[58]{0:T(128)S(1)} %copy-done.7, bf16[32,512]{1,0:T(8,128)(2,1)S(1)} %copy-done.4, bf16[4096,256]{1,0:T(8,128)(2,1)S(1)} %copy-done.2, bf16[2,144,3200]{2,1,0:T(8,128)(2,1)S(1)} %get-tuple-element.36.v_ref, ...), custom_call_target="tpu_custom_call" | custom-call | flops 3221225472 | bytes 8388608 | tf_op jit(solution)/shard_map/attention/pallas_call | solution.py:203
  43.0 0.4 collective-permute-start.10
  43.4 3.4 %collective-permute-start.13 = (bf16[32,2176]{1,0:T(8,128)(2,1)S(1)}, bf16[32,2176]{1,0:T(8,128)(2,1)S(1)}, u32[]{:S(2)}, u32[]{:S(2)}) collective-permute-start(bf16[32,2176]{1,0:T(8,128)(2,1)S(1)} %get-tuple-element.54), channel_id=1, source_target_pairs={{0,20},{4,16},{8,28},{12,24},{16,4},{20,0},{24,12},{28,8},{1,21},{... | collective-permute-start | bytes 417800 | tf_op jit(solution)/shard_map/ppermute | solution.py:347
  46.8 0.0 copy-done.3
  46.8 0.0 copy-done.5
  46.8 3.7 %attention.7.refs_0_ = bf16[32,2176]{1,0:T(8,128)(2,1)S(1)} custom-call(s32[58]{0:T(128)S(1)} %copy-done.7, bf16[32,512]{1,0:T(8,128)(2,1)S(1)} %copy-done.5, bf16[4096,256]{1,0:T(8,128)(2,1)S(1)} %copy-done.2, bf16[2,144,3200]{2,1,0:T(8,128)(2,1)S(1)} %get-tuple-element.36.v_ref, bf16[32,2048]{1,0:T(8,128)(2,1)S(1)} %copy-done.3), custom_call_target="tpu_custom_call" | custom-call | flops 1610612736 | bytes 8388608 | tf_op jit(solution)/shard_map/attention/pallas_call | solution.py:203
  50.5 0.0 collective-permute-done.11.refs_5_
  50.5 0.0 collective-permute-done.12.refs_6_
  50.5 0.0 collective-permute-done.9.refs_3_
  50.5 0.0 collective-permute-done.10.refs_4_
  50.5 3.0 %collective-permute-done.13.refs_7_ = bf16[32,2176]{1,0:T(8,128)(2,1)S(1)} collective-permute-done((bf16[32,2176]{1,0:T(8,128)(2,1)S(1)}, bf16[32,2176]{1,0:T(8,128)(2,1)S(1)}, u32[]{:S(2)}, u32[]{:S(2)}) %collective-permute-start.13) | collective-permute-done | bytes 139296 | tf_op jit(solution)/shard_map/ppermute | solution.py:347
  53.5 0.9 %merge.1.rest_0_ = bf16[32,2048]{1,0:T(8,128)(2,1)S(1)} custom-call(bf16[32,2176]{1,0:T(8,128)(2,1)S(1)} %attention.7.refs_0_, bf16[32,2176]{1,0:T(8,128)(2,1)S(1)} %collective-permute-done.7.refs_1_, bf16[32,2176]{1,0:T(8,128)(2,1)S(1)} %collective-permute-done.8.refs_2_, bf16[32,2176]{1,0:T(8,128)(2,1)S(1)} %collective-permute-done.9.refs_3_, ...), custom_call_target="tpu_custom_call" | custom-call | flops 1114112 | bytes 1114112 | tf_op jit(solution)/shard_map/merge/pallas_call | solution.py:263
  54.5 0.1 collective-permute-start.15
  54.5 3.8 %collective-permute-start.14 = (bf16[32,2048]{1,0:T(8,128)(2,1)S(1)}, bf16[32,2048]{1,0:T(8,128)(2,1)S(1)}, u32[]{:S(2)}, u32[]{:S(2)}) collective-permute-start(bf16[32,2048]{1,0:T(8,128)(2,1)S(1)} %merge.1.rest_0_), channel_id=1, source_target_pairs={{0,24},{4,28},{8,0},{12,4},{16,8},{20,12},{24,16},{28,20},{1,25},{... | collective-permute-start | bytes 393224 | tf_op jit(solution)/shard_map/ppermute | solution.py:347
  58.3 0.0 collective-permute-start.16
  58.3 3.1 %collective-permute-done.15.rest_2_ = bf16[32,2048]{1,0:T(8,128)(2,1)S(1)} collective-permute-done((bf16[32,2048]{1,0:T(8,128)(2,1)S(1)}, bf16[32,2048]{1,0:T(8,128)(2,1)S(1)}, u32[]{:S(2)}, u32[]{:S(2)}) %collective-permute-start.15) | collective-permute-done | bytes 131104 | tf_op jit(solution)/shard_map/ppermute | solution.py:347
  61.4 1.6 %collective-permute-start.19 = (bf16[32,2048]{1,0:T(8,128)(2,1)S(1)}, bf16[32,2048]{1,0:T(8,128)(2,1)S(1)}, u32[]{:S(2)}, u32[]{:S(2)}) collective-permute-start(bf16[32,2048]{1,0:T(8,128)(2,1)S(1)} %collective-permute-done.15.rest_2_), channel_id=1, source_target_pairs={{0,4},{4,0},{8,12},{12,8},{16,20},{20,16},{24,28},{28,24},{1,5},{5... | collective-permute-start | bytes 393224 | tf_op jit(solution)/shard_map/ppermute | solution.py:347
  63.0 0.5 collective-permute-start.17
  63.5 0.0 collective-permute-done.14.rest_1_
  63.5 1.6 %collective-permute-start.18 = (bf16[32,2048]{1,0:T(8,128)(2,1)S(1)}, bf16[32,2048]{1,0:T(8,128)(2,1)S(1)}, u32[]{:S(2)}, u32[]{:S(2)}) collective-permute-start(bf16[32,2048]{1,0:T(8,128)(2,1)S(1)} %collective-permute-done.14.rest_1_), channel_id=1, source_target_pairs={{0,4},{4,0},{8,12},{12,8},{16,20},{20,16},{24,28},{28,24},{1,5},{5... | collective-permute-start | bytes 393224 | tf_op jit(solution)/shard_map/ppermute | solution.py:347
  65.0 1.4 %collective-permute-done.16.rest_3_ = bf16[32,2048]{1,0:T(8,128)(2,1)S(1)} collective-permute-done((bf16[32,2048]{1,0:T(8,128)(2,1)S(1)}, bf16[32,2048]{1,0:T(8,128)(2,1)S(1)}, u32[]{:S(2)}, u32[]{:S(2)}) %collective-permute-start.16) | collective-permute-done | bytes 131104 | tf_op jit(solution)/shard_map/ppermute | solution.py:347
  66.5 0.0 collective-permute-done.19.rest_6_
  66.5 1.6 %collective-permute-start.20 = (bf16[32,2048]{1,0:T(8,128)(2,1)S(1)}, bf16[32,2048]{1,0:T(8,128)(2,1)S(1)}, u32[]{:S(2)}, u32[]{:S(2)}) collective-permute-start(bf16[32,2048]{1,0:T(8,128)(2,1)S(1)} %collective-permute-done.16.rest_3_), channel_id=1, source_target_pairs={{0,4},{4,0},{8,12},{12,8},{16,20},{20,16},{24,28},{28,24},{1,5},{5... | collective-permute-start | bytes 393224 | tf_op jit(solution)/shard_map/ppermute | solution.py:347
  68.1 1.0 %collective-permute-done.17.rest_4_ = bf16[32,2048]{1,0:T(8,128)(2,1)S(1)} collective-permute-done((bf16[32,2048]{1,0:T(8,128)(2,1)S(1)}, bf16[32,2048]{1,0:T(8,128)(2,1)S(1)}, u32[]{:S(2)}, u32[]{:S(2)}) %collective-permute-start.17) | collective-permute-done | bytes 131104 | tf_op jit(solution)/shard_map/ppermute | solution.py:347
  69.1 1.7 %collective-permute-done.18.rest_5_ = bf16[32,2048]{1,0:T(8,128)(2,1)S(1)} collective-permute-done((bf16[32,2048]{1,0:T(8,128)(2,1)S(1)}, bf16[32,2048]{1,0:T(8,128)(2,1)S(1)}, u32[]{:S(2)}, u32[]{:S(2)}) %collective-permute-start.18) | collective-permute-done | bytes 131104 | tf_op jit(solution)/shard_map/ppermute | solution.py:347
  70.8 1.4 %collective-permute-done.20.rest_7_ = bf16[32,2048]{1,0:T(8,128)(2,1)S(1)} collective-permute-done((bf16[32,2048]{1,0:T(8,128)(2,1)S(1)}, bf16[32,2048]{1,0:T(8,128)(2,1)S(1)}, u32[]{:S(2)}, u32[]{:S(2)}) %collective-permute-start.20) | collective-permute-done | bytes 131104 | tf_op jit(solution)/shard_map/ppermute | solution.py:347
  72.2 0.0 copy-done
  72.2 1.4 %projection.1 = (f32[2,64,1024]{2,1,0:T(8,128)S(1)}, bf16[2,64,1024]{2,1,0:T(8,128)(2,1)S(1)}) custom-call(bf16[2048,1024]{1,0:T(8,128)(2,1)S(1)} %copy-done, bf16[32,2048]{1,0:T(8,128)(2,1)S(1)} %merge.1.rest_0_, bf16[32,2048]{1,0:T(8,128)(2,1)S(1)} %collective-permute-done.14.rest_1_, bf16[32,2048]{1,0:T(8,128)(2,1)S(1)} %collective-permute-done.15.rest_2_, ...), custom_call_target="tpu_custom_call" | custom-call | flops 1073741824 | bytes 4194304 | tf_op jit(solution)/shard_map/projection/pallas_call | solution.py:305
  73.6 0.1 collective-permute-start.21
  73.7 1.5 %collective-permute-done.21 = bf16[2,64,1024]{2,1,0:T(8,128)(2,1)S(1)} collective-permute-done((bf16[2,64,1024]{2,1,0:T(8,128)(2,1)S(1)}, bf16[2,64,1024]{2,1,0:T(8,128)(2,1)S(1)}, u32[]{:S(2)}, u32[]{:S(2)}) %collective-permute-start.21) | collective-permute-done | bytes 262176 | tf_op jit(solution)/shard_map/ppermute | solution.py:425
  75.2 6.0 %collective-permute-start.22 = (bf16[64,1024]{1,0:T(8,128)(2,1)S(1)}, bf16[64,1024]{1,0:T(8,128)(2,1)S(1)}, u32[]{:S(2)}, u32[]{:S(2)}) collective-permute-start(bf16[64,1024]{1,0:T(8,128)(2,1)S(1)} %fusion), channel_id=1, source_target_pairs={{0,2},{1,3},{2,0},{3,1},{4,6},{5,7},{6,4},{7,5},{8,10},{9,11},{10,... | collective-permute-start | bytes 393224 | tf_op jit(solution)/shard_map/ppermute | solution.py:429
  81.2 3.8 %collective-permute-done.22 = bf16[64,1024]{1,0:T(8,128)(2,1)S(1)} collective-permute-done((bf16[64,1024]{1,0:T(8,128)(2,1)S(1)}, bf16[64,1024]{1,0:T(8,128)(2,1)S(1)}, u32[]{:S(2)}, u32[]{:S(2)}) %collective-permute-start.22) | collective-permute-done | bytes 131104 | tf_op jit(solution)/shard_map/ppermute | solution.py:429
  85.0 0.7 bitcast_add_fusion
  (7 shorter events, 0.0 us)
Async XLA Ops:
  0.0 9.3 %collective-permute-start = (bf16[32,2048]{1,0:T(8,128)(2,1)}, bf16[32,2048]{1,0:T(8,128)(2,1)S(1)}, u32[]{:S(2)}, u32[]{:S(2)}) collective-permute-start(bf16[32,2048]{1,0:T(8,128)(2,1)} %rest_0_), channel_id=1, source_target_pairs={{0,24},{4,28},{8,0},{12,4},{16,8},{20,12},{24,16},{28,20},{1,25},{... | collective-permute-start | bytes 393224 | tf_op jit(solution)/shard_map/ppermute | solution.py:347
  5.0 7.0 %collective-permute-start.1 = (bf16[32,2048]{1,0:T(8,128)(2,1)}, bf16[32,2048]{1,0:T(8,128)(2,1)S(1)}, u32[]{:S(2)}, u32[]{:S(2)}) collective-permute-start(bf16[32,2048]{1,0:T(8,128)(2,1)} %rest_0_), channel_id=1, source_target_pairs={{0,8},{4,12},{8,16},{12,20},{16,24},{20,28},{24,0},{28,4},{1,9},{5... | collective-permute-start | bytes 393224 | tf_op jit(solution)/shard_map/ppermute | solution.py:347
  5.1 28.2 %collective-permute-start.4 = (bf16[32,2048]{1,0:T(8,128)(2,1)}, bf16[32,2048]{1,0:T(8,128)(2,1)S(1)}, u32[]{:S(2)}, u32[]{:S(2)}) collective-permute-start(bf16[32,2048]{1,0:T(8,128)(2,1)} %rest_0_), channel_id=1, source_target_pairs={{0,4},{4,0},{8,12},{12,8},{16,20},{20,16},{24,28},{28,24},{1,5},{5... | collective-permute-start | bytes 393224 | tf_op jit(solution)/shard_map/ppermute | solution.py:347
  6.5 7.9 %copy-start.1 = (bf16[4096,256]{1,0:T(8,128)(2,1)S(1)}, bf16[4096,256]{1,0:T(8,128)(2,1)}, u32[]{:S(2)}) copy-start(bf16[4096,256]{1,0:T(8,128)(2,1)} %v_ref.1) | copy-start | bytes 6291460
  6.5 7.9 %copy-start.2 = (bf16[4096,256]{1,0:T(8,128)(2,1)S(1)}, bf16[4096,256]{1,0:T(8,128)(2,1)}, u32[]{:S(2)}) copy-start(bf16[4096,256]{1,0:T(8,128)(2,1)} %k_ref.7) | copy-start | bytes 6291460
  12.0 11.5 %collective-permute-start.2 = (bf16[32,2048]{1,0:T(8,128)(2,1)}, bf16[32,2048]{1,0:T(8,128)(2,1)S(1)}, u32[]{:S(2)}, u32[]{:S(2)}) collective-permute-start(bf16[32,2048]{1,0:T(8,128)(2,1)} %rest_0_), channel_id=1, source_target_pairs={{0,16},{4,20},{8,24},{12,28},{16,0},{20,4},{24,8},{28,12},{1,17},{... | collective-permute-start | bytes 393224 | tf_op jit(solution)/shard_map/ppermute | solution.py:347
  12.4 11.1 %collective-permute-start.5 = (bf16[32,2048]{1,0:T(8,128)(2,1)S(1)}, bf16[32,2048]{1,0:T(8,128)(2,1)S(1)}, u32[]{:S(2)}, u32[]{:S(2)}) collective-permute-start(bf16[32,2048]{1,0:T(8,128)(2,1)S(1)} %collective-permute-done.rest_0_), channel_id=1, source_target_pairs={{0,4},{4,0},{8,12},{12,8},{16,20},{20,16},{24,28},{28,24},{1,5},{5... | collective-permute-start | bytes 393224 | tf_op jit(solution)/shard_map/ppermute | solution.py:347
  13.9 9.7 %collective-permute-start.6 = (bf16[32,2048]{1,0:T(8,128)(2,1)S(1)}, bf16[32,2048]{1,0:T(8,128)(2,1)S(1)}, u32[]{:S(2)}, u32[]{:S(2)}) collective-permute-start(bf16[32,2048]{1,0:T(8,128)(2,1)S(1)} %collective-permute-done.1.rest_1_), channel_id=1, source_target_pairs={{0,4},{4,0},{8,12},{12,8},{16,20},{20,16},{24,28},{28,24},{1,5},{5... | collective-permute-start | bytes 393224 | tf_op jit(solution)/shard_map/ppermute | solution.py:347
  14.4 0.8 copy-start.4
  15.2 0.6 copy-start.6
  20.8 17.1 %collective-permute-start.8 = (bf16[32,2176]{1,0:T(8,128)(2,1)S(1)}, bf16[32,2176]{1,0:T(8,128)(2,1)S(1)}, u32[]{:S(2)}, u32[]{:S(2)}) collective-permute-start(bf16[32,2176]{1,0:T(8,128)(2,1)S(1)} %get-tuple-element.38), channel_id=1, source_target_pairs={{0,24},{4,28},{8,0},{12,4},{16,8},{20,12},{24,16},{28,20},{1,25},{... | collective-permute-start | bytes 417800 | tf_op jit(solution)/shard_map/ppermute | solution.py:347
  23.5 14.4 %collective-permute-start.7 = (bf16[32,2176]{1,0:T(8,128)(2,1)S(1)}, bf16[32,2176]{1,0:T(8,128)(2,1)S(1)}, u32[]{:S(2)}, u32[]{:S(2)}) collective-permute-start(bf16[32,2176]{1,0:T(8,128)(2,1)S(1)} %get-tuple-element.45), channel_id=1, source_target_pairs={{0,8},{4,12},{8,16},{12,20},{16,24},{20,28},{24,0},{28,4},{1,9},{5... | collective-permute-start | bytes 417800 | tf_op jit(solution)/shard_map/ppermute | solution.py:347
  23.6 14.4 %collective-permute-start.3 = (bf16[32,2048]{1,0:T(8,128)(2,1)S(1)}, bf16[32,2048]{1,0:T(8,128)(2,1)S(1)}, u32[]{:S(2)}, u32[]{:S(2)}) collective-permute-start(bf16[32,2048]{1,0:T(8,128)(2,1)S(1)} %collective-permute-done.2.rest_0_), channel_id=1, source_target_pairs={{0,4},{4,0},{8,12},{12,8},{16,20},{20,16},{24,28},{28,24},{1,5},{5... | collective-permute-start | bytes 393224 | tf_op jit(solution)/shard_map/ppermute | solution.py:347
  26.4 11.5 %copy-start.7 = (s32[58]{0:T(128)S(1)}, s32[58]{0:T(128)}, u32[]{:S(2)}) copy-start(s32[58]{0:T(128)} %get-tuple-element.32.table_ref) | copy-start | bytes 700
  33.2 17.3 %collective-permute-start.11 = (bf16[32,2176]{1,0:T(8,128)(2,1)S(1)}, bf16[32,2176]{1,0:T(8,128)(2,1)S(1)}, u32[]{:S(2)}, u32[]{:S(2)}) collective-permute-start(bf16[32,2176]{1,0:T(8,128)(2,1)S(1)} %get-tuple-element.53), channel_id=1, source_target_pairs={{0,12},{4,8},{8,20},{12,16},{16,28},{20,24},{24,4},{28,0},{1,13},{... | collective-permute-start | bytes 417800 | tf_op jit(solution)/shard_map/ppermute | solution.py:347
  33.2 17.2 %collective-permute-start.12 = (bf16[32,2176]{1,0:T(8,128)(2,1)S(1)}, bf16[32,2176]{1,0:T(8,128)(2,1)S(1)}, u32[]{:S(2)}, u32[]{:S(2)}) collective-permute-start(bf16[32,2176]{1,0:T(8,128)(2,1)S(1)} %get-tuple-element.42), channel_id=1, source_target_pairs={{0,28},{4,24},{8,4},{12,0},{16,12},{20,8},{24,20},{28,16},{1,29},{... | collective-permute-start | bytes 417800 | tf_op jit(solution)/shard_map/ppermute | solution.py:347
  37.9 8.9 %copy-start.3 = (bf16[32,2048]{1,0:T(8,128)(2,1)S(1)}, bf16[32,2048]{1,0:T(8,128)(2,1)}, u32[]{:S(2)}) copy-start(bf16[32,2048]{1,0:T(8,128)(2,1)} %rest_0_) | copy-start | bytes 393220
  37.9 8.9 %copy-start.5 = (bf16[32,512]{1,0:T(8,128)(2,1)S(1)}, bf16[32,512]{1,0:T(8,128)(2,1)}, u32[]{:S(2)}) copy-start(bf16[32,512]{1,0:T(8,128)(2,1)} %get-tuple-element.33.new_ref) | copy-start | bytes 98308
  37.9 12.5 %collective-permute-start.9 = (bf16[32,2176]{1,0:T(8,128)(2,1)S(1)}, bf16[32,2176]{1,0:T(8,128)(2,1)S(1)}, u32[]{:S(2)}, u32[]{:S(2)}) collective-permute-start(bf16[32,2176]{1,0:T(8,128)(2,1)S(1)} %get-tuple-element.52), channel_id=1, source_target_pairs={{0,16},{4,20},{8,24},{12,28},{16,0},{20,4},{24,8},{28,12},{1,17},{... | collective-permute-start | bytes 417800 | tf_op jit(solution)/shard_map/ppermute | solution.py:347
  43.0 7.5 %collective-permute-start.10 = (bf16[32,2176]{1,0:T(8,128)(2,1)S(1)}, bf16[32,2176]{1,0:T(8,128)(2,1)S(1)}, u32[]{:S(2)}, u32[]{:S(2)}) collective-permute-start(bf16[32,2176]{1,0:T(8,128)(2,1)S(1)} %get-tuple-element.48), channel_id=1, source_target_pairs={{0,4},{4,0},{8,12},{12,8},{16,20},{20,16},{24,28},{28,24},{1,5},{5... | collective-permute-start | bytes 417800 | tf_op jit(solution)/shard_map/ppermute | solution.py:347
  43.4 10.1 %collective-permute-start.13 = (bf16[32,2176]{1,0:T(8,128)(2,1)S(1)}, bf16[32,2176]{1,0:T(8,128)(2,1)S(1)}, u32[]{:S(2)}, u32[]{:S(2)}) collective-permute-start(bf16[32,2176]{1,0:T(8,128)(2,1)S(1)} %get-tuple-element.54), channel_id=1, source_target_pairs={{0,20},{4,16},{8,28},{12,24},{16,4},{20,0},{24,12},{28,8},{1,21},{... | collective-permute-start | bytes 417800 | tf_op jit(solution)/shard_map/ppermute | solution.py:347
  46.8 25.4 %copy-start = (bf16[2048,1024]{1,0:T(8,128)(2,1)S(1)}, bf16[2048,1024]{1,0:T(8,128)(2,1)}, u32[]{:S(2)}) copy-start(bf16[2048,1024]{1,0:T(8,128)(2,1)} %w_ref.1) | copy-start | bytes 12582916
  54.5 7.0 %collective-permute-start.15 = (bf16[32,2048]{1,0:T(8,128)(2,1)S(1)}, bf16[32,2048]{1,0:T(8,128)(2,1)S(1)}, u32[]{:S(2)}, u32[]{:S(2)}) collective-permute-start(bf16[32,2048]{1,0:T(8,128)(2,1)S(1)} %merge.1.rest_0_), channel_id=1, source_target_pairs={{0,8},{4,12},{8,16},{12,20},{16,24},{20,28},{24,0},{28,4},{1,9},{5... | collective-permute-start | bytes 393224 | tf_op jit(solution)/shard_map/ppermute | solution.py:347
  54.5 8.9 %collective-permute-start.14 = (bf16[32,2048]{1,0:T(8,128)(2,1)S(1)}, bf16[32,2048]{1,0:T(8,128)(2,1)S(1)}, u32[]{:S(2)}, u32[]{:S(2)}) collective-permute-start(bf16[32,2048]{1,0:T(8,128)(2,1)S(1)} %merge.1.rest_0_), channel_id=1, source_target_pairs={{0,24},{4,28},{8,0},{12,4},{16,8},{20,12},{24,16},{28,20},{1,25},{... | collective-permute-start | bytes 393224 | tf_op jit(solution)/shard_map/ppermute | solution.py:347
  58.3 8.1 %collective-permute-start.16 = (bf16[32,2048]{1,0:T(8,128)(2,1)S(1)}, bf16[32,2048]{1,0:T(8,128)(2,1)S(1)}, u32[]{:S(2)}, u32[]{:S(2)}) collective-permute-start(bf16[32,2048]{1,0:T(8,128)(2,1)S(1)} %merge.1.rest_0_), channel_id=1, source_target_pairs={{0,16},{4,20},{8,24},{12,28},{16,0},{20,4},{24,8},{28,12},{1,17},{... | collective-permute-start | bytes 393224 | tf_op jit(solution)/shard_map/ppermute | solution.py:347
  61.4 5.0 %collective-permute-start.19 = (bf16[32,2048]{1,0:T(8,128)(2,1)S(1)}, bf16[32,2048]{1,0:T(8,128)(2,1)S(1)}, u32[]{:S(2)}, u32[]{:S(2)}) collective-permute-start(bf16[32,2048]{1,0:T(8,128)(2,1)S(1)} %collective-permute-done.15.rest_2_), channel_id=1, source_target_pairs={{0,4},{4,0},{8,12},{12,8},{16,20},{20,16},{24,28},{28,24},{1,5},{5... | collective-permute-start | bytes 393224 | tf_op jit(solution)/shard_map/ppermute | solution.py:347
  63.0 6.1 %collective-permute-start.17 = (bf16[32,2048]{1,0:T(8,128)(2,1)S(1)}, bf16[32,2048]{1,0:T(8,128)(2,1)S(1)}, u32[]{:S(2)}, u32[]{:S(2)}) collective-permute-start(bf16[32,2048]{1,0:T(8,128)(2,1)S(1)} %merge.1.rest_0_), channel_id=1, source_target_pairs={{0,4},{4,0},{8,12},{12,8},{16,20},{20,16},{24,28},{28,24},{1,5},{5... | collective-permute-start | bytes 393224 | tf_op jit(solution)/shard_map/ppermute | solution.py:347
  63.5 7.3 %collective-permute-start.18 = (bf16[32,2048]{1,0:T(8,128)(2,1)S(1)}, bf16[32,2048]{1,0:T(8,128)(2,1)S(1)}, u32[]{:S(2)}, u32[]{:S(2)}) collective-permute-start(bf16[32,2048]{1,0:T(8,128)(2,1)S(1)} %collective-permute-done.14.rest_1_), channel_id=1, source_target_pairs={{0,4},{4,0},{8,12},{12,8},{16,20},{20,16},{24,28},{28,24},{1,5},{5... | collective-permute-start | bytes 393224 | tf_op jit(solution)/shard_map/ppermute | solution.py:347
  66.5 5.7 %collective-permute-start.20 = (bf16[32,2048]{1,0:T(8,128)(2,1)S(1)}, bf16[32,2048]{1,0:T(8,128)(2,1)S(1)}, u32[]{:S(2)}, u32[]{:S(2)}) collective-permute-start(bf16[32,2048]{1,0:T(8,128)(2,1)S(1)} %collective-permute-done.16.rest_3_), channel_id=1, source_target_pairs={{0,4},{4,0},{8,12},{12,8},{16,20},{20,16},{24,28},{28,24},{1,5},{5... | collective-permute-start | bytes 393224 | tf_op jit(solution)/shard_map/ppermute | solution.py:347
  73.6 1.6 %collective-permute-start.21 = (bf16[2,64,1024]{2,1,0:T(8,128)(2,1)S(1)}, bf16[2,64,1024]{2,1,0:T(8,128)(2,1)S(1)}, u32[]{:S(2)}, u32[]{:S(2)}) collective-permute-start(bf16[2,64,1024]{2,1,0:T(8,128)(2,1)S(1)} %get-tuple-element.58), channel_id=1, source_target_pairs={{0,1},{1,0},{2,3},{3,2},{4,5},{5,4},{6,7},{7,6},{8,9},{9,8},{10,11... | collective-permute-start | bytes 786440 | tf_op jit(solution)/shard_map/ppermute | solution.py:425
  75.2 9.8 %collective-permute-start.22 = (bf16[64,1024]{1,0:T(8,128)(2,1)S(1)}, bf16[64,1024]{1,0:T(8,128)(2,1)S(1)}, u32[]{:S(2)}, u32[]{:S(2)}) collective-permute-start(bf16[64,1024]{1,0:T(8,128)(2,1)S(1)} %fusion), channel_id=1, source_target_pairs={{0,2},{1,3},{2,0},{3,1},{4,6},{5,7},{6,4},{7,5},{8,10},{9,11},{10,... | collective-permute-start | bytes 393224 | tf_op jit(solution)/shard_map/ppermute | solution.py:429

commit v6 on v5

--- a/solution.py
+++ b/solution.py
@@ -13,6 +13,7 @@
 LANES = 128
 CHUNK = 4
 LOW = -1e30
+LIMIT = 2.0**100
 ONES = 16
 LOW_SIZE = 2
 VMEM_PACK = 58 * 2**20
@@ -48,78 +49,75 @@
     def slot_of(ctx):
         return table_ref[kv_local * (slots + 1) + ctx]
 
-    def turned(x):
-        return x.T
-
-    def fold(g, b, s, values, first=False):
-        peak = jnp.max(s, axis=0, keepdims=True) * scale
-        top = peak if first else jnp.maximum(max_ref[g, b, :1], peak)
-        p = jnp.exp2(s * scale - top).astype(jnp.bfloat16)
-        mixed = jnp.dot(values, p, preferred_element_type=jnp.float32)
-        if not first:
-            mixed += acc_ref[g, b] * jnp.exp2(max_ref[g, b, :1] - top)
-        max_ref[g, b] = jnp.broadcast_to(top, max_ref.shape[2:])
-        acc_ref[g, b] = mixed
-
     ones_tile = jnp.ones((ONES, TILE), jnp.bfloat16)
     place_key = lax.broadcasted_iota(jnp.int32, (TILE, rows), 0)
     place_row = lax.broadcasted_iota(jnp.int32, (TILE, rows), 1) % q_dev
     padding = jnp.zeros((TILE - q_dev, DH), jnp.bfloat16)
 
+    def keys_of(g, chunk):
+        cols = slice(g * DH, (g + 1) * DH)
+        parts = []
+        for i in range(CHUNK):
+            slot = chunk * CHUNK + i
+            tile = table_ref[g * slots + jnp.where(slot < count_of(g), slot, 0)]
+            parts.append(k_ref[pl.ds(pl.multiple_of(tile * TILE, TILE), TILE), cols])
+        return jnp.concatenate(parts, 0)
+
+    def values_of(g, chunk):
+        whole = pl.ds(pl.multiple_of(chunk * span, span), span)
+        if not turn:
+            return kept_ref[g, :, whole]
+        cols = slice(g * DH, (g + 1) * DH)
+        parts = []
+        for i in range(CHUNK):
+            slot = chunk * CHUNK + i
+            live = slot < count_of(g)
+            tile = table_ref[g * slots + jnp.where(live, slot, 0)]
+            at = pl.ds(pl.multiple_of(tile * TILE, TILE), TILE)
+            tail = jnp.concatenate([v_ref[at, cols].T, ones_tile], 0)
+            parts.append(jnp.where(live, tail, jnp.zeros_like(tail)))
+        values = jnp.concatenate(parts, 1)
+        kept_ref[g, :, whole] = values
+        return values
+
+    def open_state(g, b, keys, values):
+        s = jnp.dot(keys, turned_ref[g, b], preferred_element_type=jnp.float32)
+        shift = (slot_of(flipped(me, ctx_count, *members[b])) - slot_of(me)) * q_dev
+        live = (place_key < q_dev) & (place_row - place_key + shift >= 0)
+        s = jnp.concatenate([s[:span], jnp.where(live, s[span:], LOW)], 0)
+        top = jnp.max(s, axis=0, keepdims=True) * scale
+        p = jnp.exp2(s * scale - top).astype(jnp.bfloat16)
+        max_ref[g, b] = jnp.broadcast_to(top, max_ref.shape[2:])
+        acc_ref[g, b] = jnp.dot(values, p, preferred_element_type=jnp.float32)
+
+    def open_head(g, first_values):
+        fresh = jnp.concatenate([new_ref[:, g * DH : (g + 1) * DH], padding], 0)
+        keys = jnp.concatenate([keys_of(g, 0), fresh], 0)
+        values = jnp.concatenate([first_values, kept_ref[g, :, last:]], 1)
+        for b in range(blocks):
+            open_state(g, b, keys, values)
+
     for g in range(kv_local):
-        fresh_keys = jnp.concatenate([new_ref[:, g * DH : (g + 1) * DH], padding], 0)
         if turn:
             fresh_values = new_ref[:, (kv_local + g) * DH : (kv_local + g + 1) * DH]
-            fresh_values = jnp.concatenate(
-                [turned(jnp.concatenate([fresh_values, padding], 0)), ones_tile], 0
-            )
-            kept_ref[g, :, last:] = fresh_values
-        else:
-            fresh_values = kept_ref[g, :, last:]
+            fresh_values = jnp.concatenate([fresh_values, padding], 0).T
+            kept_ref[g, :, last:] = jnp.concatenate([fresh_values, ones_tile], 0)
         for b in range(blocks):
             columns = [
                 q_refs[b][:, (g * group + h) * DH : (g * group + h + 1) * DH]
                 for h in range(group)
             ]
-            turned_ref[g, b] = turned(jnp.concatenate(columns, 0))
-            s = jnp.dot(fresh_keys, turned_ref[g, b], preferred_element_type=jnp.float32)
-            shift = (slot_of(flipped(me, ctx_count, *members[b])) - slot_of(me)) * q_dev
-            live = (place_key < q_dev) & (place_row - place_key + shift >= 0)
-            fold(g, b, jnp.where(live, s, LOW), fresh_values, first=True)
-
-    def load_chunk(g, chunk):
-        cols = slice(g * DH, (g + 1) * DH)
-        whole = pl.ds(pl.multiple_of(chunk * span, span), span)
-        key_parts, value_parts = [], []
-        for i in range(CHUNK):
-            slot = chunk * CHUNK + i
-            live = slot < count_of(g)
-            tile = table_ref[g * slots + jnp.where(live, slot, 0)]
-            at = pl.ds(pl.multiple_of(tile * TILE, TILE), TILE)
-            key_parts.append(k_ref[at, cols])
-            if turn:
-                tail = jnp.concatenate([turned(v_ref[at, cols]), ones_tile], 0)
-                value_parts.append(jnp.where(live, tail, jnp.zeros_like(tail)))
-        keys = jnp.concatenate(key_parts, 0)
-        if not turn:
-            return keys, kept_ref[g, :, whole]
-        values = jnp.concatenate(value_parts, 1)
-        kept_ref[g, :, whole] = values
-        return keys, values
+            turned_ref[g, b] = jnp.concatenate(columns, 0).T
+        open_head(g, values_of(g, 0))
 
     def run(kv_heads, chunk):
-        loaded = {g: load_chunk(g, chunk) for g in kv_heads}
-        chains = [(g, b) for b in range(blocks) for g in kv_heads]
-
-        def score(g, b):
-            return jnp.dot(loaded[g][0], turned_ref[g, b], preferred_element_type=jnp.float32)
-
-        ahead = score(*chains[0])
-        for at, (g, b) in enumerate(chains):
-            s = ahead
-            if at + 1 < len(chains):
-                ahead = score(*chains[at + 1])
-            fold(g, b, s, loaded[g][1])
+        loaded = {g: (keys_of(g, chunk), values_of(g, chunk)) for g in kv_heads}
+        for b in range(blocks):
+            for g in kv_heads:
+                keys, values = loaded[g]
+                s = jnp.dot(keys, turned_ref[g, b], preferred_element_type=jnp.float32)
+                p = jnp.exp2(s * scale - max_ref[g, b, :1]).astype(jnp.bfloat16)
+                acc_ref[g, b] += jnp.dot(values, p, preferred_element_type=jnp.float32)
 
     ends = [(count_of(g) + CHUNK - 1) // CHUNK for g in range(kv_local)]
     shared = functools.reduce(jnp.minimum, ends)
@@ -128,7 +126,7 @@
         run(range(kv_local), chunk)
         return carry
 
-    lax.fori_loop(0, shared, step_all, 0)
+    lax.fori_loop(1, shared, step_all, 0)
     for g in range(kv_local):
 
         def step_one(chunk, carry, g=g):
@@ -136,6 +134,33 @@
             return carry
 
         lax.fori_loop(shared, ends[g], step_one, 0)
+
+    large = jnp.zeros((1, rows), jnp.float32)
+    for g in range(kv_local):
+        for b in range(blocks):
+            fits = acc_ref[g, b, DH : DH + 1, :] < LIMIT
+            large = jnp.maximum(large, jnp.where(fits, 0.0, 1.0))
+
+    @pl.when(jnp.max(large) > 0.0)
+    def again():
+        for g in range(kv_local):
+            open_head(g, kept_ref[g, :, :span])
+
+            def step_exact(chunk, carry, g=g):
+                keys = keys_of(g, chunk)
+                values = kept_ref[g, :, pl.ds(pl.multiple_of(chunk * span, span), span)]
+                for b in range(blocks):
+                    s = jnp.dot(keys, turned_ref[g, b], preferred_element_type=jnp.float32)
+                    old = max_ref[g, b, :1]
+                    top = jnp.maximum(old, jnp.max(s, axis=0, keepdims=True) * scale)
+                    p = jnp.exp2(s * scale - top).astype(jnp.bfloat16)
+                    max_ref[g, b] = jnp.broadcast_to(top, max_ref.shape[2:])
+                    acc_ref[g, b] = acc_ref[g, b] * jnp.exp2(old - top) + jnp.dot(
+                        values, p, preferred_element_type=jnp.float32
+                    )
+                return carry
+
+            lax.fori_loop(1, ends[g], step_exact, 0)
 
     sublane = lax.broadcasted_iota(jnp.int32, (q_dev, LANES), 0)
     parts = rows // LANES

time: 85.7 us -> 95 us (1.11)
  Pallas kernels: 24.3 us -> 30.1 us
  starting transfers between devices: 38.2 us -> 40.4 us
  waiting for transfers between devices: 20.9 us -> 22.1 us
    pallas_call x4, Pallas kernels: 20.4 us -> 26.2 us  [attention_call(): pl.pallas_call(functools.partial(attention_kernel, members, ctx_count, gr...]
    ppermute x1, starting transfers between devices: 6.01 us -> 8.32 us  [body(): piece = lax.ppermute(piece, 'tp', [(i, i ^ 2 * j) for i in range(peers)])]
    ppermute x21, waiting for transfers between devices: 15.6 us -> 16.8 us  [move(): return lax.ppermute(x, 'ctx', pairs)]
  transfers between devices with their start and end apart: 23 -> 23, of which waited for: 10 -> 10; matrix products, arithmetic and copies ran while one was open for 0% -> 0% of each run, Pallas kernels for 26% -> 29%
where the time goes in v6:
time: 95 us; the launch traced here: 94.9 us
  starting transfers between devices  40.4 us (43%)
  Pallas kernels  30.1 us (32%)
  waiting for transfers between devices  22.1 us (23%)
  local copies, waits for them, and re-layouts  1.38 us (1%)
    ppermute x21, starting transfers between devices, move(): return lax.ppermute(x, 'ctx', pairs)  32 us
    pallas_call x4, Pallas kernels, attention_call(): pl.pallas_call(functools.partial(attention_kernel, members, ctx_count, gr...  26.2 us
    ppermute x21, waiting for transfers between devices, move(): return lax.ppermute(x, 'ctx', pairs)  16.8 us
    ppermute x1, starting transfers between devices, body(): piece = lax.ppermute(piece, 'tp', [(i, i ^ 2 * j) for i in range(peers)])  8.32 us
    ppermute x1, waiting for transfers between devices, body(): piece = lax.ppermute(piece, 'tp', [(i, i ^ 2 * j) for i in range(peers)])  3.8 us
  transfers between devices with their start and end apart: 23, of which 10 were waited for; matrix products, arithmetic and copies ran while one was open for 0% of the time, Pallas kernels for 29%

profile of v6, /device:TPU:0, one launch (start us, length us, event | category | flops | bytes accessed | tf_op | source)
XLA Modules:
  0.0 94.9 jit_solution(562771537650325400)
XLA Ops:
  0.0 5.0 %collective-permute-start = (bf16[32,2048]{1,0:T(8,128)(2,1)}, bf16[32,2048]{1,0:T(8,128)(2,1)S(1)}, u32[]{:S(2)}, u32[]{:S(2)}) collective-permute-start(bf16[32,2048]{1,0:T(8,128)(2,1)} %rest_0_), channel_id=1, source_target_pairs={{0,24},{4,28},{8,0},{12,4},{16,8},{20,12},{24,16},{28,20},{1,25},{... | collective-permute-start | bytes 393224 | tf_op jit(solution)/shard_map/ppermute | solution.py:372
  5.0 0.0 collective-permute-start.1
  5.1 1.5 %collective-permute-start.4 = (bf16[32,2048]{1,0:T(8,128)(2,1)}, bf16[32,2048]{1,0:T(8,128)(2,1)S(1)}, u32[]{:S(2)}, u32[]{:S(2)}) collective-permute-start(bf16[32,2048]{1,0:T(8,128)(2,1)} %rest_0_), channel_id=1, source_target_pairs={{0,4},{4,0},{8,12},{12,8},{16,20},{20,16},{24,28},{28,24},{1,5},{5... | collective-permute-start | bytes 393224 | tf_op jit(solution)/shard_map/ppermute | solution.py:372
  6.5 0.0 copy-start.1
  6.5 0.0 copy-start.2
  6.5 1.6 %pack.1 = (s32[58]{0:T(128)}, bf16[32,512]{1,0:T(8,128)(2,1)}) custom-call(s32[8]{0:T(128)} %slot_ref.1, s32[2,24]{1,0:T(2,128)} %bitcast.6, s32[2]{0:T(128)} %bitcast.7, bf16[32,256]{1,0:T(8,128)(2,1)} %nk_ref.1, bf16[32,256]{1,0:T(8,128)(2,1)} %nv_ref.1, bf16[4096,256]{1,0:T(8,128)(2,1)} %k_ref.7, bf16[4096,256]{1,0:T(8,128)(2,1)} %v_ref.1), custom_call_target="tpu_custom_call" | custom-call | tf_op jit(solution)/shard_map/pack/pallas_call | solution.py:204
  8.1 1.2 %collective-permute-done.rest_0_ = bf16[32,2048]{1,0:T(8,128)(2,1)S(1)} collective-permute-done((bf16[32,2048]{1,0:T(8,128)(2,1)}, bf16[32,2048]{1,0:T(8,128)(2,1)S(1)}, u32[]{:S(2)}, u32[]{:S(2)}) %collective-permute-start) | collective-permute-done | bytes 131104 | tf_op jit(solution)/shard_map/ppermute | solution.py:372
  9.3 2.8 %collective-permute-done.1.rest_1_ = bf16[32,2048]{1,0:T(8,128)(2,1)S(1)} collective-permute-done((bf16[32,2048]{1,0:T(8,128)(2,1)}, bf16[32,2048]{1,0:T(8,128)(2,1)S(1)}, u32[]{:S(2)}, u32[]{:S(2)}) %collective-permute-start.1) | collective-permute-done | bytes 131104 | tf_op jit(solution)/shard_map/ppermute | solution.py:372
  12.0 0.4 collective-permute-start.2
  12.4 1.5 %collective-permute-start.5 = (bf16[32,2048]{1,0:T(8,128)(2,1)S(1)}, bf16[32,2048]{1,0:T(8,128)(2,1)S(1)}, u32[]{:S(2)}, u32[]{:S(2)}) collective-permute-start(bf16[32,2048]{1,0:T(8,128)(2,1)S(1)} %collective-permute-done.rest_0_), channel_id=1, source_target_pairs={{0,4},{4,0},{8,12},{12,8},{16,20},{20,16},{24,28},{28,24},{1,5},{5... | collective-permute-start | bytes 393224 | tf_op jit(solution)/shard_map/ppermute | solution.py:372
  13.9 0.5 collective-permute-start.6
  14.4 0.0 copy-done.1
  14.4 0.0 copy-done.2
  14.4 0.8 copy-done.4
  15.2 0.6 copy-done.6
  15.8 6.5 %attention.4 = (bf16[32,2176]{1,0:T(8,128)(2,1)S(1)}, bf16[32,2176]{1,0:T(8,128)(2,1)S(1)}, bf16[2,144,3200]{2,1,0:T(8,128)(2,1)S(1)}) custom-call(s32[58]{0:T(128)S(1)} %copy-done.6, bf16[32,512]{1,0:T(8,128)(2,1)S(1)} %copy-done.4, bf16[4096,256]{1,0:T(8,128)(2,1)S(1)} %copy-done.2, bf16[4096,256]{1,0:T(8,128)(2,1)S(1)} %copy-done.1, ...), custom_call_target="tpu_custom_call" | custom-call | flops 3221225472 | bytes 8388608 | tf_op jit(solution)/shard_map/attention/pallas_call | solution.py:228
  22.3 2.6 %collective-permute-start.8 = (bf16[32,2176]{1,0:T(8,128)(2,1)S(1)}, bf16[32,2176]{1,0:T(8,128)(2,1)S(1)}, u32[]{:S(2)}, u32[]{:S(2)}) collective-permute-start(bf16[32,2176]{1,0:T(8,128)(2,1)S(1)} %get-tuple-element.38), channel_id=1, source_target_pairs={{0,24},{4,28},{8,0},{12,4},{16,8},{20,12},{24,16},{28,20},{1,25},{... | collective-permute-start | bytes 417800 | tf_op jit(solution)/shard_map/ppermute | solution.py:372
  24.9 0.0 collective-permute-done.2.rest_0_
  24.9 0.0 collective-permute-start.7
  24.9 0.0 collective-permute-done.5.rest_1_
  24.9 0.0 collective-permute-done.6.rest_2_
  24.9 2.9 %collective-permute-start.3 = (bf16[32,2048]{1,0:T(8,128)(2,1)S(1)}, bf16[32,2048]{1,0:T(8,128)(2,1)S(1)}, u32[]{:S(2)}, u32[]{:S(2)}) collective-permute-start(bf16[32,2048]{1,0:T(8,128)(2,1)S(1)} %collective-permute-done.2.rest_0_), channel_id=1, source_target_pairs={{0,4},{4,0},{8,12},{12,8},{16,20},{20,16},{24,28},{28,24},{1,5},{5... | collective-permute-start | bytes 393224 | tf_op jit(solution)/shard_map/ppermute | solution.py:372
  27.8 9.2 %attention.5 = (bf16[32,2176]{1,0:T(8,128)(2,1)S(1)}, bf16[32,2176]{1,0:T(8,128)(2,1)S(1)}, bf16[32,2176]{1,0:T(8,128)(2,1)S(1)}) custom-call(s32[58]{0:T(128)S(1)} %copy-done.6, bf16[32,512]{1,0:T(8,128)(2,1)S(1)} %copy-done.4, bf16[4096,256]{1,0:T(8,128)(2,1)S(1)} %copy-done.2, bf16[2,144,3200]{2,1,0:T(8,128)(2,1)S(1)} %get-tuple-element.36.v_ref, ...), custom_call_target="tpu_custom_call" | custom-call | flops 4831838208 | bytes 8388608 | tf_op jit(solution)/shard_map/attention/pallas_call | solution.py:228
  37.0 0.1 collective-permute-start.11
  37.1 0.0 collective-permute-done.4.rest_1_
  37.1 4.7 %collective-permute-start.12 = (bf16[32,2176]{1,0:T(8,128)(2,1)S(1)}, bf16[32,2176]{1,0:T(8,128)(2,1)S(1)}, u32[]{:S(2)}, u32[]{:S(2)}) collective-permute-start(bf16[32,2176]{1,0:T(8,128)(2,1)S(1)} %get-tuple-element.42), channel_id=1, source_target_pairs={{0,28},{4,24},{8,4},{12,0},{16,12},{20,8},{24,20},{28,16},{1,29},{... | collective-permute-start | bytes 417800 | tf_op jit(solution)/shard_map/ppermute | solution.py:372
  41.8 0.0 collective-permute-done.3.rest_0_
  41.8 0.5 collective-permute-start.9
  42.3 0.0 collective-permute-done.8.refs_2_
  42.4 0.0 collective-permute-done.7.refs_1_
  42.4 0.0 copy-done.7
  42.4 6.7 %attention.6 = (bf16[32,2176]{1,0:T(8,128)(2,1)S(1)}, bf16[32,2176]{1,0:T(8,128)(2,1)S(1)}) custom-call(s32[58]{0:T(128)S(1)} %copy-done.7, bf16[32,512]{1,0:T(8,128)(2,1)S(1)} %copy-done.4, bf16[4096,256]{1,0:T(8,128)(2,1)S(1)} %copy-done.2, bf16[2,144,3200]{2,1,0:T(8,128)(2,1)S(1)} %get-tuple-element.36.v_ref, ...), custom_call_target="tpu_custom_call" | custom-call | flops 3221225472 | bytes 8388608 | tf_op jit(solution)/shard_map/attention/pallas_call | solution.py:228
  49.1 1.6 %collective-permute-start.10 = (bf16[32,2176]{1,0:T(8,128)(2,1)S(1)}, bf16[32,2176]{1,0:T(8,128)(2,1)S(1)}, u32[]{:S(2)}, u32[]{:S(2)}) collective-permute-start(bf16[32,2176]{1,0:T(8,128)(2,1)S(1)} %get-tuple-element.48), channel_id=1, source_target_pairs={{0,4},{4,0},{8,12},{12,8},{16,20},{20,16},{24,28},{28,24},{1,5},{5... | collective-permute-start | bytes 417800 | tf_op jit(solution)/shard_map/ppermute | solution.py:372
  50.6 3.1 %collective-permute-start.13 = (bf16[32,2176]{1,0:T(8,128)(2,1)S(1)}, bf16[32,2176]{1,0:T(8,128)(2,1)S(1)}, u32[]{:S(2)}, u32[]{:S(2)}) collective-permute-start(bf16[32,2176]{1,0:T(8,128)(2,1)S(1)} %get-tuple-element.54), channel_id=1, source_target_pairs={{0,20},{4,16},{8,28},{12,24},{16,4},{20,0},{24,12},{28,8},{1,21},{... | collective-permute-start | bytes 417800 | tf_op jit(solution)/shard_map/ppermute | solution.py:372
  53.7 0.0 copy-done.3
  53.7 0.0 copy-done.5
  53.7 3.9 %attention.7.refs_0_ = bf16[32,2176]{1,0:T(8,128)(2,1)S(1)} custom-call(s32[58]{0:T(128)S(1)} %copy-done.7, bf16[32,512]{1,0:T(8,128)(2,1)S(1)} %copy-done.5, bf16[4096,256]{1,0:T(8,128)(2,1)S(1)} %copy-done.2, bf16[2,144,3200]{2,1,0:T(8,128)(2,1)S(1)} %get-tuple-element.36.v_ref, bf16[32,2048]{1,0:T(8,128)(2,1)S(1)} %copy-done.3), custom_call_target="tpu_custom_call" | custom-call | flops 1610612736 | bytes 8388608 | tf_op jit(solution)/shard_map/attention/pallas_call | solution.py:228
  57.6 0.0 collective-permute-done.11.refs_5_
  57.6 0.0 collective-permute-done.12.refs_6_
  57.6 0.0 collective-permute-done.9.refs_3_
  57.6 0.0 collective-permute-done.10.refs_4_
  57.6 1.6 %collective-permute-done.13.refs_7_ = bf16[32,2176]{1,0:T(8,128)(2,1)S(1)} collective-permute-done((bf16[32,2176]{1,0:T(8,128)(2,1)S(1)}, bf16[32,2176]{1,0:T(8,128)(2,1)S(1)}, u32[]{:S(2)}, u32[]{:S(2)}) %collective-permute-start.13) | collective-permute-done | bytes 139296 | tf_op jit(solution)/shard_map/ppermute | solution.py:372
  59.2 0.9 merge.1.rest_0_
  60.1 0.1 collective-permute-start.15
  60.2 3.8 %collective-permute-start.14 = (bf16[32,2048]{1,0:T(8,128)(2,1)S(1)}, bf16[32,2048]{1,0:T(8,128)(2,1)S(1)}, u32[]{:S(2)}, u32[]{:S(2)}) collective-permute-start(bf16[32,2048]{1,0:T(8,128)(2,1)S(1)} %merge.1.rest_0_), channel_id=1, source_target_pairs={{0,24},{4,28},{8,0},{12,4},{16,8},{20,12},{24,16},{28,20},{1,25},{... | collective-permute-start | bytes 393224 | tf_op jit(solution)/shard_map/ppermute | solution.py:372
  64.0 0.0 collective-permute-start.16
  64.0 4.4 %collective-permute-done.15.rest_2_ = bf16[32,2048]{1,0:T(8,128)(2,1)S(1)} collective-permute-done((bf16[32,2048]{1,0:T(8,128)(2,1)S(1)}, bf16[32,2048]{1,0:T(8,128)(2,1)S(1)}, u32[]{:S(2)}, u32[]{:S(2)}) %collective-permute-start.15) | collective-permute-done | bytes 131104 | tf_op jit(solution)/shard_map/ppermute | solution.py:372
  68.4 0.8 collective-permute-start.19
  69.2 1.2 %collective-permute-start.17 = (bf16[32,2048]{1,0:T(8,128)(2,1)S(1)}, bf16[32,2048]{1,0:T(8,128)(2,1)S(1)}, u32[]{:S(2)}, u32[]{:S(2)}) collective-permute-start(bf16[32,2048]{1,0:T(8,128)(2,1)S(1)} %merge.1.rest_0_), channel_id=1, source_target_pairs={{0,4},{4,0},{8,12},{12,8},{16,20},{20,16},{24,28},{28,24},{1,5},{5... | collective-permute-start | bytes 393224 | tf_op jit(solution)/shard_map/ppermute | solution.py:372
  70.5 0.0 collective-permute-done.14.rest_1_
  70.5 0.8 collective-permute-start.18
  71.2 2.4 %collective-permute-done.16.rest_3_ = bf16[32,2048]{1,0:T(8,128)(2,1)S(1)} collective-permute-done((bf16[32,2048]{1,0:T(8,128)(2,1)S(1)}, bf16[32,2048]{1,0:T(8,128)(2,1)S(1)}, u32[]{:S(2)}, u32[]{:S(2)}) %collective-permute-start.16) | collective-permute-done | bytes 131104 | tf_op jit(solution)/shard_map/ppermute | solution.py:372
  73.6 0.0 collective-permute-done.19.rest_6_
  73.6 0.9 collective-permute-start.20
  74.6 0.2 collective-permute-done.17.rest_4_
  74.8 1.9 %collective-permute-done.18.rest_5_ = bf16[32,2048]{1,0:T(8,128)(2,1)S(1)} collective-permute-done((bf16[32,2048]{1,0:T(8,128)(2,1)S(1)}, bf16[32,2048]{1,0:T(8,128)(2,1)S(1)}, u32[]{:S(2)}, u32[]{:S(2)}) %collective-permute-start.18) | collective-permute-done | bytes 131104 | tf_op jit(solution)/shard_map/ppermute | solution.py:372
  76.7 2.3 %collective-permute-done.20.rest_7_ = bf16[32,2048]{1,0:T(8,128)(2,1)S(1)} collective-permute-done((bf16[32,2048]{1,0:T(8,128)(2,1)S(1)}, bf16[32,2048]{1,0:T(8,128)(2,1)S(1)}, u32[]{:S(2)}, u32[]{:S(2)}) %collective-permute-start.20) | collective-permute-done | bytes 131104 | tf_op jit(solution)/shard_map/ppermute | solution.py:372
  79.0 0.0 copy-done
  79.0 1.4 %projection.1 = (f32[2,64,1024]{2,1,0:T(8,128)S(1)}, bf16[2,64,1024]{2,1,0:T(8,128)(2,1)S(1)}) custom-call(bf16[2048,1024]{1,0:T(8,128)(2,1)S(1)} %copy-done, bf16[32,2048]{1,0:T(8,128)(2,1)S(1)} %merge.1.rest_0_, bf16[32,2048]{1,0:T(8,128)(2,1)S(1)} %collective-permute-done.14.rest_1_, bf16[32,2048]{1,0:T(8,128)(2,1)S(1)} %collective-permute-done.15.rest_2_, ...), custom_call_target="tpu_custom_call" | custom-call | flops 1073741824 | bytes 4194304 | tf_op jit(solution)/shard_map/projection/pallas_call | solution.py:330
  80.4 0.1 collective-permute-start.21
  80.5 1.5 %collective-permute-done.21 = bf16[2,64,1024]{2,1,0:T(8,128)(2,1)S(1)} collective-permute-done((bf16[2,64,1024]{2,1,0:T(8,128)(2,1)S(1)}, bf16[2,64,1024]{2,1,0:T(8,128)(2,1)S(1)}, u32[]{:S(2)}, u32[]{:S(2)}) %collective-permute-start.21) | collective-permute-done | bytes 262176 | tf_op jit(solution)/shard_map/ppermute | solution.py:450
  82.1 8.3 %collective-permute-start.22 = (bf16[64,1024]{1,0:T(8,128)(2,1)S(1)}, bf16[64,1024]{1,0:T(8,128)(2,1)S(1)}, u32[]{:S(2)}, u32[]{:S(2)}) collective-permute-start(bf16[64,1024]{1,0:T(8,128)(2,1)S(1)} %fusion), channel_id=1, source_target_pairs={{0,2},{1,3},{2,0},{3,1},{4,6},{5,7},{6,4},{7,5},{8,10},{9,11},{10,... | collective-permute-start | bytes 393224 | tf_op jit(solution)/shard_map/ppermute | solution.py:454
  90.4 3.8 %collective-permute-done.22 = bf16[64,1024]{1,0:T(8,128)(2,1)S(1)} collective-permute-done((bf16[64,1024]{1,0:T(8,128)(2,1)S(1)}, bf16[64,1024]{1,0:T(8,128)(2,1)S(1)}, u32[]{:S(2)}, u32[]{:S(2)}) %collective-permute-start.22) | collective-permute-done | bytes 131104 | tf_op jit(solution)/shard_map/ppermute | solution.py:454
  94.2 0.7 bitcast_add_fusion
  (7 shorter events, 0.0 us)
Async XLA Ops:
  0.0 9.3 %collective-permute-start = (bf16[32,2048]{1,0:T(8,128)(2,1)}, bf16[32,2048]{1,0:T(8,128)(2,1)S(1)}, u32[]{:S(2)}, u32[]{:S(2)}) collective-permute-start(bf16[32,2048]{1,0:T(8,128)(2,1)} %rest_0_), channel_id=1, source_target_pairs={{0,24},{4,28},{8,0},{12,4},{16,8},{20,12},{24,16},{28,20},{1,25},{... | collective-permute-start | bytes 393224 | tf_op jit(solution)/shard_map/ppermute | solution.py:372
  5.0 7.0 %collective-permute-start.1 = (bf16[32,2048]{1,0:T(8,128)(2,1)}, bf16[32,2048]{1,0:T(8,128)(2,1)S(1)}, u32[]{:S(2)}, u32[]{:S(2)}) collective-permute-start(bf16[32,2048]{1,0:T(8,128)(2,1)} %rest_0_), channel_id=1, source_target_pairs={{0,8},{4,12},{8,16},{12,20},{16,24},{20,28},{24,0},{28,4},{1,9},{5... | collective-permute-start | bytes 393224 | tf_op jit(solution)/shard_map/ppermute | solution.py:372
  5.1 32.0 %collective-permute-start.4 = (bf16[32,2048]{1,0:T(8,128)(2,1)}, bf16[32,2048]{1,0:T(8,128)(2,1)S(1)}, u32[]{:S(2)}, u32[]{:S(2)}) collective-permute-start(bf16[32,2048]{1,0:T(8,128)(2,1)} %rest_0_), channel_id=1, source_target_pairs={{0,4},{4,0},{8,12},{12,8},{16,20},{20,16},{24,28},{28,24},{1,5},{5... | collective-permute-start | bytes 393224 | tf_op jit(solution)/shard_map/ppermute | solution.py:372
  6.5 7.9 %copy-start.1 = (bf16[4096,256]{1,0:T(8,128)(2,1)S(1)}, bf16[4096,256]{1,0:T(8,128)(2,1)}, u32[]{:S(2)}) copy-start(bf16[4096,256]{1,0:T(8,128)(2,1)} %v_ref.1) | copy-start | bytes 6291460
  6.5 7.9 %copy-start.2 = (bf16[4096,256]{1,0:T(8,128)(2,1)S(1)}, bf16[4096,256]{1,0:T(8,128)(2,1)}, u32[]{:S(2)}) copy-start(bf16[4096,256]{1,0:T(8,128)(2,1)} %k_ref.7) | copy-start | bytes 6291460
  12.0 12.9 %collective-permute-start.2 = (bf16[32,2048]{1,0:T(8,128)(2,1)}, bf16[32,2048]{1,0:T(8,128)(2,1)S(1)}, u32[]{:S(2)}, u32[]{:S(2)}) collective-permute-start(bf16[32,2048]{1,0:T(8,128)(2,1)} %rest_0_), channel_id=1, source_target_pairs={{0,16},{4,20},{8,24},{12,28},{16,0},{20,4},{24,8},{28,12},{1,17},{... | collective-permute-start | bytes 393224 | tf_op jit(solution)/shard_map/ppermute | solution.py:372
  12.4 12.5 %collective-permute-start.5 = (bf16[32,2048]{1,0:T(8,128)(2,1)S(1)}, bf16[32,2048]{1,0:T(8,128)(2,1)S(1)}, u32[]{:S(2)}, u32[]{:S(2)}) collective-permute-start(bf16[32,2048]{1,0:T(8,128)(2,1)S(1)} %collective-permute-done.rest_0_), channel_id=1, source_target_pairs={{0,4},{4,0},{8,12},{12,8},{16,20},{20,16},{24,28},{28,24},{1,5},{5... | collective-permute-start | bytes 393224 | tf_op jit(solution)/shard_map/ppermute | solution.py:372
  13.9 11.0 %collective-permute-start.6 = (bf16[32,2048]{1,0:T(8,128)(2,1)S(1)}, bf16[32,2048]{1,0:T(8,128)(2,1)S(1)}, u32[]{:S(2)}, u32[]{:S(2)}) collective-permute-start(bf16[32,2048]{1,0:T(8,128)(2,1)S(1)} %collective-permute-done.1.rest_1_), channel_id=1, source_target_pairs={{0,4},{4,0},{8,12},{12,8},{16,20},{20,16},{24,28},{28,24},{1,5},{5... | collective-permute-start | bytes 393224 | tf_op jit(solution)/shard_map/ppermute | solution.py:372
  14.4 0.8 copy-start.4
  15.2 0.6 copy-start.6
  22.3 20.1 %collective-permute-start.8 = (bf16[32,2176]{1,0:T(8,128)(2,1)S(1)}, bf16[32,2176]{1,0:T(8,128)(2,1)S(1)}, u32[]{:S(2)}, u32[]{:S(2)}) collective-permute-start(bf16[32,2176]{1,0:T(8,128)(2,1)S(1)} %get-tuple-element.38), channel_id=1, source_target_pairs={{0,24},{4,28},{8,0},{12,4},{16,8},{20,12},{24,16},{28,20},{1,25},{... | collective-permute-start | bytes 417800 | tf_op jit(solution)/shard_map/ppermute | solution.py:372
  24.9 17.5 %collective-permute-start.7 = (bf16[32,2176]{1,0:T(8,128)(2,1)S(1)}, bf16[32,2176]{1,0:T(8,128)(2,1)S(1)}, u32[]{:S(2)}, u32[]{:S(2)}) collective-permute-start(bf16[32,2176]{1,0:T(8,128)(2,1)S(1)} %get-tuple-element.45), channel_id=1, source_target_pairs={{0,8},{4,12},{8,16},{12,20},{16,24},{20,28},{24,0},{28,4},{1,9},{5... | collective-permute-start | bytes 417800 | tf_op jit(solution)/shard_map/ppermute | solution.py:372
  24.9 16.9 %collective-permute-start.3 = (bf16[32,2048]{1,0:T(8,128)(2,1)S(1)}, bf16[32,2048]{1,0:T(8,128)(2,1)S(1)}, u32[]{:S(2)}, u32[]{:S(2)}) collective-permute-start(bf16[32,2048]{1,0:T(8,128)(2,1)S(1)} %collective-permute-done.2.rest_0_), channel_id=1, source_target_pairs={{0,4},{4,0},{8,12},{12,8},{16,20},{20,16},{24,28},{28,24},{1,5},{5... | collective-permute-start | bytes 393224 | tf_op jit(solution)/shard_map/ppermute | solution.py:372
  27.8 14.6 %copy-start.7 = (s32[58]{0:T(128)S(1)}, s32[58]{0:T(128)}, u32[]{:S(2)}) copy-start(s32[58]{0:T(128)} %get-tuple-element.32.table_ref) | copy-start | bytes 700
  37.0 20.6 %collective-permute-start.11 = (bf16[32,2176]{1,0:T(8,128)(2,1)S(1)}, bf16[32,2176]{1,0:T(8,128)(2,1)S(1)}, u32[]{:S(2)}, u32[]{:S(2)}) collective-permute-start(bf16[32,2176]{1,0:T(8,128)(2,1)S(1)} %get-tuple-element.53), channel_id=1, source_target_pairs={{0,12},{4,8},{8,20},{12,16},{16,28},{20,24},{24,4},{28,0},{1,13},{... | collective-permute-start | bytes 417800 | tf_op jit(solution)/shard_map/ppermute | solution.py:372
  37.1 20.5 %collective-permute-start.12 = (bf16[32,2176]{1,0:T(8,128)(2,1)S(1)}, bf16[32,2176]{1,0:T(8,128)(2,1)S(1)}, u32[]{:S(2)}, u32[]{:S(2)}) collective-permute-start(bf16[32,2176]{1,0:T(8,128)(2,1)S(1)} %get-tuple-element.42), channel_id=1, source_target_pairs={{0,28},{4,24},{8,4},{12,0},{16,12},{20,8},{24,20},{28,16},{1,29},{... | collective-permute-start | bytes 417800 | tf_op jit(solution)/shard_map/ppermute | solution.py:372
  41.8 11.9 %copy-start.3 = (bf16[32,2048]{1,0:T(8,128)(2,1)S(1)}, bf16[32,2048]{1,0:T(8,128)(2,1)}, u32[]{:S(2)}) copy-start(bf16[32,2048]{1,0:T(8,128)(2,1)} %rest_0_) | copy-start | bytes 393220
  41.8 11.9 %copy-start.5 = (bf16[32,512]{1,0:T(8,128)(2,1)S(1)}, bf16[32,512]{1,0:T(8,128)(2,1)}, u32[]{:S(2)}) copy-start(bf16[32,512]{1,0:T(8,128)(2,1)} %get-tuple-element.33.new_ref) | copy-start | bytes 98308
  41.8 15.8 %collective-permute-start.9 = (bf16[32,2176]{1,0:T(8,128)(2,1)S(1)}, bf16[32,2176]{1,0:T(8,128)(2,1)S(1)}, u32[]{:S(2)}, u32[]{:S(2)}) collective-permute-start(bf16[32,2176]{1,0:T(8,128)(2,1)S(1)} %get-tuple-element.52), channel_id=1, source_target_pairs={{0,16},{4,20},{8,24},{12,28},{16,0},{20,4},{24,8},{28,12},{1,17},{... | collective-permute-start | bytes 417800 | tf_op jit(solution)/shard_map/ppermute | solution.py:372
  49.1 8.6 %collective-permute-start.10 = (bf16[32,2176]{1,0:T(8,128)(2,1)S(1)}, bf16[32,2176]{1,0:T(8,128)(2,1)S(1)}, u32[]{:S(2)}, u32[]{:S(2)}) collective-permute-start(bf16[32,2176]{1,0:T(8,128)(2,1)S(1)} %get-tuple-element.48), channel_id=1, source_target_pairs={{0,4},{4,0},{8,12},{12,8},{16,20},{20,16},{24,28},{28,24},{1,5},{5... | collective-permute-start | bytes 417800 | tf_op jit(solution)/shard_map/ppermute | solution.py:372
  50.6 8.6 %collective-permute-start.13 = (bf16[32,2176]{1,0:T(8,128)(2,1)S(1)}, bf16[32,2176]{1,0:T(8,128)(2,1)S(1)}, u32[]{:S(2)}, u32[]{:S(2)}) collective-permute-start(bf16[32,2176]{1,0:T(8,128)(2,1)S(1)} %get-tuple-element.54), channel_id=1, source_target_pairs={{0,20},{4,16},{8,28},{12,24},{16,4},{20,0},{24,12},{28,8},{1,21},{... | collective-permute-start | bytes 417800 | tf_op jit(solution)/shard_map/ppermute | solution.py:372
  53.7 25.3 %copy-start = (bf16[2048,1024]{1,0:T(8,128)(2,1)S(1)}, bf16[2048,1024]{1,0:T(8,128)(2,1)}, u32[]{:S(2)}) copy-start(bf16[2048,1024]{1,0:T(8,128)(2,1)} %w_ref.1) | copy-start | bytes 12582916
  60.1 8.3 %collective-permute-start.15 = (bf16[32,2048]{1,0:T(8,128)(2,1)S(1)}, bf16[32,2048]{1,0:T(8,128)(2,1)S(1)}, u32[]{:S(2)}, u32[]{:S(2)}) collective-permute-start(bf16[32,2048]{1,0:T(8,128)(2,1)S(1)} %merge.1.rest_0_), channel_id=1, source_target_pairs={{0,8},{4,12},{8,16},{12,20},{16,24},{20,28},{24,0},{28,4},{1,9},{5... | collective-permute-start | bytes 393224 | tf_op jit(solution)/shard_map/ppermute | solution.py:372
  60.2 10.2 %collective-permute-start.14 = (bf16[32,2048]{1,0:T(8,128)(2,1)S(1)}, bf16[32,2048]{1,0:T(8,128)(2,1)S(1)}, u32[]{:S(2)}, u32[]{:S(2)}) collective-permute-start(bf16[32,2048]{1,0:T(8,128)(2,1)S(1)} %merge.1.rest_0_), channel_id=1, source_target_pairs={{0,24},{4,28},{8,0},{12,4},{16,8},{20,12},{24,16},{28,20},{1,25},{... | collective-permute-start | bytes 393224 | tf_op jit(solution)/shard_map/ppermute | solution.py:372
  64.0 9.6 %collective-permute-start.16 = (bf16[32,2048]{1,0:T(8,128)(2,1)S(1)}, bf16[32,2048]{1,0:T(8,128)(2,1)S(1)}, u32[]{:S(2)}, u32[]{:S(2)}) collective-permute-start(bf16[32,2048]{1,0:T(8,128)(2,1)S(1)} %merge.1.rest_0_), channel_id=1, source_target_pairs={{0,16},{4,20},{8,24},{12,28},{16,0},{20,4},{24,8},{28,12},{1,17},{... | collective-permute-start | bytes 393224 | tf_op jit(solution)/shard_map/ppermute | solution.py:372
  68.4 5.2 %collective-permute-start.19 = (bf16[32,2048]{1,0:T(8,128)(2,1)S(1)}, bf16[32,2048]{1,0:T(8,128)(2,1)S(1)}, u32[]{:S(2)}, u32[]{:S(2)}) collective-permute-start(bf16[32,2048]{1,0:T(8,128)(2,1)S(1)} %collective-permute-done.15.rest_2_), channel_id=1, source_target_pairs={{0,4},{4,0},{8,12},{12,8},{16,20},{20,16},{24,28},{28,24},{1,5},{5... | collective-permute-start | bytes 393224 | tf_op jit(solution)/shard_map/ppermute | solution.py:372
  69.2 5.6 %collective-permute-start.17 = (bf16[32,2048]{1,0:T(8,128)(2,1)S(1)}, bf16[32,2048]{1,0:T(8,128)(2,1)S(1)}, u32[]{:S(2)}, u32[]{:S(2)}) collective-permute-start(bf16[32,2048]{1,0:T(8,128)(2,1)S(1)} %merge.1.rest_0_), channel_id=1, source_target_pairs={{0,4},{4,0},{8,12},{12,8},{16,20},{20,16},{24,28},{28,24},{1,5},{5... | collective-permute-start | bytes 393224 | tf_op jit(solution)/shard_map/ppermute | solution.py:372
  70.5 6.2 %collective-permute-start.18 = (bf16[32,2048]{1,0:T(8,128)(2,1)S(1)}, bf16[32,2048]{1,0:T(8,128)(2,1)S(1)}, u32[]{:S(2)}, u32[]{:S(2)}) collective-permute-start(bf16[32,2048]{1,0:T(8,128)(2,1)S(1)} %collective-permute-done.14.rest_1_), channel_id=1, source_target_pairs={{0,4},{4,0},{8,12},{12,8},{16,20},{20,16},{24,28},{28,24},{1,5},{5... | collective-permute-start | bytes 393224 | tf_op jit(solution)/shard_map/ppermute | solution.py:372
  73.6 5.4 %collective-permute-start.20 = (bf16[32,2048]{1,0:T(8,128)(2,1)S(1)}, bf16[32,2048]{1,0:T(8,128)(2,1)S(1)}, u32[]{:S(2)}, u32[]{:S(2)}) collective-permute-start(bf16[32,2048]{1,0:T(8,128)(2,1)S(1)} %collective-permute-done.16.rest_3_), channel_id=1, source_target_pairs={{0,4},{4,0},{8,12},{12,8},{16,20},{20,16},{24,28},{28,24},{1,5},{5... | collective-permute-start | bytes 393224 | tf_op jit(solution)/shard_map/ppermute | solution.py:372
  80.4 1.6 %collective-permute-start.21 = (bf16[2,64,1024]{2,1,0:T(8,128)(2,1)S(1)}, bf16[2,64,1024]{2,1,0:T(8,128)(2,1)S(1)}, u32[]{:S(2)}, u32[]{:S(2)}) collective-permute-start(bf16[2,64,1024]{2,1,0:T(8,128)(2,1)S(1)} %get-tuple-element.58), channel_id=1, source_target_pairs={{0,1},{1,0},{2,3},{3,2},{4,5},{5,4},{6,7},{7,6},{8,9},{9,8},{10,11... | collective-permute-start | bytes 786440 | tf_op jit(solution)/shard_map/ppermute | solution.py:450
  82.1 12.1 %collective-permute-start.22 = (bf16[64,1024]{1,0:T(8,128)(2,1)S(1)}, bf16[64,1024]{1,0:T(8,128)(2,1)S(1)}, u32[]{:S(2)}, u32[]{:S(2)}) collective-permute-start(bf16[64,1024]{1,0:T(8,128)(2,1)S(1)} %fusion), channel_id=1, source_target_pairs={{0,2},{1,3},{2,0},{3,1},{4,6},{5,7},{6,4},{7,5},{8,10},{9,11},{10,... | collective-permute-start | bytes 393224 | tf_op jit(solution)/shard_map/ppermute | solution.py:454

commit v7 on v6

--- a/solution.py
+++ b/solution.py
@@ -28,10 +28,10 @@
 
 
 def attention_kernel(
-    members, ctx_count, group, kv_local, slots, turn, table_ref, new_ref, k_ref, v_ref, *rest
+    members, ctx_count, group, kv_local, slots, turn, extra, slot_ref, keep_ref, count_ref, nk_ref, nv_ref, k_ref, v_ref, *rest
 ):
     blocks = len(members)
-    q_refs, rest = rest[:blocks], rest[blocks:]
+    q_refs, rest = rest[:blocks], rest[blocks + extra :]
     out_refs, rest = rest[:blocks], rest[blocks:]
     turned_ref, acc_ref, max_ref = rest[-3:]
     kept_ref = rest[0] if turn else v_ref
@@ -44,10 +44,10 @@
     me = lax.axis_index("ctx")
 
     def count_of(g):
-        return table_ref[kv_local * slots + g]
+        return count_ref[g]
 
     def slot_of(ctx):
-        return table_ref[kv_local * (slots + 1) + ctx]
+        return slot_ref[ctx]
 
     ones_tile = jnp.ones((ONES, TILE), jnp.bfloat16)
     place_key = lax.broadcasted_iota(jnp.int32, (TILE, rows), 0)
@@ -59,7 +59,7 @@
         parts = []
         for i in range(CHUNK):
             slot = chunk * CHUNK + i
-            tile = table_ref[g * slots + jnp.where(slot < count_of(g), slot, 0)]
+            tile = keep_ref[g, jnp.where(slot < count_of(g), slot, 0)]
             parts.append(k_ref[pl.ds(pl.multiple_of(tile * TILE, TILE), TILE), cols])
         return jnp.concatenate(parts, 0)
 
@@ -72,7 +72,7 @@
         for i in range(CHUNK):
             slot = chunk * CHUNK + i
             live = slot < count_of(g)
-            tile = table_ref[g * slots + jnp.where(live, slot, 0)]
+            tile = keep_ref[g, jnp.where(live, slot, 0)]
             at = pl.ds(pl.multiple_of(tile * TILE, TILE), TILE)
             tail = jnp.concatenate([v_ref[at, cols].T, ones_tile], 0)
             parts.append(jnp.where(live, tail, jnp.zeros_like(tail)))
@@ -80,26 +80,25 @@
         kept_ref[g, :, whole] = values
         return values
 
-    def open_state(g, b, keys, values):
-        s = jnp.dot(keys, turned_ref[g, b], preferred_element_type=jnp.float32)
-        shift = (slot_of(flipped(me, ctx_count, *members[b])) - slot_of(me)) * q_dev
-        live = (place_key < q_dev) & (place_row - place_key + shift >= 0)
-        s = jnp.concatenate([s[:span], jnp.where(live, s[span:], LOW)], 0)
-        top = jnp.max(s, axis=0, keepdims=True) * scale
-        p = jnp.exp2(s * scale - top).astype(jnp.bfloat16)
-        max_ref[g, b] = jnp.broadcast_to(top, max_ref.shape[2:])
-        acc_ref[g, b] = jnp.dot(values, p, preferred_element_type=jnp.float32)
-
-    def open_head(g, first_values):
-        fresh = jnp.concatenate([new_ref[:, g * DH : (g + 1) * DH], padding], 0)
-        keys = jnp.concatenate([keys_of(g, 0), fresh], 0)
-        values = jnp.concatenate([first_values, kept_ref[g, :, last:]], 1)
+    def open_head(g):
+        cols = slice(g * DH, (g + 1) * DH)
+        first = pl.ds(pl.multiple_of(keep_ref[g, 0] * TILE, TILE), TILE)
+        keys = jnp.concatenate([nk_ref[:, cols], padding, k_ref[first, cols]], 0)
         for b in range(blocks):
-            open_state(g, b, keys, values)
+            s = jnp.dot(keys, turned_ref[g, b], preferred_element_type=jnp.float32)
+            shift = (slot_of(flipped(me, ctx_count, *members[b])) - slot_of(me)) * q_dev
+            live = (place_key < q_dev) & (place_row - place_key + shift >= 0)
+            fresh = jnp.where(live, s[:TILE], LOW)
+            top = jnp.max(jnp.maximum(fresh, s[TILE:]), axis=0, keepdims=True) * scale
+            p = jnp.exp2(fresh * scale - top).astype(jnp.bfloat16)
+            max_ref[g, b] = jnp.broadcast_to(top, max_ref.shape[2:])
+            acc_ref[g, b] = jnp.dot(
+                kept_ref[g, :, last:], p, preferred_element_type=jnp.float32
+            )
 
     for g in range(kv_local):
         if turn:
-            fresh_values = new_ref[:, (kv_local + g) * DH : (kv_local + g + 1) * DH]
+            fresh_values = nv_ref[:, g * DH : (g + 1) * DH]
             fresh_values = jnp.concatenate([fresh_values, padding], 0).T
             kept_ref[g, :, last:] = jnp.concatenate([fresh_values, ones_tile], 0)
         for b in range(blocks):
@@ -108,16 +107,22 @@
                 for h in range(group)
             ]
             turned_ref[g, b] = jnp.concatenate(columns, 0).T
-        open_head(g, values_of(g, 0))
+        open_head(g)
 
     def run(kv_heads, chunk):
         loaded = {g: (keys_of(g, chunk), values_of(g, chunk)) for g in kv_heads}
-        for b in range(blocks):
-            for g in kv_heads:
-                keys, values = loaded[g]
-                s = jnp.dot(keys, turned_ref[g, b], preferred_element_type=jnp.float32)
-                p = jnp.exp2(s * scale - max_ref[g, b, :1]).astype(jnp.bfloat16)
-                acc_ref[g, b] += jnp.dot(values, p, preferred_element_type=jnp.float32)
+        chains = [(g, b) for b in range(blocks) for g in kv_heads]
+
+        def score(g, b):
+            return jnp.dot(loaded[g][0], turned_ref[g, b], preferred_element_type=jnp.float32)
+
+        ahead = score(*chains[0])
+        for at, (g, b) in enumerate(chains):
+            s = ahead
+            if at + 1 < len(chains):
+                ahead = score(*chains[at + 1])
+            p = jnp.exp2(s * scale - max_ref[g, b, :1]).astype(jnp.bfloat16)
+            acc_ref[g, b] += jnp.dot(loaded[g][1], p, preferred_element_type=jnp.float32)
 
     ends = [(count_of(g) + CHUNK - 1) // CHUNK for g in range(kv_local)]
     shared = functools.reduce(jnp.minimum, ends)
@@ -126,7 +131,7 @@
         run(range(kv_local), chunk)
         return carry
 
-    lax.fori_loop(1, shared, step_all, 0)
+    lax.fori_loop(0, shared, step_all, 0)
     for g in range(kv_local):
 
         def step_one(chunk, carry, g=g):
@@ -144,7 +149,7 @@
     @pl.when(jnp.max(large) > 0.0)
     def again():
         for g in range(kv_local):
-            open_head(g, kept_ref[g, :, :span])
+            open_head(g)
 
             def step_exact(chunk, carry, g=g):
                 keys = keys_of(g, chunk)
@@ -160,7 +165,7 @@
                     )
                 return carry
 
-            lax.fori_loop(1, ends[g], step_exact, 0)
+            lax.fori_loop(0, ends[g], step_exact, 0)
 
     sublane = lax.broadcasted_iota(jnp.int32, (q_dev, LANES), 0)
     parts = rows // LANES
@@ -182,40 +187,23 @@
         out_refs[b][:, heads * DH :] = stats.astype(jnp.bfloat16)
 
 
-def pack_kernel(slot_ref, keep_ref, count_ref, nk_ref, nv_ref, k_hbm, v_hbm, table_ref, rows_ref):
-    kv_local, slots = keep_ref.shape
-    for g in range(kv_local):
-        for t in range(slots):
-            table_ref[g * slots + t] = keep_ref[g, t]
-        table_ref[kv_local * slots + g] = count_ref[g]
-    for c in range(slot_ref.shape[0]):
-        table_ref[kv_local * (slots + 1) + c] = slot_ref[c]
-    width = nk_ref.shape[1]
-    rows_ref[:, :width] = nk_ref[...]
-    rows_ref[:, width:] = nv_ref[...]
-
-
-def pack_call(slot, keep, count, new_keys, new_values, keys, values):
-    smem = pl.BlockSpec(memory_space=pltpu.SMEM)
-    vmem = pl.BlockSpec(memory_space=pltpu.VMEM)
-    hbm = pl.BlockSpec(memory_space=pltpu.HBM)
-    q_dev, width = new_keys.shape
-    entries = keep.size + count.size + slot.size
+def settle_kernel(k_hbm, v_hbm, nk_hbm, nv_hbm, out_ref):
+    out_ref[...] = jnp.zeros_like(out_ref)
+
+
+def settle_call(*arrays):
     return pl.pallas_call(
-        pack_kernel,
-        out_shape=[
-            jax.ShapeDtypeStruct((entries,), jnp.int32),
-            jax.ShapeDtypeStruct((q_dev, 2 * width), new_keys.dtype),
-        ],
-        in_specs=[smem] * 3 + [vmem] * 2 + [hbm] * 2,
-        out_specs=[smem, vmem],
+        settle_kernel,
+        out_shape=jax.ShapeDtypeStruct((8, LANES), jnp.float32),
+        in_specs=[pl.BlockSpec(memory_space=pltpu.HBM)] * len(arrays),
+        out_specs=pl.BlockSpec(memory_space=pltpu.VMEM),
         compiler_params=pltpu.CompilerParams(vmem_limit_bytes=VMEM_PACK),
-        name="pack",
-    )(slot, keep, count, new_keys, new_values, keys, values)
+        name="settle",
+    )(*arrays)
 
 
 def attention_call(
-    members, ctx_count, kv_local, slots, turn, blocks, table, new_rows, keys, values
+    members, ctx_count, kv_local, slots, turn, blocks, small, keys, values, extra
 ):
     n = len(blocks)
     q_dev, width = blocks[0].shape
@@ -227,11 +215,11 @@
     kept = -(-slots // CHUNK) * CHUNK + 1
     return pl.pallas_call(
         functools.partial(
-            attention_kernel, members, ctx_count, group, kv_local, slots, turn
+            attention_kernel, members, ctx_count, group, kv_local, slots, turn, len(extra)
         ),
         out_shape=[jax.ShapeDtypeStruct((q_dev, width + LANES), jnp.bfloat16)] * n
         + [jax.ShapeDtypeStruct((kv_local, DH + ONES, kept * TILE), jnp.bfloat16)] * turn,
-        in_specs=[smem] + [vmem] * (3 + n),
+        in_specs=[smem] * 3 + [vmem] * (4 + n + len(extra)),
         out_specs=[vmem] * (n + turn),
         scratch_shapes=[
             pltpu.VMEM((kv_local, n, DH, rows), jnp.bfloat16),
@@ -243,7 +231,7 @@
             flops=work * DH * 8, bytes_accessed=8 * 2**20, transcendentals=work
         ),
         name="attention",
-    )(table, new_rows, keys, values, *blocks)
+    )(*small, keys, values, *blocks, *extra)
 
 
 def merge_kernel(parts, kv_local, *refs):
@@ -401,17 +389,10 @@
     groups += [middle + flip[:2]] + [flip[i : i + 2] for i in range(2, len(flip), 2)]
     groups += [late, order[:1]]
     kv_local = new_keys.shape[1] // DH
-    table, new_rows = pack_call(
-        owner_slot,
-        keep_tiles[0],
-        tile_count[0],
-        new_keys,
-        new_values,
-        cache_keys,
-        cache_values,
-    )
-
-    def attend(members, blocks, turn, values):
+    small = (owner_slot, keep_tiles[0], tile_count[0], new_keys, new_values)
+    token = settle_call(cache_keys, cache_values, new_keys, new_values)
+
+    def attend(members, blocks, turn, values, extra):
         return attention_call(
             members,
             ctx_count,
@@ -419,10 +400,10 @@
             keep_tiles.shape[2],
             turn,
             blocks,
-            table,
-            new_rows,
+            small,
             cache_keys,
             values,
+            extra,
         )
 
     values = cache_values
@@ -430,13 +411,16 @@
     last = None
     for index, members in enumerate(groups):
         blocks = [held[m] for m in members]
+        if index == 0:
+            blocks, token = lax.optimization_barrier((blocks, token))
         if last is not None:
             blocks, parts[last] = lax.optimization_barrier((blocks, parts[last]))
         if 2 <= index < len(groups) - 1:
             returned = {m: back[m] for m in groups[index - 2] if 2 * m[0] != high}
             blocks, returned = lax.optimization_barrier((blocks, returned))
             back.update(returned)
-        outs = attend(members, blocks, index == 0, values)
+        extra = [token] if members == groups[-1] else []
+        outs = attend(members, blocks, index == 0, values, extra)
         parts.update(zip(members, outs))
         if index == 0:
             values = outs[-1]

time: 95 us -> 80.5 us (0.85)
  starting transfers between devices: 40.4 us -> 30.6 us
  Pallas kernels: 30.1 us -> 21.3 us
  waiting for transfers between devices: 22.1 us -> 27.9 us
  local copies, waits for them, and re-layouts: 1.38 us -> 0.04 us
    ppermute x1, starting transfers between devices: 8.32 us -> 0.31 us  [body(): piece = lax.ppermute(piece, 'tp', [(i, i ^ 2 * j) for i in range(peers)])]
    pallas_call x4, Pallas kernels: 26.2 us -> 18.4 us  [attention_call(): pl.pallas_call(functools.partial(attention_kernel, members, ctx_count, gr...]
    ppermute x21, waiting for transfers between devices: 16.8 us -> 21.1 us  [move(): return lax.ppermute(x, 'ctx', pairs)]
    ppermute x21, starting transfers between devices: 32 us -> 30.2 us  [move(): return lax.ppermute(x, 'ctx', pairs)]
    ppermute x1, waiting for transfers between devices: 3.8 us -> 5.29 us  [body(): piece = lax.ppermute(piece, 'tp', [(i, i ^ 2 * j) for i in range(peers)])]
    unnamed x16 -> x20, local copies, waits for them, and re-layouts: 1.38 us -> 0.04 us
    pallas_call x1, Pallas kernels: 1.55 us -> 0.59 us  [settle_call(): pl.pallas_call(settle_kernel, out_shape=jax.ShapeDtypeStruct((8, LANES),...]
  transfers between devices with their start and end apart: 23 -> 23, of which waited for: 10 -> 11; matrix products, arithmetic and copies ran while one was open for 0% -> 0% of each run, Pallas kernels for 29% -> 24%
where the time goes in v7:
time: 80.5 us; the launch traced here: 80.8 us
  starting transfers between devices  30.6 us (38%)
  waiting for transfers between devices  27.9 us (35%)
  Pallas kernels  21.3 us (26%)
    ppermute x21, starting transfers between devices, move(): return lax.ppermute(x, 'ctx', pairs)  30.2 us
    ppermute x21, waiting for transfers between devices, move(): return lax.ppermute(x, 'ctx', pairs)  21.1 us
    pallas_call x4, Pallas kernels, attention_call(): pl.pallas_call(functools.partial(attention_kernel, members, ctx_count, gr...  18.4 us
    ppermute x1, waiting for transfers between devices, body(): piece = lax.ppermute(piece, 'tp', [(i, i ^ 2 * j) for i in range(peers)])  5.29 us
  transfers between devices with their start and end apart: 23, of which 11 were waited for; matrix products, arithmetic and copies ran while one was open for 0% of the time, Pallas kernels for 24%

profile of v7, /device:TPU:0, one launch (start us, length us, event | category | flops | bytes accessed | tf_op | source)
XLA Modules:
  0.0 80.8 jit_solution(16687324437743787455)
XLA Ops:
  0.0 0.0 copy-start.9
  0.0 0.0 copy-start.8
  0.0 5.1 %collective-permute-start = (bf16[32,2048]{1,0:T(8,128)(2,1)}, bf16[32,2048]{1,0:T(8,128)(2,1)S(1)}, u32[]{:S(2)}, u32[]{:S(2)}) collective-permute-start(bf16[32,2048]{1,0:T(8,128)(2,1)} %rest_0_), channel_id=1, source_target_pairs={{0,24},{4,28},{8,0},{12,4},{16,8},{20,12},{24,16},{28,20},{1,25},{... | collective-permute-start | bytes 393224 | tf_op jit(solution)/shard_map/ppermute | solution.py:360
  5.2 0.0 collective-permute-start.1
  5.2 1.5 %collective-permute-start.4 = (bf16[32,2048]{1,0:T(8,128)(2,1)}, bf16[32,2048]{1,0:T(8,128)(2,1)S(1)}, u32[]{:S(2)}, u32[]{:S(2)}) collective-permute-start(bf16[32,2048]{1,0:T(8,128)(2,1)} %rest_0_), channel_id=1, source_target_pairs={{0,4},{4,0},{8,12},{12,8},{16,20},{20,16},{24,28},{28,24},{1,5},{5... | collective-permute-start | bytes 393224 | tf_op jit(solution)/shard_map/ppermute | solution.py:360
  6.6 0.6 settle.1.rest_1_
  7.2 2.1 %collective-permute-done.rest_0_ = bf16[32,2048]{1,0:T(8,128)(2,1)S(1)} collective-permute-done((bf16[32,2048]{1,0:T(8,128)(2,1)}, bf16[32,2048]{1,0:T(8,128)(2,1)S(1)}, u32[]{:S(2)}, u32[]{:S(2)}) %collective-permute-start) | collective-permute-done | bytes 131104 | tf_op jit(solution)/shard_map/ppermute | solution.py:360
  9.4 2.8 %collective-permute-done.1.rest_1_ = bf16[32,2048]{1,0:T(8,128)(2,1)S(1)} collective-permute-done((bf16[32,2048]{1,0:T(8,128)(2,1)}, bf16[32,2048]{1,0:T(8,128)(2,1)S(1)}, u32[]{:S(2)}, u32[]{:S(2)}) %collective-permute-start.1) | collective-permute-done | bytes 131104 | tf_op jit(solution)/shard_map/ppermute | solution.py:360
  12.1 1.5 %collective-permute-start.5 = (bf16[32,2048]{1,0:T(8,128)(2,1)S(1)}, bf16[32,2048]{1,0:T(8,128)(2,1)S(1)}, u32[]{:S(2)}, u32[]{:S(2)}) collective-permute-start(bf16[32,2048]{1,0:T(8,128)(2,1)S(1)} %collective-permute-done.rest_0_), channel_id=1, source_target_pairs={{0,4},{4,0},{8,12},{12,8},{16,20},{20,16},{24,28},{28,24},{1,5},{5... | collective-permute-start | bytes 393224 | tf_op jit(solution)/shard_map/ppermute | solution.py:360
  13.6 0.5 collective-permute-start.6
  14.2 0.4 collective-permute-start.2
  14.5 0.0 copy-done.3
  14.5 0.0 copy-done.4
  14.5 0.0 copy-done.2
  14.5 0.0 copy-done.1
  14.5 0.0 copy-done.7
  14.6 0.0 copy-done.9
  14.6 0.0 copy-done.8
  14.6 4.6 %attention.4 = (bf16[32,2176]{1,0:T(8,128)(2,1)S(1)}, bf16[32,2176]{1,0:T(8,128)(2,1)S(1)}, bf16[2,144,3200]{2,1,0:T(8,128)(2,1)S(1)}) custom-call(s32[8]{0:T(128)S(1)} %copy-done.8, s32[2,24]{1,0:T(2,128)S(1)} %bitcast.6, s32[2]{0:T(128)S(1)} %bitcast.10, bf16[32,256]{1,0:T(8,128)(2,1)S(1)} %copy-done.3, bf16[32,256]{1,0:T(8,128)(2,1)S(1)} %copy-done.4, ...), custom_call_target="tpu_custom_call" | custom-call | flops 3221225472 | bytes 8388608 | tf_op jit(solution)/shard_map/attention/pallas_call | solution.py:216
  19.1 3.4 %collective-permute-start.8 = (bf16[32,2176]{1,0:T(8,128)(2,1)S(1)}, bf16[32,2176]{1,0:T(8,128)(2,1)S(1)}, u32[]{:S(2)}, u32[]{:S(2)}) collective-permute-start(bf16[32,2176]{1,0:T(8,128)(2,1)S(1)} %get-tuple-element.39), channel_id=1, source_target_pairs={{0,24},{4,28},{8,0},{12,4},{16,8},{20,12},{24,16},{28,20},{1,25},{... | collective-permute-start | bytes 417800 | tf_op jit(solution)/shard_map/ppermute | solution.py:360
  22.5 0.0 collective-permute-done.2.rest_0_
  22.5 0.0 collective-permute-start.7
  22.5 0.0 collective-permute-done.5.rest_1_
  22.5 0.0 collective-permute-done.6.rest_2_
  22.5 1.1 %collective-permute-start.3 = (bf16[32,2048]{1,0:T(8,128)(2,1)S(1)}, bf16[32,2048]{1,0:T(8,128)(2,1)S(1)}, u32[]{:S(2)}, u32[]{:S(2)}) collective-permute-start(bf16[32,2048]{1,0:T(8,128)(2,1)S(1)} %collective-permute-done.2.rest_0_), channel_id=1, source_target_pairs={{0,4},{4,0},{8,12},{12,8},{16,20},{20,16},{24,28},{28,24},{1,5},{5... | collective-permute-start | bytes 393224 | tf_op jit(solution)/shard_map/ppermute | solution.py:360
  23.6 5.9 %attention.5 = (bf16[32,2176]{1,0:T(8,128)(2,1)S(1)}, bf16[32,2176]{1,0:T(8,128)(2,1)S(1)}, bf16[32,2176]{1,0:T(8,128)(2,1)S(1)}) custom-call(s32[8]{0:T(128)S(1)} %copy-done.8, s32[2,24]{1,0:T(2,128)S(1)} %bitcast.7, s32[2]{0:T(128)S(1)} %bitcast.11, bf16[32,256]{1,0:T(8,128)(2,1)S(1)} %copy-done.3, bf16[32,256]{1,0:T(8,128)(2,1)S(1)} %copy-done.4, ...), custom_call_target="tpu_custom_call" | custom-call | flops 4831838208 | bytes 8388608 | tf_op jit(solution)/shard_map/attention/pallas_call | solution.py:216
  29.5 0.5 collective-permute-start.11
  30.0 0.0 collective-permute-done.4.rest_1_
  30.0 4.3 %collective-permute-start.12 = (bf16[32,2176]{1,0:T(8,128)(2,1)S(1)}, bf16[32,2176]{1,0:T(8,128)(2,1)S(1)}, u32[]{:S(2)}, u32[]{:S(2)}) collective-permute-start(bf16[32,2176]{1,0:T(8,128)(2,1)S(1)} %get-tuple-element.43), channel_id=1, source_target_pairs={{0,28},{4,24},{8,4},{12,0},{16,12},{20,8},{24,20},{28,16},{1,29},{... | collective-permute-start | bytes 417800 | tf_op jit(solution)/shard_map/ppermute | solution.py:360
  34.3 0.0 collective-permute-done.3.rest_0_
  34.3 0.0 collective-permute-start.9
  34.3 0.0 collective-permute-done.8.refs_2_
  34.3 0.0 collective-permute-done.7.refs_1_
  34.3 4.7 %attention.6 = (bf16[32,2176]{1,0:T(8,128)(2,1)S(1)}, bf16[32,2176]{1,0:T(8,128)(2,1)S(1)}) custom-call(s32[8]{0:T(128)S(1)} %copy-done.8, s32[2,24]{1,0:T(2,128)S(1)} %bitcast.8, s32[2]{0:T(128)S(1)} %bitcast.12, bf16[32,256]{1,0:T(8,128)(2,1)S(1)} %copy-done.3, bf16[32,256]{1,0:T(8,128)(2,1)S(1)} %copy-done.4, bf16[4096,256]{1,0:T(8,128)(2,1)S(1)} %copy-done.2, ...), custom_call_target="tpu_custom_call" | custom-call | flops 3221225472 | bytes 8388608 | tf_op jit(solution)/shard_map/attention/pallas_call | solution.py:216
  39.0 1.2 %collective-permute-start.10 = (bf16[32,2176]{1,0:T(8,128)(2,1)S(1)}, bf16[32,2176]{1,0:T(8,128)(2,1)S(1)}, u32[]{:S(2)}, u32[]{:S(2)}) collective-permute-start(bf16[32,2176]{1,0:T(8,128)(2,1)S(1)} %get-tuple-element.49), channel_id=1, source_target_pairs={{0,4},{4,0},{8,12},{12,8},{16,20},{20,16},{24,28},{28,24},{1,5},{5... | collective-permute-start | bytes 417800 | tf_op jit(solution)/shard_map/ppermute | solution.py:360
  40.2 3.0 %collective-permute-start.13 = (bf16[32,2176]{1,0:T(8,128)(2,1)S(1)}, bf16[32,2176]{1,0:T(8,128)(2,1)S(1)}, u32[]{:S(2)}, u32[]{:S(2)}) collective-permute-start(bf16[32,2176]{1,0:T(8,128)(2,1)S(1)} %get-tuple-element.56), channel_id=1, source_target_pairs={{0,20},{4,16},{8,28},{12,24},{16,4},{20,0},{24,12},{28,8},{1,21},{... | collective-permute-start | bytes 417800 | tf_op jit(solution)/shard_map/ppermute | solution.py:360
  43.2 0.0 copy-done.5
  43.2 3.3 %attention.7.refs_0_ = bf16[32,2176]{1,0:T(8,128)(2,1)S(1)} custom-call(s32[8]{0:T(128)S(1)} %copy-done.8, s32[2,24]{1,0:T(2,128)S(1)} %bitcast.9, s32[2]{0:T(128)S(1)} %bitcast.13, bf16[32,256]{1,0:T(8,128)(2,1)S(1)} %copy-done.3, bf16[32,256]{1,0:T(8,128)(2,1)S(1)} %copy-done.4, bf16[4096,256]{1,0:T(8,128)(2,1)S(1)} %copy-done.2, ...), custom_call_target="tpu_custom_call" | custom-call | flops 1610612736 | bytes 8388608 | tf_op jit(solution)/shard_map/attention/pallas_call | solution.py:216
  46.5 0.0 collective-permute-done.11.refs_5_
  46.5 0.0 collective-permute-done.12.refs_6_
  46.5 2.3 %collective-permute-done.9.refs_3_ = bf16[32,2176]{1,0:T(8,128)(2,1)S(1)} collective-permute-done((bf16[32,2176]{1,0:T(8,128)(2,1)S(1)}, bf16[32,2176]{1,0:T(8,128)(2,1)S(1)}, u32[]{:S(2)}, u32[]{:S(2)}) %collective-permute-start.9) | collective-permute-done | bytes 139296 | tf_op jit(solution)/shard_map/ppermute | solution.py:360
  48.8 0.0 collective-permute-done.10.refs_4_
  48.8 2.7 %collective-permute-done.13.refs_7_ = bf16[32,2176]{1,0:T(8,128)(2,1)S(1)} collective-permute-done((bf16[32,2176]{1,0:T(8,128)(2,1)S(1)}, bf16[32,2176]{1,0:T(8,128)(2,1)S(1)}, u32[]{:S(2)}, u32[]{:S(2)}) %collective-permute-start.13) | collective-permute-done | bytes 139296 | tf_op jit(solution)/shard_map/ppermute | solution.py:360
  51.6 0.9 %merge.1.rest_0_ = bf16[32,2048]{1,0:T(8,128)(2,1)S(1)} custom-call(bf16[32,2176]{1,0:T(8,128)(2,1)S(1)} %attention.7.refs_0_, bf16[32,2176]{1,0:T(8,128)(2,1)S(1)} %collective-permute-done.7.refs_1_, bf16[32,2176]{1,0:T(8,128)(2,1)S(1)} %collective-permute-done.8.refs_2_, bf16[32,2176]{1,0:T(8,128)(2,1)S(1)} %collective-permute-done.9.refs_3_, ...), custom_call_target="tpu_custom_call" | custom-call | flops 1114112 | bytes 1114112 | tf_op jit(solution)/shard_map/merge/pallas_call | solution.py:276
  52.5 0.1 collective-permute-start.15
  52.6 3.8 %collective-permute-start.14 = (bf16[32,2048]{1,0:T(8,128)(2,1)S(1)}, bf16[32,2048]{1,0:T(8,128)(2,1)S(1)}, u32[]{:S(2)}, u32[]{:S(2)}) collective-permute-start(bf16[32,2048]{1,0:T(8,128)(2,1)S(1)} %merge.1.rest_0_), channel_id=1, source_target_pairs={{0,24},{4,28},{8,0},{12,4},{16,8},{20,12},{24,16},{28,20},{1,25},{... | collective-permute-start | bytes 393224 | tf_op jit(solution)/shard_map/ppermute | solution.py:360
  56.4 0.0 collective-permute-start.16
  56.4 4.4 %collective-permute-done.15.rest_2_ = bf16[32,2048]{1,0:T(8,128)(2,1)S(1)} collective-permute-done((bf16[32,2048]{1,0:T(8,128)(2,1)S(1)}, bf16[32,2048]{1,0:T(8,128)(2,1)S(1)}, u32[]{:S(2)}, u32[]{:S(2)}) %collective-permute-start.15) | collective-permute-done | bytes 131104 | tf_op jit(solution)/shard_map/ppermute | solution.py:360
  60.8 1.1 %collective-permute-start.19 = (bf16[32,2048]{1,0:T(8,128)(2,1)S(1)}, bf16[32,2048]{1,0:T(8,128)(2,1)S(1)}, u32[]{:S(2)}, u32[]{:S(2)}) collective-permute-start(bf16[32,2048]{1,0:T(8,128)(2,1)S(1)} %collective-permute-done.15.rest_2_), channel_id=1, source_target_pairs={{0,4},{4,0},{8,12},{12,8},{16,20},{20,16},{24,28},{28,24},{1,5},{5... | collective-permute-start | bytes 393224 | tf_op jit(solution)/shard_map/ppermute | solution.py:360
  61.9 1.0 %collective-permute-start.17 = (bf16[32,2048]{1,0:T(8,128)(2,1)S(1)}, bf16[32,2048]{1,0:T(8,128)(2,1)S(1)}, u32[]{:S(2)}, u32[]{:S(2)}) collective-permute-start(bf16[32,2048]{1,0:T(8,128)(2,1)S(1)} %merge.1.rest_0_), channel_id=1, source_target_pairs={{0,4},{4,0},{8,12},{12,8},{16,20},{20,16},{24,28},{28,24},{1,5},{5... | collective-permute-start | bytes 393224 | tf_op jit(solution)/shard_map/ppermute | solution.py:360
  62.8 0.0 collective-permute-done.14.rest_1_
  62.8 1.1 %collective-permute-start.18 = (bf16[32,2048]{1,0:T(8,128)(2,1)S(1)}, bf16[32,2048]{1,0:T(8,128)(2,1)S(1)}, u32[]{:S(2)}, u32[]{:S(2)}) collective-permute-start(bf16[32,2048]{1,0:T(8,128)(2,1)S(1)} %collective-permute-done.14.rest_1_), channel_id=1, source_target_pairs={{0,4},{4,0},{8,12},{12,8},{16,20},{20,16},{24,28},{28,24},{1,5},{5... | collective-permute-start | bytes 393224 | tf_op jit(solution)/shard_map/ppermute | solution.py:360
  63.9 2.4 %collective-permute-done.16.rest_3_ = bf16[32,2048]{1,0:T(8,128)(2,1)S(1)} collective-permute-done((bf16[32,2048]{1,0:T(8,128)(2,1)S(1)}, bf16[32,2048]{1,0:T(8,128)(2,1)S(1)}, u32[]{:S(2)}, u32[]{:S(2)}) %collective-permute-start.16) | collective-permute-done | bytes 131104 | tf_op jit(solution)/shard_map/ppermute | solution.py:360
  66.3 0.0 collective-permute-done.19.rest_6_
  66.4 0.8 collective-permute-start.20
  67.1 0.1 collective-permute-done.17.rest_4_
  67.2 1.9 %collective-permute-done.18.rest_5_ = bf16[32,2048]{1,0:T(8,128)(2,1)S(1)} collective-permute-done((bf16[32,2048]{1,0:T(8,128)(2,1)S(1)}, bf16[32,2048]{1,0:T(8,128)(2,1)S(1)}, u32[]{:S(2)}, u32[]{:S(2)}) %collective-permute-start.18) | collective-permute-done | bytes 131104 | tf_op jit(solution)/shard_map/ppermute | solution.py:360
  69.1 2.3 %collective-permute-done.20.rest_7_ = bf16[32,2048]{1,0:T(8,128)(2,1)S(1)} collective-permute-done((bf16[32,2048]{1,0:T(8,128)(2,1)S(1)}, bf16[32,2048]{1,0:T(8,128)(2,1)S(1)}, u32[]{:S(2)}, u32[]{:S(2)}) %collective-permute-start.20) | collective-permute-done | bytes 131104 | tf_op jit(solution)/shard_map/ppermute | solution.py:360
  71.4 1.4 %projection.1 = (f32[2,64,1024]{2,1,0:T(8,128)S(1)}, bf16[2,64,1024]{2,1,0:T(8,128)(2,1)S(1)}) custom-call(bf16[2048,1024]{1,0:T(8,128)(2,1)S(1)} %copy-done, bf16[32,2048]{1,0:T(8,128)(2,1)S(1)} %merge.1.rest_0_, bf16[32,2048]{1,0:T(8,128)(2,1)S(1)} %collective-permute-done.14.rest_1_, bf16[32,2048]{1,0:T(8,128)(2,1)S(1)} %collective-permute-done.15.rest_2_, ...), custom_call_target="tpu_custom_call" | custom-call | flops 1073741824 | bytes 4194304 | tf_op jit(solution)/shard_map/projection/pallas_call | solution.py:318
  72.8 0.1 collective-permute-start.21
  72.9 1.5 %collective-permute-done.21 = bf16[2,64,1024]{2,1,0:T(8,128)(2,1)S(1)} collective-permute-done((bf16[2,64,1024]{2,1,0:T(8,128)(2,1)S(1)}, bf16[2,64,1024]{2,1,0:T(8,128)(2,1)S(1)}, u32[]{:S(2)}, u32[]{:S(2)}) %collective-permute-start.21) | collective-permute-done | bytes 262176 | tf_op jit(solution)/shard_map/ppermute | solution.py:434
  74.4 0.3 collective-permute-start.22
  74.7 5.3 %collective-permute-done.22 = bf16[64,1024]{1,0:T(8,128)(2,1)S(1)} collective-permute-done((bf16[64,1024]{1,0:T(8,128)(2,1)S(1)}, bf16[64,1024]{1,0:T(8,128)(2,1)S(1)}, u32[]{:S(2)}, u32[]{:S(2)}) %collective-permute-start.22) | collective-permute-done | bytes 131104 | tf_op jit(solution)/shard_map/ppermute | solution.py:438
  80.0 0.7 bitcast_add_fusion
  (11 shorter events, 0.0 us)
Async XLA Ops:
  0.0 14.5 %copy-start.3 = (bf16[32,256]{1,0:T(8,128)(2,1)S(1)}, bf16[32,256]{1,0:T(8,128)(2,1)}, u32[]{:S(2)}) copy-start(bf16[32,256]{1,0:T(8,128)(2,1)} %nk_ref.7) | copy-start | bytes 49156
  0.0 14.5 %copy-start.4 = (bf16[32,256]{1,0:T(8,128)(2,1)S(1)}, bf16[32,256]{1,0:T(8,128)(2,1)}, u32[]{:S(2)}) copy-start(bf16[32,256]{1,0:T(8,128)(2,1)} %nv_ref.7) | copy-start | bytes 49156
  0.0 14.5 %copy-start.2 = (bf16[4096,256]{1,0:T(8,128)(2,1)S(1)}, bf16[4096,256]{1,0:T(8,128)(2,1)}, u32[]{:S(2)}) copy-start(bf16[4096,256]{1,0:T(8,128)(2,1)} %k_ref.7) | copy-start | bytes 6291460
  0.0 14.5 %copy-start.1 = (bf16[4096,256]{1,0:T(8,128)(2,1)S(1)}, bf16[4096,256]{1,0:T(8,128)(2,1)}, u32[]{:S(2)}) copy-start(bf16[4096,256]{1,0:T(8,128)(2,1)} %v_ref.1) | copy-start | bytes 6291460
  0.0 14.5 %copy-start.7 = (s32[1,2,24]{2,1,0:T(2,128)S(1)}, s32[1,2,24]{2,1,0:T(2,128)}, u32[]{:S(2)}) copy-start(s32[1,2,24]{2,1,0:T(2,128)} %param.14) | copy-start | bytes 580
  0.0 14.5 %copy-start.9 = (s32[1,2]{1,0:T(1,128)S(1)}, s32[1,2]{1,0:T(1,128)}, u32[]{:S(2)}) copy-start(s32[1,2]{1,0:T(1,128)} %param.15) | copy-start | bytes 28
  0.0 14.5 %copy-start.8 = (s32[8]{0:T(128)S(1)}, s32[8]{0:T(128)}, u32[]{:S(2)}) copy-start(s32[8]{0:T(128)} %slot_ref.7) | copy-start | bytes 100
  0.0 9.3 %collective-permute-start = (bf16[32,2048]{1,0:T(8,128)(2,1)}, bf16[32,2048]{1,0:T(8,128)(2,1)S(1)}, u32[]{:S(2)}, u32[]{:S(2)}) collective-permute-start(bf16[32,2048]{1,0:T(8,128)(2,1)} %rest_0_), channel_id=1, source_target_pairs={{0,24},{4,28},{8,0},{12,4},{16,8},{20,12},{24,16},{28,20},{1,25},{... | collective-permute-start | bytes 393224 | tf_op jit(solution)/shard_map/ppermute | solution.py:360
  5.2 7.0 %collective-permute-start.1 = (bf16[32,2048]{1,0:T(8,128)(2,1)}, bf16[32,2048]{1,0:T(8,128)(2,1)S(1)}, u32[]{:S(2)}, u32[]{:S(2)}) collective-permute-start(bf16[32,2048]{1,0:T(8,128)(2,1)} %rest_0_), channel_id=1, source_target_pairs={{0,8},{4,12},{8,16},{12,20},{16,24},{20,28},{24,0},{28,4},{1,9},{5... | collective-permute-start | bytes 393224 | tf_op jit(solution)/shard_map/ppermute | solution.py:360
  5.2 24.8 %collective-permute-start.4 = (bf16[32,2048]{1,0:T(8,128)(2,1)}, bf16[32,2048]{1,0:T(8,128)(2,1)S(1)}, u32[]{:S(2)}, u32[]{:S(2)}) collective-permute-start(bf16[32,2048]{1,0:T(8,128)(2,1)} %rest_0_), channel_id=1, source_target_pairs={{0,4},{4,0},{8,12},{12,8},{16,20},{20,16},{24,28},{28,24},{1,5},{5... | collective-permute-start | bytes 393224 | tf_op jit(solution)/shard_map/ppermute | solution.py:360
  12.1 10.4 %collective-permute-start.5 = (bf16[32,2048]{1,0:T(8,128)(2,1)S(1)}, bf16[32,2048]{1,0:T(8,128)(2,1)S(1)}, u32[]{:S(2)}, u32[]{:S(2)}) collective-permute-start(bf16[32,2048]{1,0:T(8,128)(2,1)S(1)} %collective-permute-done.rest_0_), channel_id=1, source_target_pairs={{0,4},{4,0},{8,12},{12,8},{16,20},{20,16},{24,28},{28,24},{1,5},{5... | collective-permute-start | bytes 393224 | tf_op jit(solution)/shard_map/ppermute | solution.py:360
  13.6 8.9 %collective-permute-start.6 = (bf16[32,2048]{1,0:T(8,128)(2,1)S(1)}, bf16[32,2048]{1,0:T(8,128)(2,1)S(1)}, u32[]{:S(2)}, u32[]{:S(2)}) collective-permute-start(bf16[32,2048]{1,0:T(8,128)(2,1)S(1)} %collective-permute-done.1.rest_1_), channel_id=1, source_target_pairs={{0,4},{4,0},{8,12},{12,8},{16,20},{20,16},{24,28},{28,24},{1,5},{5... | collective-permute-start | bytes 393224 | tf_op jit(solution)/shard_map/ppermute | solution.py:360
  14.2 8.4 %collective-permute-start.2 = (bf16[32,2048]{1,0:T(8,128)(2,1)}, bf16[32,2048]{1,0:T(8,128)(2,1)S(1)}, u32[]{:S(2)}, u32[]{:S(2)}) collective-permute-start(bf16[32,2048]{1,0:T(8,128)(2,1)} %rest_0_), channel_id=1, source_target_pairs={{0,16},{4,20},{8,24},{12,28},{16,0},{20,4},{24,8},{28,12},{1,17},{... | collective-permute-start | bytes 393224 | tf_op jit(solution)/shard_map/ppermute | solution.py:360
  19.1 15.1 %collective-permute-start.8 = (bf16[32,2176]{1,0:T(8,128)(2,1)S(1)}, bf16[32,2176]{1,0:T(8,128)(2,1)S(1)}, u32[]{:S(2)}, u32[]{:S(2)}) collective-permute-start(bf16[32,2176]{1,0:T(8,128)(2,1)S(1)} %get-tuple-element.39), channel_id=1, source_target_pairs={{0,24},{4,28},{8,0},{12,4},{16,8},{20,12},{24,16},{28,20},{1,25},{... | collective-permute-start | bytes 417800 | tf_op jit(solution)/shard_map/ppermute | solution.py:360
  22.5 11.8 %collective-permute-start.7 = (bf16[32,2176]{1,0:T(8,128)(2,1)S(1)}, bf16[32,2176]{1,0:T(8,128)(2,1)S(1)}, u32[]{:S(2)}, u32[]{:S(2)}) collective-permute-start(bf16[32,2176]{1,0:T(8,128)(2,1)S(1)} %get-tuple-element.46), channel_id=1, source_target_pairs={{0,8},{4,12},{8,16},{12,20},{16,24},{20,28},{24,0},{28,4},{1,9},{5... | collective-permute-start | bytes 417800 | tf_op jit(solution)/shard_map/ppermute | solution.py:360
  22.5 11.7 %collective-permute-start.3 = (bf16[32,2048]{1,0:T(8,128)(2,1)S(1)}, bf16[32,2048]{1,0:T(8,128)(2,1)S(1)}, u32[]{:S(2)}, u32[]{:S(2)}) collective-permute-start(bf16[32,2048]{1,0:T(8,128)(2,1)S(1)} %collective-permute-done.2.rest_0_), channel_id=1, source_target_pairs={{0,4},{4,0},{8,12},{12,8},{16,20},{20,16},{24,28},{28,24},{1,5},{5... | collective-permute-start | bytes 393224 | tf_op jit(solution)/shard_map/ppermute | solution.py:360
  29.5 17.0 %collective-permute-start.11 = (bf16[32,2176]{1,0:T(8,128)(2,1)S(1)}, bf16[32,2176]{1,0:T(8,128)(2,1)S(1)}, u32[]{:S(2)}, u32[]{:S(2)}) collective-permute-start(bf16[32,2176]{1,0:T(8,128)(2,1)S(1)} %get-tuple-element.55), channel_id=1, source_target_pairs={{0,12},{4,8},{8,20},{12,16},{16,28},{20,24},{24,4},{28,0},{1,13},{... | collective-permute-start | bytes 417800 | tf_op jit(solution)/shard_map/ppermute | solution.py:360
  30.0 16.6 %collective-permute-start.12 = (bf16[32,2176]{1,0:T(8,128)(2,1)S(1)}, bf16[32,2176]{1,0:T(8,128)(2,1)S(1)}, u32[]{:S(2)}, u32[]{:S(2)}) collective-permute-start(bf16[32,2176]{1,0:T(8,128)(2,1)S(1)} %get-tuple-element.43), channel_id=1, source_target_pairs={{0,28},{4,24},{8,4},{12,0},{16,12},{20,8},{24,20},{28,16},{1,29},{... | collective-permute-start | bytes 417800 | tf_op jit(solution)/shard_map/ppermute | solution.py:360
  34.3 8.9 %copy-start.5 = (f32[8,128]{1,0:T(8,128)S(1)}, f32[8,128]{1,0:T(8,128)}, u32[]{:S(2)}) copy-start(f32[8,128]{1,0:T(8,128)} %settle.1.rest_1_) | copy-start | bytes 12292
  34.3 8.9 %copy-start.6 = (bf16[32,2048]{1,0:T(8,128)(2,1)S(1)}, bf16[32,2048]{1,0:T(8,128)(2,1)}, u32[]{:S(2)}) copy-start(bf16[32,2048]{1,0:T(8,128)(2,1)} %rest_0_) | copy-start | bytes 393220
  34.3 14.6 %collective-permute-start.9 = (bf16[32,2176]{1,0:T(8,128)(2,1)S(1)}, bf16[32,2176]{1,0:T(8,128)(2,1)S(1)}, u32[]{:S(2)}, u32[]{:S(2)}) collective-permute-start(bf16[32,2176]{1,0:T(8,128)(2,1)S(1)} %get-tuple-element.54), channel_id=1, source_target_pairs={{0,16},{4,20},{8,24},{12,28},{16,0},{20,4},{24,8},{28,12},{1,17},{... | collective-permute-start | bytes 417800 | tf_op jit(solution)/shard_map/ppermute | solution.py:360
  39.0 9.9 %collective-permute-start.10 = (bf16[32,2176]{1,0:T(8,128)(2,1)S(1)}, bf16[32,2176]{1,0:T(8,128)(2,1)S(1)}, u32[]{:S(2)}, u32[]{:S(2)}) collective-permute-start(bf16[32,2176]{1,0:T(8,128)(2,1)S(1)} %get-tuple-element.49), channel_id=1, source_target_pairs={{0,4},{4,0},{8,12},{12,8},{16,20},{20,16},{24,28},{28,24},{1,5},{5... | collective-permute-start | bytes 417800 | tf_op jit(solution)/shard_map/ppermute | solution.py:360
  40.2 11.4 %collective-permute-start.13 = (bf16[32,2176]{1,0:T(8,128)(2,1)S(1)}, bf16[32,2176]{1,0:T(8,128)(2,1)S(1)}, u32[]{:S(2)}, u32[]{:S(2)}) collective-permute-start(bf16[32,2176]{1,0:T(8,128)(2,1)S(1)} %get-tuple-element.56), channel_id=1, source_target_pairs={{0,20},{4,16},{8,28},{12,24},{16,4},{20,0},{24,12},{28,8},{1,21},{... | collective-permute-start | bytes 417800 | tf_op jit(solution)/shard_map/ppermute | solution.py:360
  43.2 28.2 %copy-start = (bf16[2048,1024]{1,0:T(8,128)(2,1)S(1)}, bf16[2048,1024]{1,0:T(8,128)(2,1)}, u32[]{:S(2)}) copy-start(bf16[2048,1024]{1,0:T(8,128)(2,1)} %w_ref.1) | copy-start | bytes 12582916
  52.5 8.3 %collective-permute-start.15 = (bf16[32,2048]{1,0:T(8,128)(2,1)S(1)}, bf16[32,2048]{1,0:T(8,128)(2,1)S(1)}, u32[]{:S(2)}, u32[]{:S(2)}) collective-permute-start(bf16[32,2048]{1,0:T(8,128)(2,1)S(1)} %merge.1.rest_0_), channel_id=1, source_target_pairs={{0,8},{4,12},{8,16},{12,20},{16,24},{20,28},{24,0},{28,4},{1,9},{5... | collective-permute-start | bytes 393224 | tf_op jit(solution)/shard_map/ppermute | solution.py:360
  52.6 10.3 %collective-permute-start.14 = (bf16[32,2048]{1,0:T(8,128)(2,1)S(1)}, bf16[32,2048]{1,0:T(8,128)(2,1)S(1)}, u32[]{:S(2)}, u32[]{:S(2)}) collective-permute-start(bf16[32,2048]{1,0:T(8,128)(2,1)S(1)} %merge.1.rest_0_), channel_id=1, source_target_pairs={{0,24},{4,28},{8,0},{12,4},{16,8},{20,12},{24,16},{28,20},{1,25},{... | collective-permute-start | bytes 393224 | tf_op jit(solution)/shard_map/ppermute | solution.py:360
  56.4 9.9 %collective-permute-start.16 = (bf16[32,2048]{1,0:T(8,128)(2,1)S(1)}, bf16[32,2048]{1,0:T(8,128)(2,1)S(1)}, u32[]{:S(2)}, u32[]{:S(2)}) collective-permute-start(bf16[32,2048]{1,0:T(8,128)(2,1)S(1)} %merge.1.rest_0_), channel_id=1, source_target_pairs={{0,16},{4,20},{8,24},{12,28},{16,0},{20,4},{24,8},{28,12},{1,17},{... | collective-permute-start | bytes 393224 | tf_op jit(solution)/shard_map/ppermute | solution.py:360
  60.8 5.5 %collective-permute-start.19 = (bf16[32,2048]{1,0:T(8,128)(2,1)S(1)}, bf16[32,2048]{1,0:T(8,128)(2,1)S(1)}, u32[]{:S(2)}, u32[]{:S(2)}) collective-permute-start(bf16[32,2048]{1,0:T(8,128)(2,1)S(1)} %collective-permute-done.15.rest_2_), channel_id=1, source_target_pairs={{0,4},{4,0},{8,12},{12,8},{16,20},{20,16},{24,28},{28,24},{1,5},{5... | collective-permute-start | bytes 393224 | tf_op jit(solution)/shard_map/ppermute | solution.py:360
  61.9 5.3 %collective-permute-start.17 = (bf16[32,2048]{1,0:T(8,128)(2,1)S(1)}, bf16[32,2048]{1,0:T(8,128)(2,1)S(1)}, u32[]{:S(2)}, u32[]{:S(2)}) collective-permute-start(bf16[32,2048]{1,0:T(8,128)(2,1)S(1)} %merge.1.rest_0_), channel_id=1, source_target_pairs={{0,4},{4,0},{8,12},{12,8},{16,20},{20,16},{24,28},{28,24},{1,5},{5... | collective-permute-start | bytes 393224 | tf_op jit(solution)/shard_map/ppermute | solution.py:360
  62.8 6.2 %collective-permute-start.18 = (bf16[32,2048]{1,0:T(8,128)(2,1)S(1)}, bf16[32,2048]{1,0:T(8,128)(2,1)S(1)}, u32[]{:S(2)}, u32[]{:S(2)}) collective-permute-start(bf16[32,2048]{1,0:T(8,128)(2,1)S(1)} %collective-permute-done.14.rest_1_), channel_id=1, source_target_pairs={{0,4},{4,0},{8,12},{12,8},{16,20},{20,16},{24,28},{28,24},{1,5},{5... | collective-permute-start | bytes 393224 | tf_op jit(solution)/shard_map/ppermute | solution.py:360
  66.4 5.1 %collective-permute-start.20 = (bf16[32,2048]{1,0:T(8,128)(2,1)S(1)}, bf16[32,2048]{1,0:T(8,128)(2,1)S(1)}, u32[]{:S(2)}, u32[]{:S(2)}) collective-permute-start(bf16[32,2048]{1,0:T(8,128)(2,1)S(1)} %collective-permute-done.16.rest_3_), channel_id=1, source_target_pairs={{0,4},{4,0},{8,12},{12,8},{16,20},{20,16},{24,28},{28,24},{1,5},{5... | collective-permute-start | bytes 393224 | tf_op jit(solution)/shard_map/ppermute | solution.py:360
  72.8 1.6 %collective-permute-start.21 = (bf16[2,64,1024]{2,1,0:T(8,128)(2,1)S(1)}, bf16[2,64,1024]{2,1,0:T(8,128)(2,1)S(1)}, u32[]{:S(2)}, u32[]{:S(2)}) collective-permute-start(bf16[2,64,1024]{2,1,0:T(8,128)(2,1)S(1)} %get-tuple-element.60), channel_id=1, source_target_pairs={{0,1},{1,0},{2,3},{3,2},{4,5},{5,4},{6,7},{7,6},{8,9},{9,8},{10,11... | collective-permute-start | bytes 786440 | tf_op jit(solution)/shard_map/ppermute | solution.py:434
  74.4 5.6 %collective-permute-start.22 = (bf16[64,1024]{1,0:T(8,128)(2,1)S(1)}, bf16[64,1024]{1,0:T(8,128)(2,1)S(1)}, u32[]{:S(2)}, u32[]{:S(2)}) collective-permute-start(bf16[64,1024]{1,0:T(8,128)(2,1)S(1)} %fusion), channel_id=1, source_target_pairs={{0,2},{1,3},{2,0},{3,1},{4,6},{5,7},{6,4},{7,5},{8,10},{9,11},{10,... | collective-permute-start | bytes 393224 | tf_op jit(solution)/shard_map/ppermute | solution.py:438

commit v8 on v7

--- a/solution.py
+++ b/solution.py
@@ -12,6 +12,7 @@
 TILE = 128
 LANES = 128
 CHUNK = 4
+PIECE = 256
 LOW = -1e30
 LIMIT = 2.0**100
 ONES = 16
@@ -111,18 +112,29 @@
 
     def run(kv_heads, chunk):
         loaded = {g: (keys_of(g, chunk), values_of(g, chunk)) for g in kv_heads}
-        chains = [(g, b) for b in range(blocks) for g in kv_heads]
-
-        def score(g, b):
-            return jnp.dot(loaded[g][0], turned_ref[g, b], preferred_element_type=jnp.float32)
-
-        ahead = score(*chains[0])
-        for at, (g, b) in enumerate(chains):
+        pieces = [
+            (g, b, slice(at, at + PIECE))
+            for at in range(0, span, PIECE)
+            for b in range(blocks)
+            for g in kv_heads
+        ]
+
+        def score(g, b, at):
+            return jnp.dot(loaded[g][0][at], turned_ref[g, b], preferred_element_type=jnp.float32)
+
+        def add(g, b, at, p):
+            acc_ref[g, b] += jnp.dot(loaded[g][1][:, at], p, preferred_element_type=jnp.float32)
+
+        ahead, behind = score(*pieces[0]), None
+        for i, piece in enumerate(pieces):
             s = ahead
-            if at + 1 < len(chains):
-                ahead = score(*chains[at + 1])
-            p = jnp.exp2(s * scale - max_ref[g, b, :1]).astype(jnp.bfloat16)
-            acc_ref[g, b] += jnp.dot(loaded[g][1], p, preferred_element_type=jnp.float32)
+            if i + 1 < len(pieces):
+                ahead = score(*pieces[i + 1])
+            p = jnp.exp2(s * scale - max_ref[piece[0], piece[1], :1]).astype(jnp.bfloat16)
+            if behind is not None:
+                add(*behind)
+            behind = (*piece, p)
+        add(*behind)
 
     ends = [(count_of(g) + CHUNK - 1) // CHUNK for g in range(kv_local)]
     shared = functools.reduce(jnp.minimum, ends)

time: 80.5 us -> 84.8 us (1.053); the launches traced: 80.8 us -> 86.3 us
  Pallas kernels: 21.3 us -> 32 us
  waiting for transfers between devices: 27.9 us -> 19.5 us
  starting transfers between devices: 30.6 us -> 33.7 us
    pallas_call x4, Pallas kernels: 18.4 us -> 29.1 us  [attention_call(): pl.pallas_call(functools.partial(attention_kernel, members, ctx_count, gr...]
    ppermute x21, waiting for transfers between devices: 21.1 us -> 14.1 us  [move(): return lax.ppermute(x, 'ctx', pairs)]
    ppermute x21, starting transfers between devices: 30.2 us -> 31.9 us  [move(): return lax.ppermute(x, 'ctx', pairs)]
    ppermute x1, starting transfers between devices: 0.31 us -> 1.66 us  [body(): piece = lax.ppermute(piece, 'tp', [(i, i ^ 2 * j) for i in range(peers)])]
    ppermute x1, waiting for transfers between devices: 5.29 us -> 3.94 us  [body(): piece = lax.ppermute(piece, 'tp', [(i, i ^ 2 * j) for i in range(peers)])]
  transfers between devices with their start and end apart: 23 -> 23, of which waited for: 11 -> 9; matrix products, arithmetic and copies ran while one was open for 0% -> 0% of each run, Pallas kernels for 24% -> 34%
where the time goes in v8:
time: 84.8 us; the launch traced here: 86.3 us
  starting transfers between devices  33.7 us (40%)
  Pallas kernels  32 us (38%)
  waiting for transfers between devices  19.5 us (23%)
    ppermute x21, starting transfers between devices, move(): return lax.ppermute(x, 'ctx', pairs)  31.9 us
    pallas_call x4, Pallas kernels, attention_call(): pl.pallas_call(functools.partial(attention_kernel, members, ctx_count, gr...  29.1 us
    ppermute x21, waiting for transfers between devices, move(): return lax.ppermute(x, 'ctx', pairs)  14.1 us
    ppermute x1, waiting for transfers between devices, body(): piece = lax.ppermute(piece, 'tp', [(i, i ^ 2 * j) for i in range(peers)])  3.94 us
  transfers between devices with their start and end apart: 23, of which 9 were waited for; matrix products, arithmetic and copies ran while one was open for 0% of the time, Pallas kernels for 34%

profile of v8, /device:TPU:0, one launch (start us, length us, event | category | flops | bytes accessed | tf_op | source)
XLA Modules:
  0.0 86.3 jit_solution(1311566706324632766)
XLA Ops:
  0.0 0.0 copy-start.9
  0.0 0.0 copy-start.8
  0.0 5.1 %collective-permute-start = (bf16[32,2048]{1,0:T(8,128)(2,1)}, bf16[32,2048]{1,0:T(8,128)(2,1)S(1)}, u32[]{:S(2)}, u32[]{:S(2)}) collective-permute-start(bf16[32,2048]{1,0:T(8,128)(2,1)} %rest_0_), channel_id=1, source_target_pairs={{0,24},{4,28},{8,0},{12,4},{16,8},{20,12},{24,16},{28,20},{1,25},{... | collective-permute-start | bytes 393224 | tf_op jit(solution)/shard_map/ppermute | solution.py:372
  5.2 0.0 collective-permute-start.1
  5.2 1.5 %collective-permute-start.4 = (bf16[32,2048]{1,0:T(8,128)(2,1)}, bf16[32,2048]{1,0:T(8,128)(2,1)S(1)}, u32[]{:S(2)}, u32[]{:S(2)}) collective-permute-start(bf16[32,2048]{1,0:T(8,128)(2,1)} %rest_0_), channel_id=1, source_target_pairs={{0,4},{4,0},{8,12},{12,8},{16,20},{20,16},{24,28},{28,24},{1,5},{5... | collective-permute-start | bytes 393224 | tf_op jit(solution)/shard_map/ppermute | solution.py:372
  6.6 0.6 settle.1.rest_1_
  7.2 2.1 %collective-permute-done.rest_0_ = bf16[32,2048]{1,0:T(8,128)(2,1)S(1)} collective-permute-done((bf16[32,2048]{1,0:T(8,128)(2,1)}, bf16[32,2048]{1,0:T(8,128)(2,1)S(1)}, u32[]{:S(2)}, u32[]{:S(2)}) %collective-permute-start) | collective-permute-done | bytes 131104 | tf_op jit(solution)/shard_map/ppermute | solution.py:372
  9.4 2.8 %collective-permute-done.1.rest_1_ = bf16[32,2048]{1,0:T(8,128)(2,1)S(1)} collective-permute-done((bf16[32,2048]{1,0:T(8,128)(2,1)}, bf16[32,2048]{1,0:T(8,128)(2,1)S(1)}, u32[]{:S(2)}, u32[]{:S(2)}) %collective-permute-start.1) | collective-permute-done | bytes 131104 | tf_op jit(solution)/shard_map/ppermute | solution.py:372
  12.1 1.5 %collective-permute-start.5 = (bf16[32,2048]{1,0:T(8,128)(2,1)S(1)}, bf16[32,2048]{1,0:T(8,128)(2,1)S(1)}, u32[]{:S(2)}, u32[]{:S(2)}) collective-permute-start(bf16[32,2048]{1,0:T(8,128)(2,1)S(1)} %collective-permute-done.rest_0_), channel_id=1, source_target_pairs={{0,4},{4,0},{8,12},{12,8},{16,20},{20,16},{24,28},{28,24},{1,5},{5... | collective-permute-start | bytes 393224 | tf_op jit(solution)/shard_map/ppermute | solution.py:372
  13.6 0.5 collective-permute-start.6
  14.2 0.4 collective-permute-start.2
  14.5 0.0 copy-done.3
  14.5 0.0 copy-done.4
  14.5 0.0 copy-done.2
  14.5 0.0 copy-done.1
  14.5 0.0 copy-done.7
  14.6 0.0 copy-done.9
  14.6 0.0 copy-done.8
  14.6 7.3 %attention.4 = (bf16[32,2176]{1,0:T(8,128)(2,1)S(1)}, bf16[32,2176]{1,0:T(8,128)(2,1)S(1)}, bf16[2,144,3200]{2,1,0:T(8,128)(2,1)S(1)}) custom-call(s32[8]{0:T(128)S(1)} %copy-done.8, s32[2,24]{1,0:T(2,128)S(1)} %bitcast.6, s32[2]{0:T(128)S(1)} %bitcast.10, bf16[32,256]{1,0:T(8,128)(2,1)S(1)} %copy-done.3, bf16[32,256]{1,0:T(8,128)(2,1)S(1)} %copy-done.4, ...), custom_call_target="tpu_custom_call" | custom-call | flops 3221225472 | bytes 8388608 | tf_op jit(solution)/shard_map/attention/pallas_call | solution.py:228
  21.8 1.5 %collective-permute-start.8 = (bf16[32,2176]{1,0:T(8,128)(2,1)S(1)}, bf16[32,2176]{1,0:T(8,128)(2,1)S(1)}, u32[]{:S(2)}, u32[]{:S(2)}) collective-permute-start(bf16[32,2176]{1,0:T(8,128)(2,1)S(1)} %get-tuple-element.39), channel_id=1, source_target_pairs={{0,24},{4,28},{8,0},{12,4},{16,8},{20,12},{24,16},{28,20},{1,25},{... | collective-permute-start | bytes 417800 | tf_op jit(solution)/shard_map/ppermute | solution.py:372
  23.4 0.0 collective-permute-done.2.rest_0_
  23.4 0.6 collective-permute-start.7
  23.9 0.0 collective-permute-done.5.rest_1_
  23.9 0.0 collective-permute-done.6.rest_2_
  23.9 2.3 %collective-permute-start.3 = (bf16[32,2048]{1,0:T(8,128)(2,1)S(1)}, bf16[32,2048]{1,0:T(8,128)(2,1)S(1)}, u32[]{:S(2)}, u32[]{:S(2)}) collective-permute-start(bf16[32,2048]{1,0:T(8,128)(2,1)S(1)} %collective-permute-done.2.rest_0_), channel_id=1, source_target_pairs={{0,4},{4,0},{8,12},{12,8},{16,20},{20,16},{24,28},{28,24},{1,5},{5... | collective-permute-start | bytes 393224 | tf_op jit(solution)/shard_map/ppermute | solution.py:372
  26.2 9.6 %attention.5 = (bf16[32,2176]{1,0:T(8,128)(2,1)S(1)}, bf16[32,2176]{1,0:T(8,128)(2,1)S(1)}, bf16[32,2176]{1,0:T(8,128)(2,1)S(1)}) custom-call(s32[8]{0:T(128)S(1)} %copy-done.8, s32[2,24]{1,0:T(2,128)S(1)} %bitcast.7, s32[2]{0:T(128)S(1)} %bitcast.11, bf16[32,256]{1,0:T(8,128)(2,1)S(1)} %copy-done.3, bf16[32,256]{1,0:T(8,128)(2,1)S(1)} %copy-done.4, ...), custom_call_target="tpu_custom_call" | custom-call | flops 4831838208 | bytes 8388608 | tf_op jit(solution)/shard_map/attention/pallas_call | solution.py:228
  35.8 0.1 collective-permute-start.11
  35.8 0.0 collective-permute-done.4.rest_1_
  35.9 4.7 %collective-permute-start.12 = (bf16[32,2176]{1,0:T(8,128)(2,1)S(1)}, bf16[32,2176]{1,0:T(8,128)(2,1)S(1)}, u32[]{:S(2)}, u32[]{:S(2)}) collective-permute-start(bf16[32,2176]{1,0:T(8,128)(2,1)S(1)} %get-tuple-element.43), channel_id=1, source_target_pairs={{0,28},{4,24},{8,4},{12,0},{16,12},{20,8},{24,20},{28,16},{1,29},{... | collective-permute-start | bytes 417800 | tf_op jit(solution)/shard_map/ppermute | solution.py:372
  40.6 0.0 collective-permute-done.3.rest_0_
  40.6 0.0 collective-permute-start.9
  40.6 0.0 collective-permute-done.8.refs_2_
  40.6 0.0 collective-permute-done.7.refs_1_
  40.6 7.4 %attention.6 = (bf16[32,2176]{1,0:T(8,128)(2,1)S(1)}, bf16[32,2176]{1,0:T(8,128)(2,1)S(1)}) custom-call(s32[8]{0:T(128)S(1)} %copy-done.8, s32[2,24]{1,0:T(2,128)S(1)} %bitcast.8, s32[2]{0:T(128)S(1)} %bitcast.12, bf16[32,256]{1,0:T(8,128)(2,1)S(1)} %copy-done.3, bf16[32,256]{1,0:T(8,128)(2,1)S(1)} %copy-done.4, bf16[4096,256]{1,0:T(8,128)(2,1)S(1)} %copy-done.2, ...), custom_call_target="tpu_custom_call" | custom-call | flops 3221225472 | bytes 8388608 | tf_op jit(solution)/shard_map/attention/pallas_call | solution.py:228
  48.0 0.1 collective-permute-start.10
  48.1 2.5 %collective-permute-start.13 = (bf16[32,2176]{1,0:T(8,128)(2,1)S(1)}, bf16[32,2176]{1,0:T(8,128)(2,1)S(1)}, u32[]{:S(2)}, u32[]{:S(2)}) collective-permute-start(bf16[32,2176]{1,0:T(8,128)(2,1)S(1)} %get-tuple-element.56), channel_id=1, source_target_pairs={{0,20},{4,16},{8,28},{12,24},{16,4},{20,0},{24,12},{28,8},{1,21},{... | collective-permute-start | bytes 417800 | tf_op jit(solution)/shard_map/ppermute | solution.py:372
  50.6 0.0 copy-done.5
  50.6 4.9 %attention.7.refs_0_ = bf16[32,2176]{1,0:T(8,128)(2,1)S(1)} custom-call(s32[8]{0:T(128)S(1)} %copy-done.8, s32[2,24]{1,0:T(2,128)S(1)} %bitcast.9, s32[2]{0:T(128)S(1)} %bitcast.13, bf16[32,256]{1,0:T(8,128)(2,1)S(1)} %copy-done.3, bf16[32,256]{1,0:T(8,128)(2,1)S(1)} %copy-done.4, bf16[4096,256]{1,0:T(8,128)(2,1)S(1)} %copy-done.2, ...), custom_call_target="tpu_custom_call" | custom-call | flops 1610612736 | bytes 8388608 | tf_op jit(solution)/shard_map/attention/pallas_call | solution.py:228
  55.5 0.0 collective-permute-done.11.refs_5_
  55.6 0.0 collective-permute-done.12.refs_6_
  55.6 0.0 collective-permute-done.9.refs_3_
  55.6 0.0 collective-permute-done.10.refs_4_
  55.6 2.3 %collective-permute-done.13.refs_7_ = bf16[32,2176]{1,0:T(8,128)(2,1)S(1)} collective-permute-done((bf16[32,2176]{1,0:T(8,128)(2,1)S(1)}, bf16[32,2176]{1,0:T(8,128)(2,1)S(1)}, u32[]{:S(2)}, u32[]{:S(2)}) %collective-permute-start.13) | collective-permute-done | bytes 139296 | tf_op jit(solution)/shard_map/ppermute | solution.py:372
  57.8 0.9 %merge.1.rest_0_ = bf16[32,2048]{1,0:T(8,128)(2,1)S(1)} custom-call(bf16[32,2176]{1,0:T(8,128)(2,1)S(1)} %attention.7.refs_0_, bf16[32,2176]{1,0:T(8,128)(2,1)S(1)} %collective-permute-done.7.refs_1_, bf16[32,2176]{1,0:T(8,128)(2,1)S(1)} %collective-permute-done.8.refs_2_, bf16[32,2176]{1,0:T(8,128)(2,1)S(1)} %collective-permute-done.9.refs_3_, ...), custom_call_target="tpu_custom_call" | custom-call | flops 1114112 | bytes 1114112 | tf_op jit(solution)/shard_map/merge/pallas_call | solution.py:288
  58.8 0.1 collective-permute-start.15
  58.8 3.8 %collective-permute-start.14 = (bf16[32,2048]{1,0:T(8,128)(2,1)S(1)}, bf16[32,2048]{1,0:T(8,128)(2,1)S(1)}, u32[]{:S(2)}, u32[]{:S(2)}) collective-permute-start(bf16[32,2048]{1,0:T(8,128)(2,1)S(1)} %merge.1.rest_0_), channel_id=1, source_target_pairs={{0,24},{4,28},{8,0},{12,4},{16,8},{20,12},{24,16},{28,20},{1,25},{... | collective-permute-start | bytes 393224 | tf_op jit(solution)/shard_map/ppermute | solution.py:372
  62.7 0.0 collective-permute-start.16
  62.7 3.0 %collective-permute-done.15.rest_2_ = bf16[32,2048]{1,0:T(8,128)(2,1)S(1)} collective-permute-done((bf16[32,2048]{1,0:T(8,128)(2,1)S(1)}, bf16[32,2048]{1,0:T(8,128)(2,1)S(1)}, u32[]{:S(2)}, u32[]{:S(2)}) %collective-permute-start.15) | collective-permute-done | bytes 131104 | tf_op jit(solution)/shard_map/ppermute | solution.py:372
  65.7 3.3 %collective-permute-start.19 = (bf16[32,2048]{1,0:T(8,128)(2,1)S(1)}, bf16[32,2048]{1,0:T(8,128)(2,1)S(1)}, u32[]{:S(2)}, u32[]{:S(2)}) collective-permute-start(bf16[32,2048]{1,0:T(8,128)(2,1)S(1)} %collective-permute-done.15.rest_2_), channel_id=1, source_target_pairs={{0,4},{4,0},{8,12},{12,8},{16,20},{20,16},{24,28},{28,24},{1,5},{5... | collective-permute-start | bytes 393224 | tf_op jit(solution)/shard_map/ppermute | solution.py:372
  69.0 0.0 collective-permute-start.17
  69.0 0.0 collective-permute-done.14.rest_1_
  69.0 2.0 %collective-permute-start.18 = (bf16[32,2048]{1,0:T(8,128)(2,1)S(1)}, bf16[32,2048]{1,0:T(8,128)(2,1)S(1)}, u32[]{:S(2)}, u32[]{:S(2)}) collective-permute-start(bf16[32,2048]{1,0:T(8,128)(2,1)S(1)} %collective-permute-done.14.rest_1_), channel_id=1, source_target_pairs={{0,4},{4,0},{8,12},{12,8},{16,20},{20,16},{24,28},{28,24},{1,5},{5... | collective-permute-start | bytes 393224 | tf_op jit(solution)/shard_map/ppermute | solution.py:372
  71.0 0.0 collective-permute-done.16.rest_3_
  71.0 0.9 %collective-permute-done.19.rest_6_ = bf16[32,2048]{1,0:T(8,128)(2,1)S(1)} collective-permute-done((bf16[32,2048]{1,0:T(8,128)(2,1)S(1)}, bf16[32,2048]{1,0:T(8,128)(2,1)S(1)}, u32[]{:S(2)}, u32[]{:S(2)}) %collective-permute-start.19) | collective-permute-done | bytes 131104 | tf_op jit(solution)/shard_map/ppermute | solution.py:372
  71.9 2.0 %collective-permute-start.20 = (bf16[32,2048]{1,0:T(8,128)(2,1)S(1)}, bf16[32,2048]{1,0:T(8,128)(2,1)S(1)}, u32[]{:S(2)}, u32[]{:S(2)}) collective-permute-start(bf16[32,2048]{1,0:T(8,128)(2,1)S(1)} %collective-permute-done.16.rest_3_), channel_id=1, source_target_pairs={{0,4},{4,0},{8,12},{12,8},{16,20},{20,16},{24,28},{28,24},{1,5},{5... | collective-permute-start | bytes 393224 | tf_op jit(solution)/shard_map/ppermute | solution.py:372
  74.0 0.0 collective-permute-done.17.rest_4_
  74.0 1.4 %collective-permute-done.18.rest_5_ = bf16[32,2048]{1,0:T(8,128)(2,1)S(1)} collective-permute-done((bf16[32,2048]{1,0:T(8,128)(2,1)S(1)}, bf16[32,2048]{1,0:T(8,128)(2,1)S(1)}, u32[]{:S(2)}, u32[]{:S(2)}) %collective-permute-start.18) | collective-permute-done | bytes 131104 | tf_op jit(solution)/shard_map/ppermute | solution.py:372
  75.4 1.5 %collective-permute-done.20.rest_7_ = bf16[32,2048]{1,0:T(8,128)(2,1)S(1)} collective-permute-done((bf16[32,2048]{1,0:T(8,128)(2,1)S(1)}, bf16[32,2048]{1,0:T(8,128)(2,1)S(1)}, u32[]{:S(2)}, u32[]{:S(2)}) %collective-permute-start.20) | collective-permute-done | bytes 131104 | tf_op jit(solution)/shard_map/ppermute | solution.py:372
  76.9 1.4 %projection.1 = (f32[2,64,1024]{2,1,0:T(8,128)S(1)}, bf16[2,64,1024]{2,1,0:T(8,128)(2,1)S(1)}) custom-call(bf16[2048,1024]{1,0:T(8,128)(2,1)S(1)} %copy-done, bf16[32,2048]{1,0:T(8,128)(2,1)S(1)} %merge.1.rest_0_, bf16[32,2048]{1,0:T(8,128)(2,1)S(1)} %collective-permute-done.14.rest_1_, bf16[32,2048]{1,0:T(8,128)(2,1)S(1)} %collective-permute-done.15.rest_2_, ...), custom_call_target="tpu_custom_call" | custom-call | flops 1073741824 | bytes 4194304 | tf_op jit(solution)/shard_map/projection/pallas_call | solution.py:330
  78.3 0.1 collective-permute-start.21
  78.4 1.5 %collective-permute-done.21 = bf16[2,64,1024]{2,1,0:T(8,128)(2,1)S(1)} collective-permute-done((bf16[2,64,1024]{2,1,0:T(8,128)(2,1)S(1)}, bf16[2,64,1024]{2,1,0:T(8,128)(2,1)S(1)}, u32[]{:S(2)}, u32[]{:S(2)}) %collective-permute-start.21) | collective-permute-done | bytes 262176 | tf_op jit(solution)/shard_map/ppermute | solution.py:446
  79.9 1.7 %collective-permute-start.22 = (bf16[64,1024]{1,0:T(8,128)(2,1)S(1)}, bf16[64,1024]{1,0:T(8,128)(2,1)S(1)}, u32[]{:S(2)}, u32[]{:S(2)}) collective-permute-start(bf16[64,1024]{1,0:T(8,128)(2,1)S(1)} %fusion), channel_id=1, source_target_pairs={{0,2},{1,3},{2,0},{3,1},{4,6},{5,7},{6,4},{7,5},{8,10},{9,11},{10,... | collective-permute-start | bytes 393224 | tf_op jit(solution)/shard_map/ppermute | solution.py:450
  81.6 3.9 %collective-permute-done.22 = bf16[64,1024]{1,0:T(8,128)(2,1)S(1)} collective-permute-done((bf16[64,1024]{1,0:T(8,128)(2,1)S(1)}, bf16[64,1024]{1,0:T(8,128)(2,1)S(1)}, u32[]{:S(2)}, u32[]{:S(2)}) %collective-permute-start.22) | collective-permute-done | bytes 131104 | tf_op jit(solution)/shard_map/ppermute | solution.py:450
  85.5 0.7 bitcast_add_fusion
  (11 shorter events, 0.0 us)
Async XLA Ops:
  0.0 14.5 %copy-start.3 = (bf16[32,256]{1,0:T(8,128)(2,1)S(1)}, bf16[32,256]{1,0:T(8,128)(2,1)}, u32[]{:S(2)}) copy-start(bf16[32,256]{1,0:T(8,128)(2,1)} %nk_ref.7) | copy-start | bytes 49156
  0.0 14.5 %copy-start.4 = (bf16[32,256]{1,0:T(8,128)(2,1)S(1)}, bf16[32,256]{1,0:T(8,128)(2,1)}, u32[]{:S(2)}) copy-start(bf16[32,256]{1,0:T(8,128)(2,1)} %nv_ref.7) | copy-start | bytes 49156
  0.0 14.5 %copy-start.2 = (bf16[4096,256]{1,0:T(8,128)(2,1)S(1)}, bf16[4096,256]{1,0:T(8,128)(2,1)}, u32[]{:S(2)}) copy-start(bf16[4096,256]{1,0:T(8,128)(2,1)} %k_ref.7) | copy-start | bytes 6291460
  0.0 14.5 %copy-start.1 = (bf16[4096,256]{1,0:T(8,128)(2,1)S(1)}, bf16[4096,256]{1,0:T(8,128)(2,1)}, u32[]{:S(2)}) copy-start(bf16[4096,256]{1,0:T(8,128)(2,1)} %v_ref.1) | copy-start | bytes 6291460
  0.0 14.5 %copy-start.7 = (s32[1,2,24]{2,1,0:T(2,128)S(1)}, s32[1,2,24]{2,1,0:T(2,128)}, u32[]{:S(2)}) copy-start(s32[1,2,24]{2,1,0:T(2,128)} %param.14) | copy-start | bytes 580
  0.0 14.5 %copy-start.9 = (s32[1,2]{1,0:T(1,128)S(1)}, s32[1,2]{1,0:T(1,128)}, u32[]{:S(2)}) copy-start(s32[1,2]{1,0:T(1,128)} %param.15) | copy-start | bytes 28
  0.0 14.5 %copy-start.8 = (s32[8]{0:T(128)S(1)}, s32[8]{0:T(128)}, u32[]{:S(2)}) copy-start(s32[8]{0:T(128)} %slot_ref.7) | copy-start | bytes 100
  0.0 9.3 %collective-permute-start = (bf16[32,2048]{1,0:T(8,128)(2,1)}, bf16[32,2048]{1,0:T(8,128)(2,1)S(1)}, u32[]{:S(2)}, u32[]{:S(2)}) collective-permute-start(bf16[32,2048]{1,0:T(8,128)(2,1)} %rest_0_), channel_id=1, source_target_pairs={{0,24},{4,28},{8,0},{12,4},{16,8},{20,12},{24,16},{28,20},{1,25},{... | collective-permute-start | bytes 393224 | tf_op jit(solution)/shard_map/ppermute | solution.py:372
  5.2 7.0 %collective-permute-start.1 = (bf16[32,2048]{1,0:T(8,128)(2,1)}, bf16[32,2048]{1,0:T(8,128)(2,1)S(1)}, u32[]{:S(2)}, u32[]{:S(2)}) collective-permute-start(bf16[32,2048]{1,0:T(8,128)(2,1)} %rest_0_), channel_id=1, source_target_pairs={{0,8},{4,12},{8,16},{12,20},{16,24},{20,28},{24,0},{28,4},{1,9},{5... | collective-permute-start | bytes 393224 | tf_op jit(solution)/shard_map/ppermute | solution.py:372
  5.2 30.7 %collective-permute-start.4 = (bf16[32,2048]{1,0:T(8,128)(2,1)}, bf16[32,2048]{1,0:T(8,128)(2,1)S(1)}, u32[]{:S(2)}, u32[]{:S(2)}) collective-permute-start(bf16[32,2048]{1,0:T(8,128)(2,1)} %rest_0_), channel_id=1, source_target_pairs={{0,4},{4,0},{8,12},{12,8},{16,20},{20,16},{24,28},{28,24},{1,5},{5... | collective-permute-start | bytes 393224 | tf_op jit(solution)/shard_map/ppermute | solution.py:372
  12.1 11.8 %collective-permute-start.5 = (bf16[32,2048]{1,0:T(8,128)(2,1)S(1)}, bf16[32,2048]{1,0:T(8,128)(2,1)S(1)}, u32[]{:S(2)}, u32[]{:S(2)}) collective-permute-start(bf16[32,2048]{1,0:T(8,128)(2,1)S(1)} %collective-permute-done.rest_0_), channel_id=1, source_target_pairs={{0,4},{4,0},{8,12},{12,8},{16,20},{20,16},{24,28},{28,24},{1,5},{5... | collective-permute-start | bytes 393224 | tf_op jit(solution)/shard_map/ppermute | solution.py:372
  13.6 10.3 %collective-permute-start.6 = (bf16[32,2048]{1,0:T(8,128)(2,1)S(1)}, bf16[32,2048]{1,0:T(8,128)(2,1)S(1)}, u32[]{:S(2)}, u32[]{:S(2)}) collective-permute-start(bf16[32,2048]{1,0:T(8,128)(2,1)S(1)} %collective-permute-done.1.rest_1_), channel_id=1, source_target_pairs={{0,4},{4,0},{8,12},{12,8},{16,20},{20,16},{24,28},{28,24},{1,5},{5... | collective-permute-start | bytes 393224 | tf_op jit(solution)/shard_map/ppermute | solution.py:372
  14.2 9.2 %collective-permute-start.2 = (bf16[32,2048]{1,0:T(8,128)(2,1)}, bf16[32,2048]{1,0:T(8,128)(2,1)S(1)}, u32[]{:S(2)}, u32[]{:S(2)}) collective-permute-start(bf16[32,2048]{1,0:T(8,128)(2,1)} %rest_0_), channel_id=1, source_target_pairs={{0,16},{4,20},{8,24},{12,28},{16,0},{20,4},{24,8},{28,12},{1,17},{... | collective-permute-start | bytes 393224 | tf_op jit(solution)/shard_map/ppermute | solution.py:372
  21.8 18.7 %collective-permute-start.8 = (bf16[32,2176]{1,0:T(8,128)(2,1)S(1)}, bf16[32,2176]{1,0:T(8,128)(2,1)S(1)}, u32[]{:S(2)}, u32[]{:S(2)}) collective-permute-start(bf16[32,2176]{1,0:T(8,128)(2,1)S(1)} %get-tuple-element.39), channel_id=1, source_target_pairs={{0,24},{4,28},{8,0},{12,4},{16,8},{20,12},{24,16},{28,20},{1,25},{... | collective-permute-start | bytes 417800 | tf_op jit(solution)/shard_map/ppermute | solution.py:372
  23.4 17.2 %collective-permute-start.7 = (bf16[32,2176]{1,0:T(8,128)(2,1)S(1)}, bf16[32,2176]{1,0:T(8,128)(2,1)S(1)}, u32[]{:S(2)}, u32[]{:S(2)}) collective-permute-start(bf16[32,2176]{1,0:T(8,128)(2,1)S(1)} %get-tuple-element.46), channel_id=1, source_target_pairs={{0,8},{4,12},{8,16},{12,20},{16,24},{20,28},{24,0},{28,4},{1,9},{5... | collective-permute-start | bytes 417800 | tf_op jit(solution)/shard_map/ppermute | solution.py:372
  23.9 16.6 %collective-permute-start.3 = (bf16[32,2048]{1,0:T(8,128)(2,1)S(1)}, bf16[32,2048]{1,0:T(8,128)(2,1)S(1)}, u32[]{:S(2)}, u32[]{:S(2)}) collective-permute-start(bf16[32,2048]{1,0:T(8,128)(2,1)S(1)} %collective-permute-done.2.rest_0_), channel_id=1, source_target_pairs={{0,4},{4,0},{8,12},{12,8},{16,20},{20,16},{24,28},{28,24},{1,5},{5... | collective-permute-start | bytes 393224 | tf_op jit(solution)/shard_map/ppermute | solution.py:372
  35.8 19.8 %collective-permute-start.11 = (bf16[32,2176]{1,0:T(8,128)(2,1)S(1)}, bf16[32,2176]{1,0:T(8,128)(2,1)S(1)}, u32[]{:S(2)}, u32[]{:S(2)}) collective-permute-start(bf16[32,2176]{1,0:T(8,128)(2,1)S(1)} %get-tuple-element.55), channel_id=1, source_target_pairs={{0,12},{4,8},{8,20},{12,16},{16,28},{20,24},{24,4},{28,0},{1,13},{... | collective-permute-start | bytes 417800 | tf_op jit(solution)/shard_map/ppermute | solution.py:372
  35.9 19.7 %collective-permute-start.12 = (bf16[32,2176]{1,0:T(8,128)(2,1)S(1)}, bf16[32,2176]{1,0:T(8,128)(2,1)S(1)}, u32[]{:S(2)}, u32[]{:S(2)}) collective-permute-start(bf16[32,2176]{1,0:T(8,128)(2,1)S(1)} %get-tuple-element.43), channel_id=1, source_target_pairs={{0,28},{4,24},{8,4},{12,0},{16,12},{20,8},{24,20},{28,16},{1,29},{... | collective-permute-start | bytes 417800 | tf_op jit(solution)/shard_map/ppermute | solution.py:372
  40.6 10.0 %copy-start.5 = (f32[8,128]{1,0:T(8,128)S(1)}, f32[8,128]{1,0:T(8,128)}, u32[]{:S(2)}) copy-start(f32[8,128]{1,0:T(8,128)} %settle.1.rest_1_) | copy-start | bytes 12292
  40.6 10.0 %copy-start.6 = (bf16[32,2048]{1,0:T(8,128)(2,1)S(1)}, bf16[32,2048]{1,0:T(8,128)(2,1)}, u32[]{:S(2)}) copy-start(bf16[32,2048]{1,0:T(8,128)(2,1)} %rest_0_) | copy-start | bytes 393220
  40.6 15.0 %collective-permute-start.9 = (bf16[32,2176]{1,0:T(8,128)(2,1)S(1)}, bf16[32,2176]{1,0:T(8,128)(2,1)S(1)}, u32[]{:S(2)}, u32[]{:S(2)}) collective-permute-start(bf16[32,2176]{1,0:T(8,128)(2,1)S(1)} %get-tuple-element.54), channel_id=1, source_target_pairs={{0,16},{4,20},{8,24},{12,28},{16,0},{20,4},{24,8},{28,12},{1,17},{... | collective-permute-start | bytes 417800 | tf_op jit(solution)/shard_map/ppermute | solution.py:372
  48.0 7.6 %collective-permute-start.10 = (bf16[32,2176]{1,0:T(8,128)(2,1)S(1)}, bf16[32,2176]{1,0:T(8,128)(2,1)S(1)}, u32[]{:S(2)}, u32[]{:S(2)}) collective-permute-start(bf16[32,2176]{1,0:T(8,128)(2,1)S(1)} %get-tuple-element.49), channel_id=1, source_target_pairs={{0,4},{4,0},{8,12},{12,8},{16,20},{20,16},{24,28},{28,24},{1,5},{5... | collective-permute-start | bytes 417800 | tf_op jit(solution)/shard_map/ppermute | solution.py:372
  48.1 9.8 %collective-permute-start.13 = (bf16[32,2176]{1,0:T(8,128)(2,1)S(1)}, bf16[32,2176]{1,0:T(8,128)(2,1)S(1)}, u32[]{:S(2)}, u32[]{:S(2)}) collective-permute-start(bf16[32,2176]{1,0:T(8,128)(2,1)S(1)} %get-tuple-element.56), channel_id=1, source_target_pairs={{0,20},{4,16},{8,28},{12,24},{16,4},{20,0},{24,12},{28,8},{1,21},{... | collective-permute-start | bytes 417800 | tf_op jit(solution)/shard_map/ppermute | solution.py:372
  50.6 26.3 %copy-start = (bf16[2048,1024]{1,0:T(8,128)(2,1)S(1)}, bf16[2048,1024]{1,0:T(8,128)(2,1)}, u32[]{:S(2)}) copy-start(bf16[2048,1024]{1,0:T(8,128)(2,1)} %w_ref.1) | copy-start | bytes 12582916
  58.8 6.9 %collective-permute-start.15 = (bf16[32,2048]{1,0:T(8,128)(2,1)S(1)}, bf16[32,2048]{1,0:T(8,128)(2,1)S(1)}, u32[]{:S(2)}, u32[]{:S(2)}) collective-permute-start(bf16[32,2048]{1,0:T(8,128)(2,1)S(1)} %merge.1.rest_0_), channel_id=1, source_target_pairs={{0,8},{4,12},{8,16},{12,20},{16,24},{20,28},{24,0},{28,4},{1,9},{5... | collective-permute-start | bytes 393224 | tf_op jit(solution)/shard_map/ppermute | solution.py:372
  58.8 10.2 %collective-permute-start.14 = (bf16[32,2048]{1,0:T(8,128)(2,1)S(1)}, bf16[32,2048]{1,0:T(8,128)(2,1)S(1)}, u32[]{:S(2)}, u32[]{:S(2)}) collective-permute-start(bf16[32,2048]{1,0:T(8,128)(2,1)S(1)} %merge.1.rest_0_), channel_id=1, source_target_pairs={{0,24},{4,28},{8,0},{12,4},{16,8},{20,12},{24,16},{28,20},{1,25},{... | collective-permute-start | bytes 393224 | tf_op jit(solution)/shard_map/ppermute | solution.py:372
  62.7 8.4 %collective-permute-start.16 = (bf16[32,2048]{1,0:T(8,128)(2,1)S(1)}, bf16[32,2048]{1,0:T(8,128)(2,1)S(1)}, u32[]{:S(2)}, u32[]{:S(2)}) collective-permute-start(bf16[32,2048]{1,0:T(8,128)(2,1)S(1)} %merge.1.rest_0_), channel_id=1, source_target_pairs={{0,16},{4,20},{8,24},{12,28},{16,0},{20,4},{24,8},{28,12},{1,17},{... | collective-permute-start | bytes 393224 | tf_op jit(solution)/shard_map/ppermute | solution.py:372
  65.7 6.2 %collective-permute-start.19 = (bf16[32,2048]{1,0:T(8,128)(2,1)S(1)}, bf16[32,2048]{1,0:T(8,128)(2,1)S(1)}, u32[]{:S(2)}, u32[]{:S(2)}) collective-permute-start(bf16[32,2048]{1,0:T(8,128)(2,1)S(1)} %collective-permute-done.15.rest_2_), channel_id=1, source_target_pairs={{0,4},{4,0},{8,12},{12,8},{16,20},{20,16},{24,28},{28,24},{1,5},{5... | collective-permute-start | bytes 393224 | tf_op jit(solution)/shard_map/ppermute | solution.py:372
  69.0 5.0 %collective-permute-start.17 = (bf16[32,2048]{1,0:T(8,128)(2,1)S(1)}, bf16[32,2048]{1,0:T(8,128)(2,1)S(1)}, u32[]{:S(2)}, u32[]{:S(2)}) collective-permute-start(bf16[32,2048]{1,0:T(8,128)(2,1)S(1)} %merge.1.rest_0_), channel_id=1, source_target_pairs={{0,4},{4,0},{8,12},{12,8},{16,20},{20,16},{24,28},{28,24},{1,5},{5... | collective-permute-start | bytes 393224 | tf_op jit(solution)/shard_map/ppermute | solution.py:372
  69.0 6.3 %collective-permute-start.18 = (bf16[32,2048]{1,0:T(8,128)(2,1)S(1)}, bf16[32,2048]{1,0:T(8,128)(2,1)S(1)}, u32[]{:S(2)}, u32[]{:S(2)}) collective-permute-start(bf16[32,2048]{1,0:T(8,128)(2,1)S(1)} %collective-permute-done.14.rest_1_), channel_id=1, source_target_pairs={{0,4},{4,0},{8,12},{12,8},{16,20},{20,16},{24,28},{28,24},{1,5},{5... | collective-permute-start | bytes 393224 | tf_op jit(solution)/shard_map/ppermute | solution.py:372
  71.9 5.0 %collective-permute-start.20 = (bf16[32,2048]{1,0:T(8,128)(2,1)S(1)}, bf16[32,2048]{1,0:T(8,128)(2,1)S(1)}, u32[]{:S(2)}, u32[]{:S(2)}) collective-permute-start(bf16[32,2048]{1,0:T(8,128)(2,1)S(1)} %collective-permute-done.16.rest_3_), channel_id=1, source_target_pairs={{0,4},{4,0},{8,12},{12,8},{16,20},{20,16},{24,28},{28,24},{1,5},{5... | collective-permute-start | bytes 393224 | tf_op jit(solution)/shard_map/ppermute | solution.py:372
  78.3 1.6 %collective-permute-start.21 = (bf16[2,64,1024]{2,1,0:T(8,128)(2,1)S(1)}, bf16[2,64,1024]{2,1,0:T(8,128)(2,1)S(1)}, u32[]{:S(2)}, u32[]{:S(2)}) collective-permute-start(bf16[2,64,1024]{2,1,0:T(8,128)(2,1)S(1)} %get-tuple-element.60), channel_id=1, source_target_pairs={{0,1},{1,0},{2,3},{3,2},{4,5},{5,4},{6,7},{7,6},{8,9},{9,8},{10,11... | collective-permute-start | bytes 786440 | tf_op jit(solution)/shard_map/ppermute | solution.py:446
  79.9 5.6 %collective-permute-start.22 = (bf16[64,1024]{1,0:T(8,128)(2,1)S(1)}, bf16[64,1024]{1,0:T(8,128)(2,1)S(1)}, u32[]{:S(2)}, u32[]{:S(2)}) collective-permute-start(bf16[64,1024]{1,0:T(8,128)(2,1)S(1)} %fusion), channel_id=1, source_target_pairs={{0,2},{1,3},{2,0},{3,1},{4,6},{5,7},{6,4},{7,5},{8,10},{9,11},{10,... | collective-permute-start | bytes 393224 | tf_op jit(solution)/shard_map/ppermute | solution.py:450

commit v9 on v7

--- a/solution.py
+++ b/solution.py
@@ -11,7 +11,7 @@
 DH = 128
 TILE = 128
 LANES = 128
-CHUNK = 4
+CHUNK = 6
 LOW = -1e30
 LIMIT = 2.0**100
 ONES = 16

time: 80.5 us -> 80 us (level)
  waiting for transfers between devices: 27.9 us -> 19.3 us
  Pallas kernels: 21.3 us -> 26.6 us
  starting transfers between devices: 30.6 us -> 33.3 us
    ppermute x21, waiting for transfers between devices: 21.1 us -> 13.6 us  [move(): return lax.ppermute(x, 'ctx', pairs)]
    pallas_call x4, Pallas kernels: 18.4 us -> 23.7 us  [attention_call(): pl.pallas_call(functools.partial(attention_kernel, members, ctx_count, gr...]
    ppermute x21, starting transfers between devices: 30.2 us -> 31.8 us  [move(): return lax.ppermute(x, 'ctx', pairs)]
    ppermute x1, starting transfers between devices: 0.31 us -> 1.38 us  [body(): piece = lax.ppermute(piece, 'tp', [(i, i ^ 2 * j) for i in range(peers)])]
    ppermute x1, waiting for transfers between devices: 5.29 us -> 4.23 us  [body(): piece = lax.ppermute(piece, 'tp', [(i, i ^ 2 * j) for i in range(peers)])]
  transfers between devices with their start and end apart: 23 -> 23, of which waited for: 11 -> 10; matrix products, arithmetic and copies ran while one was open for 0% -> 0% of each run, Pallas kernels for 24% -> 30%
where the time goes in v9:
time: 80 us; the launch traced here: 80.2 us
  starting transfers between devices  33.3 us (42%)
  Pallas kernels  26.6 us (33%)
  waiting for transfers between devices  19.3 us (24%)
    ppermute x21, starting transfers between devices, move(): return lax.ppermute(x, 'ctx', pairs)  31.8 us
    pallas_call x4, Pallas kernels, attention_call(): pl.pallas_call(functools.partial(attention_kernel, members, ctx_count, gr...  23.7 us
    ppermute x21, waiting for transfers between devices, move(): return lax.ppermute(x, 'ctx', pairs)  13.6 us
    ppermute x1, waiting for transfers between devices, body(): piece = lax.ppermute(piece, 'tp', [(i, i ^ 2 * j) for i in range(peers)])  4.23 us
  transfers between devices with their start and end apart: 23, of which 10 were waited for; matrix products, arithmetic and copies ran while one was open for 0% of the time, Pallas kernels for 30%

profile of v9, /device:TPU:0, one launch (start us, length us, event | category | flops | bytes accessed | tf_op | source)
XLA Modules:
  0.0 80.2 jit_solution(4052847140070799774)
XLA Ops:
  0.0 0.0 copy-start.9
  0.0 0.0 copy-start.8
  0.0 5.1 %collective-permute-start = (bf16[32,2048]{1,0:T(8,128)(2,1)}, bf16[32,2048]{1,0:T(8,128)(2,1)S(1)}, u32[]{:S(2)}, u32[]{:S(2)}) collective-permute-start(bf16[32,2048]{1,0:T(8,128)(2,1)} %rest_0_), channel_id=1, source_target_pairs={{0,24},{4,28},{8,0},{12,4},{16,8},{20,12},{24,16},{28,20},{1,25},{... | collective-permute-start | bytes 393224 | tf_op jit(solution)/shard_map/ppermute | solution.py:360
  5.2 0.0 collective-permute-start.1
  5.2 1.5 %collective-permute-start.4 = (bf16[32,2048]{1,0:T(8,128)(2,1)}, bf16[32,2048]{1,0:T(8,128)(2,1)S(1)}, u32[]{:S(2)}, u32[]{:S(2)}) collective-permute-start(bf16[32,2048]{1,0:T(8,128)(2,1)} %rest_0_), channel_id=1, source_target_pairs={{0,4},{4,0},{8,12},{12,8},{16,20},{20,16},{24,28},{28,24},{1,5},{5... | collective-permute-start | bytes 393224 | tf_op jit(solution)/shard_map/ppermute | solution.py:360
  6.6 0.6 settle.1.rest_1_
  7.2 2.1 %collective-permute-done.rest_0_ = bf16[32,2048]{1,0:T(8,128)(2,1)S(1)} collective-permute-done((bf16[32,2048]{1,0:T(8,128)(2,1)}, bf16[32,2048]{1,0:T(8,128)(2,1)S(1)}, u32[]{:S(2)}, u32[]{:S(2)}) %collective-permute-start) | collective-permute-done | bytes 131104 | tf_op jit(solution)/shard_map/ppermute | solution.py:360
  9.4 2.8 %collective-permute-done.1.rest_1_ = bf16[32,2048]{1,0:T(8,128)(2,1)S(1)} collective-permute-done((bf16[32,2048]{1,0:T(8,128)(2,1)}, bf16[32,2048]{1,0:T(8,128)(2,1)S(1)}, u32[]{:S(2)}, u32[]{:S(2)}) %collective-permute-start.1) | collective-permute-done | bytes 131104 | tf_op jit(solution)/shard_map/ppermute | solution.py:360
  12.1 1.5 %collective-permute-start.5 = (bf16[32,2048]{1,0:T(8,128)(2,1)S(1)}, bf16[32,2048]{1,0:T(8,128)(2,1)S(1)}, u32[]{:S(2)}, u32[]{:S(2)}) collective-permute-start(bf16[32,2048]{1,0:T(8,128)(2,1)S(1)} %collective-permute-done.rest_0_), channel_id=1, source_target_pairs={{0,4},{4,0},{8,12},{12,8},{16,20},{20,16},{24,28},{28,24},{1,5},{5... | collective-permute-start | bytes 393224 | tf_op jit(solution)/shard_map/ppermute | solution.py:360
  13.6 0.5 collective-permute-start.6
  14.2 0.4 collective-permute-start.2
  14.5 0.0 copy-done.3
  14.5 0.0 copy-done.4
  14.5 0.0 copy-done.2
  14.5 0.0 copy-done.1
  14.5 0.0 copy-done.7
  14.6 0.0 copy-done.9
  14.6 0.0 copy-done.8
  14.6 6.0 %attention.4 = (bf16[32,2176]{1,0:T(8,128)(2,1)S(1)}, bf16[32,2176]{1,0:T(8,128)(2,1)S(1)}, bf16[2,144,3200]{2,1,0:T(8,128)(2,1)S(1)}) custom-call(s32[8]{0:T(128)S(1)} %copy-done.8, s32[2,24]{1,0:T(2,128)S(1)} %bitcast.6, s32[2]{0:T(128)S(1)} %bitcast.10, bf16[32,256]{1,0:T(8,128)(2,1)S(1)} %copy-done.3, bf16[32,256]{1,0:T(8,128)(2,1)S(1)} %copy-done.4, ...), custom_call_target="tpu_custom_call" | custom-call | flops 3221225472 | bytes 8388608 | tf_op jit(solution)/shard_map/attention/pallas_call | solution.py:216
  20.6 2.9 %collective-permute-start.8 = (bf16[32,2176]{1,0:T(8,128)(2,1)S(1)}, bf16[32,2176]{1,0:T(8,128)(2,1)S(1)}, u32[]{:S(2)}, u32[]{:S(2)}) collective-permute-start(bf16[32,2176]{1,0:T(8,128)(2,1)S(1)} %get-tuple-element.39), channel_id=1, source_target_pairs={{0,24},{4,28},{8,0},{12,4},{16,8},{20,12},{24,16},{28,20},{1,25},{... | collective-permute-start | bytes 417800 | tf_op jit(solution)/shard_map/ppermute | solution.py:360
  23.5 0.0 collective-permute-done.2.rest_0_
  23.5 0.0 collective-permute-start.7
  23.5 0.0 collective-permute-done.5.rest_1_
  23.5 0.0 collective-permute-done.6.rest_2_
  23.5 1.6 %collective-permute-start.3 = (bf16[32,2048]{1,0:T(8,128)(2,1)S(1)}, bf16[32,2048]{1,0:T(8,128)(2,1)S(1)}, u32[]{:S(2)}, u32[]{:S(2)}) collective-permute-start(bf16[32,2048]{1,0:T(8,128)(2,1)S(1)} %collective-permute-done.2.rest_0_), channel_id=1, source_target_pairs={{0,4},{4,0},{8,12},{12,8},{16,20},{20,16},{24,28},{28,24},{1,5},{5... | collective-permute-start | bytes 393224 | tf_op jit(solution)/shard_map/ppermute | solution.py:360
  25.1 8.1 %attention.5 = (bf16[32,2176]{1,0:T(8,128)(2,1)S(1)}, bf16[32,2176]{1,0:T(8,128)(2,1)S(1)}, bf16[32,2176]{1,0:T(8,128)(2,1)S(1)}) custom-call(s32[8]{0:T(128)S(1)} %copy-done.8, s32[2,24]{1,0:T(2,128)S(1)} %bitcast.7, s32[2]{0:T(128)S(1)} %bitcast.11, bf16[32,256]{1,0:T(8,128)(2,1)S(1)} %copy-done.3, bf16[32,256]{1,0:T(8,128)(2,1)S(1)} %copy-done.4, ...), custom_call_target="tpu_custom_call" | custom-call | flops 4831838208 | bytes 8388608 | tf_op jit(solution)/shard_map/attention/pallas_call | solution.py:216
  33.2 0.2 collective-permute-start.11
  33.5 0.0 collective-permute-done.4.rest_1_
  33.5 4.5 %collective-permute-start.12 = (bf16[32,2176]{1,0:T(8,128)(2,1)S(1)}, bf16[32,2176]{1,0:T(8,128)(2,1)S(1)}, u32[]{:S(2)}, u32[]{:S(2)}) collective-permute-start(bf16[32,2176]{1,0:T(8,128)(2,1)S(1)} %get-tuple-element.43), channel_id=1, source_target_pairs={{0,28},{4,24},{8,4},{12,0},{16,12},{20,8},{24,20},{28,16},{1,29},{... | collective-permute-start | bytes 417800 | tf_op jit(solution)/shard_map/ppermute | solution.py:360
  38.0 0.0 collective-permute-done.3.rest_0_
  38.0 0.0 collective-permute-start.9
  38.0 0.0 collective-permute-done.8.refs_2_
  38.0 0.0 collective-permute-done.7.refs_1_
  38.0 5.9 %attention.6 = (bf16[32,2176]{1,0:T(8,128)(2,1)S(1)}, bf16[32,2176]{1,0:T(8,128)(2,1)S(1)}) custom-call(s32[8]{0:T(128)S(1)} %copy-done.8, s32[2,24]{1,0:T(2,128)S(1)} %bitcast.8, s32[2]{0:T(128)S(1)} %bitcast.12, bf16[32,256]{1,0:T(8,128)(2,1)S(1)} %copy-done.3, bf16[32,256]{1,0:T(8,128)(2,1)S(1)} %copy-done.4, bf16[4096,256]{1,0:T(8,128)(2,1)S(1)} %copy-done.2, ...), custom_call_target="tpu_custom_call" | custom-call | flops 3221225472 | bytes 8388608 | tf_op jit(solution)/shard_map/attention/pallas_call | solution.py:216
  44.0 0.6 collective-permute-start.10
  44.6 3.8 %collective-permute-start.13 = (bf16[32,2176]{1,0:T(8,128)(2,1)S(1)}, bf16[32,2176]{1,0:T(8,128)(2,1)S(1)}, u32[]{:S(2)}, u32[]{:S(2)}) collective-permute-start(bf16[32,2176]{1,0:T(8,128)(2,1)S(1)} %get-tuple-element.56), channel_id=1, source_target_pairs={{0,20},{4,16},{8,28},{12,24},{16,4},{20,0},{24,12},{28,8},{1,21},{... | collective-permute-start | bytes 417800 | tf_op jit(solution)/shard_map/ppermute | solution.py:360
  48.4 0.0 copy-done.5
  48.4 3.7 %attention.7.refs_0_ = bf16[32,2176]{1,0:T(8,128)(2,1)S(1)} custom-call(s32[8]{0:T(128)S(1)} %copy-done.8, s32[2,24]{1,0:T(2,128)S(1)} %bitcast.9, s32[2]{0:T(128)S(1)} %bitcast.13, bf16[32,256]{1,0:T(8,128)(2,1)S(1)} %copy-done.3, bf16[32,256]{1,0:T(8,128)(2,1)S(1)} %copy-done.4, bf16[4096,256]{1,0:T(8,128)(2,1)S(1)} %copy-done.2, ...), custom_call_target="tpu_custom_call" | custom-call | flops 1610612736 | bytes 8388608 | tf_op jit(solution)/shard_map/attention/pallas_call | solution.py:216
  52.1 0.0 collective-permute-done.11.refs_5_
  52.1 0.0 collective-permute-done.12.refs_6_
  52.1 0.0 collective-permute-done.9.refs_3_
  52.1 0.0 collective-permute-done.10.refs_4_
  52.1 0.9 %collective-permute-done.13.refs_7_ = bf16[32,2176]{1,0:T(8,128)(2,1)S(1)} collective-permute-done((bf16[32,2176]{1,0:T(8,128)(2,1)S(1)}, bf16[32,2176]{1,0:T(8,128)(2,1)S(1)}, u32[]{:S(2)}, u32[]{:S(2)}) %collective-permute-start.13) | collective-permute-done | bytes 139296 | tf_op jit(solution)/shard_map/ppermute | solution.py:360
  53.0 0.9 %merge.1.rest_0_ = bf16[32,2048]{1,0:T(8,128)(2,1)S(1)} custom-call(bf16[32,2176]{1,0:T(8,128)(2,1)S(1)} %attention.7.refs_0_, bf16[32,2176]{1,0:T(8,128)(2,1)S(1)} %collective-permute-done.7.refs_1_, bf16[32,2176]{1,0:T(8,128)(2,1)S(1)} %collective-permute-done.8.refs_2_, bf16[32,2176]{1,0:T(8,128)(2,1)S(1)} %collective-permute-done.9.refs_3_, ...), custom_call_target="tpu_custom_call" | custom-call | flops 1114112 | bytes 1114112 | tf_op jit(solution)/shard_map/merge/pallas_call | solution.py:276
  54.0 0.4 collective-permute-start.15
  54.3 3.5 %collective-permute-start.14 = (bf16[32,2048]{1,0:T(8,128)(2,1)S(1)}, bf16[32,2048]{1,0:T(8,128)(2,1)S(1)}, u32[]{:S(2)}, u32[]{:S(2)}) collective-permute-start(bf16[32,2048]{1,0:T(8,128)(2,1)S(1)} %merge.1.rest_0_), channel_id=1, source_target_pairs={{0,24},{4,28},{8,0},{12,4},{16,8},{20,12},{24,16},{28,20},{1,25},{... | collective-permute-start | bytes 393224 | tf_op jit(solution)/shard_map/ppermute | solution.py:360
  57.8 0.3 collective-permute-start.16
  58.1 2.8 %collective-permute-done.15.rest_2_ = bf16[32,2048]{1,0:T(8,128)(2,1)S(1)} collective-permute-done((bf16[32,2048]{1,0:T(8,128)(2,1)S(1)}, bf16[32,2048]{1,0:T(8,128)(2,1)S(1)}, u32[]{:S(2)}, u32[]{:S(2)}) %collective-permute-start.15) | collective-permute-done | bytes 131104 | tf_op jit(solution)/shard_map/ppermute | solution.py:360
  60.9 1.5 %collective-permute-start.19 = (bf16[32,2048]{1,0:T(8,128)(2,1)S(1)}, bf16[32,2048]{1,0:T(8,128)(2,1)S(1)}, u32[]{:S(2)}, u32[]{:S(2)}) collective-permute-start(bf16[32,2048]{1,0:T(8,128)(2,1)S(1)} %collective-permute-done.15.rest_2_), channel_id=1, source_target_pairs={{0,4},{4,0},{8,12},{12,8},{16,20},{20,16},{24,28},{28,24},{1,5},{5... | collective-permute-start | bytes 393224 | tf_op jit(solution)/shard_map/ppermute | solution.py:360
  62.4 0.5 collective-permute-start.17
  63.0 0.0 collective-permute-done.14.rest_1_
  63.0 1.5 %collective-permute-start.18 = (bf16[32,2048]{1,0:T(8,128)(2,1)S(1)}, bf16[32,2048]{1,0:T(8,128)(2,1)S(1)}, u32[]{:S(2)}, u32[]{:S(2)}) collective-permute-start(bf16[32,2048]{1,0:T(8,128)(2,1)S(1)} %collective-permute-done.14.rest_1_), channel_id=1, source_target_pairs={{0,4},{4,0},{8,12},{12,8},{16,20},{20,16},{24,28},{28,24},{1,5},{5... | collective-permute-start | bytes 393224 | tf_op jit(solution)/shard_map/ppermute | solution.py:360
  64.4 0.5 collective-permute-done.16.rest_3_
  65.0 0.9 %collective-permute-done.19.rest_6_ = bf16[32,2048]{1,0:T(8,128)(2,1)S(1)} collective-permute-done((bf16[32,2048]{1,0:T(8,128)(2,1)S(1)}, bf16[32,2048]{1,0:T(8,128)(2,1)S(1)}, u32[]{:S(2)}, u32[]{:S(2)}) %collective-permute-start.19) | collective-permute-done | bytes 131104 | tf_op jit(solution)/shard_map/ppermute | solution.py:360
  65.9 1.5 %collective-permute-start.20 = (bf16[32,2048]{1,0:T(8,128)(2,1)S(1)}, bf16[32,2048]{1,0:T(8,128)(2,1)S(1)}, u32[]{:S(2)}, u32[]{:S(2)}) collective-permute-start(bf16[32,2048]{1,0:T(8,128)(2,1)S(1)} %collective-permute-done.16.rest_3_), channel_id=1, source_target_pairs={{0,4},{4,0},{8,12},{12,8},{16,20},{20,16},{24,28},{28,24},{1,5},{5... | collective-permute-start | bytes 393224 | tf_op jit(solution)/shard_map/ppermute | solution.py:360
  67.4 0.0 collective-permute-done.17.rest_4_
  67.4 1.4 %collective-permute-done.18.rest_5_ = bf16[32,2048]{1,0:T(8,128)(2,1)S(1)} collective-permute-done((bf16[32,2048]{1,0:T(8,128)(2,1)S(1)}, bf16[32,2048]{1,0:T(8,128)(2,1)S(1)}, u32[]{:S(2)}, u32[]{:S(2)}) %collective-permute-start.18) | collective-permute-done | bytes 131104 | tf_op jit(solution)/shard_map/ppermute | solution.py:360
  68.8 2.1 %collective-permute-done.20.rest_7_ = bf16[32,2048]{1,0:T(8,128)(2,1)S(1)} collective-permute-done((bf16[32,2048]{1,0:T(8,128)(2,1)S(1)}, bf16[32,2048]{1,0:T(8,128)(2,1)S(1)}, u32[]{:S(2)}, u32[]{:S(2)}) %collective-permute-start.20) | collective-permute-done | bytes 131104 | tf_op jit(solution)/shard_map/ppermute | solution.py:360
  70.9 1.4 %projection.1 = (f32[2,64,1024]{2,1,0:T(8,128)S(1)}, bf16[2,64,1024]{2,1,0:T(8,128)(2,1)S(1)}) custom-call(bf16[2048,1024]{1,0:T(8,128)(2,1)S(1)} %copy-done, bf16[32,2048]{1,0:T(8,128)(2,1)S(1)} %merge.1.rest_0_, bf16[32,2048]{1,0:T(8,128)(2,1)S(1)} %collective-permute-done.14.rest_1_, bf16[32,2048]{1,0:T(8,128)(2,1)S(1)} %collective-permute-done.15.rest_2_, ...), custom_call_target="tpu_custom_call" | custom-call | flops 1073741824 | bytes 4194304 | tf_op jit(solution)/shard_map/projection/pallas_call | solution.py:318
  72.2 0.1 collective-permute-start.21
  72.3 1.5 %collective-permute-done.21 = bf16[2,64,1024]{2,1,0:T(8,128)(2,1)S(1)} collective-permute-done((bf16[2,64,1024]{2,1,0:T(8,128)(2,1)S(1)}, bf16[2,64,1024]{2,1,0:T(8,128)(2,1)S(1)}, u32[]{:S(2)}, u32[]{:S(2)}) %collective-permute-start.21) | collective-permute-done | bytes 262176 | tf_op jit(solution)/shard_map/ppermute | solution.py:434
  73.9 1.4 %collective-permute-start.22 = (bf16[64,1024]{1,0:T(8,128)(2,1)S(1)}, bf16[64,1024]{1,0:T(8,128)(2,1)S(1)}, u32[]{:S(2)}, u32[]{:S(2)}) collective-permute-start(bf16[64,1024]{1,0:T(8,128)(2,1)S(1)} %fusion), channel_id=1, source_target_pairs={{0,2},{1,3},{2,0},{3,1},{4,6},{5,7},{6,4},{7,5},{8,10},{9,11},{10,... | collective-permute-start | bytes 393224 | tf_op jit(solution)/shard_map/ppermute | solution.py:438
  75.3 4.2 %collective-permute-done.22 = bf16[64,1024]{1,0:T(8,128)(2,1)S(1)} collective-permute-done((bf16[64,1024]{1,0:T(8,128)(2,1)S(1)}, bf16[64,1024]{1,0:T(8,128)(2,1)S(1)}, u32[]{:S(2)}, u32[]{:S(2)}) %collective-permute-start.22) | collective-permute-done | bytes 131104 | tf_op jit(solution)/shard_map/ppermute | solution.py:438
  79.5 0.7 bitcast_add_fusion
  (11 shorter events, 0.0 us)
Async XLA Ops:
  0.0 14.5 %copy-start.3 = (bf16[32,256]{1,0:T(8,128)(2,1)S(1)}, bf16[32,256]{1,0:T(8,128)(2,1)}, u32[]{:S(2)}) copy-start(bf16[32,256]{1,0:T(8,128)(2,1)} %nk_ref.7) | copy-start | bytes 49156
  0.0 14.5 %copy-start.4 = (bf16[32,256]{1,0:T(8,128)(2,1)S(1)}, bf16[32,256]{1,0:T(8,128)(2,1)}, u32[]{:S(2)}) copy-start(bf16[32,256]{1,0:T(8,128)(2,1)} %nv_ref.7) | copy-start | bytes 49156
  0.0 14.5 %copy-start.2 = (bf16[4096,256]{1,0:T(8,128)(2,1)S(1)}, bf16[4096,256]{1,0:T(8,128)(2,1)}, u32[]{:S(2)}) copy-start(bf16[4096,256]{1,0:T(8,128)(2,1)} %k_ref.7) | copy-start | bytes 6291460
  0.0 14.5 %copy-start.1 = (bf16[4096,256]{1,0:T(8,128)(2,1)S(1)}, bf16[4096,256]{1,0:T(8,128)(2,1)}, u32[]{:S(2)}) copy-start(bf16[4096,256]{1,0:T(8,128)(2,1)} %v_ref.1) | copy-start | bytes 6291460
  0.0 14.5 %copy-start.7 = (s32[1,2,24]{2,1,0:T(2,128)S(1)}, s32[1,2,24]{2,1,0:T(2,128)}, u32[]{:S(2)}) copy-start(s32[1,2,24]{2,1,0:T(2,128)} %param.14) | copy-start | bytes 580
  0.0 14.5 %copy-start.9 = (s32[1,2]{1,0:T(1,128)S(1)}, s32[1,2]{1,0:T(1,128)}, u32[]{:S(2)}) copy-start(s32[1,2]{1,0:T(1,128)} %param.15) | copy-start | bytes 28
  0.0 14.5 %copy-start.8 = (s32[8]{0:T(128)S(1)}, s32[8]{0:T(128)}, u32[]{:S(2)}) copy-start(s32[8]{0:T(128)} %slot_ref.7) | copy-start | bytes 100
  0.0 9.3 %collective-permute-start = (bf16[32,2048]{1,0:T(8,128)(2,1)}, bf16[32,2048]{1,0:T(8,128)(2,1)S(1)}, u32[]{:S(2)}, u32[]{:S(2)}) collective-permute-start(bf16[32,2048]{1,0:T(8,128)(2,1)} %rest_0_), channel_id=1, source_target_pairs={{0,24},{4,28},{8,0},{12,4},{16,8},{20,12},{24,16},{28,20},{1,25},{... | collective-permute-start | bytes 393224 | tf_op jit(solution)/shard_map/ppermute | solution.py:360
  5.2 7.0 %collective-permute-start.1 = (bf16[32,2048]{1,0:T(8,128)(2,1)}, bf16[32,2048]{1,0:T(8,128)(2,1)S(1)}, u32[]{:S(2)}, u32[]{:S(2)}) collective-permute-start(bf16[32,2048]{1,0:T(8,128)(2,1)} %rest_0_), channel_id=1, source_target_pairs={{0,8},{4,12},{8,16},{12,20},{16,24},{20,28},{24,0},{28,4},{1,9},{5... | collective-permute-start | bytes 393224 | tf_op jit(solution)/shard_map/ppermute | solution.py:360
  5.2 28.3 %collective-permute-start.4 = (bf16[32,2048]{1,0:T(8,128)(2,1)}, bf16[32,2048]{1,0:T(8,128)(2,1)S(1)}, u32[]{:S(2)}, u32[]{:S(2)}) collective-permute-start(bf16[32,2048]{1,0:T(8,128)(2,1)} %rest_0_), channel_id=1, source_target_pairs={{0,4},{4,0},{8,12},{12,8},{16,20},{20,16},{24,28},{28,24},{1,5},{5... | collective-permute-start | bytes 393224 | tf_op jit(solution)/shard_map/ppermute | solution.py:360
  12.1 11.4 %collective-permute-start.5 = (bf16[32,2048]{1,0:T(8,128)(2,1)S(1)}, bf16[32,2048]{1,0:T(8,128)(2,1)S(1)}, u32[]{:S(2)}, u32[]{:S(2)}) collective-permute-start(bf16[32,2048]{1,0:T(8,128)(2,1)S(1)} %collective-permute-done.rest_0_), channel_id=1, source_target_pairs={{0,4},{4,0},{8,12},{12,8},{16,20},{20,16},{24,28},{28,24},{1,5},{5... | collective-permute-start | bytes 393224 | tf_op jit(solution)/shard_map/ppermute | solution.py:360
  13.6 9.9 %collective-permute-start.6 = (bf16[32,2048]{1,0:T(8,128)(2,1)S(1)}, bf16[32,2048]{1,0:T(8,128)(2,1)S(1)}, u32[]{:S(2)}, u32[]{:S(2)}) collective-permute-start(bf16[32,2048]{1,0:T(8,128)(2,1)S(1)} %collective-permute-done.1.rest_1_), channel_id=1, source_target_pairs={{0,4},{4,0},{8,12},{12,8},{16,20},{20,16},{24,28},{28,24},{1,5},{5... | collective-permute-start | bytes 393224 | tf_op jit(solution)/shard_map/ppermute | solution.py:360
  14.2 9.3 %collective-permute-start.2 = (bf16[32,2048]{1,0:T(8,128)(2,1)}, bf16[32,2048]{1,0:T(8,128)(2,1)S(1)}, u32[]{:S(2)}, u32[]{:S(2)}) collective-permute-start(bf16[32,2048]{1,0:T(8,128)(2,1)} %rest_0_), channel_id=1, source_target_pairs={{0,16},{4,20},{8,24},{12,28},{16,0},{20,4},{24,8},{28,12},{1,17},{... | collective-permute-start | bytes 393224 | tf_op jit(solution)/shard_map/ppermute | solution.py:360
  20.6 17.4 %collective-permute-start.8 = (bf16[32,2176]{1,0:T(8,128)(2,1)S(1)}, bf16[32,2176]{1,0:T(8,128)(2,1)S(1)}, u32[]{:S(2)}, u32[]{:S(2)}) collective-permute-start(bf16[32,2176]{1,0:T(8,128)(2,1)S(1)} %get-tuple-element.39), channel_id=1, source_target_pairs={{0,24},{4,28},{8,0},{12,4},{16,8},{20,12},{24,16},{28,20},{1,25},{... | collective-permute-start | bytes 417800 | tf_op jit(solution)/shard_map/ppermute | solution.py:360
  23.5 14.5 %collective-permute-start.7 = (bf16[32,2176]{1,0:T(8,128)(2,1)S(1)}, bf16[32,2176]{1,0:T(8,128)(2,1)S(1)}, u32[]{:S(2)}, u32[]{:S(2)}) collective-permute-start(bf16[32,2176]{1,0:T(8,128)(2,1)S(1)} %get-tuple-element.46), channel_id=1, source_target_pairs={{0,8},{4,12},{8,16},{12,20},{16,24},{20,28},{24,0},{28,4},{1,9},{5... | collective-permute-start | bytes 417800 | tf_op jit(solution)/shard_map/ppermute | solution.py:360
  23.5 14.5 %collective-permute-start.3 = (bf16[32,2048]{1,0:T(8,128)(2,1)S(1)}, bf16[32,2048]{1,0:T(8,128)(2,1)S(1)}, u32[]{:S(2)}, u32[]{:S(2)}) collective-permute-start(bf16[32,2048]{1,0:T(8,128)(2,1)S(1)} %collective-permute-done.2.rest_0_), channel_id=1, source_target_pairs={{0,4},{4,0},{8,12},{12,8},{16,20},{20,16},{24,28},{28,24},{1,5},{5... | collective-permute-start | bytes 393224 | tf_op jit(solution)/shard_map/ppermute | solution.py:360
  33.2 18.8 %collective-permute-start.11 = (bf16[32,2176]{1,0:T(8,128)(2,1)S(1)}, bf16[32,2176]{1,0:T(8,128)(2,1)S(1)}, u32[]{:S(2)}, u32[]{:S(2)}) collective-permute-start(bf16[32,2176]{1,0:T(8,128)(2,1)S(1)} %get-tuple-element.55), channel_id=1, source_target_pairs={{0,12},{4,8},{8,20},{12,16},{16,28},{20,24},{24,4},{28,0},{1,13},{... | collective-permute-start | bytes 417800 | tf_op jit(solution)/shard_map/ppermute | solution.py:360
  33.5 18.6 %collective-permute-start.12 = (bf16[32,2176]{1,0:T(8,128)(2,1)S(1)}, bf16[32,2176]{1,0:T(8,128)(2,1)S(1)}, u32[]{:S(2)}, u32[]{:S(2)}) collective-permute-start(bf16[32,2176]{1,0:T(8,128)(2,1)S(1)} %get-tuple-element.43), channel_id=1, source_target_pairs={{0,28},{4,24},{8,4},{12,0},{16,12},{20,8},{24,20},{28,16},{1,29},{... | collective-permute-start | bytes 417800 | tf_op jit(solution)/shard_map/ppermute | solution.py:360
  38.0 10.4 %copy-start.5 = (f32[8,128]{1,0:T(8,128)S(1)}, f32[8,128]{1,0:T(8,128)}, u32[]{:S(2)}) copy-start(f32[8,128]{1,0:T(8,128)} %settle.1.rest_1_) | copy-start | bytes 12292
  38.0 10.4 %copy-start.6 = (bf16[32,2048]{1,0:T(8,128)(2,1)S(1)}, bf16[32,2048]{1,0:T(8,128)(2,1)}, u32[]{:S(2)}) copy-start(bf16[32,2048]{1,0:T(8,128)(2,1)} %rest_0_) | copy-start | bytes 393220
  38.0 14.1 %collective-permute-start.9 = (bf16[32,2176]{1,0:T(8,128)(2,1)S(1)}, bf16[32,2176]{1,0:T(8,128)(2,1)S(1)}, u32[]{:S(2)}, u32[]{:S(2)}) collective-permute-start(bf16[32,2176]{1,0:T(8,128)(2,1)S(1)} %get-tuple-element.54), channel_id=1, source_target_pairs={{0,16},{4,20},{8,24},{12,28},{16,0},{20,4},{24,8},{28,12},{1,17},{... | collective-permute-start | bytes 417800 | tf_op jit(solution)/shard_map/ppermute | solution.py:360
  44.0 8.1 %collective-permute-start.10 = (bf16[32,2176]{1,0:T(8,128)(2,1)S(1)}, bf16[32,2176]{1,0:T(8,128)(2,1)S(1)}, u32[]{:S(2)}, u32[]{:S(2)}) collective-permute-start(bf16[32,2176]{1,0:T(8,128)(2,1)S(1)} %get-tuple-element.49), channel_id=1, source_target_pairs={{0,4},{4,0},{8,12},{12,8},{16,20},{20,16},{24,28},{28,24},{1,5},{5... | collective-permute-start | bytes 417800 | tf_op jit(solution)/shard_map/ppermute | solution.py:360
  44.6 8.5 %collective-permute-start.13 = (bf16[32,2176]{1,0:T(8,128)(2,1)S(1)}, bf16[32,2176]{1,0:T(8,128)(2,1)S(1)}, u32[]{:S(2)}, u32[]{:S(2)}) collective-permute-start(bf16[32,2176]{1,0:T(8,128)(2,1)S(1)} %get-tuple-element.56), channel_id=1, source_target_pairs={{0,20},{4,16},{8,28},{12,24},{16,4},{20,0},{24,12},{28,8},{1,21},{... | collective-permute-start | bytes 417800 | tf_op jit(solution)/shard_map/ppermute | solution.py:360
  48.4 22.5 %copy-start = (bf16[2048,1024]{1,0:T(8,128)(2,1)S(1)}, bf16[2048,1024]{1,0:T(8,128)(2,1)}, u32[]{:S(2)}) copy-start(bf16[2048,1024]{1,0:T(8,128)(2,1)} %w_ref.1) | copy-start | bytes 12582916
  54.0 7.0 %collective-permute-start.15 = (bf16[32,2048]{1,0:T(8,128)(2,1)S(1)}, bf16[32,2048]{1,0:T(8,128)(2,1)S(1)}, u32[]{:S(2)}, u32[]{:S(2)}) collective-permute-start(bf16[32,2048]{1,0:T(8,128)(2,1)S(1)} %merge.1.rest_0_), channel_id=1, source_target_pairs={{0,8},{4,12},{8,16},{12,20},{16,24},{20,28},{24,0},{28,4},{1,9},{5... | collective-permute-start | bytes 393224 | tf_op jit(solution)/shard_map/ppermute | solution.py:360
  54.3 8.6 %collective-permute-start.14 = (bf16[32,2048]{1,0:T(8,128)(2,1)S(1)}, bf16[32,2048]{1,0:T(8,128)(2,1)S(1)}, u32[]{:S(2)}, u32[]{:S(2)}) collective-permute-start(bf16[32,2048]{1,0:T(8,128)(2,1)S(1)} %merge.1.rest_0_), channel_id=1, source_target_pairs={{0,24},{4,28},{8,0},{12,4},{16,8},{20,12},{24,16},{28,20},{1,25},{... | collective-permute-start | bytes 393224 | tf_op jit(solution)/shard_map/ppermute | solution.py:360
  57.8 7.2 %collective-permute-start.16 = (bf16[32,2048]{1,0:T(8,128)(2,1)S(1)}, bf16[32,2048]{1,0:T(8,128)(2,1)S(1)}, u32[]{:S(2)}, u32[]{:S(2)}) collective-permute-start(bf16[32,2048]{1,0:T(8,128)(2,1)S(1)} %merge.1.rest_0_), channel_id=1, source_target_pairs={{0,16},{4,20},{8,24},{12,28},{16,0},{20,4},{24,8},{28,12},{1,17},{... | collective-permute-start | bytes 393224 | tf_op jit(solution)/shard_map/ppermute | solution.py:360
  60.9 5.0 %collective-permute-start.19 = (bf16[32,2048]{1,0:T(8,128)(2,1)S(1)}, bf16[32,2048]{1,0:T(8,128)(2,1)S(1)}, u32[]{:S(2)}, u32[]{:S(2)}) collective-permute-start(bf16[32,2048]{1,0:T(8,128)(2,1)S(1)} %collective-permute-done.15.rest_2_), channel_id=1, source_target_pairs={{0,4},{4,0},{8,12},{12,8},{16,20},{20,16},{24,28},{28,24},{1,5},{5... | collective-permute-start | bytes 393224 | tf_op jit(solution)/shard_map/ppermute | solution.py:360
  62.4 5.0 %collective-permute-start.17 = (bf16[32,2048]{1,0:T(8,128)(2,1)S(1)}, bf16[32,2048]{1,0:T(8,128)(2,1)S(1)}, u32[]{:S(2)}, u32[]{:S(2)}) collective-permute-start(bf16[32,2048]{1,0:T(8,128)(2,1)S(1)} %merge.1.rest_0_), channel_id=1, source_target_pairs={{0,4},{4,0},{8,12},{12,8},{16,20},{20,16},{24,28},{28,24},{1,5},{5... | collective-permute-start | bytes 393224 | tf_op jit(solution)/shard_map/ppermute | solution.py:360
  63.0 5.8 %collective-permute-start.18 = (bf16[32,2048]{1,0:T(8,128)(2,1)S(1)}, bf16[32,2048]{1,0:T(8,128)(2,1)S(1)}, u32[]{:S(2)}, u32[]{:S(2)}) collective-permute-start(bf16[32,2048]{1,0:T(8,128)(2,1)S(1)} %collective-permute-done.14.rest_1_), channel_id=1, source_target_pairs={{0,4},{4,0},{8,12},{12,8},{16,20},{20,16},{24,28},{28,24},{1,5},{5... | collective-permute-start | bytes 393224 | tf_op jit(solution)/shard_map/ppermute | solution.py:360
  65.9 5.0 %collective-permute-start.20 = (bf16[32,2048]{1,0:T(8,128)(2,1)S(1)}, bf16[32,2048]{1,0:T(8,128)(2,1)S(1)}, u32[]{:S(2)}, u32[]{:S(2)}) collective-permute-start(bf16[32,2048]{1,0:T(8,128)(2,1)S(1)} %collective-permute-done.16.rest_3_), channel_id=1, source_target_pairs={{0,4},{4,0},{8,12},{12,8},{16,20},{20,16},{24,28},{28,24},{1,5},{5... | collective-permute-start | bytes 393224 | tf_op jit(solution)/shard_map/ppermute | solution.py:360
  72.2 1.6 %collective-permute-start.21 = (bf16[2,64,1024]{2,1,0:T(8,128)(2,1)S(1)}, bf16[2,64,1024]{2,1,0:T(8,128)(2,1)S(1)}, u32[]{:S(2)}, u32[]{:S(2)}) collective-permute-start(bf16[2,64,1024]{2,1,0:T(8,128)(2,1)S(1)} %get-tuple-element.60), channel_id=1, source_target_pairs={{0,1},{1,0},{2,3},{3,2},{4,5},{5,4},{6,7},{7,6},{8,9},{9,8},{10,11... | collective-permute-start | bytes 786440 | tf_op jit(solution)/shard_map/ppermute | solution.py:434
  73.9 5.6 %collective-permute-start.22 = (bf16[64,1024]{1,0:T(8,128)(2,1)S(1)}, bf16[64,1024]{1,0:T(8,128)(2,1)S(1)}, u32[]{:S(2)}, u32[]{:S(2)}) collective-permute-start(bf16[64,1024]{1,0:T(8,128)(2,1)S(1)} %fusion), channel_id=1, source_target_pairs={{0,2},{1,3},{2,0},{3,1},{4,6},{5,7},{6,4},{7,5},{8,10},{9,11},{10,... | collective-permute-start | bytes 393224 | tf_op jit(solution)/shard_map/ppermute | solution.py:438

commit v10 on v9

--- a/solution.py
+++ b/solution.py
@@ -385,6 +385,7 @@
     middle = [m for m in order[1:] if not m[1] and 2 * m[0] == high]
     flip = [m for m in order if m[1] and m[0] and 2 * m[0] != high]
     late = [m for m in order if m[1] and 2 * m[0] == high] + [(0, 1)]
+    late = late[::-1]
     groups = [near[i : i + 2] for i in range(0, len(near), 2)]
     groups += [middle + flip[:2]] + [flip[i : i + 2] for i in range(2, len(flip), 2)]
     groups += [late, order[:1]]

time: 80 us -> 79.5 us (level); the launches traced: 80.2 us -> 78.9 us
  Pallas kernels: 26.6 us -> 25 us
    pallas_call x4, Pallas kernels: 23.7 us -> 22.1 us  [attention_call(): pl.pallas_call(functools.partial(attention_kernel, members, ctx_count, gr...]
  transfers between devices with their start and end apart: 23 -> 23, of which waited for: 10 -> 11; matrix products, arithmetic and copies ran while one was open for 0% -> 0% of each run, Pallas kernels for 30% -> 29%
where the time goes in v10:
time: 79.5 us; the launch traced here: 78.9 us
  starting transfers between devices  34 us (43%)
  Pallas kernels  25 us (31%)
  waiting for transfers between devices  18.9 us (24%)
    ppermute x21, starting transfers between devices, move(): return lax.ppermute(x, 'ctx', pairs)  32 us
    pallas_call x4, Pallas kernels, attention_call(): pl.pallas_call(functools.partial(attention_kernel, members, ctx_count, gr...  22.1 us
    ppermute x21, waiting for transfers between devices, move(): return lax.ppermute(x, 'ctx', pairs)  13.6 us
    ppermute x1, waiting for transfers between devices, body(): piece = lax.ppermute(piece, 'tp', [(i, i ^ 2 * j) for i in range(peers)])  3.8 us
    ppermute x1, starting transfers between devices, body(): piece = lax.ppermute(piece, 'tp', [(i, i ^ 2 * j) for i in range(peers)])  1.97 us
  transfers between devices with their start and end apart: 23, of which 11 were waited for; matrix products, arithmetic and copies ran while one was open for 0% of the time, Pallas kernels for 29%

profile of v10, /device:TPU:0, one launch (start us, length us, event | category | flops | bytes accessed | tf_op | source)
XLA Modules:
  0.0 78.9 jit_solution(14487098671996277742)
XLA Ops:
  0.0 0.0 copy-start.9
  0.0 0.0 copy-start.8
  0.0 5.1 %collective-permute-start = (bf16[32,2048]{1,0:T(8,128)(2,1)}, bf16[32,2048]{1,0:T(8,128)(2,1)S(1)}, u32[]{:S(2)}, u32[]{:S(2)}) collective-permute-start(bf16[32,2048]{1,0:T(8,128)(2,1)} %rest_0_), channel_id=1, source_target_pairs={{0,24},{4,28},{8,0},{12,4},{16,8},{20,12},{24,16},{28,20},{1,25},{... | collective-permute-start | bytes 393224 | tf_op jit(solution)/shard_map/ppermute | solution.py:360
  5.2 0.0 collective-permute-start.1
  5.2 1.5 %collective-permute-start.2 = (bf16[32,2048]{1,0:T(8,128)(2,1)}, bf16[32,2048]{1,0:T(8,128)(2,1)S(1)}, u32[]{:S(2)}, u32[]{:S(2)}) collective-permute-start(bf16[32,2048]{1,0:T(8,128)(2,1)} %rest_0_), channel_id=1, source_target_pairs={{0,4},{4,0},{8,12},{12,8},{16,20},{20,16},{24,28},{28,24},{1,5},{5... | collective-permute-start | bytes 393224 | tf_op jit(solution)/shard_map/ppermute | solution.py:360
  6.6 0.6 settle.1.rest_1_
  7.2 2.1 %collective-permute-done.rest_0_ = bf16[32,2048]{1,0:T(8,128)(2,1)S(1)} collective-permute-done((bf16[32,2048]{1,0:T(8,128)(2,1)}, bf16[32,2048]{1,0:T(8,128)(2,1)S(1)}, u32[]{:S(2)}, u32[]{:S(2)}) %collective-permute-start) | collective-permute-done | bytes 131104 | tf_op jit(solution)/shard_map/ppermute | solution.py:360
  9.4 2.8 %collective-permute-done.1.rest_1_ = bf16[32,2048]{1,0:T(8,128)(2,1)S(1)} collective-permute-done((bf16[32,2048]{1,0:T(8,128)(2,1)}, bf16[32,2048]{1,0:T(8,128)(2,1)S(1)}, u32[]{:S(2)}, u32[]{:S(2)}) %collective-permute-start.1) | collective-permute-done | bytes 131104 | tf_op jit(solution)/shard_map/ppermute | solution.py:360
  12.1 1.5 %collective-permute-start.5 = (bf16[32,2048]{1,0:T(8,128)(2,1)S(1)}, bf16[32,2048]{1,0:T(8,128)(2,1)S(1)}, u32[]{:S(2)}, u32[]{:S(2)}) collective-permute-start(bf16[32,2048]{1,0:T(8,128)(2,1)S(1)} %collective-permute-done.rest_0_), channel_id=1, source_target_pairs={{0,4},{4,0},{8,12},{12,8},{16,20},{20,16},{24,28},{28,24},{1,5},{5... | collective-permute-start | bytes 393224 | tf_op jit(solution)/shard_map/ppermute | solution.py:360
  13.6 0.5 collective-permute-start.6
  14.2 0.4 collective-permute-start.3
  14.5 0.0 copy-done.3
  14.5 0.0 copy-done.4
  14.5 0.0 copy-done.2
  14.5 0.0 copy-done.1
  14.5 0.0 copy-done.7
  14.6 0.0 copy-done.9
  14.6 0.0 copy-done.8
  14.6 5.6 %attention.4 = (bf16[32,2176]{1,0:T(8,128)(2,1)S(1)}, bf16[32,2176]{1,0:T(8,128)(2,1)S(1)}, bf16[2,144,3200]{2,1,0:T(8,128)(2,1)S(1)}) custom-call(s32[8]{0:T(128)S(1)} %copy-done.8, s32[2,24]{1,0:T(2,128)S(1)} %bitcast.6, s32[2]{0:T(128)S(1)} %bitcast.10, bf16[32,256]{1,0:T(8,128)(2,1)S(1)} %copy-done.3, bf16[32,256]{1,0:T(8,128)(2,1)S(1)} %copy-done.4, ...), custom_call_target="tpu_custom_call" | custom-call | flops 3221225472 | bytes 8388608 | tf_op jit(solution)/shard_map/attention/pallas_call | solution.py:216
  20.1 2.4 %collective-permute-start.8 = (bf16[32,2176]{1,0:T(8,128)(2,1)S(1)}, bf16[32,2176]{1,0:T(8,128)(2,1)S(1)}, u32[]{:S(2)}, u32[]{:S(2)}) collective-permute-start(bf16[32,2176]{1,0:T(8,128)(2,1)S(1)} %get-tuple-element.39), channel_id=1, source_target_pairs={{0,24},{4,28},{8,0},{12,4},{16,8},{20,12},{24,16},{28,20},{1,25},{... | collective-permute-start | bytes 417800 | tf_op jit(solution)/shard_map/ppermute | solution.py:360
  22.5 0.0 collective-permute-done.3.rest_0_
  22.5 0.0 collective-permute-start.7
  22.5 0.0 collective-permute-done.5.rest_1_
  22.5 0.0 collective-permute-done.6.rest_2_
  22.5 1.6 %collective-permute-start.4 = (bf16[32,2048]{1,0:T(8,128)(2,1)S(1)}, bf16[32,2048]{1,0:T(8,128)(2,1)S(1)}, u32[]{:S(2)}, u32[]{:S(2)}) collective-permute-start(bf16[32,2048]{1,0:T(8,128)(2,1)S(1)} %collective-permute-done.3.rest_0_), channel_id=1, source_target_pairs={{0,4},{4,0},{8,12},{12,8},{16,20},{20,16},{24,28},{28,24},{1,5},{5... | collective-permute-start | bytes 393224 | tf_op jit(solution)/shard_map/ppermute | solution.py:360
  24.1 7.5 %attention.5 = (bf16[32,2176]{1,0:T(8,128)(2,1)S(1)}, bf16[32,2176]{1,0:T(8,128)(2,1)S(1)}, bf16[32,2176]{1,0:T(8,128)(2,1)S(1)}) custom-call(s32[8]{0:T(128)S(1)} %copy-done.8, s32[2,24]{1,0:T(2,128)S(1)} %bitcast.7, s32[2]{0:T(128)S(1)} %bitcast.11, bf16[32,256]{1,0:T(8,128)(2,1)S(1)} %copy-done.3, bf16[32,256]{1,0:T(8,128)(2,1)S(1)} %copy-done.4, ...), custom_call_target="tpu_custom_call" | custom-call | flops 4831838208 | bytes 8388608 | tf_op jit(solution)/shard_map/attention/pallas_call | solution.py:216
  31.6 0.2 collective-permute-start.11
  31.8 0.0 collective-permute-done.2.rest_0_
  31.8 4.6 %collective-permute-start.12 = (bf16[32,2176]{1,0:T(8,128)(2,1)S(1)}, bf16[32,2176]{1,0:T(8,128)(2,1)S(1)}, u32[]{:S(2)}, u32[]{:S(2)}) collective-permute-start(bf16[32,2176]{1,0:T(8,128)(2,1)S(1)} %get-tuple-element.43), channel_id=1, source_target_pairs={{0,28},{4,24},{8,4},{12,0},{16,12},{20,8},{24,20},{28,16},{1,29},{... | collective-permute-start | bytes 417800 | tf_op jit(solution)/shard_map/ppermute | solution.py:360
  36.4 0.0 collective-permute-done.4.rest_1_
  36.4 0.0 collective-permute-start.9
  36.4 0.0 collective-permute-done.8.refs_2_
  36.4 0.0 collective-permute-done.7.refs_1_
  36.4 5.5 %attention.6 = (bf16[32,2176]{1,0:T(8,128)(2,1)S(1)}, bf16[32,2176]{1,0:T(8,128)(2,1)S(1)}) custom-call(s32[8]{0:T(128)S(1)} %copy-done.8, s32[2,24]{1,0:T(2,128)S(1)} %bitcast.8, s32[2]{0:T(128)S(1)} %bitcast.12, bf16[32,256]{1,0:T(8,128)(2,1)S(1)} %copy-done.3, bf16[32,256]{1,0:T(8,128)(2,1)S(1)} %copy-done.4, bf16[4096,256]{1,0:T(8,128)(2,1)S(1)} %copy-done.2, ...), custom_call_target="tpu_custom_call" | custom-call | flops 3221225472 | bytes 8388608 | tf_op jit(solution)/shard_map/attention/pallas_call | solution.py:216
  41.9 1.3 %collective-permute-start.13 = (bf16[32,2176]{1,0:T(8,128)(2,1)S(1)}, bf16[32,2176]{1,0:T(8,128)(2,1)S(1)}, u32[]{:S(2)}, u32[]{:S(2)}) collective-permute-start(bf16[32,2176]{1,0:T(8,128)(2,1)S(1)} %get-tuple-element.49), channel_id=1, source_target_pairs={{0,20},{4,16},{8,28},{12,24},{16,4},{20,0},{24,12},{28,8},{1,21},{... | collective-permute-start | bytes 417800 | tf_op jit(solution)/shard_map/ppermute | solution.py:360
  43.2 2.6 %collective-permute-start.10 = (bf16[32,2176]{1,0:T(8,128)(2,1)S(1)}, bf16[32,2176]{1,0:T(8,128)(2,1)S(1)}, u32[]{:S(2)}, u32[]{:S(2)}) collective-permute-start(bf16[32,2176]{1,0:T(8,128)(2,1)S(1)} %get-tuple-element.55), channel_id=1, source_target_pairs={{0,4},{4,0},{8,12},{12,8},{16,20},{20,16},{24,28},{28,24},{1,5},{5... | collective-permute-start | bytes 417800 | tf_op jit(solution)/shard_map/ppermute | solution.py:360
  45.8 0.0 copy-done.5
  45.8 3.6 %attention.7.refs_0_ = bf16[32,2176]{1,0:T(8,128)(2,1)S(1)} custom-call(s32[8]{0:T(128)S(1)} %copy-done.8, s32[2,24]{1,0:T(2,128)S(1)} %bitcast.9, s32[2]{0:T(128)S(1)} %bitcast.13, bf16[32,256]{1,0:T(8,128)(2,1)S(1)} %copy-done.3, bf16[32,256]{1,0:T(8,128)(2,1)S(1)} %copy-done.4, bf16[4096,256]{1,0:T(8,128)(2,1)S(1)} %copy-done.2, ...), custom_call_target="tpu_custom_call" | custom-call | flops 1610612736 | bytes 8388608 | tf_op jit(solution)/shard_map/attention/pallas_call | solution.py:216
  49.4 0.0 collective-permute-done.11.refs_5_
  49.4 0.0 collective-permute-done.12.refs_6_
  49.4 0.0 collective-permute-done.9.refs_3_
  49.4 0.4 collective-permute-done.10.refs_4_
  49.8 0.5 collective-permute-done.13.refs_7_
  50.3 0.9 %merge.1.rest_0_ = bf16[32,2048]{1,0:T(8,128)(2,1)S(1)} custom-call(bf16[32,2176]{1,0:T(8,128)(2,1)S(1)} %attention.7.refs_0_, bf16[32,2176]{1,0:T(8,128)(2,1)S(1)} %collective-permute-done.7.refs_1_, bf16[32,2176]{1,0:T(8,128)(2,1)S(1)} %collective-permute-done.8.refs_2_, bf16[32,2176]{1,0:T(8,128)(2,1)S(1)} %collective-permute-done.9.refs_3_, ...), custom_call_target="tpu_custom_call" | custom-call | flops 1114112 | bytes 1114112 | tf_op jit(solution)/shard_map/merge/pallas_call | solution.py:276
  51.2 0.2 collective-permute-start.15
  51.5 3.6 %collective-permute-start.14 = (bf16[32,2048]{1,0:T(8,128)(2,1)S(1)}, bf16[32,2048]{1,0:T(8,128)(2,1)S(1)}, u32[]{:S(2)}, u32[]{:S(2)}) collective-permute-start(bf16[32,2048]{1,0:T(8,128)(2,1)S(1)} %merge.1.rest_0_), channel_id=1, source_target_pairs={{0,24},{4,28},{8,0},{12,4},{16,8},{20,12},{24,16},{28,20},{1,25},{... | collective-permute-start | bytes 393224 | tf_op jit(solution)/shard_map/ppermute | solution.py:360
  55.1 0.1 collective-permute-start.16
  55.2 2.9 %collective-permute-done.15.rest_2_ = bf16[32,2048]{1,0:T(8,128)(2,1)S(1)} collective-permute-done((bf16[32,2048]{1,0:T(8,128)(2,1)S(1)}, bf16[32,2048]{1,0:T(8,128)(2,1)S(1)}, u32[]{:S(2)}, u32[]{:S(2)}) %collective-permute-start.15) | collective-permute-done | bytes 131104 | tf_op jit(solution)/shard_map/ppermute | solution.py:360
  58.1 2.2 %collective-permute-start.19 = (bf16[32,2048]{1,0:T(8,128)(2,1)S(1)}, bf16[32,2048]{1,0:T(8,128)(2,1)S(1)}, u32[]{:S(2)}, u32[]{:S(2)}) collective-permute-start(bf16[32,2048]{1,0:T(8,128)(2,1)S(1)} %collective-permute-done.15.rest_2_), channel_id=1, source_target_pairs={{0,4},{4,0},{8,12},{12,8},{16,20},{20,16},{24,28},{28,24},{1,5},{5... | collective-permute-start | bytes 393224 | tf_op jit(solution)/shard_map/ppermute | solution.py:360
  60.2 0.0 collective-permute-start.17
  60.3 0.0 collective-permute-done.14.rest_1_
  60.3 2.0 %collective-permute-start.18 = (bf16[32,2048]{1,0:T(8,128)(2,1)S(1)}, bf16[32,2048]{1,0:T(8,128)(2,1)S(1)}, u32[]{:S(2)}, u32[]{:S(2)}) collective-permute-start(bf16[32,2048]{1,0:T(8,128)(2,1)S(1)} %collective-permute-done.14.rest_1_), channel_id=1, source_target_pairs={{0,4},{4,0},{8,12},{12,8},{16,20},{20,16},{24,28},{28,24},{1,5},{5... | collective-permute-start | bytes 393224 | tf_op jit(solution)/shard_map/ppermute | solution.py:360
  62.3 0.8 %collective-permute-done.16.rest_3_ = bf16[32,2048]{1,0:T(8,128)(2,1)S(1)} collective-permute-done((bf16[32,2048]{1,0:T(8,128)(2,1)S(1)}, bf16[32,2048]{1,0:T(8,128)(2,1)S(1)}, u32[]{:S(2)}, u32[]{:S(2)}) %collective-permute-start.16) | collective-permute-done | bytes 131104 | tf_op jit(solution)/shard_map/ppermute | solution.py:360
  63.1 1.1 %collective-permute-done.19.rest_6_ = bf16[32,2048]{1,0:T(8,128)(2,1)S(1)} collective-permute-done((bf16[32,2048]{1,0:T(8,128)(2,1)S(1)}, bf16[32,2048]{1,0:T(8,128)(2,1)S(1)}, u32[]{:S(2)}, u32[]{:S(2)}) %collective-permute-start.19) | collective-permute-done | bytes 131104 | tf_op jit(solution)/shard_map/ppermute | solution.py:360
  64.2 2.2 %collective-permute-start.20 = (bf16[32,2048]{1,0:T(8,128)(2,1)S(1)}, bf16[32,2048]{1,0:T(8,128)(2,1)S(1)}, u32[]{:S(2)}, u32[]{:S(2)}) collective-permute-start(bf16[32,2048]{1,0:T(8,128)(2,1)S(1)} %collective-permute-done.16.rest_3_), channel_id=1, source_target_pairs={{0,4},{4,0},{8,12},{12,8},{16,20},{20,16},{24,28},{28,24},{1,5},{5... | collective-permute-start | bytes 393224 | tf_op jit(solution)/shard_map/ppermute | solution.py:360
  66.4 0.0 collective-permute-done.17.rest_4_
  66.4 1.0 %collective-permute-done.18.rest_5_ = bf16[32,2048]{1,0:T(8,128)(2,1)S(1)} collective-permute-done((bf16[32,2048]{1,0:T(8,128)(2,1)S(1)}, bf16[32,2048]{1,0:T(8,128)(2,1)S(1)}, u32[]{:S(2)}, u32[]{:S(2)}) %collective-permute-start.18) | collective-permute-done | bytes 131104 | tf_op jit(solution)/shard_map/ppermute | solution.py:360
  67.4 2.0 %collective-permute-done.20.rest_7_ = bf16[32,2048]{1,0:T(8,128)(2,1)S(1)} collective-permute-done((bf16[32,2048]{1,0:T(8,128)(2,1)S(1)}, bf16[32,2048]{1,0:T(8,128)(2,1)S(1)}, u32[]{:S(2)}, u32[]{:S(2)}) %collective-permute-start.20) | collective-permute-done | bytes 131104 | tf_op jit(solution)/shard_map/ppermute | solution.py:360
  69.4 1.4 %projection.1 = (f32[2,64,1024]{2,1,0:T(8,128)S(1)}, bf16[2,64,1024]{2,1,0:T(8,128)(2,1)S(1)}) custom-call(bf16[2048,1024]{1,0:T(8,128)(2,1)S(1)} %copy-done, bf16[32,2048]{1,0:T(8,128)(2,1)S(1)} %merge.1.rest_0_, bf16[32,2048]{1,0:T(8,128)(2,1)S(1)} %collective-permute-done.14.rest_1_, bf16[32,2048]{1,0:T(8,128)(2,1)S(1)} %collective-permute-done.15.rest_2_, ...), custom_call_target="tpu_custom_call" | custom-call | flops 1073741824 | bytes 4194304 | tf_op jit(solution)/shard_map/projection/pallas_call | solution.py:318
  70.8 0.1 collective-permute-start.21
  70.8 1.5 %collective-permute-done.21 = bf16[2,64,1024]{2,1,0:T(8,128)(2,1)S(1)} collective-permute-done((bf16[2,64,1024]{2,1,0:T(8,128)(2,1)S(1)}, bf16[2,64,1024]{2,1,0:T(8,128)(2,1)S(1)}, u32[]{:S(2)}, u32[]{:S(2)}) %collective-permute-start.21) | collective-permute-done | bytes 262176 | tf_op jit(solution)/shard_map/ppermute | solution.py:435
  72.4 2.0 %collective-permute-start.22 = (bf16[64,1024]{1,0:T(8,128)(2,1)S(1)}, bf16[64,1024]{1,0:T(8,128)(2,1)S(1)}, u32[]{:S(2)}, u32[]{:S(2)}) collective-permute-start(bf16[64,1024]{1,0:T(8,128)(2,1)S(1)} %fusion), channel_id=1, source_target_pairs={{0,2},{1,3},{2,0},{3,1},{4,6},{5,7},{6,4},{7,5},{8,10},{9,11},{10,... | collective-permute-start | bytes 393224 | tf_op jit(solution)/shard_map/ppermute | solution.py:439
  74.4 3.8 %collective-permute-done.22 = bf16[64,1024]{1,0:T(8,128)(2,1)S(1)} collective-permute-done((bf16[64,1024]{1,0:T(8,128)(2,1)S(1)}, bf16[64,1024]{1,0:T(8,128)(2,1)S(1)}, u32[]{:S(2)}, u32[]{:S(2)}) %collective-permute-start.22) | collective-permute-done | bytes 131104 | tf_op jit(solution)/shard_map/ppermute | solution.py:439
  78.2 0.7 bitcast_add_fusion
  (11 shorter events, 0.0 us)
Async XLA Ops:
  0.0 14.5 %copy-start.3 = (bf16[32,256]{1,0:T(8,128)(2,1)S(1)}, bf16[32,256]{1,0:T(8,128)(2,1)}, u32[]{:S(2)}) copy-start(bf16[32,256]{1,0:T(8,128)(2,1)} %nk_ref.7) | copy-start | bytes 49156
  0.0 14.5 %copy-start.4 = (bf16[32,256]{1,0:T(8,128)(2,1)S(1)}, bf16[32,256]{1,0:T(8,128)(2,1)}, u32[]{:S(2)}) copy-start(bf16[32,256]{1,0:T(8,128)(2,1)} %nv_ref.7) | copy-start | bytes 49156
  0.0 14.5 %copy-start.2 = (bf16[4096,256]{1,0:T(8,128)(2,1)S(1)}, bf16[4096,256]{1,0:T(8,128)(2,1)}, u32[]{:S(2)}) copy-start(bf16[4096,256]{1,0:T(8,128)(2,1)} %k_ref.7) | copy-start | bytes 6291460
  0.0 14.5 %copy-start.1 = (bf16[4096,256]{1,0:T(8,128)(2,1)S(1)}, bf16[4096,256]{1,0:T(8,128)(2,1)}, u32[]{:S(2)}) copy-start(bf16[4096,256]{1,0:T(8,128)(2,1)} %v_ref.1) | copy-start | bytes 6291460
  0.0 14.5 %copy-start.7 = (s32[1,2,24]{2,1,0:T(2,128)S(1)}, s32[1,2,24]{2,1,0:T(2,128)}, u32[]{:S(2)}) copy-start(s32[1,2,24]{2,1,0:T(2,128)} %param.14) | copy-start | bytes 580
  0.0 14.5 %copy-start.9 = (s32[1,2]{1,0:T(1,128)S(1)}, s32[1,2]{1,0:T(1,128)}, u32[]{:S(2)}) copy-start(s32[1,2]{1,0:T(1,128)} %param.15) | copy-start | bytes 28
  0.0 14.5 %copy-start.8 = (s32[8]{0:T(128)S(1)}, s32[8]{0:T(128)}, u32[]{:S(2)}) copy-start(s32[8]{0:T(128)} %slot_ref.7) | copy-start | bytes 100
  0.0 9.3 %collective-permute-start = (bf16[32,2048]{1,0:T(8,128)(2,1)}, bf16[32,2048]{1,0:T(8,128)(2,1)S(1)}, u32[]{:S(2)}, u32[]{:S(2)}) collective-permute-start(bf16[32,2048]{1,0:T(8,128)(2,1)} %rest_0_), channel_id=1, source_target_pairs={{0,24},{4,28},{8,0},{12,4},{16,8},{20,12},{24,16},{28,20},{1,25},{... | collective-permute-start | bytes 393224 | tf_op jit(solution)/shard_map/ppermute | solution.py:360
  5.2 7.0 %collective-permute-start.1 = (bf16[32,2048]{1,0:T(8,128)(2,1)}, bf16[32,2048]{1,0:T(8,128)(2,1)S(1)}, u32[]{:S(2)}, u32[]{:S(2)}) collective-permute-start(bf16[32,2048]{1,0:T(8,128)(2,1)} %rest_0_), channel_id=1, source_target_pairs={{0,8},{4,12},{8,16},{12,20},{16,24},{20,28},{24,0},{28,4},{1,9},{5... | collective-permute-start | bytes 393224 | tf_op jit(solution)/shard_map/ppermute | solution.py:360
  5.2 26.6 %collective-permute-start.2 = (bf16[32,2048]{1,0:T(8,128)(2,1)}, bf16[32,2048]{1,0:T(8,128)(2,1)S(1)}, u32[]{:S(2)}, u32[]{:S(2)}) collective-permute-start(bf16[32,2048]{1,0:T(8,128)(2,1)} %rest_0_), channel_id=1, source_target_pairs={{0,4},{4,0},{8,12},{12,8},{16,20},{20,16},{24,28},{28,24},{1,5},{5... | collective-permute-start | bytes 393224 | tf_op jit(solution)/shard_map/ppermute | solution.py:360
  12.1 10.4 %collective-permute-start.5 = (bf16[32,2048]{1,0:T(8,128)(2,1)S(1)}, bf16[32,2048]{1,0:T(8,128)(2,1)S(1)}, u32[]{:S(2)}, u32[]{:S(2)}) collective-permute-start(bf16[32,2048]{1,0:T(8,128)(2,1)S(1)} %collective-permute-done.rest_0_), channel_id=1, source_target_pairs={{0,4},{4,0},{8,12},{12,8},{16,20},{20,16},{24,28},{28,24},{1,5},{5... | collective-permute-start | bytes 393224 | tf_op jit(solution)/shard_map/ppermute | solution.py:360
  13.6 8.9 %collective-permute-start.6 = (bf16[32,2048]{1,0:T(8,128)(2,1)S(1)}, bf16[32,2048]{1,0:T(8,128)(2,1)S(1)}, u32[]{:S(2)}, u32[]{:S(2)}) collective-permute-start(bf16[32,2048]{1,0:T(8,128)(2,1)S(1)} %collective-permute-done.1.rest_1_), channel_id=1, source_target_pairs={{0,4},{4,0},{8,12},{12,8},{16,20},{20,16},{24,28},{28,24},{1,5},{5... | collective-permute-start | bytes 393224 | tf_op jit(solution)/shard_map/ppermute | solution.py:360
  14.2 8.4 %collective-permute-start.3 = (bf16[32,2048]{1,0:T(8,128)(2,1)}, bf16[32,2048]{1,0:T(8,128)(2,1)S(1)}, u32[]{:S(2)}, u32[]{:S(2)}) collective-permute-start(bf16[32,2048]{1,0:T(8,128)(2,1)} %rest_0_), channel_id=1, source_target_pairs={{0,16},{4,20},{8,24},{12,28},{16,0},{20,4},{24,8},{28,12},{1,17},{... | collective-permute-start | bytes 393224 | tf_op jit(solution)/shard_map/ppermute | solution.py:360
  20.1 16.2 %collective-permute-start.8 = (bf16[32,2176]{1,0:T(8,128)(2,1)S(1)}, bf16[32,2176]{1,0:T(8,128)(2,1)S(1)}, u32[]{:S(2)}, u32[]{:S(2)}) collective-permute-start(bf16[32,2176]{1,0:T(8,128)(2,1)S(1)} %get-tuple-element.39), channel_id=1, source_target_pairs={{0,24},{4,28},{8,0},{12,4},{16,8},{20,12},{24,16},{28,20},{1,25},{... | collective-permute-start | bytes 417800 | tf_op jit(solution)/shard_map/ppermute | solution.py:360
  22.5 13.9 %collective-permute-start.7 = (bf16[32,2176]{1,0:T(8,128)(2,1)S(1)}, bf16[32,2176]{1,0:T(8,128)(2,1)S(1)}, u32[]{:S(2)}, u32[]{:S(2)}) collective-permute-start(bf16[32,2176]{1,0:T(8,128)(2,1)S(1)} %get-tuple-element.46), channel_id=1, source_target_pairs={{0,8},{4,12},{8,16},{12,20},{16,24},{20,28},{24,0},{28,4},{1,9},{5... | collective-permute-start | bytes 417800 | tf_op jit(solution)/shard_map/ppermute | solution.py:360
  22.5 13.8 %collective-permute-start.4 = (bf16[32,2048]{1,0:T(8,128)(2,1)S(1)}, bf16[32,2048]{1,0:T(8,128)(2,1)S(1)}, u32[]{:S(2)}, u32[]{:S(2)}) collective-permute-start(bf16[32,2048]{1,0:T(8,128)(2,1)S(1)} %collective-permute-done.3.rest_0_), channel_id=1, source_target_pairs={{0,4},{4,0},{8,12},{12,8},{16,20},{20,16},{24,28},{28,24},{1,5},{5... | collective-permute-start | bytes 393224 | tf_op jit(solution)/shard_map/ppermute | solution.py:360
  31.6 17.8 %collective-permute-start.11 = (bf16[32,2176]{1,0:T(8,128)(2,1)S(1)}, bf16[32,2176]{1,0:T(8,128)(2,1)S(1)}, u32[]{:S(2)}, u32[]{:S(2)}) collective-permute-start(bf16[32,2176]{1,0:T(8,128)(2,1)S(1)} %get-tuple-element.56), channel_id=1, source_target_pairs={{0,12},{4,8},{8,20},{12,16},{16,28},{20,24},{24,4},{28,0},{1,13},{... | collective-permute-start | bytes 417800 | tf_op jit(solution)/shard_map/ppermute | solution.py:360
  31.8 17.7 %collective-permute-start.12 = (bf16[32,2176]{1,0:T(8,128)(2,1)S(1)}, bf16[32,2176]{1,0:T(8,128)(2,1)S(1)}, u32[]{:S(2)}, u32[]{:S(2)}) collective-permute-start(bf16[32,2176]{1,0:T(8,128)(2,1)S(1)} %get-tuple-element.43), channel_id=1, source_target_pairs={{0,28},{4,24},{8,4},{12,0},{16,12},{20,8},{24,20},{28,16},{1,29},{... | collective-permute-start | bytes 417800 | tf_op jit(solution)/shard_map/ppermute | solution.py:360
  36.4 9.4 %copy-start.5 = (f32[8,128]{1,0:T(8,128)S(1)}, f32[8,128]{1,0:T(8,128)}, u32[]{:S(2)}) copy-start(f32[8,128]{1,0:T(8,128)} %settle.1.rest_1_) | copy-start | bytes 12292
  36.4 9.4 %copy-start.6 = (bf16[32,2048]{1,0:T(8,128)(2,1)S(1)}, bf16[32,2048]{1,0:T(8,128)(2,1)}, u32[]{:S(2)}) copy-start(bf16[32,2048]{1,0:T(8,128)(2,1)} %rest_0_) | copy-start | bytes 393220
  36.4 13.1 %collective-permute-start.9 = (bf16[32,2176]{1,0:T(8,128)(2,1)S(1)}, bf16[32,2176]{1,0:T(8,128)(2,1)S(1)}, u32[]{:S(2)}, u32[]{:S(2)}) collective-permute-start(bf16[32,2176]{1,0:T(8,128)(2,1)S(1)} %get-tuple-element.54), channel_id=1, source_target_pairs={{0,16},{4,20},{8,24},{12,28},{16,0},{20,4},{24,8},{28,12},{1,17},{... | collective-permute-start | bytes 417800 | tf_op jit(solution)/shard_map/ppermute | solution.py:360
  41.9 8.4 %collective-permute-start.13 = (bf16[32,2176]{1,0:T(8,128)(2,1)S(1)}, bf16[32,2176]{1,0:T(8,128)(2,1)S(1)}, u32[]{:S(2)}, u32[]{:S(2)}) collective-permute-start(bf16[32,2176]{1,0:T(8,128)(2,1)S(1)} %get-tuple-element.49), channel_id=1, source_target_pairs={{0,20},{4,16},{8,28},{12,24},{16,4},{20,0},{24,12},{28,8},{1,21},{... | collective-permute-start | bytes 417800 | tf_op jit(solution)/shard_map/ppermute | solution.py:360
  43.2 6.6 %collective-permute-start.10 = (bf16[32,2176]{1,0:T(8,128)(2,1)S(1)}, bf16[32,2176]{1,0:T(8,128)(2,1)S(1)}, u32[]{:S(2)}, u32[]{:S(2)}) collective-permute-start(bf16[32,2176]{1,0:T(8,128)(2,1)S(1)} %get-tuple-element.55), channel_id=1, source_target_pairs={{0,4},{4,0},{8,12},{12,8},{16,20},{20,16},{24,28},{28,24},{1,5},{5... | collective-permute-start | bytes 417800 | tf_op jit(solution)/shard_map/ppermute | solution.py:360
  45.8 23.6 %copy-start = (bf16[2048,1024]{1,0:T(8,128)(2,1)S(1)}, bf16[2048,1024]{1,0:T(8,128)(2,1)}, u32[]{:S(2)}) copy-start(bf16[2048,1024]{1,0:T(8,128)(2,1)} %w_ref.1) | copy-start | bytes 12582916
  51.2 6.8 %collective-permute-start.15 = (bf16[32,2048]{1,0:T(8,128)(2,1)S(1)}, bf16[32,2048]{1,0:T(8,128)(2,1)S(1)}, u32[]{:S(2)}, u32[]{:S(2)}) collective-permute-start(bf16[32,2048]{1,0:T(8,128)(2,1)S(1)} %merge.1.rest_0_), channel_id=1, source_target_pairs={{0,8},{4,12},{8,16},{12,20},{16,24},{20,28},{24,0},{28,4},{1,9},{5... | collective-permute-start | bytes 393224 | tf_op jit(solution)/shard_map/ppermute | solution.py:360
  51.5 8.8 %collective-permute-start.14 = (bf16[32,2048]{1,0:T(8,128)(2,1)S(1)}, bf16[32,2048]{1,0:T(8,128)(2,1)S(1)}, u32[]{:S(2)}, u32[]{:S(2)}) collective-permute-start(bf16[32,2048]{1,0:T(8,128)(2,1)S(1)} %merge.1.rest_0_), channel_id=1, source_target_pairs={{0,24},{4,28},{8,0},{12,4},{16,8},{20,12},{24,16},{28,20},{1,25},{... | collective-permute-start | bytes 393224 | tf_op jit(solution)/shard_map/ppermute | solution.py:360
  55.1 8.0 %collective-permute-start.16 = (bf16[32,2048]{1,0:T(8,128)(2,1)S(1)}, bf16[32,2048]{1,0:T(8,128)(2,1)S(1)}, u32[]{:S(2)}, u32[]{:S(2)}) collective-permute-start(bf16[32,2048]{1,0:T(8,128)(2,1)S(1)} %merge.1.rest_0_), channel_id=1, source_target_pairs={{0,16},{4,20},{8,24},{12,28},{16,0},{20,4},{24,8},{28,12},{1,17},{... | collective-permute-start | bytes 393224 | tf_op jit(solution)/shard_map/ppermute | solution.py:360
  58.1 6.1 %collective-permute-start.19 = (bf16[32,2048]{1,0:T(8,128)(2,1)S(1)}, bf16[32,2048]{1,0:T(8,128)(2,1)S(1)}, u32[]{:S(2)}, u32[]{:S(2)}) collective-permute-start(bf16[32,2048]{1,0:T(8,128)(2,1)S(1)} %collective-permute-done.15.rest_2_), channel_id=1, source_target_pairs={{0,4},{4,0},{8,12},{12,8},{16,20},{20,16},{24,28},{28,24},{1,5},{5... | collective-permute-start | bytes 393224 | tf_op jit(solution)/shard_map/ppermute | solution.py:360
  60.2 6.2 %collective-permute-start.17 = (bf16[32,2048]{1,0:T(8,128)(2,1)S(1)}, bf16[32,2048]{1,0:T(8,128)(2,1)S(1)}, u32[]{:S(2)}, u32[]{:S(2)}) collective-permute-start(bf16[32,2048]{1,0:T(8,128)(2,1)S(1)} %merge.1.rest_0_), channel_id=1, source_target_pairs={{0,4},{4,0},{8,12},{12,8},{16,20},{20,16},{24,28},{28,24},{1,5},{5... | collective-permute-start | bytes 393224 | tf_op jit(solution)/shard_map/ppermute | solution.py:360
  60.3 7.1 %collective-permute-start.18 = (bf16[32,2048]{1,0:T(8,128)(2,1)S(1)}, bf16[32,2048]{1,0:T(8,128)(2,1)S(1)}, u32[]{:S(2)}, u32[]{:S(2)}) collective-permute-start(bf16[32,2048]{1,0:T(8,128)(2,1)S(1)} %collective-permute-done.14.rest_1_), channel_id=1, source_target_pairs={{0,4},{4,0},{8,12},{12,8},{16,20},{20,16},{24,28},{28,24},{1,5},{5... | collective-permute-start | bytes 393224 | tf_op jit(solution)/shard_map/ppermute | solution.py:360
  64.2 5.2 %collective-permute-start.20 = (bf16[32,2048]{1,0:T(8,128)(2,1)S(1)}, bf16[32,2048]{1,0:T(8,128)(2,1)S(1)}, u32[]{:S(2)}, u32[]{:S(2)}) collective-permute-start(bf16[32,2048]{1,0:T(8,128)(2,1)S(1)} %collective-permute-done.16.rest_3_), channel_id=1, source_target_pairs={{0,4},{4,0},{8,12},{12,8},{16,20},{20,16},{24,28},{28,24},{1,5},{5... | collective-permute-start | bytes 393224 | tf_op jit(solution)/shard_map/ppermute | solution.py:360
  70.8 1.6 %collective-permute-start.21 = (bf16[2,64,1024]{2,1,0:T(8,128)(2,1)S(1)}, bf16[2,64,1024]{2,1,0:T(8,128)(2,1)S(1)}, u32[]{:S(2)}, u32[]{:S(2)}) collective-permute-start(bf16[2,64,1024]{2,1,0:T(8,128)(2,1)S(1)} %get-tuple-element.60), channel_id=1, source_target_pairs={{0,1},{1,0},{2,3},{3,2},{4,5},{5,4},{6,7},{7,6},{8,9},{9,8},{10,11... | collective-permute-start | bytes 786440 | tf_op jit(solution)/shard_map/ppermute | solution.py:435
  72.4 5.8 %collective-permute-start.22 = (bf16[64,1024]{1,0:T(8,128)(2,1)S(1)}, bf16[64,1024]{1,0:T(8,128)(2,1)S(1)}, u32[]{:S(2)}, u32[]{:S(2)}) collective-permute-start(bf16[64,1024]{1,0:T(8,128)(2,1)S(1)} %fusion), channel_id=1, source_target_pairs={{0,2},{1,3},{2,0},{3,1},{4,6},{5,7},{6,4},{7,5},{8,10},{9,11},{10,... | collective-permute-start | bytes 393224 | tf_op jit(solution)/shard_map/ppermute | solution.py:439

commit v11 on v10

--- a/solution.py
+++ b/solution.py
@@ -374,6 +374,8 @@
         behind = None
         for k in steps:
             block = held[k, 0]
+            if chained and behind is None:
+                block, held[0, 1] = lax.optimization_barrier((block, held[0, 1]))
             if chained and 2 * k == high and behind is not None:
                 block, held[behind] = lax.optimization_barrier((block, held[behind]))
             held[k, 1] = move(block, 0, 1)

time: 79.5 us -> 80.3 us (1.010)
  waiting for transfers between devices: 18.9 us -> 27.2 us
  Pallas kernels: 25 us -> 18.9 us
  starting transfers between devices: 34 us -> 32.8 us
    ppermute x21, waiting for transfers between devices: 13.6 us -> 21.9 us  [move(): return lax.ppermute(x, 'ctx', pairs)]
    pallas_call x4, Pallas kernels: 22.1 us -> 16 us  [attention_call(): pl.pallas_call(functools.partial(attention_kernel, members, ctx_count, gr...]
    ppermute x21, starting transfers between devices: 32 us -> 30.9 us  [move(): return lax.ppermute(x, 'ctx', pairs)]
  transfers between devices with their start and end apart: 23 -> 23, of which waited for: 11 -> 12; matrix products, arithmetic and copies ran while one was open for 0% -> 0% of each run, Pallas kernels for 29% -> 21%
where the time goes in v11:
time: 80.3 us; the launch traced here: 79.9 us
  starting transfers between devices  32.8 us (41%)
  waiting for transfers between devices  27.2 us (34%)
  Pallas kernels  18.9 us (24%)
    ppermute x21, starting transfers between devices, move(): return lax.ppermute(x, 'ctx', pairs)  30.9 us
    ppermute x21, waiting for transfers between devices, move(): return lax.ppermute(x, 'ctx', pairs)  21.9 us
    pallas_call x4, Pallas kernels, attention_call(): pl.pallas_call(functools.partial(attention_kernel, members, ctx_count, gr...  16 us
    ppermute x1, waiting for transfers between devices, body(): piece = lax.ppermute(piece, 'tp', [(i, i ^ 2 * j) for i in range(peers)])  3.85 us
    ppermute x1, starting transfers between devices, body(): piece = lax.ppermute(piece, 'tp', [(i, i ^ 2 * j) for i in range(peers)])  1.75 us
  transfers between devices with their start and end apart: 23, of which 12 were waited for; matrix products, arithmetic and copies ran while one was open for 0% of the time, Pallas kernels for 21%

profile of v11, /device:TPU:0, one launch (start us, length us, event | category | flops | bytes accessed | tf_op | source)
XLA Modules:
  0.0 79.9 jit_solution(1087949748201199632)
XLA Ops:
  0.0 0.0 copy-start.9
  0.0 0.0 copy-start.8
  0.0 5.1 %collective-permute-start = (bf16[32,2048]{1,0:T(8,128)(2,1)}, bf16[32,2048]{1,0:T(8,128)(2,1)S(1)}, u32[]{:S(2)}, u32[]{:S(2)}) collective-permute-start(bf16[32,2048]{1,0:T(8,128)(2,1)} %rest_0_), channel_id=1, source_target_pairs={{0,24},{4,28},{8,0},{12,4},{16,8},{20,12},{24,16},{28,20},{1,25},{... | collective-permute-start | bytes 393224 | tf_op jit(solution)/shard_map/ppermute | solution.py:360
  5.2 0.0 collective-permute-start.1
  5.2 1.5 %collective-permute-start.2 = (bf16[32,2048]{1,0:T(8,128)(2,1)}, bf16[32,2048]{1,0:T(8,128)(2,1)S(1)}, u32[]{:S(2)}, u32[]{:S(2)}) collective-permute-start(bf16[32,2048]{1,0:T(8,128)(2,1)} %rest_0_), channel_id=1, source_target_pairs={{0,4},{4,0},{8,12},{12,8},{16,20},{20,16},{24,28},{28,24},{1,5},{5... | collective-permute-start | bytes 393224 | tf_op jit(solution)/shard_map/ppermute | solution.py:360
  6.6 0.6 settle.1.rest_1_
  7.2 2.1 %collective-permute-done.rest_0_ = bf16[32,2048]{1,0:T(8,128)(2,1)S(1)} collective-permute-done((bf16[32,2048]{1,0:T(8,128)(2,1)}, bf16[32,2048]{1,0:T(8,128)(2,1)S(1)}, u32[]{:S(2)}, u32[]{:S(2)}) %collective-permute-start) | collective-permute-done | bytes 131104 | tf_op jit(solution)/shard_map/ppermute | solution.py:360
  9.4 2.8 %collective-permute-done.1.rest_1_ = bf16[32,2048]{1,0:T(8,128)(2,1)S(1)} collective-permute-done((bf16[32,2048]{1,0:T(8,128)(2,1)}, bf16[32,2048]{1,0:T(8,128)(2,1)S(1)}, u32[]{:S(2)}, u32[]{:S(2)}) %collective-permute-start.1) | collective-permute-done | bytes 131104 | tf_op jit(solution)/shard_map/ppermute | solution.py:360
  12.1 1.5 %collective-permute-start.5 = (bf16[32,2048]{1,0:T(8,128)(2,1)S(1)}, bf16[32,2048]{1,0:T(8,128)(2,1)S(1)}, u32[]{:S(2)}, u32[]{:S(2)}) collective-permute-start(bf16[32,2048]{1,0:T(8,128)(2,1)S(1)} %collective-permute-done.rest_0_), channel_id=1, source_target_pairs={{0,4},{4,0},{8,12},{12,8},{16,20},{20,16},{24,28},{28,24},{1,5},{5... | collective-permute-start | bytes 393224 | tf_op jit(solution)/shard_map/ppermute | solution.py:360
  13.6 0.5 collective-permute-start.6
  14.2 0.4 collective-permute-start.3
  14.5 0.0 copy-done.3
  14.5 0.0 copy-done.4
  14.5 0.0 copy-done.2
  14.5 0.0 copy-done.1
  14.5 0.0 copy-done.7
  14.6 0.0 copy-done.9
  14.6 0.0 copy-done.8
  14.6 4.0 %attention.4 = (bf16[32,2176]{1,0:T(8,128)(2,1)S(1)}, bf16[32,2176]{1,0:T(8,128)(2,1)S(1)}, bf16[2,144,3200]{2,1,0:T(8,128)(2,1)S(1)}) custom-call(s32[8]{0:T(128)S(1)} %copy-done.8, s32[2,24]{1,0:T(2,128)S(1)} %bitcast.6, s32[2]{0:T(128)S(1)} %bitcast.10, bf16[32,256]{1,0:T(8,128)(2,1)S(1)} %copy-done.3, bf16[32,256]{1,0:T(8,128)(2,1)S(1)} %copy-done.4, ...), custom_call_target="tpu_custom_call" | custom-call | flops 3221225472 | bytes 8388608 | tf_op jit(solution)/shard_map/attention/pallas_call | solution.py:216
  18.6 3.4 %collective-permute-start.8 = (bf16[32,2176]{1,0:T(8,128)(2,1)S(1)}, bf16[32,2176]{1,0:T(8,128)(2,1)S(1)}, u32[]{:S(2)}, u32[]{:S(2)}) collective-permute-start(bf16[32,2176]{1,0:T(8,128)(2,1)S(1)} %get-tuple-element.41), channel_id=1, source_target_pairs={{0,24},{4,28},{8,0},{12,4},{16,8},{20,12},{24,16},{28,20},{1,25},{... | collective-permute-start | bytes 417800 | tf_op jit(solution)/shard_map/ppermute | solution.py:360
  22.0 0.2 collective-permute-done.3.rest_0_
  22.1 0.0 collective-permute-start.7
  22.1 0.0 collective-permute-done.5.rest_1_
  22.1 0.0 collective-permute-done.6.rest_2_
  22.1 2.0 %collective-permute-start.4 = (bf16[32,2048]{1,0:T(8,128)(2,1)S(1)}, bf16[32,2048]{1,0:T(8,128)(2,1)S(1)}, u32[]{:S(2)}, u32[]{:S(2)}) collective-permute-start(bf16[32,2048]{1,0:T(8,128)(2,1)S(1)} %collective-permute-done.3.rest_0_), channel_id=1, source_target_pairs={{0,4},{4,0},{8,12},{12,8},{16,20},{20,16},{24,28},{28,24},{1,5},{5... | collective-permute-start | bytes 393224 | tf_op jit(solution)/shard_map/ppermute | solution.py:360
  24.1 5.4 %attention.5 = (bf16[32,2176]{1,0:T(8,128)(2,1)S(1)}, bf16[32,2176]{1,0:T(8,128)(2,1)S(1)}, bf16[32,2176]{1,0:T(8,128)(2,1)S(1)}) custom-call(s32[8]{0:T(128)S(1)} %copy-done.8, s32[2,24]{1,0:T(2,128)S(1)} %bitcast.7, s32[2]{0:T(128)S(1)} %bitcast.11, bf16[32,256]{1,0:T(8,128)(2,1)S(1)} %copy-done.3, bf16[32,256]{1,0:T(8,128)(2,1)S(1)} %copy-done.4, ...), custom_call_target="tpu_custom_call" | custom-call | flops 4831838208 | bytes 8388608 | tf_op jit(solution)/shard_map/attention/pallas_call | solution.py:216
  29.5 0.1 collective-permute-start.11
  29.6 0.0 collective-permute-done.2.rest_0_
  29.6 4.7 %collective-permute-start.12 = (bf16[32,2176]{1,0:T(8,128)(2,1)S(1)}, bf16[32,2176]{1,0:T(8,128)(2,1)S(1)}, u32[]{:S(2)}, u32[]{:S(2)}) collective-permute-start(bf16[32,2176]{1,0:T(8,128)(2,1)S(1)} %get-tuple-element.45), channel_id=1, source_target_pairs={{0,28},{4,24},{8,4},{12,0},{16,12},{20,8},{24,20},{28,16},{1,29},{... | collective-permute-start | bytes 417800 | tf_op jit(solution)/shard_map/ppermute | solution.py:360
  34.3 0.0 collective-permute-done.4.rest_1_
  34.3 0.0 collective-permute-start.9
  34.3 0.0 collective-permute-done.8.refs_2_
  34.3 0.0 collective-permute-done.7.refs_1_
  34.3 4.0 %attention.6 = (bf16[32,2176]{1,0:T(8,128)(2,1)S(1)}, bf16[32,2176]{1,0:T(8,128)(2,1)S(1)}) custom-call(s32[8]{0:T(128)S(1)} %copy-done.8, s32[2,24]{1,0:T(2,128)S(1)} %bitcast.8, s32[2]{0:T(128)S(1)} %bitcast.12, bf16[32,256]{1,0:T(8,128)(2,1)S(1)} %copy-done.3, bf16[32,256]{1,0:T(8,128)(2,1)S(1)} %copy-done.4, bf16[4096,256]{1,0:T(8,128)(2,1)S(1)} %copy-done.2, ...), custom_call_target="tpu_custom_call" | custom-call | flops 3221225472 | bytes 8388608 | tf_op jit(solution)/shard_map/attention/pallas_call | solution.py:216
  38.3 3.0 %collective-permute-start.13 = (bf16[32,2176]{1,0:T(8,128)(2,1)S(1)}, bf16[32,2176]{1,0:T(8,128)(2,1)S(1)}, u32[]{:S(2)}, u32[]{:S(2)}) collective-permute-start(bf16[32,2176]{1,0:T(8,128)(2,1)S(1)} %get-tuple-element.51), channel_id=1, source_target_pairs={{0,20},{4,16},{8,28},{12,24},{16,4},{20,0},{24,12},{28,8},{1,21},{... | collective-permute-start | bytes 417800 | tf_op jit(solution)/shard_map/ppermute | solution.py:360
  41.3 2.0 %collective-permute-start.10 = (bf16[32,2176]{1,0:T(8,128)(2,1)S(1)}, bf16[32,2176]{1,0:T(8,128)(2,1)S(1)}, u32[]{:S(2)}, u32[]{:S(2)}) collective-permute-start(bf16[32,2176]{1,0:T(8,128)(2,1)S(1)} %get-tuple-element.57), channel_id=1, source_target_pairs={{0,4},{4,0},{8,12},{12,8},{16,20},{20,16},{24,28},{28,24},{1,5},{5... | collective-permute-start | bytes 417800 | tf_op jit(solution)/shard_map/ppermute | solution.py:360
  43.3 0.0 copy-done.5
  43.3 2.6 %attention.7.refs_0_ = bf16[32,2176]{1,0:T(8,128)(2,1)S(1)} custom-call(s32[8]{0:T(128)S(1)} %copy-done.8, s32[2,24]{1,0:T(2,128)S(1)} %bitcast.9, s32[2]{0:T(128)S(1)} %bitcast.13, bf16[32,256]{1,0:T(8,128)(2,1)S(1)} %copy-done.3, bf16[32,256]{1,0:T(8,128)(2,1)S(1)} %copy-done.4, bf16[4096,256]{1,0:T(8,128)(2,1)S(1)} %copy-done.2, ...), custom_call_target="tpu_custom_call" | custom-call | flops 1610612736 | bytes 8388608 | tf_op jit(solution)/shard_map/attention/pallas_call | solution.py:216
  45.9 0.0 collective-permute-done.11.refs_5_
  45.9 0.0 collective-permute-done.12.refs_6_
  45.9 2.9 %collective-permute-done.9.refs_3_ = bf16[32,2176]{1,0:T(8,128)(2,1)S(1)} collective-permute-done((bf16[32,2176]{1,0:T(8,128)(2,1)S(1)}, bf16[32,2176]{1,0:T(8,128)(2,1)S(1)}, u32[]{:S(2)}, u32[]{:S(2)}) %collective-permute-start.9) | collective-permute-done | bytes 139296 | tf_op jit(solution)/shard_map/ppermute | solution.py:360
  48.8 0.0 collective-permute-done.10.refs_4_
  48.8 2.5 %collective-permute-done.13.refs_7_ = bf16[32,2176]{1,0:T(8,128)(2,1)S(1)} collective-permute-done((bf16[32,2176]{1,0:T(8,128)(2,1)S(1)}, bf16[32,2176]{1,0:T(8,128)(2,1)S(1)}, u32[]{:S(2)}, u32[]{:S(2)}) %collective-permute-start.13) | collective-permute-done | bytes 139296 | tf_op jit(solution)/shard_map/ppermute | solution.py:360
  51.3 0.9 %merge.1.rest_0_ = bf16[32,2048]{1,0:T(8,128)(2,1)S(1)} custom-call(bf16[32,2176]{1,0:T(8,128)(2,1)S(1)} %attention.7.refs_0_, bf16[32,2176]{1,0:T(8,128)(2,1)S(1)} %collective-permute-done.7.refs_1_, bf16[32,2176]{1,0:T(8,128)(2,1)S(1)} %collective-permute-done.8.refs_2_, bf16[32,2176]{1,0:T(8,128)(2,1)S(1)} %collective-permute-done.9.refs_3_, ...), custom_call_target="tpu_custom_call" | custom-call | flops 1114112 | bytes 1114112 | tf_op jit(solution)/shard_map/merge/pallas_call | solution.py:276
  52.2 0.1 collective-permute-start.15
  52.3 3.8 %collective-permute-start.14 = (bf16[32,2048]{1,0:T(8,128)(2,1)S(1)}, bf16[32,2048]{1,0:T(8,128)(2,1)S(1)}, u32[]{:S(2)}, u32[]{:S(2)}) collective-permute-start(bf16[32,2048]{1,0:T(8,128)(2,1)S(1)} %merge.1.rest_0_), channel_id=1, source_target_pairs={{0,24},{4,28},{8,0},{12,4},{16,8},{20,12},{24,16},{28,20},{1,25},{... | collective-permute-start | bytes 393224 | tf_op jit(solution)/shard_map/ppermute | solution.py:360
  56.1 0.6 collective-permute-start.17
  56.7 0.0 collective-permute-start.16
  56.7 3.9 %collective-permute-done.15.rest_2_ = bf16[32,2048]{1,0:T(8,128)(2,1)S(1)} collective-permute-done((bf16[32,2048]{1,0:T(8,128)(2,1)S(1)}, bf16[32,2048]{1,0:T(8,128)(2,1)S(1)}, u32[]{:S(2)}, u32[]{:S(2)}) %collective-permute-start.15) | collective-permute-done | bytes 131104 | tf_op jit(solution)/shard_map/ppermute | solution.py:360
  60.6 0.6 collective-permute-start.19
  61.2 0.0 collective-permute-done.14.rest_1_
  61.2 1.3 %collective-permute-done.17.rest_4_ = bf16[32,2048]{1,0:T(8,128)(2,1)S(1)} collective-permute-done((bf16[32,2048]{1,0:T(8,128)(2,1)S(1)}, bf16[32,2048]{1,0:T(8,128)(2,1)S(1)}, u32[]{:S(2)}, u32[]{:S(2)}) %collective-permute-start.17) | collective-permute-done | bytes 131104 | tf_op jit(solution)/shard_map/ppermute | solution.py:360
  62.5 0.6 collective-permute-start.18
  63.1 2.5 %collective-permute-done.16.rest_3_ = bf16[32,2048]{1,0:T(8,128)(2,1)S(1)} collective-permute-done((bf16[32,2048]{1,0:T(8,128)(2,1)S(1)}, bf16[32,2048]{1,0:T(8,128)(2,1)S(1)}, u32[]{:S(2)}, u32[]{:S(2)}) %collective-permute-start.16) | collective-permute-done | bytes 131104 | tf_op jit(solution)/shard_map/ppermute | solution.py:360
  65.5 0.0 collective-permute-done.19.rest_6_
  65.6 1.3 %collective-permute-start.20 = (bf16[32,2048]{1,0:T(8,128)(2,1)S(1)}, bf16[32,2048]{1,0:T(8,128)(2,1)S(1)}, u32[]{:S(2)}, u32[]{:S(2)}) collective-permute-start(bf16[32,2048]{1,0:T(8,128)(2,1)S(1)} %collective-permute-done.16.rest_3_), channel_id=1, source_target_pairs={{0,4},{4,0},{8,12},{12,8},{16,20},{20,16},{24,28},{28,24},{1,5},{5... | collective-permute-start | bytes 393224 | tf_op jit(solution)/shard_map/ppermute | solution.py:360
  66.8 0.6 collective-permute-done.18.rest_5_
  67.4 3.1 %collective-permute-done.20.rest_7_ = bf16[32,2048]{1,0:T(8,128)(2,1)S(1)} collective-permute-done((bf16[32,2048]{1,0:T(8,128)(2,1)S(1)}, bf16[32,2048]{1,0:T(8,128)(2,1)S(1)}, u32[]{:S(2)}, u32[]{:S(2)}) %collective-permute-start.20) | collective-permute-done | bytes 131104 | tf_op jit(solution)/shard_map/ppermute | solution.py:360
  70.5 1.4 %projection.1 = (f32[2,64,1024]{2,1,0:T(8,128)S(1)}, bf16[2,64,1024]{2,1,0:T(8,128)(2,1)S(1)}) custom-call(bf16[2048,1024]{1,0:T(8,128)(2,1)S(1)} %copy-done, bf16[32,2048]{1,0:T(8,128)(2,1)S(1)} %merge.1.rest_0_, bf16[32,2048]{1,0:T(8,128)(2,1)S(1)} %collective-permute-done.14.rest_1_, bf16[32,2048]{1,0:T(8,128)(2,1)S(1)} %collective-permute-done.15.rest_2_, ...), custom_call_target="tpu_custom_call" | custom-call | flops 1073741824 | bytes 4194304 | tf_op jit(solution)/shard_map/projection/pallas_call | solution.py:318
  71.9 0.1 collective-permute-start.21
  72.0 1.5 %collective-permute-done.21 = bf16[2,64,1024]{2,1,0:T(8,128)(2,1)S(1)} collective-permute-done((bf16[2,64,1024]{2,1,0:T(8,128)(2,1)S(1)}, bf16[2,64,1024]{2,1,0:T(8,128)(2,1)S(1)}, u32[]{:S(2)}, u32[]{:S(2)}) %collective-permute-start.21) | collective-permute-done | bytes 262176 | tf_op jit(solution)/shard_map/ppermute | solution.py:437
  73.6 1.8 %collective-permute-start.22 = (bf16[64,1024]{1,0:T(8,128)(2,1)S(1)}, bf16[64,1024]{1,0:T(8,128)(2,1)S(1)}, u32[]{:S(2)}, u32[]{:S(2)}) collective-permute-start(bf16[64,1024]{1,0:T(8,128)(2,1)S(1)} %fusion), channel_id=1, source_target_pairs={{0,2},{1,3},{2,0},{3,1},{4,6},{5,7},{6,4},{7,5},{8,10},{9,11},{10,... | collective-permute-start | bytes 393224 | tf_op jit(solution)/shard_map/ppermute | solution.py:441
  75.3 3.8 %collective-permute-done.22 = bf16[64,1024]{1,0:T(8,128)(2,1)S(1)} collective-permute-done((bf16[64,1024]{1,0:T(8,128)(2,1)S(1)}, bf16[64,1024]{1,0:T(8,128)(2,1)S(1)}, u32[]{:S(2)}, u32[]{:S(2)}) %collective-permute-start.22) | collective-permute-done | bytes 131104 | tf_op jit(solution)/shard_map/ppermute | solution.py:441
  79.2 0.7 bitcast_add_fusion
  (11 shorter events, 0.0 us)
Async XLA Ops:
  0.0 14.5 %copy-start.3 = (bf16[32,256]{1,0:T(8,128)(2,1)S(1)}, bf16[32,256]{1,0:T(8,128)(2,1)}, u32[]{:S(2)}) copy-start(bf16[32,256]{1,0:T(8,128)(2,1)} %nk_ref.7) | copy-start | bytes 49156
  0.0 14.5 %copy-start.4 = (bf16[32,256]{1,0:T(8,128)(2,1)S(1)}, bf16[32,256]{1,0:T(8,128)(2,1)}, u32[]{:S(2)}) copy-start(bf16[32,256]{1,0:T(8,128)(2,1)} %nv_ref.7) | copy-start | bytes 49156
  0.0 14.5 %copy-start.2 = (bf16[4096,256]{1,0:T(8,128)(2,1)S(1)}, bf16[4096,256]{1,0:T(8,128)(2,1)}, u32[]{:S(2)}) copy-start(bf16[4096,256]{1,0:T(8,128)(2,1)} %k_ref.7) | copy-start | bytes 6291460
  0.0 14.5 %copy-start.1 = (bf16[4096,256]{1,0:T(8,128)(2,1)S(1)}, bf16[4096,256]{1,0:T(8,128)(2,1)}, u32[]{:S(2)}) copy-start(bf16[4096,256]{1,0:T(8,128)(2,1)} %v_ref.1) | copy-start | bytes 6291460
  0.0 14.5 %copy-start.7 = (s32[1,2,24]{2,1,0:T(2,128)S(1)}, s32[1,2,24]{2,1,0:T(2,128)}, u32[]{:S(2)}) copy-start(s32[1,2,24]{2,1,0:T(2,128)} %param.14) | copy-start | bytes 580
  0.0 14.5 %copy-start.9 = (s32[1,2]{1,0:T(1,128)S(1)}, s32[1,2]{1,0:T(1,128)}, u32[]{:S(2)}) copy-start(s32[1,2]{1,0:T(1,128)} %param.15) | copy-start | bytes 28
  0.0 14.5 %copy-start.8 = (s32[8]{0:T(128)S(1)}, s32[8]{0:T(128)}, u32[]{:S(2)}) copy-start(s32[8]{0:T(128)} %slot_ref.7) | copy-start | bytes 100
  0.0 9.3 %collective-permute-start = (bf16[32,2048]{1,0:T(8,128)(2,1)}, bf16[32,2048]{1,0:T(8,128)(2,1)S(1)}, u32[]{:S(2)}, u32[]{:S(2)}) collective-permute-start(bf16[32,2048]{1,0:T(8,128)(2,1)} %rest_0_), channel_id=1, source_target_pairs={{0,24},{4,28},{8,0},{12,4},{16,8},{20,12},{24,16},{28,20},{1,25},{... | collective-permute-start | bytes 393224 | tf_op jit(solution)/shard_map/ppermute | solution.py:360
  5.2 7.0 %collective-permute-start.1 = (bf16[32,2048]{1,0:T(8,128)(2,1)}, bf16[32,2048]{1,0:T(8,128)(2,1)S(1)}, u32[]{:S(2)}, u32[]{:S(2)}) collective-permute-start(bf16[32,2048]{1,0:T(8,128)(2,1)} %rest_0_), channel_id=1, source_target_pairs={{0,8},{4,12},{8,16},{12,20},{16,24},{20,28},{24,0},{28,4},{1,9},{5... | collective-permute-start | bytes 393224 | tf_op jit(solution)/shard_map/ppermute | solution.py:360
  5.2 24.4 %collective-permute-start.2 = (bf16[32,2048]{1,0:T(8,128)(2,1)}, bf16[32,2048]{1,0:T(8,128)(2,1)S(1)}, u32[]{:S(2)}, u32[]{:S(2)}) collective-permute-start(bf16[32,2048]{1,0:T(8,128)(2,1)} %rest_0_), channel_id=1, source_target_pairs={{0,4},{4,0},{8,12},{12,8},{16,20},{20,16},{24,28},{28,24},{1,5},{5... | collective-permute-start | bytes 393224 | tf_op jit(solution)/shard_map/ppermute | solution.py:360
  12.1 10.0 %collective-permute-start.5 = (bf16[32,2048]{1,0:T(8,128)(2,1)S(1)}, bf16[32,2048]{1,0:T(8,128)(2,1)S(1)}, u32[]{:S(2)}, u32[]{:S(2)}) collective-permute-start(bf16[32,2048]{1,0:T(8,128)(2,1)S(1)} %collective-permute-done.rest_0_), channel_id=1, source_target_pairs={{0,4},{4,0},{8,12},{12,8},{16,20},{20,16},{24,28},{28,24},{1,5},{5... | collective-permute-start | bytes 393224 | tf_op jit(solution)/shard_map/ppermute | solution.py:360
  13.6 8.5 %collective-permute-start.6 = (bf16[32,2048]{1,0:T(8,128)(2,1)S(1)}, bf16[32,2048]{1,0:T(8,128)(2,1)S(1)}, u32[]{:S(2)}, u32[]{:S(2)}) collective-permute-start(bf16[32,2048]{1,0:T(8,128)(2,1)S(1)} %collective-permute-done.1.rest_1_), channel_id=1, source_target_pairs={{0,4},{4,0},{8,12},{12,8},{16,20},{20,16},{24,28},{28,24},{1,5},{5... | collective-permute-start | bytes 393224 | tf_op jit(solution)/shard_map/ppermute | solution.py:360
  14.2 8.0 %collective-permute-start.3 = (bf16[32,2048]{1,0:T(8,128)(2,1)}, bf16[32,2048]{1,0:T(8,128)(2,1)S(1)}, u32[]{:S(2)}, u32[]{:S(2)}) collective-permute-start(bf16[32,2048]{1,0:T(8,128)(2,1)} %rest_0_), channel_id=1, source_target_pairs={{0,16},{4,20},{8,24},{12,28},{16,0},{20,4},{24,8},{28,12},{1,17},{... | collective-permute-start | bytes 393224 | tf_op jit(solution)/shard_map/ppermute | solution.py:360
  18.6 15.7 %collective-permute-start.8 = (bf16[32,2176]{1,0:T(8,128)(2,1)S(1)}, bf16[32,2176]{1,0:T(8,128)(2,1)S(1)}, u32[]{:S(2)}, u32[]{:S(2)}) collective-permute-start(bf16[32,2176]{1,0:T(8,128)(2,1)S(1)} %get-tuple-element.41), channel_id=1, source_target_pairs={{0,24},{4,28},{8,0},{12,4},{16,8},{20,12},{24,16},{28,20},{1,25},{... | collective-permute-start | bytes 417800 | tf_op jit(solution)/shard_map/ppermute | solution.py:360
  22.1 12.2 %collective-permute-start.7 = (bf16[32,2176]{1,0:T(8,128)(2,1)S(1)}, bf16[32,2176]{1,0:T(8,128)(2,1)S(1)}, u32[]{:S(2)}, u32[]{:S(2)}) collective-permute-start(bf16[32,2176]{1,0:T(8,128)(2,1)S(1)} %get-tuple-element.48), channel_id=1, source_target_pairs={{0,8},{4,12},{8,16},{12,20},{16,24},{20,28},{24,0},{28,4},{1,9},{5... | collective-permute-start | bytes 417800 | tf_op jit(solution)/shard_map/ppermute | solution.py:360
  22.1 12.2 %collective-permute-start.4 = (bf16[32,2048]{1,0:T(8,128)(2,1)S(1)}, bf16[32,2048]{1,0:T(8,128)(2,1)S(1)}, u32[]{:S(2)}, u32[]{:S(2)}) collective-permute-start(bf16[32,2048]{1,0:T(8,128)(2,1)S(1)} %collective-permute-done.3.rest_0_), channel_id=1, source_target_pairs={{0,4},{4,0},{8,12},{12,8},{16,20},{20,16},{24,28},{28,24},{1,5},{5... | collective-permute-start | bytes 393224 | tf_op jit(solution)/shard_map/ppermute | solution.py:360
  29.5 16.4 %collective-permute-start.11 = (bf16[32,2176]{1,0:T(8,128)(2,1)S(1)}, bf16[32,2176]{1,0:T(8,128)(2,1)S(1)}, u32[]{:S(2)}, u32[]{:S(2)}) collective-permute-start(bf16[32,2176]{1,0:T(8,128)(2,1)S(1)} %get-tuple-element.58), channel_id=1, source_target_pairs={{0,12},{4,8},{8,20},{12,16},{16,28},{20,24},{24,4},{28,0},{1,13},{... | collective-permute-start | bytes 417800 | tf_op jit(solution)/shard_map/ppermute | solution.py:360
  29.6 16.3 %collective-permute-start.12 = (bf16[32,2176]{1,0:T(8,128)(2,1)S(1)}, bf16[32,2176]{1,0:T(8,128)(2,1)S(1)}, u32[]{:S(2)}, u32[]{:S(2)}) collective-permute-start(bf16[32,2176]{1,0:T(8,128)(2,1)S(1)} %get-tuple-element.45), channel_id=1, source_target_pairs={{0,28},{4,24},{8,4},{12,0},{16,12},{20,8},{24,20},{28,16},{1,29},{... | collective-permute-start | bytes 417800 | tf_op jit(solution)/shard_map/ppermute | solution.py:360
  34.3 9.0 %copy-start.5 = (f32[8,128]{1,0:T(8,128)S(1)}, f32[8,128]{1,0:T(8,128)}, u32[]{:S(2)}) copy-start(f32[8,128]{1,0:T(8,128)} %settle.1.rest_1_) | copy-start | bytes 12292
  34.3 9.0 %copy-start.6 = (bf16[32,2048]{1,0:T(8,128)(2,1)S(1)}, bf16[32,2048]{1,0:T(8,128)(2,1)}, u32[]{:S(2)}) copy-start(bf16[32,2048]{1,0:T(8,128)(2,1)} %rest_0_) | copy-start | bytes 393220
  34.3 14.5 %collective-permute-start.9 = (bf16[32,2176]{1,0:T(8,128)(2,1)S(1)}, bf16[32,2176]{1,0:T(8,128)(2,1)S(1)}, u32[]{:S(2)}, u32[]{:S(2)}) collective-permute-start(bf16[32,2176]{1,0:T(8,128)(2,1)S(1)} %get-tuple-element.56), channel_id=1, source_target_pairs={{0,16},{4,20},{8,24},{12,28},{16,0},{20,4},{24,8},{28,12},{1,17},{... | collective-permute-start | bytes 417800 | tf_op jit(solution)/shard_map/ppermute | solution.py:360
  38.3 13.0 %collective-permute-start.13 = (bf16[32,2176]{1,0:T(8,128)(2,1)S(1)}, bf16[32,2176]{1,0:T(8,128)(2,1)S(1)}, u32[]{:S(2)}, u32[]{:S(2)}) collective-permute-start(bf16[32,2176]{1,0:T(8,128)(2,1)S(1)} %get-tuple-element.51), channel_id=1, source_target_pairs={{0,20},{4,16},{8,28},{12,24},{16,4},{20,0},{24,12},{28,8},{1,21},{... | collective-permute-start | bytes 417800 | tf_op jit(solution)/shard_map/ppermute | solution.py:360
  41.3 7.5 %collective-permute-start.10 = (bf16[32,2176]{1,0:T(8,128)(2,1)S(1)}, bf16[32,2176]{1,0:T(8,128)(2,1)S(1)}, u32[]{:S(2)}, u32[]{:S(2)}) collective-permute-start(bf16[32,2176]{1,0:T(8,128)(2,1)S(1)} %get-tuple-element.57), channel_id=1, source_target_pairs={{0,4},{4,0},{8,12},{12,8},{16,20},{20,16},{24,28},{28,24},{1,5},{5... | collective-permute-start | bytes 417800 | tf_op jit(solution)/shard_map/ppermute | solution.py:360
  43.3 27.2 %copy-start = (bf16[2048,1024]{1,0:T(8,128)(2,1)S(1)}, bf16[2048,1024]{1,0:T(8,128)(2,1)}, u32[]{:S(2)}) copy-start(bf16[2048,1024]{1,0:T(8,128)(2,1)} %w_ref.1) | copy-start | bytes 12582916
  52.2 8.4 %collective-permute-start.15 = (bf16[32,2048]{1,0:T(8,128)(2,1)S(1)}, bf16[32,2048]{1,0:T(8,128)(2,1)S(1)}, u32[]{:S(2)}, u32[]{:S(2)}) collective-permute-start(bf16[32,2048]{1,0:T(8,128)(2,1)S(1)} %merge.1.rest_0_), channel_id=1, source_target_pairs={{0,8},{4,12},{8,16},{12,20},{16,24},{20,28},{24,0},{28,4},{1,9},{5... | collective-permute-start | bytes 393224 | tf_op jit(solution)/shard_map/ppermute | solution.py:360
  52.3 8.9 %collective-permute-start.14 = (bf16[32,2048]{1,0:T(8,128)(2,1)S(1)}, bf16[32,2048]{1,0:T(8,128)(2,1)S(1)}, u32[]{:S(2)}, u32[]{:S(2)}) collective-permute-start(bf16[32,2048]{1,0:T(8,128)(2,1)S(1)} %merge.1.rest_0_), channel_id=1, source_target_pairs={{0,24},{4,28},{8,0},{12,4},{16,8},{20,12},{24,16},{28,20},{1,25},{... | collective-permute-start | bytes 393224 | tf_op jit(solution)/shard_map/ppermute | solution.py:360
  56.1 6.4 %collective-permute-start.17 = (bf16[32,2048]{1,0:T(8,128)(2,1)S(1)}, bf16[32,2048]{1,0:T(8,128)(2,1)S(1)}, u32[]{:S(2)}, u32[]{:S(2)}) collective-permute-start(bf16[32,2048]{1,0:T(8,128)(2,1)S(1)} %merge.1.rest_0_), channel_id=1, source_target_pairs={{0,4},{4,0},{8,12},{12,8},{16,20},{20,16},{24,28},{28,24},{1,5},{5... | collective-permute-start | bytes 393224 | tf_op jit(solution)/shard_map/ppermute | solution.py:360
  56.7 8.8 %collective-permute-start.16 = (bf16[32,2048]{1,0:T(8,128)(2,1)S(1)}, bf16[32,2048]{1,0:T(8,128)(2,1)S(1)}, u32[]{:S(2)}, u32[]{:S(2)}) collective-permute-start(bf16[32,2048]{1,0:T(8,128)(2,1)S(1)} %merge.1.rest_0_), channel_id=1, source_target_pairs={{0,16},{4,20},{8,24},{12,28},{16,0},{20,4},{24,8},{28,12},{1,17},{... | collective-permute-start | bytes 393224 | tf_op jit(solution)/shard_map/ppermute | solution.py:360
  60.6 5.0 %collective-permute-start.19 = (bf16[32,2048]{1,0:T(8,128)(2,1)S(1)}, bf16[32,2048]{1,0:T(8,128)(2,1)S(1)}, u32[]{:S(2)}, u32[]{:S(2)}) collective-permute-start(bf16[32,2048]{1,0:T(8,128)(2,1)S(1)} %collective-permute-done.15.rest_2_), channel_id=1, source_target_pairs={{0,4},{4,0},{8,12},{12,8},{16,20},{20,16},{24,28},{28,24},{1,5},{5... | collective-permute-start | bytes 393224 | tf_op jit(solution)/shard_map/ppermute | solution.py:360
  62.5 5.0 %collective-permute-start.18 = (bf16[32,2048]{1,0:T(8,128)(2,1)S(1)}, bf16[32,2048]{1,0:T(8,128)(2,1)S(1)}, u32[]{:S(2)}, u32[]{:S(2)}) collective-permute-start(bf16[32,2048]{1,0:T(8,128)(2,1)S(1)} %collective-permute-done.14.rest_1_), channel_id=1, source_target_pairs={{0,4},{4,0},{8,12},{12,8},{16,20},{20,16},{24,28},{28,24},{1,5},{5... | collective-permute-start | bytes 393224 | tf_op jit(solution)/shard_map/ppermute | solution.py:360
  65.6 5.0 %collective-permute-start.20 = (bf16[32,2048]{1,0:T(8,128)(2,1)S(1)}, bf16[32,2048]{1,0:T(8,128)(2,1)S(1)}, u32[]{:S(2)}, u32[]{:S(2)}) collective-permute-start(bf16[32,2048]{1,0:T(8,128)(2,1)S(1)} %collective-permute-done.16.rest_3_), channel_id=1, source_target_pairs={{0,4},{4,0},{8,12},{12,8},{16,20},{20,16},{24,28},{28,24},{1,5},{5... | collective-permute-start | bytes 393224 | tf_op jit(solution)/shard_map/ppermute | solution.py:360
  71.9 1.6 %collective-permute-start.21 = (bf16[2,64,1024]{2,1,0:T(8,128)(2,1)S(1)}, bf16[2,64,1024]{2,1,0:T(8,128)(2,1)S(1)}, u32[]{:S(2)}, u32[]{:S(2)}) collective-permute-start(bf16[2,64,1024]{2,1,0:T(8,128)(2,1)S(1)} %get-tuple-element.64), channel_id=1, source_target_pairs={{0,1},{1,0},{2,3},{3,2},{4,5},{5,4},{6,7},{7,6},{8,9},{9,8},{10,11... | collective-permute-start | bytes 786440 | tf_op jit(solution)/shard_map/ppermute | solution.py:437
  73.6 5.6 %collective-permute-start.22 = (bf16[64,1024]{1,0:T(8,128)(2,1)S(1)}, bf16[64,1024]{1,0:T(8,128)(2,1)S(1)}, u32[]{:S(2)}, u32[]{:S(2)}) collective-permute-start(bf16[64,1024]{1,0:T(8,128)(2,1)S(1)} %fusion), channel_id=1, source_target_pairs={{0,2},{1,3},{2,0},{3,1},{4,6},{5,7},{6,4},{7,5},{8,10},{9,11},{10,... | collective-permute-start | bytes 393224 | tf_op jit(solution)/shard_map/ppermute | solution.py:441
